TPU v7x, 128 devices: a whole 4x4x4 slice. The times are simulated.
128 devices in a mesh: fsdp: 4 (over z), ctx: 8 (over y, x_hi), tp: 4 (over x_lo, core).
Axes of the slice: x: 4 (x_hi: 2, x_lo: 2; x = x_hi * 2 + x_lo), y: 4, z: 4, core: 2. Of those that a mesh axis runs over, the one named last changes fastest.
Arguments:
- inputs: bfloat16 [8192, 1024], P(('fsdp', 'ctx')), may hold values from -6 to 6
- cotangent: bfloat16 [8192, 1024], P(('fsdp', 'ctx')), may hold values from -6 to 6
- lengths: int32 [4, 4], P('fsdp'), may hold values from 1 to 2048, as said below
- expert_ids: int32 [8192, 8], P(('fsdp', 'ctx')), may hold values from 0 to 31, all different within a row; in each aligned block of 256 rows (0 to 255, 256 to 511, ...) at most 128 rows name the same one
- attn_gain: bfloat16 [1024], P('fsdp'), may hold values from 0.5 to 1.5
- w_query: bfloat16 [1024, 1024], P('fsdp', 'tp'), may hold values from -0.1875 to 0.1875
- key_weight: bfloat16 [1024, 512], P('fsdp', 'tp'), may hold values from -0.1875 to 0.1875
- value_weight: bfloat16 [1024, 512], P('fsdp', 'tp'), may hold values from -0.1875 to 0.1875
- w_output: bfloat16 [1024, 1024], P('fsdp', 'tp'), may hold values from -2 to 2
- ffn_gain: bfloat16 [1024], P('fsdp'), may hold values from 0.5 to 1.5
- w_router: bfloat16 [1024, 32], P('fsdp'), may hold values from -0.09375 to 0.09375
- w_gate: bfloat16 [1024, 32, 512], P('fsdp', None, 'tp'), may hold values from -0.1875 to 0.1875
- w_up: bfloat16 [1024, 32, 512], P('fsdp', None, 'tp'), may hold values from -0.1875 to 0.1875
- w_down: bfloat16 [1024, 32, 512], P('fsdp', None, 'tp'), may hold values from -4 to 4
Outputs:
- output: bfloat16 [8192, 1024], P(('fsdp', 'ctx'))
- input_grad: bfloat16 [8192, 1024], P(('fsdp', 'ctx'))
- grad_attn_gain: float32 [1024], P('fsdp')
- grad_query: float32 [1024, 1024], P('fsdp', 'tp')
- grad_key: float32 [1024, 512], P('fsdp', 'tp')
- grad_value: float32 [1024, 512], P('fsdp', 'tp')
- grad_output: float32 [1024, 1024], P('fsdp', 'tp')
- grad_ffn_gain: float32 [1024], P('fsdp')
- grad_router: float32 [1024, 32], P('fsdp')
- grad_gate: float32 [1024, 32, 512], P('fsdp', None, 'tp')
- grad_up: float32 [1024, 32, 512], P('fsdp', None, 'tp')
- grad_down: float32 [1024, 32, 512], P('fsdp', None, 'tp')
Inputs may be any that keep to these rules, and one draw needn't show every extreme that they name: Each row's 4 lengths sum to 2048. `expert_ids`: each row names 8 different experts; the rows of one device name no expert more than 128 times, and in some device's rows one expert is named exactly 128 times.
All inputs are finite; a program needn't handle non-finite values.
Results may differ from a plain program's by a relative error of at most 0.03.
Values may be sent and summed in bfloat16 or wider, within the bound.
A program may use at most 192 MiB of HBM per device.

v0:
```python
import math

import jax
import jax.numpy as jnp
from jax import lax
from jax.sharding import PartitionSpec as P

HEAD_SIZE = 64


norm_eps = 1e-06
rope_base = 10000.0
branch_scale = 0.22
highest = lax.Precision.HIGHEST


def doc_places(lengths_row, rows_global):
    seq_ends = jnp.cumsum(lengths_row)
    passed = (rows_global[:, None] >= seq_ends[None, :]).astype(jnp.int32)
    docs = jnp.sum(passed, axis=1)
    starts = jnp.sum(passed * lengths_row[None, :], axis=1)
    return (docs, rows_global - starts)


def rope_tables(places):
    frequencies = jnp.exp(
        jnp.arange(HEAD_SIZE // 2, dtype=jnp.float32) * (-2.0 * math.log(rope_base) / HEAD_SIZE)
    )
    angles = places.astype(jnp.float32)[:, None] * frequencies[None, :]
    return (jnp.cos(angles)[:, None, :], jnp.sin(angles)[:, None, :])


def apply_rotary(values, cosine_table, sine_table):
    row_count = values.shape[0]
    head_view = values.reshape(row_count, -1, HEAD_SIZE)
    first_half = head_view[..., : HEAD_SIZE // 2]
    second_half = head_view[..., HEAD_SIZE // 2 :]
    turned = jnp.concatenate(
        [
            first_half * cosine_table - second_half * sine_table,
            second_half * cosine_table + first_half * sine_table,
        ],
        axis=-1,
    )
    return turned.reshape(row_count, -1)


def rotate_back(gradient, cosine_table, sine_table):
    row_count = gradient.shape[0]
    head_view = gradient.reshape(row_count, -1, HEAD_SIZE)
    first_half = head_view[..., : HEAD_SIZE // 2]
    second_half = head_view[..., HEAD_SIZE // 2 :]
    turned = jnp.concatenate(
        [
            first_half * cosine_table + second_half * sine_table,
            second_half * cosine_table - first_half * sine_table,
        ],
        axis=-1,
    )
    return turned.reshape(row_count, -1)


def reduce_grads(gain_part, first_part, second_part, third_part, fourth_part):
    gain_part, first_part, second_part, third_part, fourth_part = (
        lax.psum_scatter(
            gain_part.astype(jnp.bfloat16), ("fsdp", "ctx"), scatter_dimension=0, tiled=True
        ).astype(jnp.float32),
        lax.psum_scatter(
            first_part.astype(jnp.bfloat16), ("fsdp", "ctx"), scatter_dimension=0, tiled=True
        ).astype(jnp.float32),
        lax.psum_scatter(
            second_part.astype(jnp.bfloat16), ("fsdp", "ctx"), scatter_dimension=0, tiled=True
        ).astype(jnp.float32),
        lax.psum_scatter(
            third_part.astype(jnp.bfloat16), ("fsdp", "ctx"), scatter_dimension=0, tiled=True
        ).astype(jnp.float32),
        lax.psum_scatter(
            fourth_part.astype(jnp.bfloat16), ("fsdp", "ctx"), scatter_dimension=0, tiled=True
        ).astype(jnp.float32),
    )
    return (
        lax.all_gather(gain_part.astype(jnp.bfloat16), "ctx", axis=0, tiled=True).astype(
            gain_part.dtype
        ),
        lax.all_gather(first_part.astype(jnp.bfloat16), "ctx", axis=0, tiled=True).astype(
            first_part.dtype
        ),
        lax.all_gather(second_part.astype(jnp.bfloat16), "ctx", axis=0, tiled=True).astype(
            second_part.dtype
        ),
        lax.all_gather(third_part.astype(jnp.bfloat16), "ctx", axis=0, tiled=True).astype(
            third_part.dtype
        ),
        lax.all_gather(fourth_part.astype(jnp.bfloat16), "ctx", axis=0, tiled=True).astype(
            fourth_part.dtype
        ),
    )


def contract_rows(left, right, precision=None):
    return lax.dot_general(
        left,
        right,
        (((0,), (0,)), ((), ())),
        precision=precision,
        preferred_element_type=jnp.float32,
    )


def contract_cols(left, right, precision=None):
    return lax.dot_general(
        left,
        right,
        (((1,), (1,)), ((), ())),
        precision=precision,
        preferred_element_type=jnp.float32,
    )


def local(
    inputs,
    cotangent,
    lengths,
    expert_ids,
    attn_gain,
    w_query,
    key_weight,
    value_weight,
    w_output,
    ffn_gain,
    w_router,
    w_gate,
    w_up,
    w_down,
):
    local_rows = inputs.shape[0]
    gain_one, query_w, key_w, value_w, output_w = (
        lax.all_gather(attn_gain, "fsdp", axis=0, tiled=True),
        lax.all_gather(w_query, "fsdp", axis=0, tiled=True),
        lax.all_gather(key_weight, "fsdp", axis=0, tiled=True),
        lax.all_gather(value_weight, "fsdp", axis=0, tiled=True),
        lax.all_gather(w_output, "fsdp", axis=0, tiled=True),
    )
    lengths_row = lengths[0]
    query_rows = lax.axis_index("ctx") * local_rows + jnp.arange(local_rows, dtype=jnp.int32)
    query_docs, query_places = doc_places(lengths_row, query_rows)
    cosine_table, sine_table = rope_tables(query_places)
    hidden_in = inputs.astype(jnp.float32)
    scale_one = lax.rsqrt(jnp.mean(hidden_in * hidden_in, axis=-1, keepdims=True) + norm_eps)
    normed_one = (hidden_in * scale_one * gain_one.astype(jnp.float32)).astype(jnp.bfloat16)
    query_pre = jnp.dot(normed_one, query_w, preferred_element_type=jnp.float32)
    key_unrotated = jnp.dot(normed_one, key_w, preferred_element_type=jnp.float32)
    value_projected = jnp.dot(normed_one, value_w, preferred_element_type=jnp.float32)
    queries = apply_rotary(query_pre, cosine_table, sine_table).astype(jnp.bfloat16)
    keys_local = apply_rotary(key_unrotated, cosine_table, sine_table).astype(jnp.bfloat16)
    pairs_local = jnp.concatenate([keys_local, value_projected.astype(jnp.bfloat16)], axis=1)
    pairs_all = lax.all_gather(pairs_local, "ctx", axis=0, tiled=True)
    pair_width = keys_local.shape[1]
    total_rows = pairs_all.shape[0]
    key_rows = jnp.arange(total_rows, dtype=jnp.int32)
    key_docs, key_places = doc_places(lengths_row, key_rows)
    key_heads = pair_width // HEAD_SIZE
    groups = queries.shape[1] // pair_width
    keys_all = pairs_all[:, :pair_width].reshape(total_rows, key_heads, HEAD_SIZE)
    values_all = pairs_all[:, pair_width:].reshape(total_rows, key_heads, HEAD_SIZE)
    query_head_rows = queries.reshape(local_rows, key_heads, groups, HEAD_SIZE)
    allowed = (query_docs[:, None] == key_docs[None, :]) & (
        key_rows[None, :] <= query_rows[:, None]
    )

    def masked_scores():
        raw_scores = jnp.einsum(
            "rkgd,skd->kgrs", query_head_rows, keys_all, preferred_element_type=jnp.float32
        )
        return jnp.where(allowed, raw_scores * HEAD_SIZE ** (-0.5), -1e30)

    masked = masked_scores()
    row_top = jnp.max(masked, axis=-1, keepdims=True)
    shifted_exp = jnp.exp(masked - row_top)
    row_total = jnp.sum(shifted_exp, axis=-1, keepdims=True)
    attn_probs = shifted_exp / row_total
    log_total = row_top + jnp.log(row_total)
    attended = jnp.einsum(
        "kgrs,skd->rkgd",
        attn_probs.astype(jnp.bfloat16),
        values_all,
        preferred_element_type=jnp.float32,
    )
    attended = attended.reshape(local_rows, -1).astype(jnp.bfloat16)
    attn_part = contract_cols(attended, output_w)
    attn_out = lax.psum(attn_part.astype(jnp.bfloat16), "tp").astype(jnp.float32)
    residual = hidden_in + branch_scale * attn_out
    expert_count = w_router.shape[1]
    gain_two, router_w, gate_w, up_w, down_w = (
        lax.all_gather(ffn_gain, "fsdp", axis=0, tiled=True),
        lax.all_gather(w_router, "fsdp", axis=0, tiled=True),
        lax.all_gather(w_gate, "fsdp", axis=0, tiled=True),
        lax.all_gather(w_up, "fsdp", axis=0, tiled=True),
        lax.all_gather(w_down, "fsdp", axis=0, tiled=True),
    )
    scale_two = lax.rsqrt(jnp.mean(residual * residual, axis=-1, keepdims=True) + norm_eps)
    normed_two = (residual * scale_two * gain_two.astype(jnp.float32)).astype(jnp.bfloat16)
    logits = jnp.dot(normed_two, router_w, preferred_element_type=jnp.float32)
    chosen = jnp.any(
        expert_ids[:, :, None] == jnp.arange(expert_count, dtype=jnp.int32)[None, None, :], axis=1
    )
    route_masked = jnp.where(chosen, logits, -1e30)
    route_exp = jnp.exp(route_masked - jnp.max(route_masked, axis=-1, keepdims=True))
    gate_probs = route_exp / jnp.sum(route_exp, axis=-1, keepdims=True)
    out_grad = cotangent.astype(jnp.float32)
    branch_grad = branch_scale * out_grad
    gate_pre = jnp.einsum("rd,def->ref", normed_two, gate_w, preferred_element_type=jnp.float32)
    up_pre = jnp.einsum("rd,def->ref", normed_two, up_w, preferred_element_type=jnp.float32)
    sigmoid_gate = jax.nn.sigmoid(gate_pre)
    silu_gate = gate_pre * sigmoid_gate
    activation = (silu_gate * up_pre).astype(jnp.bfloat16)
    expert_block = 8
    block_count = expert_count // expert_block

    def expert_block_out(block_index):
        first_expert = block_index * expert_block
        block_acts = lax.dynamic_slice_in_dim(activation, first_expert, expert_block, 1)
        block_weights = lax.dynamic_slice_in_dim(down_w, first_expert, expert_block, 1)
        block_gates = lax.dynamic_slice_in_dim(gate_probs, first_expert, expert_block, 1)
        outputs = jnp.einsum(
            "ref,def->red", block_acts, block_weights, preferred_element_type=jnp.float32
        )
        return (
            jnp.sum(block_gates[:, :, None] * outputs, axis=1),
            jnp.sum(outputs * branch_grad[:, None, :], axis=2),
        )

    mixed_parts, gate_grad_parts = lax.map(
        expert_block_out, jnp.arange(block_count, dtype=jnp.int32)
    )
    sum_part = jnp.sum(mixed_parts, axis=0)
    gate_grad_part = jnp.transpose(gate_grad_parts, (1, 0, 2)).reshape(local_rows, expert_count)
    down_in = (gate_probs[:, :, None] * branch_grad[:, None, :]).astype(jnp.bfloat16)
    act_grad = jnp.einsum("red,def->ref", down_in, down_w, preferred_element_type=jnp.float32)
    grad_down = jnp.einsum("red,ref->def", down_in, activation, preferred_element_type=jnp.float32)
    gate_in = (act_grad * up_pre * sigmoid_gate * (1.0 + gate_pre * (1.0 - sigmoid_gate))).astype(
        jnp.bfloat16
    )
    up_in = (act_grad * silu_gate).astype(jnp.bfloat16)
    normed_grad_part = jnp.einsum(
        "ref,def->rd", gate_in, gate_w, preferred_element_type=jnp.float32
    ) + jnp.einsum("ref,def->rd", up_in, up_w, preferred_element_type=jnp.float32)
    grad_gate = jnp.einsum("rd,ref->def", normed_two, gate_in, preferred_element_type=jnp.float32)
    grad_up = jnp.einsum("rd,ref->def", normed_two, up_in, preferred_element_type=jnp.float32)
    expert_sum, gate_grads, normed_grad_sum = (
        lax.psum(sum_part.astype(jnp.bfloat16), "tp").astype(jnp.float32),
        lax.psum(gate_grad_part.astype(jnp.bfloat16), "tp").astype(jnp.float32),
        lax.psum(normed_grad_part.astype(jnp.bfloat16), "tp").astype(jnp.float32),
    )
    output = residual + branch_scale * expert_sum
    route_grad = gate_probs * (
        gate_grads - jnp.sum(gate_probs * gate_grads, axis=-1, keepdims=True)
    )
    grad_router = contract_rows(normed_two.astype(jnp.float32), route_grad, highest)
    router_back = contract_cols(route_grad, router_w.astype(jnp.float32), highest)
    normed_grad = normed_grad_sum + router_back
    weighted_two = normed_grad * gain_two.astype(jnp.float32)
    grad_ffn_gain = jnp.sum(normed_grad * residual * scale_two, axis=0)
    residual_grad = (
        out_grad
        + scale_two * weighted_two
        - residual * scale_two**3 * jnp.mean(weighted_two * residual, axis=-1, keepdims=True)
    )
    moe_gain, moe_router, moe_gate, moe_up, moe_down = reduce_grads(
        grad_ffn_gain, grad_router, grad_gate, grad_up, grad_down
    )
    attn_in = (branch_scale * residual_grad).astype(jnp.bfloat16)
    grad_output = contract_rows(attn_in, attended)
    attended_grad = jnp.dot(attn_in, output_w, preferred_element_type=jnp.float32).astype(
        jnp.bfloat16
    )
    grad_heads = attended_grad.reshape(local_rows, key_heads, groups, HEAD_SIZE)
    attn_probs = jnp.exp(masked_scores() - log_total)
    value_grad_all = jnp.einsum(
        "kgrs,rkgd->skd",
        attn_probs.astype(jnp.bfloat16),
        grad_heads,
        preferred_element_type=jnp.float32,
    )
    prob_grad = jnp.einsum(
        "rkgd,skd->kgrs", grad_heads, values_all, preferred_element_type=jnp.float32
    )
    score_grad = (
        attn_probs * (prob_grad - jnp.sum(attn_probs * prob_grad, axis=-1, keepdims=True))
    ).astype(jnp.bfloat16)
    query_grad_rot = jnp.einsum(
        "kgrs,skd->rkgd", score_grad, keys_all, preferred_element_type=jnp.float32
    ).reshape(local_rows, -1) * HEAD_SIZE ** (-0.5)
    key_grad_all = jnp.einsum(
        "kgrs,rkgd->skd", score_grad, query_head_rows, preferred_element_type=jnp.float32
    ) * HEAD_SIZE ** (-0.5)
    pair_grads = jnp.concatenate(
        [
            key_grad_all.reshape(total_rows, pair_width),
            value_grad_all.reshape(total_rows, pair_width),
        ],
        axis=1,
    )
    pair_owned = lax.psum_scatter(
        pair_grads.astype(jnp.bfloat16), "ctx", scatter_dimension=0, tiled=True
    ).astype(jnp.float32)
    key_grad = rotate_back(pair_owned[:, :pair_width], cosine_table, sine_table).astype(
        jnp.bfloat16
    )
    value_grad = pair_owned[:, pair_width:].astype(jnp.bfloat16)
    query_grad = rotate_back(query_grad_rot, cosine_table, sine_table).astype(jnp.bfloat16)
    normed_one_part = (
        contract_cols(query_grad, query_w)
        + contract_cols(key_grad, key_w)
        + contract_cols(value_grad, value_w)
    )
    grad_query = contract_rows(normed_one, query_grad)
    grad_key = contract_rows(normed_one, key_grad)
    grad_value = contract_rows(normed_one, value_grad)
    normed_one_grad = lax.psum(normed_one_part.astype(jnp.bfloat16), "tp").astype(jnp.float32)
    weighted_one = normed_one_grad * gain_one.astype(jnp.float32)
    grad_attn_gain = jnp.sum(normed_one_grad * hidden_in * scale_one, axis=0)
    input_grad = (
        residual_grad
        + scale_one * weighted_one
        - hidden_in * scale_one**3 * jnp.mean(weighted_one * hidden_in, axis=-1, keepdims=True)
    )
    attn_gain_sum, attn_query, attn_key, attn_value, attn_output = reduce_grads(
        grad_attn_gain, grad_query, grad_key, grad_value, grad_output
    )
    return (
        output.astype(jnp.bfloat16),
        input_grad.astype(jnp.bfloat16),
        attn_gain_sum,
        attn_query,
        attn_key,
        attn_value,
        attn_output,
        moe_gain,
        moe_router,
        moe_gate,
        moe_up,
        moe_down,
    )


def solution(mesh):
    return jax.shard_map(
        local,
        mesh=mesh,
        in_specs=(
            P(("fsdp", "ctx"), None),
            P(("fsdp", "ctx"), None),
            P("fsdp", None),
            P(("fsdp", "ctx"), None),
            P("fsdp"),
            P("fsdp", "tp"),
            P("fsdp", "tp"),
            P("fsdp", "tp"),
            P("fsdp", "tp"),
            P("fsdp"),
            P("fsdp", None),
            P("fsdp", None, "tp"),
            P("fsdp", None, "tp"),
            P("fsdp", None, "tp"),
        ),
        out_specs=(
            P(("fsdp", "ctx"), None),
            P(("fsdp", "ctx"), None),
            P("fsdp"),
            P("fsdp", "tp"),
            P("fsdp", "tp"),
            P("fsdp", "tp"),
            P("fsdp", "tp"),
            P("fsdp"),
            P("fsdp", None),
            P("fsdp", None, "tp"),
            P("fsdp", None, "tp"),
            P("fsdp", None, "tp"),
        ),
        check_vma=False,
    )
```

profile of v0, /device:TPU:1, one launch (start us, length us, event | category | flops | bytes accessed | tf_op | source)
XLA Modules:
  0.0 2286.0 jit_solution(1724778251910976230)
XLA Ops:
  8.1 12.7 all_gather.65
  21.4 6.8 all-gather
  30.1 9.6 all_gather.64
  45.4 9.9 all_gather.67
  56.1 11.0 all_gather.68
  67.6 30.0 %all-gather.10.cloned.1.call-done = bf16[2048,256]{0,1:T(8,128)(2,1)} async-done(((bf16[256,256]{0,1:T(8,128)(2,1)}), bf16[2048,256]{0,1:T(8,128)(2,1)}) %all-gather.10.cloned.1.call-update) | async-done | bytes 1048592 | tf_op jit(solution)/shard_map/all_gather | solution.py:157
  109.3 3.9 copy.76
  115.5 7.9 all-gather.1
  126.0 10.6 all_gather.70
  137.2 7.9 all-reduce.11.cloned.1.call-done
  149.2 43.3 %all-gather.14.cloned.1.call-done = bf16[1024,32,128]{2,0,1:T(8,128)(2,1)} async-done(((bf16[256,32,128]{2,0,1:T(8,128)(2,1)}), bf16[1024,32,128]{2,0,1:T(8,128)(2,1)}) %all-gather.14.cloned.1.call-update) | async-done | bytes 8388624 | tf_op jit(solution)/shard_map/all_gather | solution.py:197
  192.5 7.7 fusion.56
  200.3 78.4 %all-gather.12.cloned.1.call-done = bf16[1024,32,128]{2,0,1:T(8,128)(2,1)} async-done(((bf16[256,32,128]{2,0,1:T(8,128)(2,1)}), bf16[1024,32,128]{2,0,1:T(8,128)(2,1)}) %all-gather.12.cloned.1.call-update) | async-done | bytes 8388624 | tf_op jit(solution)/shard_map/all_gather | solution.py:199
  278.6 8.3 fusion.7
  287.0 77.2 %all-gather.16.cloned.1.call-done = bf16[1024,32,128]{2,0,1:T(8,128)(2,1)} async-done(((bf16[256,32,128]{2,0,1:T(8,128)(2,1)}), bf16[1024,32,128]{2,0,1:T(8,128)(2,1)}) %all-gather.16.cloned.1.call-update) | async-done | bytes 8388624 | tf_op jit(solution)/shard_map/all_gather | solution.py:198
  364.2 10.6 fusion.21
  377.2 6.6 fusion.37
  384.3 24.2 %while.12 = (s32[]{:T(128)}, f32[4,256,1024]{1,2,0:T(8,128)}, bf16[4,256,8]{1,2,0:T(8,128)(2,1)}, s32[4]{0:T(128)S(1)}, f32[256,32]{0,1:T(8,128)S(1)}, /*index=5...) while((s32[]{:T(128)}, f32[4,256,1024]{1,2,0:T(8,128)}, ...), condition=%wide.region_15.16_spmd, body=%wide.region_12.15_spmd.sunk | while | flops 544995328 | bytes 6853827 | solution.py:233
  385.6 3.1 fusion.125
  391.6 3.1 fusion.125
  397.7 3.2 fusion.125
  408.5 10.9 psum.38
  427.7 5.0 fusion.31
  441.0 7.3 convolution_convert_fusion.1
  448.5 7.2 convolution_convert_fusion
  455.8 7.3 convert_bitcast_fusion
  463.1 12.5 copy.87
  483.5 27.8 %reduce-scatter.10.cloned.1.call-done = bf16[256,256]{0,1:T(8,128)(2,1)} async-done(((bf16[2048,256]{0,1:T(8,128)(2,1)}), bf16[256,256]{0,1:T(8,128)(2,1)}) %reduce-scatter.10.cloned.1.call-update) | async-done | bytes 131088 | tf_op jit(solution)/shard_map/reduce_scatter | solution.py:304
  525.2 182.3 %reduce-scatter.22.cloned.1.call-done = bf16[32,32,128]{2,0,1:T(8,128)(2,1)} async-done(((bf16[1024,32,128]{2,0,1:T(8,128)(2,1)}), bf16[32,32,128]{2,0,1:T(8,128)(2,1)}) %reduce-scatter.22.cloned.1.call-update) | async-done | bytes 262160 | tf_op jit(solution)/shard_map/reduce_scatter | solution.py:71
  707.6 214.1 %reduce-scatter.24.cloned.1.call-done = bf16[32,32,128]{2,0,1:T(8,128)(2,1)} async-done(((bf16[1024,32,128]{2,0,1:T(8,128)(2,1)}), bf16[32,32,128]{2,0,1:T(8,128)(2,1)}) %reduce-scatter.24.cloned.1.call-update) | async-done | bytes 262160 | tf_op jit(solution)/shard_map/reduce_scatter | solution.py:74
  921.9 214.8 %reduce-scatter.26.cloned.1.call-done = bf16[32,32,128]{2,1,0:T(8,128)(2,1)} async-done(((bf16[1024,32,128]{2,1,0:T(8,128)(2,1)}), bf16[32,32,128]{2,1,0:T(8,128)(2,1)}) %reduce-scatter.26.cloned.1.call-update) | async-done | bytes 262160 | tf_op jit(solution)/shard_map/reduce_scatter | solution.py:77
  1139.2 178.2 %reduce-scatter.20.cloned.1.call-done = bf16[32,32]{1,0:T(8,128)(2,1)} async-done(((bf16[1024,32]{1,0:T(8,128)(2,1)}), bf16[32,32]{1,0:T(8,128)(2,1)}) %reduce-scatter.20.cloned.1.call-update) | async-done | bytes 2064 | tf_op jit(solution)/shard_map/reduce_scatter | solution.py:68
  1317.4 28.5 %all_gather.80 = bf16[256,32]{1,0:T(8,128)(2,1)S(1)} all-gather(bf16[32,32]{1,0:T(8,128)(2,1)} %reduce-scatter.20.cloned.1.call-done), channel_id=1, replica_groups=mesh['fsdp'=4,'ctx'=8,'tp'=4] {'ctx'}, dimensions={0}, use_global_device_ids=true | all-gather | bytes 18432 | tf_op jit(solution)/shard_map/all_gather | solution.py:85
  1346.5 152.9 %reduce-scatter.12.cloned.1.call-done = bf16[32,256]{1,0:T(8,128)(2,1)} async-done(((bf16[1024,256]{1,0:T(8,128)(2,1)}), bf16[32,256]{1,0:T(8,128)(2,1)}) %reduce-scatter.12.cloned.1.call-update) | async-done | bytes 16400 | tf_op jit(solution)/shard_map/reduce_scatter | solution.py:68
  1499.4 28.6 %all_gather.75 = bf16[256,256]{1,0:T(8,128)(2,1)S(1)} all-gather(bf16[32,256]{1,0:T(8,128)(2,1)} %reduce-scatter.12.cloned.1.call-done), channel_id=1, replica_groups=mesh['fsdp'=4,'ctx'=8,'tp'=4] {'ctx'}, dimensions={0}, use_global_device_ids=true | all-gather | bytes 147456 | tf_op jit(solution)/shard_map/all_gather | solution.py:85
  1528.7 153.1 %reduce-scatter.18.cloned.1.call-done = bf16[32,256]{1,0:T(8,128)(2,1)} async-done(((bf16[1024,256]{1,0:T(8,128)(2,1)}), bf16[32,256]{1,0:T(8,128)(2,1)}) %reduce-scatter.18.cloned.1.call-update) | async-done | bytes 16400 | tf_op jit(solution)/shard_map/reduce_scatter | solution.py:77
  1681.8 28.6 %all_gather.78 = bf16[256,256]{1,0:T(8,128)(2,1)S(1)} all-gather(bf16[32,256]{1,0:T(8,128)(2,1)} %reduce-scatter.18.cloned.1.call-done), channel_id=1, replica_groups=mesh['fsdp'=4,'ctx'=8,'tp'=4] {'ctx'}, dimensions={0}, use_global_device_ids=true | all-gather | bytes 147456 | tf_op jit(solution)/shard_map/all_gather | solution.py:94
  1711.0 151.5 %reduce-scatter.14.cloned.1.call-done = bf16[32,128]{1,0:T(8,128)(2,1)} async-done(((bf16[1024,128]{1,0:T(8,128)(2,1)}), bf16[32,128]{1,0:T(8,128)(2,1)}) %reduce-scatter.14.cloned.1.call-update) | async-done | bytes 8208 | tf_op jit(solution)/shard_map/reduce_scatter | solution.py:71
  1862.5 28.5 %all_gather.76 = bf16[256,128]{1,0:T(8,128)(2,1)S(1)} all-gather(bf16[32,128]{1,0:T(8,128)(2,1)} %reduce-scatter.14.cloned.1.call-done), channel_id=1, replica_groups=mesh['fsdp'=4,'ctx'=8,'tp'=4] {'ctx'}, dimensions={0}, use_global_device_ids=true | all-gather | bytes 73728 | tf_op jit(solution)/shard_map/all_gather | solution.py:88
  1891.6 151.1 %reduce-scatter.16.cloned.1.call-done = bf16[32,128]{1,0:T(8,128)(2,1)} async-done(((bf16[1024,128]{1,0:T(8,128)(2,1)}), bf16[32,128]{1,0:T(8,128)(2,1)}) %reduce-scatter.16.cloned.1.call-update) | async-done | bytes 8208 | tf_op jit(solution)/shard_map/reduce_scatter | solution.py:74
  2042.7 28.5 %all_gather.77 = bf16[256,128]{1,0:T(8,128)(2,1)S(1)} all-gather(bf16[32,128]{1,0:T(8,128)(2,1)} %reduce-scatter.16.cloned.1.call-done), channel_id=1, replica_groups=mesh['fsdp'=4,'ctx'=8,'tp'=4] {'ctx'}, dimensions={0}, use_global_device_ids=true | all-gather | bytes 73728 | tf_op jit(solution)/shard_map/all_gather | solution.py:91
  2071.9 35.7 %all-reduce.15.cloned.1.call-done = (bf16[256,1024]{1,0:T(8,128)(2,1)}, bf16[256,1024]{1,0:T(8,128)(2,1)}) async-done(((bf16[256,1024]{1,0:T(8,128)(2,1)}, bf16[256,1024]{1,0:T(8,128)(2,1)}), (bf16[256,1024]{1,0:T(8,128)(2,1)}, bf16[256,1024]{1,0:T(8,128)(2,1)})) %all-reduce.15.cloned.1.call-update) | async-done | bytes 1048592 | tf_op jit(solution)/shard_map/psum | solution.py:251
  2109.0 83.2 %all-reduce.4 = (bf16[1024]{0:T(1024)(128)(2,1)S(1)}, bf16[1024]{0:T(1024)(128)(2,1)S(1)}) all-reduce(bf16[1024]{0:T(1024)(128)(2,1)S(1)} %get-tuple-element.141, bf16[1024]{0:T(1024)(128)(2,1)S(1)} %copy-done.43), channel_id=3, replica_groups=mesh['fsdp'=4,'ctx'=8,'tp'=4] {'fsdp','ctx'}, use_global_device_ids=true, to_apply=%region_27.28.clone | all-reduce | flops 2048 | bytes 8192
  2192.7 16.0 all-reduce.5
  2212.6 4.8 copy.89
  2220.0 4.8 copy.90
  2224.8 49.5 %all-gather.22.cloned.1.call-done = bf16[256,32,128]{2,1,0:T(8,128)(2,1)} async-done(((bf16[32,32,128]{2,1,0:T(8,128)(2,1)}), bf16[256,32,128]{2,1,0:T(8,128)(2,1)}) %all-gather.22.cloned.1.call-update) | async-done | bytes 2097168 | tf_op jit(solution)/shard_map/all_gather | solution.py:94
  2274.3 4.2 convert_element_type.279
  (246 shorter events, 96.9 us)
Async XLA Ops:
  8.0 47.3 %copy-start.2 = (bf16[256,1024]{1,0:T(8,128)(2,1)S(1)}, bf16[256,1024]{1,0:T(8,128)(2,1)}, u32[]{:S(2)}) copy-start(bf16[256,1024]{1,0:T(8,128)(2,1)} %param.16) | copy-start | bytes 1572868
  8.0 37.3 %copy-start.25 = (bf16[256,256]{1,0:T(8,128)(2,1)S(1)}, bf16[256,256]{1,0:T(8,128)(2,1)}, u32[]{:S(2)}) copy-start(bf16[256,256]{1,0:T(8,128)(2,1)} %param.21) | copy-start | bytes 393220
  8.0 48.1 %copy-start.26 = (bf16[256,256]{1,0:T(8,128)(2,1)S(1)}, bf16[256,256]{1,0:T(8,128)(2,1)}, u32[]{:S(2)}) copy-start(bf16[256,256]{1,0:T(8,128)(2,1)} %param.24) | copy-start | bytes 393220
  8.0 89.6 %all-gather.10.cloned.1.call-start = ((), (), s32[]{:S(2)}) async-start(), calls=%async_computation.9 | async-start | bytes 1179648 | tf_op jit(solution)/shard_map/all_gather | solution.py:157
  28.3 38.8 %copy-start.28 = (f32[4,1,256]{2,1,0:T(1,128)}, f32[4,1,256]{2,1,0:T(1,128)S(1)}, u32[]{:S(2)}) copy-start(f32[4,1,256]{2,1,0:T(1,128)S(1)} %convert_element_type.280) | copy-start | bytes 12292
  30.1 37.0 %copy-start.35 = (f32[256]{0:T(256)}, f32[256]{0:T(256)S(1)}, u32[]{:S(2)}) copy-start(f32[256]{0:T(256)S(1)} %get-tuple-element.185) | copy-start | bytes 3076
  45.2 99.9 %all-reduce.11.cloned.1.call-start = ((), (), s32[]{:S(2)}) async-start(), calls=%async_computation.10 | async-start | bytes 1048576 | tf_op jit(solution)/shard_map/psum | solution.py:191
  56.1 44.3 %copy-start.17 = (bf16[256,4,64]{0,2,1:T(8,128)(2,1)}, bf16[256,4,64]{0,2,1:T(8,128)(2,1)S(1)}, u32[]{:S(2)}) copy-start(bf16[256,4,64]{0,2,1:T(8,128)(2,1)S(1)} %pad_maximum_fusion.2) | copy-start | bytes 393220
  107.1 85.5 %all-gather.14.cloned.1.call-start = ((), (), s32[]{:S(2)}) async-start(), calls=%async_computation.12 | async-start | bytes 10485760 | tf_op jit(solution)/shard_map/all_gather | solution.py:197
  109.3 169.4 %all-gather.12.cloned.1.call-start = ((), (), s32[]{:S(2)}) async-start(), calls=%async_computation.11 | async-start | bytes 10485760 | tf_op jit(solution)/shard_map/all_gather | solution.py:199
  113.2 12.8 copy-start.33
  113.2 23.3 %copy-start.39 = (s32[256,8]{0,1:T(8,128)S(1)}, s32[256,8]{0,1:T(8,128)}, u32[]{:S(2)}) copy-start(s32[256,8]{0,1:T(8,128)} %param.19) | copy-start | bytes 24580
  113.2 251.0 %all-gather.16.cloned.1.call-start = ((), (), s32[]{:S(2)}) async-start(), calls=%async_computation.13 | async-start | bytes 10485760 | tf_op jit(solution)/shard_map/all_gather | solution.py:198
  115.4 307.5 %all-reduce.13.cloned.1.call-start = ((), (), s32[]{:S(2)}) async-start(), calls=%async_computation.14 | async-start | bytes 1048576 | tf_op jit(solution)/shard_map/psum | solution.py:253
  123.4 76.8 %copy-start.31 = (f32[4,1,256]{2,1,0:T(1,128)}, f32[4,1,256]{2,1,0:T(1,128)S(1)}, u32[]{:S(2)}) copy-start(f32[4,1,256]{2,1,0:T(1,128)S(1)} %convert_element_type.281) | copy-start | bytes 12292
  124.7 154.0 %copy-start.4 = (f32[256,1024]{1,0:T(8,128)}, f32[256,1024]{1,0:T(8,128)S(1)}, u32[]{:S(2)}) copy-start(f32[256,1024]{1,0:T(8,128)S(1)} %convert_multiply_fusion.6) | copy-start | bytes 3145732
  136.5 63.7 %copy-start.23 = (bf16[1024,32]{0,1:T(8,128)(2,1)}, bf16[1024,32]{0,1:T(8,128)(2,1)S(1)}, u32[]{:S(2)}) copy-start(bf16[1024,32]{0,1:T(8,128)(2,1)S(1)} %all_gather.70) | copy-start | bytes 196612
  149.2 51.1 %copy-start.32 = (f32[256]{0:T(256)}, f32[256]{0:T(256)S(1)}, u32[]{:S(2)}) copy-start(f32[256]{0:T(256)S(1)} %get-tuple-element.190) | copy-start | bytes 3076
  149.2 51.0 %copy-start.34 = (f32[256]{0:T(256)}, f32[256]{0:T(256)S(1)}, u32[]{:S(2)}) copy-start(f32[256]{0:T(256)S(1)} %fusion.65) | copy-start | bytes 3076
  364.2 10.6 copy-start.44
  377.2 7.1 copy-start.15
  383.8 127.5 %reduce-scatter.10.cloned.1.call-start = ((), (), s32[]{:S(2)}) async-start(), calls=%async_computation.15 | async-start | bytes 1179648 | tf_op jit(solution)/shard_map/reduce_scatter | solution.py:304
  384.3 38.7 %copy-start.3 = (bf16[256,1024]{1,0:T(8,128)(2,1)S(1)}, bf16[256,1024]{1,0:T(8,128)(2,1)}, u32[]{:S(2)}) copy-start(bf16[256,1024]{1,0:T(8,128)(2,1)} %all-reduce.11.cloned.1.call-done) | copy-start | bytes 1572868
  420.1 5.8 copy-start.41
  420.1 7.6 copy-start.27
  423.0 9.7 slice-start
  440.9 266.6 %reduce-scatter.22.cloned.1.call-start = ((), (), s32[]{:S(2)}) async-start(), calls=%async_computation.21 | async-start | bytes 8650752 | tf_op jit(solution)/shard_map/reduce_scatter | solution.py:71
  448.3 473.5 %reduce-scatter.24.cloned.1.call-start = ((), (), s32[]{:S(2)}) async-start(), calls=%async_computation.23 | async-start | bytes 8650752 | tf_op jit(solution)/shard_map/reduce_scatter | solution.py:74
  455.7 681.0 %reduce-scatter.26.cloned.1.call-start = ((), (), s32[]{:S(2)}) async-start(), calls=%async_computation.25 | async-start | bytes 8650752 | tf_op jit(solution)/shard_map/reduce_scatter | solution.py:77
  475.7 5.3 copy-start.29
  475.7 841.7 %reduce-scatter.20.cloned.1.call-start = ((), (), s32[]{:S(2)}) async-start(), calls=%async_computation.20 | async-start | bytes 270336 | tf_op jit(solution)/shard_map/reduce_scatter | solution.py:68
  477.7 1021.7 %reduce-scatter.12.cloned.1.call-start = ((), (), s32[]{:S(2)}) async-start(), calls=%async_computation.16 | async-start | bytes 540672 | tf_op jit(solution)/shard_map/reduce_scatter | solution.py:68
  480.9 32.6 %copy-start.19 = (bf16[256,4,64]{0,2,1:T(8,128)(2,1)}, bf16[256,4,64]{0,2,1:T(8,128)(2,1)S(1)}, u32[]{:S(2)}) copy-start(bf16[256,4,64]{0,2,1:T(8,128)(2,1)S(1)} %pad_maximum_fusion.3) | copy-start | bytes 393220
  482.2 1199.6 %reduce-scatter.18.cloned.1.call-start = ((), (), s32[]{:S(2)}) async-start(), calls=%async_computation.19 | async-start | bytes 540672 | tf_op jit(solution)/shard_map/reduce_scatter | solution.py:77
  483.4 33.7 %copy-start.30 = (f32[4,1,256]{2,1,0:T(1,128)S(1)}, f32[4,1,256]{2,1,0:T(1,128)}, u32[]{:S(2)}) copy-start(f32[4,1,256]{2,1,0:T(1,128)} %copy-done.28) | copy-start | bytes 12292
  483.4 33.7 %copy-start.37 = (f32[256]{0:T(256)S(1)}, f32[256]{0:T(256)}, u32[]{:S(2)}) copy-start(f32[256]{0:T(256)} %copy-done.35) | copy-start | bytes 3076
  483.4 1379.1 %reduce-scatter.14.cloned.1.call-start = ((), (), s32[]{:S(2)}) async-start(), calls=%async_computation.17 | async-start | bytes 270336 | tf_op jit(solution)/shard_map/reduce_scatter | solution.py:71
  513.4 1529.3 %reduce-scatter.16.cloned.1.call-start = ((), (), s32[]{:S(2)}) async-start(), calls=%async_computation.18 | async-start | bytes 270336 | tf_op jit(solution)/shard_map/reduce_scatter | solution.py:74
  513.5 9.1 copy-start.8
  513.5 9.1 copy-start.20
  519.1 617.6 %copy-start.47 = (u32[128]{0:T(128)S(1)}, u32[128]{0:T(128)}, u32[]{:S(2)}) copy-start(u32[128]{0:T(128)} %constant.75) | copy-start | bytes 1540
  519.1 618.9 %copy-start.46 = (u32[128]{0:T(128)S(1)}, u32[128]{0:T(128)}, u32[]{:S(2)}) copy-start(u32[128]{0:T(128)} %constant.63) | copy-start | bytes 1540
  521.4 1586.2 %all-reduce.15.cloned.1.call-start = ((), (), s32[]{:S(2)}) async-start(), calls=%async_computation.27 | async-start | bytes 2097152 | tf_op jit(solution)/shard_map/psum | solution.py:251
  522.6 1586.3 %copy-start.43 = (bf16[1024]{0:T(1024)(128)(2,1)S(1)}, bf16[1024]{0:T(1024)(128)(2,1)}, u32[]{:S(2)}) copy-start(bf16[1024]{0:T(1024)(128)(2,1)} %get-tuple-element.139) | copy-start | bytes 6148
  522.7 1687.2 %copy-start.40 = (f32[256]{0:T(256)S(1)}, f32[256]{0:T(256)}, u32[]{:S(2)}) copy-start(f32[256]{0:T(256)} %get-tuple-element.184) | copy-start | bytes 3076
  525.2 1687.4 %all-gather.18.cloned.1.call-start = ((), (), s32[]{:S(2)}) async-start(), calls=%async_computation.22 | async-start | bytes 2359296 | tf_op jit(solution)/shard_map/all_gather | solution.py:88
  707.6 1512.4 %all-gather.20.cloned.1.call-start = ((), (), s32[]{:S(2)}) async-start(), calls=%async_computation.24 | async-start | bytes 2359296 | tf_op jit(solution)/shard_map/all_gather | solution.py:91
  921.8 1352.5 %all-gather.22.cloned.1.call-start = ((), (), s32[]{:S(2)}) async-start(), calls=%async_computation.26 | async-start | bytes 2359296 | tf_op jit(solution)/shard_map/all_gather | solution.py:94
  (21 other events, 55.2 us)
Sparse Core Ops, SparseCore 0:
  45.3 52.2 all-gather.9
  107.2 37.9 all-reduce.10
  383.9 38.9 all-reduce.12
  441.1 70.2 reduce-scatter.9
  513.7 193.8 reduce-scatter.21
  710.0 211.7 reduce-scatter.23
  924.3 212.2 reduce-scatter.25
  1139.7 177.6 reduce-scatter.19
  1320.3 179.0 reduce-scatter.11
  1502.3 179.4 reduce-scatter.17
  1684.1 178.3 reduce-scatter.13
  1864.8 177.8 reduce-scatter.15
  2045.9 61.6 all-reduce.14
  2109.9 55.2 all-gather.17
  2167.4 52.5 all-gather.19
  2222.4 51.7 all-gather.21
Sparse Core Ops, SparseCore 1:
  109.8 82.7 all-gather.13
  194.6 84.0 all-gather.11
  280.2 84.0 all-gather.15
where the time goes:
time: 2290 us
  waiting for transfers between devices  1750 us (76%)
  blocking collectives  321 us (14%)
  matrix products  105 us (5%)
  local copies, waits for them, and re-layouts  53.2 us (2%)
  other arithmetic  31 us (1%)
    reduce_scatter x2, waiting for transfers between devices, reduce_grads(): lax.psum_scatter(fourth_part.astype(jnp.bfloat16), ('fsdp', 'ctx'), scatt...  368 us
    reduce_scatter x2, waiting for transfers between devices, reduce_grads(): lax.psum_scatter(third_part.astype(jnp.bfloat16), ('fsdp', 'ctx'), scatte...  365 us
    reduce_scatter x2, waiting for transfers between devices, reduce_grads(): lax.psum_scatter(second_part.astype(jnp.bfloat16), ('fsdp', 'ctx'), scatt...  334 us
    reduce_scatter x2, waiting for transfers between devices, reduce_grads(): lax.psum_scatter(first_part.astype(jnp.bfloat16), ('fsdp', 'ctx'), scatte...  331 us
    unnamed x2, blocking collectives  99.2 us
    all_gather x1, waiting for transfers between devices, local(): lax.all_gather(w_down, 'fsdp', axis=0, tiled=True)  78.4 us
    all_gather x1, waiting for transfers between devices, local(): lax.all_gather(w_up, 'fsdp', axis=0, tiled=True)  77.2 us
    all_gather x2, blocking collectives, reduce_grads(): lax.all_gather(first_part.astype(jnp.bfloat16), 'ctx', axis=0, tiled=True)  57 us
  transfers between devices with their start and end apart: 19, of which 18 were waited for; matrix products, arithmetic and copies ran while one was open for 6% of the time, Pallas kernels for 0%

commit v1 on v0

v1 whole, which is shorter than its diff:
```python
import functools
import math

import jax
import jax.numpy as jnp
from jax import lax
from jax.experimental import pallas as pl
from jax.experimental.pallas import tpu as pltpu
from jax.sharding import PartitionSpec as P

HEAD_SIZE = 64
CAP = 128
MESH = pl.DeviceIdType.MESH

norm_eps = 1e-06
rope_base = 10000.0
branch_scale = 0.22
highest = lax.Precision.HIGHEST
bf16 = jnp.bfloat16
f32 = jnp.float32


def exchange_kernel(plan, sizes, *refs):
    count = len(plan)
    ins, outs = refs[:count], refs[count : 2 * count]
    send_sem, recv_sem, self_sem = refs[2 * count :]

    def place(axes, step):
        offsets = []
        for axis in reversed(axes):
            offsets.append(step % sizes[axis])
            step //= sizes[axis]
        coords = {}
        for axis, offset in zip(axes, offsets[::-1]):
            here = lax.axis_index(axis)
            coords[axis] = lax.rem(here + offset, sizes[axis]) if offset else here
        return coords

    def flat(axes, coords):
        index = 0
        for axis in axes:
            index = index * sizes[axis] + coords[axis]
        return index

    groups = {}
    for axes, _ in plan:
        for step in range(1, math.prod(sizes[a] for a in axes)):
            full, rest = {}, step
            for axis in reversed(axes):
                full[axis] = rest % sizes[axis]
                rest //= sizes[axis]
            key = tuple(sorted((a, o) for a, o in full.items() if o))
            groups[key] = (axes, step)
    barrier = pltpu.get_barrier_semaphore()
    for axes, step in groups.values():
        pl.semaphore_signal(barrier, inc=1, device_id=place(axes, step), device_id_type=MESH)
    pl.semaphore_wait(barrier, len(groups))

    copies = []
    for at, (axes, mode) in enumerate(plan):
        mine = flat(axes, place(axes, 0))
        for step in range(1, math.prod(sizes[a] for a in axes)):
            peer = place(axes, step)
            copy = pltpu.make_async_remote_copy(
                src_ref=ins[at] if mode == "g" else ins[at].at[flat(axes, peer)],
                dst_ref=outs[at].at[mine],
                send_sem=send_sem.at[at, step],
                recv_sem=recv_sem.at[at, step],
                device_id=peer,
                device_id_type=MESH,
            )
            copy.start()
            copies.append(copy)
        own = pltpu.make_async_copy(
            ins[at] if mode == "g" else ins[at].at[mine], outs[at].at[mine], self_sem.at[at]
        )
        own.start()
        copies.append(own)
    for copy in copies:
        copy.wait()


def exchange(sizes, collective_id, *items):
    plan = [(axes, mode) for axes, mode, _ in items]
    arrays = [array for _, _, array in items]
    outs = []
    most = 1
    for axes, mode, array in items:
        n = math.prod(sizes[a] for a in axes)
        most = max(most, n)
        shape = (n,) + array.shape if mode == "g" else array.shape
        outs.append(jax.ShapeDtypeStruct(shape, array.dtype))
    count = len(items)
    moved = sum(math.prod(o.shape) * o.dtype.itemsize for o in outs)
    return pl.pallas_call(
        functools.partial(exchange_kernel, plan, sizes),
        out_shape=outs,
        in_specs=[pl.BlockSpec(memory_space=pl.ANY)] * count,
        out_specs=[pl.BlockSpec(memory_space=pl.ANY)] * count,
        scratch_shapes=[
            pltpu.SemaphoreType.DMA((count, most)),
            pltpu.SemaphoreType.DMA((count, most)),
            pltpu.SemaphoreType.DMA((count,)),
        ],
        compiler_params=pltpu.CompilerParams(collective_id=collective_id, has_side_effects=True),
        cost_estimate=pl.CostEstimate(flops=0, bytes_accessed=20 * moved, transcendentals=0),
        name="exchange_%d" % collective_id,
    )(*arrays)


def rope_tables(places):
    frequencies = jnp.exp(
        jnp.arange(HEAD_SIZE // 2, dtype=jnp.float32) * (-2.0 * math.log(rope_base) / HEAD_SIZE)
    )
    angles = places.astype(jnp.float32)[:, None] * frequencies[None, :]
    return (jnp.cos(angles)[:, None, :], jnp.sin(angles)[:, None, :])


def turn(values, cosine_table, sine_table):
    row_count = values.shape[0]
    head_view = values.reshape(row_count, -1, HEAD_SIZE)
    first_half = head_view[..., : HEAD_SIZE // 2]
    second_half = head_view[..., HEAD_SIZE // 2 :]
    turned = jnp.concatenate(
        [
            first_half * cosine_table - second_half * sine_table,
            second_half * cosine_table + first_half * sine_table,
        ],
        axis=-1,
    )
    return turned.reshape(row_count, -1)


def contract_rows(left, right, precision=None):
    return lax.dot_general(
        left, right, (((0,), (0,)), ((), ())), precision=precision, preferred_element_type=f32
    )


def contract_cols(left, right, precision=None):
    return lax.dot_general(
        left, right, (((1,), (1,)), ((), ())), precision=precision, preferred_element_type=f32
    )


def mm(left, right):
    return jnp.dot(left, right, preferred_element_type=f32)


def local(
    sizes,
    inputs,
    cotangent,
    lengths,
    expert_ids,
    attn_gain,
    w_query,
    key_weight,
    value_weight,
    w_output,
    ffn_gain,
    w_router,
    w_gate,
    w_up,
    w_down,
):
    rows, width = inputs.shape
    n_fsdp, n_ctx, n_tp = sizes["fsdp"], sizes["ctx"], sizes["tp"]
    experts = w_router.shape[1]
    depth, _, ff = w_gate.shape
    per_ctx = experts // n_ctx
    send = functools.partial(exchange, sizes)
    ctx_at, tp_at = lax.axis_index("ctx"), lax.axis_index("tp")

    chosen = jnp.any(
        expert_ids[:, :, None] == jnp.arange(experts, dtype=jnp.int32)[None, None, :], axis=1
    )
    mine = jnp.arange(n_ctx, dtype=jnp.int32) * per_ctx + tp_at
    chosen_mine = jnp.any(expert_ids[None, :, :] == mine[:, None, None], axis=2)
    earlier = jnp.arange(rows)[:, None] < jnp.arange(rows)[None, :]
    rank = mm(chosen_mine.astype(bf16), earlier.astype(bf16))
    slots = jnp.arange(CAP, dtype=f32)
    picks = (chosen_mine[:, None, :] & (rank[:, None, :] == slots[None, :, None])).astype(bf16)
    picks_flat = picks.reshape(n_ctx * CAP, rows)
    grads_sent = mm(picks_flat, cotangent).astype(bf16).reshape(n_ctx, CAP, width)

    first = ctx_at * per_ctx
    own_slices = jnp.stack(
        [
            lax.dynamic_slice_in_dim(w, first, per_ctx, 1).transpose(1, 0, 2)
            for w in (w_gate, w_up, w_down)
        ],
        axis=1,
    )
    gains = jnp.concatenate(
        [
            attn_gain.reshape(-1, 128),
            ffn_gain.reshape(-1, 128),
            jnp.zeros((16 - 2 * depth // 128, 128), bf16),
        ],
        axis=0,
    )
    router_pad = jnp.pad(w_router, ((0, 0), (0, 128 - experts)))
    query_w, key_w, value_w, gains_all, router_all, expert_slices, grads_got = send(
        0,
        (("fsdp",), "g", w_query),
        (("fsdp",), "g", key_weight),
        (("fsdp",), "g", value_weight),
        (("fsdp",), "g", gains),
        (("fsdp",), "g", router_pad),
        (("tp",), "a", own_slices),
        (("ctx",), "a", grads_sent),
    )
    query_w = query_w.reshape(width, -1)
    key_w = key_w.reshape(width, -1)
    value_w = value_w.reshape(width, -1)
    lines = depth // 128
    gain_one = gains_all[:, :lines].reshape(width).astype(f32)
    gain_two = gains_all[:, lines : 2 * lines].reshape(width).astype(f32)
    router_w = router_all.reshape(width, 128)[:, :experts]
    grad_rows = grads_got.reshape(n_ctx * CAP, width)

    output_w = lax.all_gather(w_output, "fsdp", axis=0, tiled=True)
    output_full = lax.all_gather(output_w, "tp", axis=1, tiled=True)
    expert_cat = expert_slices.transpose(2, 1, 0, 3).reshape(depth, 3 * n_tp * ff)
    expert_w = lax.all_gather(expert_cat, "fsdp", axis=0, tiled=True)
    hidden_units = n_tp * ff
    gate_up_w, down_w = expert_w[:, : 2 * hidden_units], expert_w[:, 2 * hidden_units :]

    lengths_row = lengths[0]
    query_rows = ctx_at * rows + jnp.arange(rows, dtype=jnp.int32)
    seq_ends = jnp.cumsum(lengths_row)
    passed = (query_rows[:, None] >= seq_ends[None, :]).astype(jnp.int32)
    starts = jnp.sum(passed * lengths_row[None, :], axis=1)
    cosine_table, sine_table = rope_tables(query_rows - starts)
    hidden_in = inputs.astype(f32)
    scale_one = lax.rsqrt(jnp.mean(hidden_in * hidden_in, axis=-1, keepdims=True) + norm_eps)
    normed_one = (hidden_in * scale_one * gain_one).astype(bf16)
    queries = turn(mm(normed_one, query_w), cosine_table, sine_table).astype(bf16)
    keys_local = turn(mm(normed_one, key_w), cosine_table, sine_table).astype(bf16)
    values_local = mm(normed_one, value_w).astype(bf16)
    pairs_local = jnp.concatenate([keys_local, values_local], axis=1)
    pair_width = keys_local.shape[1]
    (pairs_all,) = send(1, (("ctx",), "g", pairs_local))
    total_rows = n_ctx * rows
    pairs_all = pairs_all.reshape(total_rows, 2 * pair_width)
    key_heads = pair_width // HEAD_SIZE
    groups = queries.shape[1] // pair_width
    keys_all = pairs_all[:, :pair_width].reshape(total_rows, key_heads, HEAD_SIZE)
    values_all = pairs_all[:, pair_width:].reshape(total_rows, key_heads, HEAD_SIZE)
    query_head_rows = queries.reshape(rows, key_heads, groups, HEAD_SIZE)
    key_rows = jnp.arange(total_rows, dtype=jnp.int32)
    allowed = (key_rows[None, :] >= starts[:, None]) & (key_rows[None, :] <= query_rows[:, None])

    def masked_scores():
        raw_scores = jnp.einsum(
            "rkgd,skd->kgrs", query_head_rows, keys_all, preferred_element_type=f32
        )
        return jnp.where(allowed, raw_scores * HEAD_SIZE ** (-0.5), -1e30)

    masked = masked_scores()
    row_top = jnp.max(masked, axis=-1, keepdims=True)
    shifted_exp = jnp.exp(masked - row_top)
    row_total = jnp.sum(shifted_exp, axis=-1, keepdims=True)
    attn_probs = shifted_exp / row_total
    log_total = row_top + jnp.log(row_total)
    attended = jnp.einsum(
        "kgrs,skd->rkgd", attn_probs.astype(bf16), values_all, preferred_element_type=f32
    )
    attended = attended.reshape(rows, -1).astype(bf16)
    (attended_all,) = send(2, (("tp",), "g", attended))
    attended_all = attended_all.transpose(1, 0, 2).reshape(rows, -1)
    residual = hidden_in + branch_scale * contract_cols(attended_all, output_full)

    scale_two = lax.rsqrt(jnp.mean(residual * residual, axis=-1, keepdims=True) + norm_eps)
    normed_two = (residual * scale_two * gain_two).astype(bf16)
    logits = mm(normed_two, router_w)
    route_masked = jnp.where(chosen, logits, -1e30)
    route_exp = jnp.exp(route_masked - jnp.max(route_masked, axis=-1, keepdims=True))
    gate_probs = route_exp / jnp.sum(route_exp, axis=-1, keepdims=True)
    probs_mine = lax.dynamic_index_in_dim(
        gate_probs.T.reshape(n_ctx, per_ctx, rows), tp_at, 1, keepdims=False
    )
    probs_sent = jnp.sum(picks.astype(f32) * probs_mine[:, None, :], axis=2)
    rows_sent = mm(picks_flat, normed_two).astype(bf16).reshape(n_ctx, CAP, width)
    rows_got, probs_got = send(
        3,
        (("ctx",), "a", rows_sent),
        (("ctx",), "a", jnp.broadcast_to(probs_sent[:, None, :], (n_ctx, 8, CAP))),
    )

    norm_rows = rows_got.reshape(n_ctx * CAP, width)
    probs_col = probs_got[:, 0, :].reshape(n_ctx * CAP, 1)
    gate_up = mm(norm_rows, gate_up_w)
    gate_pre, up_pre = gate_up[:, :hidden_units], gate_up[:, hidden_units:]
    down_back = mm(grad_rows, down_w)
    sigmoid_gate = jax.nn.sigmoid(gate_pre)
    silu_gate = gate_pre * sigmoid_gate
    activation = silu_gate * up_pre
    gate_grad_rows = branch_scale * jnp.sum(activation * down_back, axis=1)
    act_grad = (branch_scale * probs_col) * down_back
    gate_in = act_grad * up_pre * sigmoid_gate * (1.0 + gate_pre * (1.0 - sigmoid_gate))
    both_in = jnp.concatenate([gate_in, act_grad * silu_gate], axis=1).astype(bf16)
    weighted = (probs_col * activation).astype(bf16)
    mixed = contract_cols(weighted, down_w).astype(bf16)
    norm_grad = contract_cols(both_in, gate_up_w).astype(bf16)
    gate_grad_rows = jnp.broadcast_to(gate_grad_rows.reshape(n_ctx, 1, CAP), (n_ctx, 8, CAP))
    grad_gate_up = contract_rows(norm_rows, both_in)
    grad_down = contract_rows(grad_rows, weighted) * branch_scale
    expert_grad = jnp.concatenate([grad_gate_up, grad_down], axis=1).astype(bf16)

    norm_grad_got, mixed_got, gate_grad_got = send(
        4,
        (("ctx",), "a", norm_grad.reshape(n_ctx, CAP, width)),
        (("ctx",), "a", mixed.reshape(n_ctx, CAP, width)),
        (("ctx",), "a", gate_grad_rows),
    )

    expert_grad = lax.psum_scatter(expert_grad, "fsdp", scatter_dimension=0, tiled=True)
    expert_grad = expert_grad.reshape(depth, 3, n_tp, ff).transpose(2, 1, 0, 3)
    pieces = [lax.dynamic_index_in_dim(expert_grad, tp_at, 0, keepdims=False)]
    for step in range(1, n_tp):
        piece = lax.dynamic_index_in_dim(
            expert_grad, lax.rem(tp_at + step, n_tp), 0, keepdims=False
        )
        pieces.append(lax.ppermute(piece, "tp", [(s, (s + step) % n_tp) for s in range(n_tp)]))
    pieces = jnp.stack(pieces)
    pieces = jnp.take(pieces, lax.rem(tp_at - jnp.arange(n_tp) + n_tp, n_tp), axis=0)
    expert_all = lax.all_gather(pieces, "ctx", axis=0, tiled=True)
    expert_all = expert_all.transpose(1, 2, 0, 3).astype(f32)

    norm_grad_part = contract_rows(picks_flat, norm_grad_got.reshape(n_ctx * CAP, width))
    mixed_part = contract_rows(picks_flat, mixed_got.reshape(n_ctx * CAP, width)).astype(bf16)
    gate_grad_part = jnp.sum(picks.astype(f32) * gate_grad_got[:, 0, :, None], axis=1)
    norm_grad_parts, gate_grad_parts = send(
        5, (("tp",), "g", norm_grad_part.astype(bf16)), (("tp",), "g", gate_grad_part)
    )
    gate_grads = gate_grad_parts.transpose(2, 1, 0).reshape(rows, experts)
    route_grad = gate_probs * (
        gate_grads - jnp.sum(gate_probs * gate_grads, axis=-1, keepdims=True)
    )
    grad_router = contract_rows(normed_two.astype(f32), route_grad, highest)
    router_back = contract_cols(route_grad, router_w.astype(f32), highest)
    out_grad = cotangent.astype(f32)
    normed_grad = jnp.sum(norm_grad_parts.astype(f32), axis=0) + router_back
    weighted_two = normed_grad * gain_two
    grad_ffn_gain = jnp.sum(normed_grad * residual * scale_two, axis=0)
    residual_grad = (
        out_grad
        + scale_two * weighted_two
        - residual * scale_two**3 * jnp.mean(weighted_two * residual, axis=-1, keepdims=True)
    )
    attn_in = (branch_scale * residual_grad).astype(bf16)
    grad_output = contract_rows(attn_in, attended)
    attended_grad = mm(attn_in, output_w).astype(bf16)

    grad_heads = attended_grad.reshape(rows, key_heads, groups, HEAD_SIZE)
    attn_probs = jnp.exp(masked_scores() - log_total)
    value_grad_all = jnp.einsum(
        "kgrs,rkgd->skd", attn_probs.astype(bf16), grad_heads, preferred_element_type=f32
    )
    prob_grad = jnp.einsum("rkgd,skd->kgrs", grad_heads, values_all, preferred_element_type=f32)
    score_grad = (
        attn_probs * (prob_grad - jnp.sum(attn_probs * prob_grad, axis=-1, keepdims=True))
    ).astype(bf16)
    query_grad_rot = jnp.einsum(
        "kgrs,skd->rkgd", score_grad, keys_all, preferred_element_type=f32
    ).reshape(rows, -1) * HEAD_SIZE ** (-0.5)
    key_grad_all = jnp.einsum(
        "kgrs,rkgd->skd", score_grad, query_head_rows, preferred_element_type=f32
    ) * HEAD_SIZE ** (-0.5)
    pair_grads = jnp.concatenate(
        [
            key_grad_all.reshape(total_rows, pair_width),
            value_grad_all.reshape(total_rows, pair_width),
        ],
        axis=1,
    ).astype(bf16)
    (pair_got,) = send(6, (("ctx",), "a", pair_grads.reshape(n_ctx, rows, 2 * pair_width)))
    pair_owned = jnp.sum(pair_got.astype(f32), axis=0)
    query_grad = turn(query_grad_rot, cosine_table, -sine_table).astype(bf16)
    key_grad = turn(pair_owned[:, :pair_width], cosine_table, -sine_table).astype(bf16)
    value_grad = pair_owned[:, pair_width:].astype(bf16)
    normed_one_part = (
        contract_cols(query_grad, query_w)
        + contract_cols(key_grad, key_w)
        + contract_cols(value_grad, value_w)
    )
    grad_gain_part = jnp.sum(normed_one_part * hidden_in * scale_one, axis=0)
    grad_query = contract_rows(normed_one, query_grad)
    grad_key = contract_rows(normed_one, key_grad)
    grad_value = contract_rows(normed_one, value_grad)

    n_rows = n_fsdp * n_ctx
    share = width // n_rows
    side = jnp.concatenate(
        [grad_router, grad_ffn_gain[:, None], jnp.zeros((width, 128 - experts - 1), f32)], axis=1
    )
    small = jnp.concatenate([grad_query, grad_key, grad_value, grad_output, side], axis=1)
    small = small.astype(bf16).reshape(n_rows, share, -1)
    gain_chunks = jnp.broadcast_to(
        jnp.pad(grad_gain_part.reshape(n_rows, 1, share), ((0, 0), (0, 0), (0, 128 - share))),
        (n_rows, 8, 128),
    )
    one_parts, mixed_parts, small_got, gain_got = send(
        7,
        (("tp",), "g", normed_one_part.astype(bf16)),
        (("tp",), "g", mixed_part),
        (("fsdp", "ctx"), "a", small),
        (("fsdp", "ctx"), "a", gain_chunks),
    )
    small_sum = jnp.sum(small_got.astype(f32), axis=0).astype(bf16)
    gain_sum = jnp.sum(gain_got, axis=0)
    small_all, gain_all = send(
        8, (("ctx",), "g", small_sum), (("ctx", "tp"), "g", gain_sum)
    )
    small_all = small_all.reshape(depth, -1).astype(f32)
    gain_all = gain_all[:, 0, :share].reshape(n_ctx, n_tp, share)
    grad_attn_gain = jnp.sum(gain_all, axis=1).reshape(depth)

    output = residual + branch_scale * jnp.sum(mixed_parts.astype(f32), axis=0)
    normed_one_grad = jnp.sum(one_parts.astype(f32), axis=0)
    weighted_one = normed_one_grad * gain_one
    input_grad = (
        residual_grad
        + scale_one * weighted_one
        - hidden_in * scale_one**3 * jnp.mean(weighted_one * hidden_in, axis=-1, keepdims=True)
    )
    q_end = queries.shape[1]
    k_end, v_end = q_end + pair_width, q_end + 2 * pair_width
    o_end = v_end + attended.shape[1]
    return (
        output.astype(bf16),
        input_grad.astype(bf16),
        grad_attn_gain,
        small_all[:, :q_end],
        small_all[:, q_end:k_end],
        small_all[:, k_end:v_end],
        small_all[:, v_end:o_end],
        small_all[:, o_end + experts],
        small_all[:, o_end : o_end + experts],
        expert_all[0],
        expert_all[1],
        expert_all[2],
    )


def solution(mesh):
    sizes = dict(mesh.shape)
    return jax.shard_map(
        functools.partial(local, sizes),
        mesh=mesh,
        in_specs=(
            P(("fsdp", "ctx"), None),
            P(("fsdp", "ctx"), None),
            P("fsdp", None),
            P(("fsdp", "ctx"), None),
            P("fsdp"),
            P("fsdp", "tp"),
            P("fsdp", "tp"),
            P("fsdp", "tp"),
            P("fsdp", "tp"),
            P("fsdp"),
            P("fsdp", None),
            P("fsdp", None, "tp"),
            P("fsdp", None, "tp"),
            P("fsdp", None, "tp"),
        ),
        out_specs=(
            P(("fsdp", "ctx"), None),
            P(("fsdp", "ctx"), None),
            P("fsdp"),
            P("fsdp", "tp"),
            P("fsdp", "tp"),
            P("fsdp", "tp"),
            P("fsdp", "tp"),
            P("fsdp"),
            P("fsdp", None),
            P("fsdp", None, "tp"),
            P("fsdp", None, "tp"),
            P("fsdp", None, "tp"),
        ),
        check_vma=False,
    )
```

time: 2290 us -> 599 us (0.26)
  waiting for transfers between devices: 1750 us -> 37.5 us
  Pallas kernels: 0 us -> 338 us
  blocking collectives: 321 us -> 14.5 us
  matrix products: 105 us -> 66.1 us
  local copies, waits for them, and re-layouts: 53.2 us -> 77.2 us
    reduce_scatter x9 -> x1, waiting for transfers between devices: 1430 us -> 35.6 us  [local(): lax.psum_scatter(expert_grad, 'fsdp', scatter_dimension=0, tiled=True)]
    pallas_call x0 -> x9, Pallas kernels: none -> 338 us  [exchange(): pl.pallas_call(functools.partial(exchange_kernel, plan, sizes), out_shape...]
    all_gather x7 -> x3, waiting for transfers between devices: 281 us -> 0.02 us  [the longest x1 0.02 us: local(): output_full = lax.all_gather(output_w, 'tp', axis=1, tiled=True)]
    all_gather x12 -> x1, blocking collectives: 211 us -> 14.5 us  [local(): output_w = lax.all_gather(w_output, 'fsdp', axis=0, tiled=True)]
    unnamed x2 -> x0, blocking collectives: 99.2 us -> none
    dot_general x19 -> x12, matrix products: 80.4 us -> 21 us  [the longest x10 14.7 us: mm(): return jnp.dot(left, right, preferred_element_type=f32)]
    psum x3 -> x0, waiting for transfers between devices: 46.6 us -> none  [the longest x1 35.7 us: local(): lax.psum(sum_part.astype(jnp.bfloat16), 'tp').astype(jnp.float32)]
  transfers between devices with their start and end apart: 19 -> 7, of which waited for: 18 -> 2; matrix products, arithmetic and copies ran while one was open for 6% -> 21% of each run, Pallas kernels for 0% -> 57%
where the time goes in v1:
time: 599 us; the launch traced here: 595 us
  Pallas kernels  338 us (56%)
  local copies, waits for them, and re-layouts  77.2 us (13%)
  matrix products  66.1 us (11%)
  other arithmetic  43.3 us (7%)
  waiting for transfers between devices  37.5 us (6%)
  between operations  15.1 us (3%)
  blocking collectives  14.5 us (2%)
    pallas_call x9, Pallas kernels, exchange(): pl.pallas_call(functools.partial(exchange_kernel, plan, sizes), out_shape...  338 us
    reduce_scatter x1, waiting for transfers between devices, local(): lax.psum_scatter(expert_grad, 'fsdp', scatter_dimension=0, tiled=True)  35.6 us
    unnamed x125, local copies, waits for them, and re-layouts  29.2 us
    dot_general x7, matrix products, contract_cols(): lax.dot_general(left, right, (((1,), (1,)), ((), ())), precision=precisio...  17 us
    dot_general x9, matrix products, contract_rows(): lax.dot_general(left, right, (((0,), (0,)), ((), ())), precision=precisio...  16.5 us
    dot_general x10, matrix products, mm(): return jnp.dot(left, right, preferred_element_type=f32)  14.7 us
    all_gather x1, blocking collectives, local(): output_w = lax.all_gather(w_output, 'fsdp', axis=0, tiled=True)  14.5 us
  transfers between devices with their start and end apart: 7, of which 2 were waited for; matrix products, arithmetic and copies ran while one was open for 21% of the time, Pallas kernels for 57%

profile of v1, /device:TPU:1, one launch (start us, length us, event | category | flops | bytes accessed | tf_op | source)
XLA Modules:
  0.0 594.9 jit_solution(2206305057479612525)
XLA Ops:
  7.2 14.5 %all_gather.12 = bf16[1024,256]{1,0:T(8,128)(2,1)} all-gather(bf16[256,256]{1,0:T(8,128)(2,1)} %param.22), channel_id=1, replica_groups=mesh['fsdp'=4,'ctx'=8,'tp'=4] {'fsdp'}, dimensions={0}, use_global_device_ids=true | all-gather | bytes 655360 | tf_op jit(solution)/shard_map/all_gather | solution.py:223
  27.4 2.0 convolution_convert_fusion.4
  29.4 56.1 %exchange_0.1 = (bf16[4,256,256]{2,1,0:T(8,128)(2,1)}, bf16[4,256,128]{2,1,0:T(8,128)(2,1)}, bf16[4,256,128]{2,1,0:T(8,128)(2,1)}, bf16[4,16,128]{2,1,0:T(8,128)...) custom-call(bf16[256,256]{1,0:T(8,128)(2,1)} %refs_0_.1, ...), custom_call_target="tpu_custom_call" | custom-call | bytes 84213760 | tf_op jit(solution)/shard_map/exchange_0/pallas_call | solution.py:95
  85.6 2.3 copy.145
  92.6 17.8 %exchange_1.1 = bf16[8,256,256]{2,1,0:T(8,128)(2,1)} custom-call(bf16[256,256]{1,0:T(8,128)(2,1)} %pad_maximum_fusion.7.refs_0_), custom_call_target="tpu_custom_call" | custom-call | bytes 20971520 | tf_op jit(solution)/shard_map/exchange_1/pallas_call | solution.py:95
  116.1 2.1 copy-done.2
  120.4 10.7 %exchange_2.1 = bf16[4,256,256]{2,1,0:T(8,128)(2,1)} custom-call(bf16[256,256]{1,0:T(8,128)(2,1)} %copy.143.refs_0_), custom_call_target="tpu_custom_call" | custom-call | bytes 10485760 | tf_op jit(solution)/shard_map/exchange_2/pallas_call | solution.py:95
  132.5 2.5 multiply_reduce_fusion.3
  136.0 2.0 convolution_convert_fusion.3
  138.6 29.2 %exchange_3.1 = (bf16[8,128,1024]{2,1,0:T(8,128)(2,1)}, f32[8,8,128]{2,1,0:T(8,128)}) custom-call(bf16[8,128,1024]{2,1,0:T(8,128)(2,1)} %bitcast.222, f32[8,8,128]{2,1,0:T(8,128)} %broadcast_in_dim.37.refs_1_), custom_call_target="tpu_custom_call" | custom-call | bytes 42598400 | tf_op jit(solution)/shard_map/exchange_3/pallas_call | solution.py:95
  168.6 4.7 fusion.20
  173.3 4.0 multiply_convert_fusion.3
  180.0 2.3 convolution_convert_fusion
  182.4 2.0 pad_maximum_fusion
  184.5 35.6 %reduce-scatter.2.cloned.1.call-done = bf16[256,1536]{0,1:T(8,128)(2,1)} async-done(((bf16[1024,1536]{0,1:T(8,128)(2,1)}), bf16[256,1536]{0,1:T(8,128)(2,1)}) %reduce-scatter.2.cloned.1.call-update) | async-done | bytes 786448 | tf_op jit(solution)/shard_map/reduce_scatter | solution.py:319
  227.1 4.2 convolution_convert_fusion.1
  231.5 1.8 collective-permute-done
  236.7 2.3 broadcast_select_fusion
  239.0 5.6 convolution_convert_fusion.2
  245.2 65.3 %exchange_4.1 = (bf16[8,128,1024]{2,1,0:T(8,128)(2,1)}, bf16[8,128,1024]{2,1,0:T(8,128)(2,1)}, f32[8,8,128]{2,1,0:T(8,128)}) custom-call(bf16[8,128,1024]{2,1,0:T(8,128)(2,1)} %bitcast.237, bf16[8,128,1024]{2,1,0:T(8,128)(2,1)} %bitcast.236, f32[8,8,128]{2,1,0:T(8,128)} %broadcast_in_dim.38.refs_2_), custom_call_target="tpu_custom_call" | custom-call | bytes 84541440 | tf_op jit(solution)/shard_map/exchange_4/pallas_call | solution.py:95
  312.1 3.1 fusion.23.refs_0_
  315.3 49.9 %exchange_5.1 = (bf16[4,256,1024]{2,1,0:T(8,128)(2,1)}, f32[4,8,256]{2,1,0:T(8,128)}) custom-call(bf16[256,1024]{1,0:T(8,128)(2,1)} %fusion.23.refs_0_, f32[8,256]{1,0:T(8,128)} %fusion.27.refs_1_), custom_call_target="tpu_custom_call" | custom-call | bytes 42598400 | tf_op jit(solution)/shard_map/exchange_5/pallas_call | solution.py:95
  366.1 2.1 convert_reduce_fusion.2
  368.2 2.5 multiply_reduce_fusion.1
  372.2 4.8 fusion.14
  378.0 2.2 copy.152
  380.2 5.5 fusion
  385.7 4.6 fusion.2
  393.2 2.3 copy.151
  395.5 2.3 pad_maximum_fusion.4.refs_0_
  397.8 16.8 %exchange_6.1 = bf16[8,256,256]{2,1,0:T(8,128)(2,1)} custom-call(bf16[8,256,256]{2,1,0:T(8,128)(2,1)} %pad_maximum_fusion.4.refs_0_), custom_call_target="tpu_custom_call" | custom-call | bytes 20971520 | tf_op jit(solution)/shard_map/exchange_6/pallas_call | solution.py:95
  416.9 3.2 convolution_multiply_fusion.1
  423.0 2.1 copy.155
  425.1 2.0 copy.158
  429.2 1.9 concatenate.65
  431.7 2.1 convolution_convert_fusion.8
  433.8 2.1 convolution_convert_fusion.7
  438.1 3.8 concatenate.63.refs_2_
  441.9 3.2 fusion.24.refs_1_
  445.7 75.4 %exchange_7.1 = (bf16[4,256,1024]{2,1,0:T(8,128)(2,1)}, bf16[4,256,1024]{2,1,0:T(8,128)(2,1)}, bf16[32,32,896]{2,1,0:T(8,128)(2,1)}, f32[32,8,128]{2,1,0:T(8,128)}) custom-call(bf16[256,1024]{1,0:T(8,128)(2,1)} %get-tuple-element.100.refs_0_, bf16[256,1024]{1,0:T(8,128)(2,1)} %fusion.24.refs_1_, bf16[32,32,896]{2,1,0:T(8,128)(2,1)} %concatenate.63.refs_2_, ...), custom_call_target="tpu_custom_call" | custom-call | bytes 123207680 | tf_op jit(solution)/shard_map/exchange_7/pallas_call | solution.py:95
  521.2 2.4 reduce_sum.210.refs_0_
  525.1 16.5 %exchange_8.1 = (bf16[8,32,896]{2,1,0:T(8,128)(2,1)}, f32[32,8,128]{2,1,0:T(8,128)}) custom-call(bf16[32,896]{1,0:T(8,128)(2,1)} %reduce_sum.210.refs_0_, f32[8,128]{1,0:T(8,128)} %reduce_sum.211.refs_1_), custom_call_target="tpu_custom_call" | custom-call | bytes 11796480 | tf_op jit(solution)/shard_map/exchange_8/pallas_call | solution.py:95
  547.3 2.3 convert_reduce_fusion
  553.8 9.1 %convert_bitcast_fusion = f32[3,256,32,128]{3,1,0,2:T(8,128)} fusion(bf16[32,3,256,128]{3,2,1,0:T(8,128)(2,1)} %all-gather.8.cloned.1.call-done), kind=kLoop, calls=%fused_computation.1 | loop fusion | flops 3145728 | bytes 18874368 | tf_op jit(solution)/shard_map/convert_element_type | solution.py:330
  562.9 9.3 %slice_bitcast_fusion = (f32[256,32,128]{2,0,1:T(8,128)S(1)}, f32[256,32,128]{2,0,1:T(8,128)}, f32[256,32,128]{2,0,1:T(8,128)}) fusion(f32[3,256,32,128]{3,1,0,2:T(8,128)} %convert_bitcast_fusion), kind=kLoop, calls=%fused_computation.14 | loop fusion | bytes 25165824 | tf_op jit(solution)/shard_map/squeeze | solution.py:444
  572.3 6.8 %copy.166 = f32[256,32,128]{2,1,0:T(8,128)} copy(f32[256,32,128]{2,0,1:T(8,128)} %get-tuple-element.94) | data formatting | bytes 8388608
  579.0 4.7 copy.167
  583.7 4.4 copy.168
  (243 shorter events, 65.5 us)
Async XLA Ops:
  7.2 17.1 %copy-start = (bf16[256,32,128]{2,1,0:T(8,128)(2,1)S(1)}, bf16[256,32,128]{2,1,0:T(8,128)(2,1)}, u32[]{:S(2)}) copy-start(bf16[256,32,128]{2,1,0:T(8,128)(2,1)} %param.25) | copy-start | bytes 6291460
  7.2 125.3 %all-gather.4.cloned.1.call-start = ((), (), s32[]{:S(2)}) async-start(), calls=%async_computation.1 | async-start | bytes 2621440 | tf_op jit(solution)/shard_map/all_gather | solution.py:224
  21.7 3.5 copy-start.35
  21.7 146.8 %all-gather.6.cloned.1.call-start = ((), (), s32[]{:S(2)}) async-start(), calls=%async_computation.2 | async-start | bytes 3932160 | tf_op jit(solution)/shard_map/all_gather | solution.py:226
  24.1 2.6 copy-start.47
  24.1 2.6 copy-start.48
  24.2 3.2 copy-start.13
  25.3 110.3 %copy-start.32 = (pred[8,256]{1,0:T(8,128)(4,1)}, pred[8,256]{1,0:T(8,128)(4,1)S(1)}, u32[]{:S(2)}) copy-start(pred[8,256]{1,0:T(8,128)(4,1)S(1)} %compare_reduce_fusion) | copy-start | bytes 6148
  29.4 60.1 %copy-start.5 = (bf16[256,1024]{1,0:T(8,128)(2,1)S(1)}, bf16[256,1024]{1,0:T(8,128)(2,1)}, u32[]{:S(2)}) copy-start(bf16[256,1024]{1,0:T(8,128)(2,1)} %param.14) | copy-start | bytes 1572868
  85.5 4.8 copy-start.19
  85.6 4.9 copy-start.24
  87.9 3.4 copy-start.46
  87.9 132.2 %reduce-scatter.2.cloned.1.call-start = ((), (), s32[]{:S(2)}) async-start(), calls=%async_computation.3 | async-start | bytes 3932160 | tf_op jit(solution)/shard_map/reduce_scatter | solution.py:319
  90.3 22.1 %copy-start.39 = (f32[256]{0:T(256)}, f32[256]{0:T(256)S(1)}, u32[]{:S(2)}) copy-start(f32[256]{0:T(256)S(1)} %get-tuple-element.126) | copy-start | bytes 3076
  111.9 4.1 copy-start.11
  112.2 2.8 copy-start.10
  114.9 3.2 copy-start.2
  118.2 14.2 %copy-start.44 = (bf16[4,2,128]{2,1,0:T(2,128)(2,1)S(1)}, bf16[4,2,128]{2,1,0:T(2,128)(2,1)}, u32[]{:S(2)}) copy-start(bf16[4,2,128]{2,1,0:T(2,128)(2,1)} %get-tuple-element.120) | copy-start | bytes 6148
  118.2 14.2 %copy-start.36 = (s32[256,8]{0,1:T(8,128)S(1)}, s32[256,8]{0,1:T(8,128)}, u32[]{:S(2)}) copy-start(s32[256,8]{0,1:T(8,128)} %param.17) | copy-start | bytes 24580
  119.7 12.8 %copy-start.22 = (bf16[2,64,2,256]{3,1,2,0:T(8,128)(2,1)}, bf16[2,64,2,256]{3,1,2,0:T(8,128)(2,1)S(1)}, u32[]{:S(2)}) copy-start(bf16[2,64,2,256]{3,1,2,0:T(8,128)(2,1)S(1)} %fusion.25) | copy-start | bytes 393220
  132.5 2.7 copy-start.16
  135.5 232.6 %copy-start.30 = (f32[256]{0:T(256)}, f32[256]{0:T(256)S(1)}, u32[]{:S(2)}) copy-start(f32[256]{0:T(256)S(1)} %get-tuple-element.133) | copy-start | bytes 3076
  135.6 232.6 %copy-start.37 = (f32[256]{0:T(256)}, f32[256]{0:T(256)S(1)}, u32[]{:S(2)}) copy-start(f32[256]{0:T(256)S(1)} %fusion.59) | copy-start | bytes 3076
  168.6 4.7 copy-start.49
  177.3 2.7 copy-start.50
  184.4 369.5 %all-gather.8.cloned.1.call-start = ((), (), s32[]{:S(2)}) async-start(), calls=%async_computation.4 | async-start | bytes 7077888 | tf_op jit(solution)/shard_map/all_gather | solution.py:329
  222.3 9.2 %collective-permute-start.2 = (bf16[3,256,128]{2,1,0:T(8,128)(2,1)}, bf16[3,256,128]{2,1,0:T(8,128)(2,1)S(1)}, u32[]{:S(2)}, u32[]{:S(2)}) collective-permute-start(bf16[3,256,128]{2,1,0:T(8,128)(2,1)} %bitcast.95), channel_id=1, source_target_pairs={{0,3},{1,0},{2,1},{3,2},{4,7},{5,4},{6,5},{7,6},{8,11},{9,8},{10,9... | collective-permute-start | bytes 589832 | tf_op jit(solution)/shard_map/ppermute | solution.py:326
  223.7 7.8 %collective-permute-start.1 = (bf16[3,256,128]{2,1,0:T(8,128)(2,1)}, bf16[3,256,128]{2,1,0:T(8,128)(2,1)S(1)}, u32[]{:S(2)}, u32[]{:S(2)}) collective-permute-start(bf16[3,256,128]{2,1,0:T(8,128)(2,1)} %bitcast.92), channel_id=1, source_target_pairs={{0,2},{1,3},{2,0},{3,1},{4,6},{5,7},{6,4},{7,5},{8,10},{9,11},{10,... | collective-permute-start | bytes 589832 | tf_op jit(solution)/shard_map/ppermute | solution.py:326
  225.7 7.6 %collective-permute-start = (bf16[3,256,128]{2,1,0:T(8,128)(2,1)}, bf16[3,256,128]{2,1,0:T(8,128)(2,1)S(1)}, u32[]{:S(2)}, u32[]{:S(2)}) collective-permute-start(bf16[3,256,128]{2,1,0:T(8,128)(2,1)} %bitcast.89), channel_id=1, source_target_pairs={{0,1},{1,2},{2,3},{3,0},{4,5},{5,6},{6,7},{7,4},{8,9},{9,10},{10,1... | collective-permute-start | bytes 589832 | tf_op jit(solution)/shard_map/ppermute | solution.py:326
  236.7 2.3 copy-start.53
  245.2 66.1 %copy-start.33 = (pred[8,256]{1,0:T(8,128)(4,1)S(1)}, pred[8,256]{1,0:T(8,128)(4,1)}, u32[]{:S(2)}) copy-start(pred[8,256]{1,0:T(8,128)(4,1)} %copy-done.32) | copy-start | bytes 6148
  366.0 4.7 copy-start.42
  368.2 2.5 copy-start.14
  416.8 3.3 copy-start.21
  416.8 3.3 copy-start.20
  423.0 4.1 copy-start.31
  423.0 4.1 copy-start.38
  423.0 4.1 copy-start.43
  428.1 7.8 %copy-start.7 = (bf16[1024,256]{1,0:T(8,128)(2,1)S(1)}, bf16[1024,256]{1,0:T(8,128)(2,1)}, u32[]{:S(2)}) copy-start(bf16[1024,256]{1,0:T(8,128)(2,1)} %copy.155) | copy-start | bytes 1572868
  431.7 5.3 copy-start.15
  431.7 5.3 copy-start.23
  438.1 3.8 copy-start.29
  438.1 3.8 copy-start.34
  547.3 2.5 copy-start.12
  550.2 2.5 copy-start.41
  550.2 2.5 copy-start.45
  572.3 6.8 %copy-start.4 = (f32[256,32,128]{2,0,1:T(8,128)S(1)}, f32[256,32,128]{2,0,1:T(8,128)}, u32[]{:S(2)}) copy-start(f32[256,32,128]{2,0,1:T(8,128)} %get-tuple-element.93) | copy-start | bytes 12582916
  583.7 4.4 copy-start.1
  (14 other events, 19.1 us)
Sparse Core Ops, SparseCore 0:
  21.9 48.4 all-gather.3
  88.1 41.8 all-gather.5
  184.5 35.6 reduce-scatter.1
  239.1 148.3 all-gather.7

commit v2 on v1

--- a/solution.py
+++ b/solution.py
@@ -60,10 +60,16 @@
     for at, (axes, mode) in enumerate(plan):
         mine = flat(axes, place(axes, 0))
         for step in range(1, math.prod(sizes[a] for a in axes)):
-            peer = place(axes, step)
+            if mode in "fb":
+                peer = place(axes, step if mode == "f" else sizes[axes[0]] - step)
+                source, slot = ins[at].at[step], step
+            else:
+                peer = place(axes, step)
+                source = ins[at] if mode == "g" else ins[at].at[flat(axes, peer)]
+                slot = mine
             copy = pltpu.make_async_remote_copy(
-                src_ref=ins[at] if mode == "g" else ins[at].at[flat(axes, peer)],
-                dst_ref=outs[at].at[mine],
+                src_ref=source,
+                dst_ref=outs[at].at[slot],
                 send_sem=send_sem.at[at, step],
                 recv_sem=recv_sem.at[at, step],
                 device_id=peer,
@@ -71,6 +77,8 @@
             )
             copy.start()
             copies.append(copy)
+        if mode in "fb":
+            mine = 0
         own = pltpu.make_async_copy(
             ins[at] if mode == "g" else ins[at].at[mine], outs[at].at[mine], self_sem.at[at]
         )
@@ -108,6 +116,32 @@
     )(*arrays)
 
 
+def spread_kernel(n_ctx, n_tp, pieces_ref, *out_refs):
+    experts = n_ctx * n_tp
+    tp_at = lax.axis_index("tp")
+    depth = pieces_ref.shape[2]
+    for which, out_ref in enumerate(out_refs):
+        for place in range(experts):
+            step = place % n_tp
+            expert = place - step + lax.rem(tp_at + n_tp - step, n_tp)
+            out_ref[pl.ds(expert, depth, stride=experts), :] = pieces_ref[place, which].astype(f32)
+
+
+def spread(pieces, n_ctx, n_tp):
+    experts, count, depth, ff = pieces.shape
+    block = 64
+    outs = pl.pallas_call(
+        functools.partial(spread_kernel, n_ctx, n_tp),
+        grid=(depth // block,),
+        out_shape=[jax.ShapeDtypeStruct((depth * experts, ff), f32)] * count,
+        in_specs=[pl.BlockSpec((experts, count, block, ff), lambda i: (0, 0, i, 0))],
+        out_specs=[pl.BlockSpec((block * experts, ff), lambda i: (i, 0))] * count,
+        compiler_params=pltpu.CompilerParams(vmem_limit_bytes=32 * 1024 * 1024),
+        name="spread",
+    )(pieces)
+    return [out.reshape(depth, experts, ff) for out in outs]
+
+
 def rope_tables(places):
     frequencies = jnp.exp(
         jnp.arange(HEAD_SIZE // 2, dtype=jnp.float32) * (-2.0 * math.log(rope_base) / HEAD_SIZE)
@@ -175,16 +209,27 @@
     chosen = jnp.any(
         expert_ids[:, :, None] == jnp.arange(experts, dtype=jnp.int32)[None, None, :], axis=1
     )
-    mine = jnp.arange(n_ctx, dtype=jnp.int32) * per_ctx + tp_at
+    ctx_order = lax.rem(ctx_at + jnp.arange(n_ctx, dtype=jnp.int32), n_ctx)
+    mine = ctx_order * per_ctx + tp_at
     chosen_mine = jnp.any(expert_ids[None, :, :] == mine[:, None, None], axis=2)
     earlier = jnp.arange(rows)[:, None] < jnp.arange(rows)[None, :]
     rank = mm(chosen_mine.astype(bf16), earlier.astype(bf16))
     slots = jnp.arange(CAP, dtype=f32)
     picks = (chosen_mine[:, None, :] & (rank[:, None, :] == slots[None, :, None])).astype(bf16)
     picks_flat = picks.reshape(n_ctx * CAP, rows)
-    grads_sent = mm(picks_flat, cotangent).astype(bf16).reshape(n_ctx, CAP, width)
+
+    def shifted(chunks, axis, direction):
+        n = chunks.shape[0]
+        return jnp.stack(
+            [chunks[0]]
+            + [
+                lax.ppermute(chunks[k], axis, [(s, (s + direction * k) % n) for s in range(n)])
+                for k in range(1, n)
+            ]
+        )
 
     first = ctx_at * per_ctx
+    tp_order = lax.rem(tp_at + jnp.arange(n_tp, dtype=jnp.int32), n_tp)
     own_slices = jnp.stack(
         [
             lax.dynamic_slice_in_dim(w, first, per_ctx, 1).transpose(1, 0, 2)
@@ -201,26 +246,29 @@
         axis=0,
     )
     router_pad = jnp.pad(w_router, ((0, 0), (0, 128 - experts)))
-    query_w, key_w, value_w, gains_all, router_all, expert_slices, grads_got = send(
+    grads_sent = mm(picks_flat, cotangent).astype(bf16).reshape(n_ctx, CAP, width)
+    query_w, key_w, value_w, output_w, gains_all, router_all, expert_slices, grad_rows = send(
         0,
         (("fsdp",), "g", w_query),
         (("fsdp",), "g", key_weight),
         (("fsdp",), "g", value_weight),
+        (("fsdp",), "g", w_output),
         (("fsdp",), "g", gains),
         (("fsdp",), "g", router_pad),
         (("tp",), "a", own_slices),
-        (("ctx",), "a", grads_sent),
+        (("ctx",), "f", grads_sent),
     )
     query_w = query_w.reshape(width, -1)
     key_w = key_w.reshape(width, -1)
     value_w = value_w.reshape(width, -1)
+    output_w = output_w.reshape(width, -1)
     lines = depth // 128
     gain_one = gains_all[:, :lines].reshape(width).astype(f32)
     gain_two = gains_all[:, lines : 2 * lines].reshape(width).astype(f32)
     router_w = router_all.reshape(width, 128)[:, :experts]
-    grad_rows = grads_got.reshape(n_ctx * CAP, width)
-
-    output_w = lax.all_gather(w_output, "fsdp", axis=0, tiled=True)
+
+    grad_rows = grad_rows.reshape(n_ctx * CAP, width)
+
     output_full = lax.all_gather(output_w, "tp", axis=1, tiled=True)
     expert_cat = expert_slices.transpose(2, 1, 0, 3).reshape(depth, 3 * n_tp * ff)
     expert_w = lax.all_gather(expert_cat, "fsdp", axis=0, tiled=True)
@@ -281,12 +329,13 @@
     probs_mine = lax.dynamic_index_in_dim(
         gate_probs.T.reshape(n_ctx, per_ctx, rows), tp_at, 1, keepdims=False
     )
+    probs_mine = jnp.take(probs_mine, ctx_order, axis=0)
     probs_sent = jnp.sum(picks.astype(f32) * probs_mine[:, None, :], axis=2)
     rows_sent = mm(picks_flat, normed_two).astype(bf16).reshape(n_ctx, CAP, width)
     rows_got, probs_got = send(
         3,
-        (("ctx",), "a", rows_sent),
-        (("ctx",), "a", jnp.broadcast_to(probs_sent[:, None, :], (n_ctx, 8, CAP))),
+        (("ctx",), "f", rows_sent),
+        (("ctx",), "f", jnp.broadcast_to(probs_sent[:, None, :], (n_ctx, 8, CAP))),
     )
 
     norm_rows = rows_got.reshape(n_ctx * CAP, width)
@@ -302,55 +351,59 @@
     gate_in = act_grad * up_pre * sigmoid_gate * (1.0 + gate_pre * (1.0 - sigmoid_gate))
     both_in = jnp.concatenate([gate_in, act_grad * silu_gate], axis=1).astype(bf16)
     weighted = (probs_col * activation).astype(bf16)
-    mixed = contract_cols(weighted, down_w).astype(bf16)
+    mixed = contract_cols(weighted, down_w).astype(bf16).reshape(n_ctx, CAP, width)
     norm_grad = contract_cols(both_in, gate_up_w).astype(bf16)
     gate_grad_rows = jnp.broadcast_to(gate_grad_rows.reshape(n_ctx, 1, CAP), (n_ctx, 8, CAP))
     grad_gate_up = contract_rows(norm_rows, both_in)
     grad_down = contract_rows(grad_rows, weighted) * branch_scale
     expert_grad = jnp.concatenate([grad_gate_up, grad_down], axis=1).astype(bf16)
-
-    norm_grad_got, mixed_got, gate_grad_got = send(
+    expert_grad = lax.psum_scatter(expert_grad, "fsdp", scatter_dimension=0, tiled=True)
+
+    norm_grad_got, gate_grad_got, mixed_got = send(
         4,
-        (("ctx",), "a", norm_grad.reshape(n_ctx, CAP, width)),
-        (("ctx",), "a", mixed.reshape(n_ctx, CAP, width)),
-        (("ctx",), "a", gate_grad_rows),
-    )
-
-    expert_grad = lax.psum_scatter(expert_grad, "fsdp", scatter_dimension=0, tiled=True)
-    expert_grad = expert_grad.reshape(depth, 3, n_tp, ff).transpose(2, 1, 0, 3)
-    pieces = [lax.dynamic_index_in_dim(expert_grad, tp_at, 0, keepdims=False)]
-    for step in range(1, n_tp):
-        piece = lax.dynamic_index_in_dim(
-            expert_grad, lax.rem(tp_at + step, n_tp), 0, keepdims=False
-        )
-        pieces.append(lax.ppermute(piece, "tp", [(s, (s + step) % n_tp) for s in range(n_tp)]))
-    pieces = jnp.stack(pieces)
-    pieces = jnp.take(pieces, lax.rem(tp_at - jnp.arange(n_tp) + n_tp, n_tp), axis=0)
-    expert_all = lax.all_gather(pieces, "ctx", axis=0, tiled=True)
-    expert_all = expert_all.transpose(1, 2, 0, 3).astype(f32)
-
+        (("ctx",), "b", norm_grad.reshape(n_ctx, CAP, width)),
+        (("ctx",), "b", gate_grad_rows),
+        (("ctx",), "b", mixed),
+    )
+
+    quarter = rows // n_tp
     norm_grad_part = contract_rows(picks_flat, norm_grad_got.reshape(n_ctx * CAP, width))
-    mixed_part = contract_rows(picks_flat, mixed_got.reshape(n_ctx * CAP, width)).astype(bf16)
     gate_grad_part = jnp.sum(picks.astype(f32) * gate_grad_got[:, 0, :, None], axis=1)
     norm_grad_parts, gate_grad_parts = send(
-        5, (("tp",), "g", norm_grad_part.astype(bf16)), (("tp",), "g", gate_grad_part)
-    )
-    gate_grads = gate_grad_parts.transpose(2, 1, 0).reshape(rows, experts)
+        5,
+        (("tp",), "a", norm_grad_part.astype(bf16).reshape(n_tp, quarter, width)),
+        (("tp",), "g", gate_grad_part),
+    )
+
+    expert_grad, _ = lax.optimization_barrier((expert_grad, gate_grad_parts))
+    expert_grad = expert_grad.reshape(depth, 3, n_tp, ff).transpose(2, 1, 0, 3)
+    pieces = shifted(jnp.take(expert_grad, tp_order, axis=0), "tp", 1)
+    expert_all = lax.all_gather(pieces, "ctx", axis=0, tiled=True)
+
+    def quarter_of(array):
+        return lax.dynamic_slice_in_dim(array, tp_at * quarter, quarter, 0)
+
+    back_order = lax.rem(jnp.arange(n_ctx, dtype=jnp.int32) + n_ctx - ctx_at, n_ctx)
+    gate_grads = jnp.take(gate_grad_parts, back_order, axis=1)
+    gate_grads = gate_grads.transpose(2, 1, 0).reshape(rows, experts)
     route_grad = gate_probs * (
         gate_grads - jnp.sum(gate_probs * gate_grads, axis=-1, keepdims=True)
     )
     grad_router = contract_rows(normed_two.astype(f32), route_grad, highest)
-    router_back = contract_cols(route_grad, router_w.astype(f32), highest)
-    out_grad = cotangent.astype(f32)
+    router_back = contract_cols(quarter_of(route_grad), router_w.astype(f32), highest)
     normed_grad = jnp.sum(norm_grad_parts.astype(f32), axis=0) + router_back
     weighted_two = normed_grad * gain_two
-    grad_ffn_gain = jnp.sum(normed_grad * residual * scale_two, axis=0)
+    residual_own, scale_two_own = quarter_of(residual), quarter_of(scale_two)
+    grad_ffn_part = jnp.sum(normed_grad * residual_own * scale_two_own, axis=0)
     residual_grad = (
-        out_grad
-        + scale_two * weighted_two
-        - residual * scale_two**3 * jnp.mean(weighted_two * residual, axis=-1, keepdims=True)
-    )
-    attn_in = (branch_scale * residual_grad).astype(bf16)
+        quarter_of(cotangent).astype(f32)
+        + scale_two_own * weighted_two
+        - residual_own
+        * scale_two_own**3
+        * jnp.mean(weighted_two * residual_own, axis=-1, keepdims=True)
+    )
+    (attn_in,) = send(6, (("tp",), "g", (branch_scale * residual_grad).astype(bf16)))
+    attn_in = attn_in.reshape(rows, width)
     grad_output = contract_rows(attn_in, attended)
     attended_grad = mm(attn_in, output_w).astype(bf16)
 
@@ -376,7 +429,7 @@
         ],
         axis=1,
     ).astype(bf16)
-    (pair_got,) = send(6, (("ctx",), "a", pair_grads.reshape(n_ctx, rows, 2 * pair_width)))
+    (pair_got,) = send(7, (("ctx",), "a", pair_grads.reshape(n_ctx, rows, 2 * pair_width)))
     pair_owned = jnp.sum(pair_got.astype(f32), axis=0)
     query_grad = turn(query_grad_rot, cosine_table, -sine_table).astype(bf16)
     key_grad = turn(pair_owned[:, :pair_width], cosine_table, -sine_table).astype(bf16)
@@ -390,58 +443,62 @@
     grad_query = contract_rows(normed_one, query_grad)
     grad_key = contract_rows(normed_one, key_grad)
     grad_value = contract_rows(normed_one, value_grad)
+    mixed_part = contract_rows(picks_flat, mixed_got.reshape(n_ctx * CAP, width)).astype(bf16)
 
     n_rows = n_fsdp * n_ctx
     share = width // n_rows
-    side = jnp.concatenate(
-        [grad_router, grad_ffn_gain[:, None], jnp.zeros((width, 128 - experts - 1), f32)], axis=1
-    )
+    side = jnp.pad(grad_router, ((0, 0), (0, 128 - experts)))
     small = jnp.concatenate([grad_query, grad_key, grad_value, grad_output, side], axis=1)
     small = small.astype(bf16).reshape(n_rows, share, -1)
-    gain_chunks = jnp.broadcast_to(
-        jnp.pad(grad_gain_part.reshape(n_rows, 1, share), ((0, 0), (0, 0), (0, 128 - share))),
-        (n_rows, 8, 128),
-    )
+    gain_parts = jnp.stack([grad_gain_part, grad_ffn_part]).reshape(2, n_rows, share)
+    gain_chunks = jnp.pad(gain_parts.transpose(1, 0, 2), ((0, 0), (0, 6), (0, 128 - share)))
     one_parts, mixed_parts, small_got, gain_got = send(
-        7,
-        (("tp",), "g", normed_one_part.astype(bf16)),
-        (("tp",), "g", mixed_part),
+        8,
+        (("tp",), "a", normed_one_part.astype(bf16).reshape(n_tp, quarter, width)),
+        (("tp",), "a", mixed_part.reshape(n_tp, quarter, width)),
         (("fsdp", "ctx"), "a", small),
         (("fsdp", "ctx"), "a", gain_chunks),
     )
     small_sum = jnp.sum(small_got.astype(f32), axis=0).astype(bf16)
     gain_sum = jnp.sum(gain_got, axis=0)
-    small_all, gain_all = send(
-        8, (("ctx",), "g", small_sum), (("ctx", "tp"), "g", gain_sum)
-    )
-    small_all = small_all.reshape(depth, -1).astype(f32)
-    gain_all = gain_all[:, 0, :share].reshape(n_ctx, n_tp, share)
-    grad_attn_gain = jnp.sum(gain_all, axis=1).reshape(depth)
-
-    output = residual + branch_scale * jnp.sum(mixed_parts.astype(f32), axis=0)
+    output = residual_own + branch_scale * jnp.sum(mixed_parts.astype(f32), axis=0)
     normed_one_grad = jnp.sum(one_parts.astype(f32), axis=0)
     weighted_one = normed_one_grad * gain_one
+    hidden_own, scale_one_own = quarter_of(hidden_in), quarter_of(scale_one)
     input_grad = (
         residual_grad
-        + scale_one * weighted_one
-        - hidden_in * scale_one**3 * jnp.mean(weighted_one * hidden_in, axis=-1, keepdims=True)
-    )
+        + scale_one_own * weighted_one
+        - hidden_own
+        * scale_one_own**3
+        * jnp.mean(weighted_one * hidden_own, axis=-1, keepdims=True)
+    )
+    small_all, gain_all, output, input_grad = send(
+        9,
+        (("ctx",), "g", small_sum),
+        (("ctx", "tp"), "g", gain_sum),
+        (("tp",), "g", output.astype(bf16)),
+        (("tp",), "g", input_grad.astype(bf16)),
+    )
+    small_all = small_all.reshape(depth, -1).astype(f32)
+    gain_all = jnp.sum(gain_all[:, :2, :share].reshape(n_ctx, n_tp, 2, share), axis=1)
+    gain_all = gain_all.transpose(1, 0, 2).reshape(2, depth)
+    grad_gate, grad_up, grad_down = spread(expert_all, n_ctx, n_tp)
     q_end = queries.shape[1]
     k_end, v_end = q_end + pair_width, q_end + 2 * pair_width
     o_end = v_end + attended.shape[1]
     return (
-        output.astype(bf16),
-        input_grad.astype(bf16),
-        grad_attn_gain,
+        output.reshape(rows, width),
+        input_grad.reshape(rows, width),
+        gain_all[0],
         small_all[:, :q_end],
         small_all[:, q_end:k_end],
         small_all[:, k_end:v_end],
         small_all[:, v_end:o_end],
-        small_all[:, o_end + experts],
+        gain_all[1],
         small_all[:, o_end : o_end + experts],
-        expert_all[0],
-        expert_all[1],
-        expert_all[2],
+        grad_gate,
+        grad_up,
+        grad_down,
     )
 
 

time: 599 us -> 478 us (0.80)
  Pallas kernels: 338 us -> 300 us
  local copies, waits for them, and re-layouts: 77.2 us -> 39.7 us
  waiting for transfers between devices: 37.5 us -> 7.27 us
  blocking collectives: 14.5 us -> 0 us
    pallas_call x9 -> x10, Pallas kernels: 338 us -> 286 us  [exchange(): pl.pallas_call(functools.partial(exchange_kernel, plan, sizes), out_shape...]
    reduce_scatter x1, waiting for transfers between devices: 35.6 us -> 0.02 us  [local(): lax.psum_scatter(expert_grad, 'fsdp', scatter_dimension=0, tiled=True)]
    unnamed x125 -> x158, local copies, waits for them, and re-layouts: 29.2 us -> 12.8 us
    pallas_call x0 -> x1, Pallas kernels: none -> 14.5 us  [spread(): pl.pallas_call(functools.partial(spread_kernel, n_ctx, n_tp), grid=(depth...]
    all_gather x1 -> x0, blocking collectives: 14.5 us -> none  [local(): output_w = lax.all_gather(w_output, 'fsdp', axis=0, tiled=True)]
    squeeze x1 -> x2, local copies, waits for them, and re-layouts: 9.34 us -> 1.28 us  [the longest x1 0.64 us: local(): gain_all[0]]
    convert_element_type x1 -> x2, other arithmetic: 9.06 us -> 2.93 us  [the longest x1 1.84 us: local(): (branch_scale * residual_grad).astype(bf16)]
  transfers between devices with their start and end apart: 7 -> 7, of which waited for: 2 -> 2; matrix products, arithmetic and copies ran while one was open for 21% -> 22% of each run, Pallas kernels for 57% -> 52%
where the time goes in v2:
time: 478 us; the launch traced here: 469 us
  Pallas kernels  300 us (63%)
  matrix products  64 us (13%)
  local copies, waits for them, and re-layouts  39.7 us (8%)
  other arithmetic  38.2 us (8%)
  between operations  15.3 us (3%)
  waiting for transfers between devices  7.27 us (2%)
    pallas_call x10, Pallas kernels, exchange(): pl.pallas_call(functools.partial(exchange_kernel, plan, sizes), out_shape...  286 us
    dot_general x10, matrix products, mm(): return jnp.dot(left, right, preferred_element_type=f32)  15.8 us
    dot_general x7, matrix products, contract_cols(): lax.dot_general(left, right, (((1,), (1,)), ((), ())), precision=precisio...  15 us
    pallas_call x1, Pallas kernels, spread(): pl.pallas_call(functools.partial(spread_kernel, n_ctx, n_tp), grid=(depth...  14.5 us
    unnamed x158, local copies, waits for them, and re-layouts  12.8 us
    dot_general x9, matrix products, contract_rows(): lax.dot_general(left, right, (((0,), (0,)), ((), ())), precision=precisio...  12.4 us
  transfers between devices with their start and end apart: 7, of which 2 were waited for; matrix products, arithmetic and copies ran while one was open for 22% of the time, Pallas kernels for 52%

profile of v2, /device:TPU:1, one launch (start us, length us, event | category | flops | bytes accessed | tf_op | source)
XLA Modules:
  0.0 468.6 jit_solution(10197281054191790259)
XLA Ops:
  8.3 1.5 constant_dynamic-slice_fusion.1
  11.4 2.0 convolution_convert_fusion.4
  15.1 40.8 %exchange_0.1 = (bf16[4,256,256]{2,1,0:T(8,128)(2,1)}, bf16[4,256,128]{2,1,0:T(8,128)(2,1)}, bf16[4,256,128]{2,1,0:T(8,128)(2,1)}, bf16[4,256,256]{2,1,0:T(8,128...) custom-call(bf16[256,256]{1,0:T(8,128)(2,1)} %refs_0_.1, ...), custom_call_target="tpu_custom_call" | custom-call | bytes 94699520 | tf_op jit(solution)/shard_map/exchange_0/pallas_call | solution.py:103
  55.9 2.4 copy.128
  62.9 24.2 %exchange_1.1 = bf16[8,256,256]{2,1,0:T(8,128)(2,1)} custom-call(bf16[256,256]{1,0:T(8,128)(2,1)} %pad_maximum_fusion.7.refs_0_), custom_call_target="tpu_custom_call" | custom-call | bytes 20971520 | tf_op jit(solution)/shard_map/exchange_1/pallas_call | solution.py:103
  89.3 4.8 %fusion.78 = (f32[2,2,256]{2,1,0:T(2,128)S(1)}, f32[2,2,256,2048]{2,3,1,0:T(8,128)}) fusion(bf16[2048,2,64,1]{0,2,3,1:T(8,128)(2,1)S(1)} %bitcast.246, bf16[256,2,2,64]{0,3,2,1:T(8,128)(2,1)S(1)} %bitcast.281, pred[256,2048]{0,1:T(8,128)(4,1)S(1)} %fusion.18), kind=kOutput, calls=%fused_computation.217 | convolution fusion | flops 274725888 | bytes 9572352 | tf_op jit(solution)/shard_map/rkgd,skd->kgrs/dot_general | solution.py:304
  94.4 4.7 %fusion.3 = f32[2,2,256]{2,1,0:T(2,128)S(1)} fusion(f32[2,2,256,2048]{2,3,1,0:T(8,128)} %get-tuple-element.107, f32[2,2,256]{2,1,0:T(2,128)S(1)} %get-tuple-element.106), kind=kLoop, calls=%fused_computation.12 | loop fusion | flops 4193280 | bytes 8396800 | tf_op jit(solution)/shard_map/reduce_sum | solution.py:312
  100.3 1.5 fusion.29
  102.6 14.0 %exchange_2.1 = bf16[4,256,256]{2,1,0:T(8,128)(2,1)} custom-call(bf16[256,256]{1,0:T(8,128)(2,1)} %copy.126.refs_0_), custom_call_target="tpu_custom_call" | custom-call | bytes 10485760 | tf_op jit(solution)/shard_map/exchange_2/pallas_call | solution.py:103
  116.7 2.0 copy.127
  119.9 2.7 multiply_reduce_fusion.2
  124.5 2.0 convolution_convert_fusion.3
  127.1 29.5 %exchange_3.1 = (bf16[8,128,1024]{2,1,0:T(8,128)(2,1)}, f32[8,8,128]{2,1,0:T(8,128)}) custom-call(bf16[8,128,1024]{2,1,0:T(8,128)(2,1)} %bitcast.238, f32[8,8,128]{2,1,0:T(8,128)} %broadcast_in_dim.50.refs_1_), custom_call_target="tpu_custom_call" | custom-call | bytes 42598400 | tf_op jit(solution)/shard_map/exchange_3/pallas_call | solution.py:103
  157.4 4.7 %fusion.20 = f32[1024,1024]{0,1:T(8,128)S(1)} fusion(bf16[1024,1024]{1,0:T(8,128)(2,1)} %bitcast.316, bf16[1024,1536]{0,1:T(8,128)(2,1)} %all-gather.6.cloned.1.call-done), kind=kOutput, calls=%fused_computation.42 | convolution fusion | flops 2147483648 | bytes 8388608 | tf_op jit(solution)/shard_map/dot_general | solution.py:181
  162.2 4.0 multiply_convert_fusion.3
  168.9 2.3 convolution_convert_fusion
  171.2 2.0 pad_maximum_fusion
  173.4 4.3 convolution_convert_fusion.1
  177.7 3.8 convolution_convert_fusion.2
  182.1 52.1 %exchange_4.1 = (bf16[8,128,1024]{2,1,0:T(8,128)(2,1)}, f32[8,8,128]{2,1,0:T(8,128)}, bf16[8,128,1024]{2,1,0:T(8,128)(2,1)}) custom-call(bf16[8,128,1024]{2,1,0:T(8,128)(2,1)} %bitcast.254, f32[8,8,128]{2,1,0:T(8,128)} %broadcast_in_dim.54.refs_1_, bf16[8,128,1024]{2,1,0:T(8,128)(2,1)} %bitcast.253), custom_call_target="tpu_custom_call" | custom-call | bytes 84541440 | tf_op jit(solution)/shard_map/exchange_4/pallas_call | solution.py:103
  235.8 3.1 fusion.24
  238.9 11.4 %exchange_5.1 = (bf16[4,64,1024]{2,1,0:T(8,128)(2,1)}, f32[4,8,256]{2,1,0:T(8,128)}) custom-call(bf16[4,64,1024]{2,1,0:T(8,128)(2,1)} %bitcast.288, f32[8,256]{1,0:T(8,128)} %fusion.31.refs_1_), custom_call_target="tpu_custom_call" | custom-call | bytes 11141120 | tf_op jit(solution)/shard_map/exchange_5/pallas_call | solution.py:103
  250.3 2.3 copy.144
  252.6 1.8 gather_fusion.2
  255.2 1.4 collective-permute-start.1
  256.6 1.6 collective-permute-start
  258.2 4.1 collective-permute-done.2
  262.3 3.1 collective-permute-done
  272.0 2.1 multiply_reduce_fusion.5
  274.1 1.8 multiply_convert_fusion.6
  276.0 15.9 %exchange_6.1 = bf16[4,64,1024]{2,1,0:T(8,128)(2,1)} custom-call(bf16[64,1024]{1,0:T(8,128)(2,1)} %get-tuple-element.72.refs_0_), custom_call_target="tpu_custom_call" | custom-call | bytes 10485760 | tf_op jit(solution)/shard_map/exchange_6/pallas_call | solution.py:103
  291.9 1.4 convolution_convert_fusion.9
  293.3 4.9 %fusion.14 = bf16[2,64,2048]{2,1,0:T(8,128)(2,1)S(1)} fusion(bf16[256,2,2,64]{0,3,2,1:T(8,128)(2,1)S(1)} %bitcast.263, f32[2,2,256,2048]{2,3,1,0:T(8,128)} %get-tuple-element.107, f32[2,2,256]{2,1,0:T(2,128)S(1)} %copy-done.35), kind=kOutput, calls=%fused_computation.22 | convolution fusion | flops 272891904 | bytes 9048064 | tf_op jit(solution)/shard_map/kgrs,rkgd->skd/dot_general | solution.py:412
  299.5 5.2 %fusion = (f32[2,2,256]{2,1,0:T(2,128)S(1)}, f32[2,2048,256,2]{2,1,3,0:T(8,128)S(1)}) fusion(f32[2,2,256,2048]{2,3,1,0:T(8,128)} %get-tuple-element.107, f32[2,2,256]{2,1,0:T(2,128)S(1)} %copy-done.35, bf16[2048,2,64,1]{0,2,3,1:T(8,128)(2,1)S(1)} %bitcast.249, bf16[256,2,2,64]{0,3,2,1:T(8,128)(2,1)S(1)} %bitcast.264), kind=kOutput, calls=%fused_computation.5 | convolution fusion | flops 274725888 | bytes 17440768 | tf_op jit(solution)/shard_map/rkgd,skd->kgrs/dot_general | solution.py:415
  304.8 4.6 fusion.2
  309.5 1.4 fusion.13
  313.7 27.1 %exchange_7.1 = bf16[8,256,256]{2,1,0:T(8,128)(2,1)} custom-call(bf16[8,256,256]{2,1,0:T(8,128)(2,1)} %pad_maximum_fusion.4.refs_0_), custom_call_target="tpu_custom_call" | custom-call | bytes 20971520 | tf_op jit(solution)/shard_map/exchange_7/pallas_call | solution.py:103
  340.8 1.4 convert_reduce_fusion
  342.9 3.1 convolution_multiply_fusion.1
  347.3 1.5 multiply_reduce_fusion.1
  357.1 1.6 fusion.25
  358.6 44.7 %exchange_8.1 = (bf16[4,64,1024]{2,1,0:T(8,128)(2,1)}, bf16[4,64,1024]{2,1,0:T(8,128)(2,1)}, bf16[32,32,896]{2,1,0:T(8,128)(2,1)}, f32[32,8,128]{2,1,0:T(8,128)}) custom-call(bf16[4,64,1024]{2,1,0:T(8,128)(2,1)} %bitcast.257, bf16[4,64,1024]{2,1,0:T(8,128)(2,1)} %bitcast.291, bf16[32,32,896]{2,1,0:T(8,128)(2,1)} %constant_dynamic-update-slice_fusion.refs_2_, ...), custom_call_target="tpu_custom_call" | custom-call | bytes 60293120 | tf_op jit(solution)/shard_map/exchange_8/pallas_call | solution.py:103
  403.4 2.5 reduce_sum.207.refs_0_
  405.9 1.5 reduce_sum.208.refs_1_
  408.9 1.6 add_convert_fusion.refs_2_
  411.3 26.1 %exchange_9.1 = (bf16[8,32,896]{2,1,0:T(8,128)(2,1)}, f32[32,8,128]{2,1,0:T(8,128)}, bf16[4,64,1024]{2,1,0:T(8,128)(2,1)}, bf16[4,64,1024]{2,1,0:T(8,128)(2,1)}) custom-call(bf16[32,896]{1,0:T(8,128)(2,1)} %reduce_sum.207.refs_0_, f32[8,128]{1,0:T(8,128)} %reduce_sum.208.refs_1_, bf16[64,1024]{1,0:T(8,128)(2,1)} %add_convert_fusion.refs_2_, ...), custom_call_target="tpu_custom_call" | custom-call | bytes 32768000 | tf_op jit(solution)/shard_map/exchange_9/pallas_call | solution.py:103
  443.0 2.8 copy-done.2
  445.8 14.5 %spread.1 = (f32[8192,128]{1,0:T(8,128)}, f32[8192,128]{1,0:T(8,128)}, f32[8192,128]{1,0:T(8,128)}) custom-call(bf16[32,3,256,128]{3,2,1,0:T(8,128)(2,1)S(1)} %copy-done.2), custom_call_target="tpu_custom_call" | custom-call | tf_op jit(solution)/shard_map/spread/pallas_call | solution.py:133
  (287 shorter events, 53.2 us)
Async XLA Ops:
  7.2 112.7 %all-gather.4.cloned.1.call-start = ((), (), s32[]{:S(2)}) async-start(), calls=%async_computation.1 | async-start | bytes 2621440 | tf_op jit(solution)/shard_map/all_gather | solution.py:272
  10.2 4.8 %copy-start.36 = (pred[8,256]{1,0:T(8,128)(4,1)}, pred[8,256]{1,0:T(8,128)(4,1)S(1)}, u32[]{:S(2)}) copy-start(pred[8,256]{1,0:T(8,128)(4,1)S(1)} %compare_reduce_fusion) | copy-start | bytes 6148
  55.8 5.1 %copy-start.20 = (bf16[4,256,128]{2,1,0:T(8,128)(2,1)S(1)}, bf16[4,256,128]{2,1,0:T(8,128)(2,1)}, u32[]{:S(2)}) copy-start(bf16[4,256,128]{2,1,0:T(8,128)(2,1)} %get-tuple-element.40) | copy-start | bytes 786436
  55.9 5.2 %copy-start.31 = (bf16[4,256,128]{2,1,0:T(8,128)(2,1)S(1)}, bf16[4,256,128]{2,1,0:T(8,128)(2,1)}, u32[]{:S(2)}) copy-start(bf16[4,256,128]{2,1,0:T(8,128)(2,1)} %get-tuple-element.41) | copy-start | bytes 786436
  55.9 101.5 %all-gather.6.cloned.1.call-start = ((), (), s32[]{:S(2)}) async-start(), calls=%async_computation.2 | async-start | bytes 3932160 | tf_op jit(solution)/shard_map/all_gather | solution.py:274
  58.3 192.0 %reduce-scatter.2.cloned.1.call-start = ((), (), s32[]{:S(2)}) async-start(), calls=%async_computation.3 | async-start | bytes 3932160 | tf_op jit(solution)/shard_map/reduce_scatter | solution.py:360
  59.6 29.3 %copy-start.52 = (f32[256]{0:T(256)}, f32[256]{0:T(256)S(1)}, u32[]{:S(2)}) copy-start(f32[256]{0:T(256)S(1)} %add_rsqrt_fusion.1) | copy-start | bytes 3076
  62.9 25.7 %copy-start.9 = (bf16[4,256,256]{2,1,0:T(8,128)(2,1)S(1)}, bf16[4,256,256]{2,1,0:T(8,128)(2,1)}, u32[]{:S(2)}) copy-start(bf16[4,256,256]{2,1,0:T(8,128)(2,1)} %get-tuple-element.42) | copy-start | bytes 1572868
  88.6 5.5 %copy-start.10 = (bf16[2048,128]{0,1:T(8,128)(2,1)}, bf16[2048,128]{0,1:T(8,128)(2,1)S(1)}, u32[]{:S(2)}) copy-start(bf16[2048,128]{0,1:T(8,128)(2,1)S(1)} %copy.122) | copy-start | bytes 1572868
  89.3 4.8 %copy-start.26 = (bf16[256,4,64]{0,2,1:T(8,128)(2,1)}, bf16[256,4,64]{0,2,1:T(8,128)(2,1)S(1)}, u32[]{:S(2)}) copy-start(bf16[256,4,64]{0,2,1:T(8,128)(2,1)S(1)} %pad_maximum_fusion.8) | copy-start | bytes 393220
  94.1 5.0 %copy-start.44 = (f32[2,2,256]{2,1,0:T(2,128)}, f32[2,2,256]{2,1,0:T(2,128)S(1)}, u32[]{:S(2)}) copy-start(f32[2,2,256]{2,1,0:T(2,128)S(1)} %get-tuple-element.106) | copy-start | bytes 12292
  94.4 4.8 %copy-start.12 = (bf16[2048,128]{0,1:T(8,128)(2,1)}, bf16[2048,128]{0,1:T(8,128)(2,1)S(1)}, u32[]{:S(2)}) copy-start(bf16[2048,128]{0,1:T(8,128)(2,1)S(1)} %copy.124) | copy-start | bytes 1572868
  94.4 6.0 %copy-start.3 = (f32[2,2,256,2048]{2,3,1,0:T(8,128)S(1)}, f32[2,2,256,2048]{2,3,1,0:T(8,128)}, u32[]{:S(2)}) copy-start(f32[2,2,256,2048]{2,3,1,0:T(8,128)} %get-tuple-element.107) | copy-start | bytes 25165828
  100.3 18.4 %copy-start.51 = (bf16[4,2,128]{2,1,0:T(2,128)(2,1)S(1)}, bf16[4,2,128]{2,1,0:T(2,128)(2,1)}, u32[]{:S(2)}) copy-start(bf16[4,2,128]{2,1,0:T(2,128)(2,1)} %get-tuple-element.101) | copy-start | bytes 6148
  100.3 19.5 %copy-start.41 = (s32[256,8]{0,1:T(8,128)S(1)}, s32[256,8]{0,1:T(8,128)}, u32[]{:S(2)}) copy-start(s32[256,8]{0,1:T(8,128)} %param.17) | copy-start | bytes 24580
  101.8 20.8 %copy-start.24 = (bf16[2,64,2,256]{3,1,2,0:T(8,128)(2,1)}, bf16[2,64,2,256]{3,1,2,0:T(8,128)(2,1)S(1)}, u32[]{:S(2)}) copy-start(bf16[2,64,2,256]{3,1,2,0:T(8,128)(2,1)S(1)} %fusion.29) | copy-start | bytes 393220
  122.7 151.5 %copy-start.7 = (f32[256,1024]{1,0:T(8,128)}, f32[256,1024]{1,0:T(8,128)S(1)}, u32[]{:S(2)}) copy-start(f32[256,1024]{1,0:T(8,128)S(1)} %get-tuple-element.109) | copy-start | bytes 3145732
  123.2 33.5 %copy-start.42 = (f32[256]{0:T(256)}, f32[256]{0:T(256)S(1)}, u32[]{:S(2)}) copy-start(f32[256]{0:T(256)S(1)} %get-tuple-element.110) | copy-start | bytes 3076
  123.4 33.2 %copy-start.48 = (f32[256]{0:T(256)}, f32[256]{0:T(256)S(1)}, u32[]{:S(2)}) copy-start(f32[256]{0:T(256)S(1)} %fusion.53) | copy-start | bytes 3076
  157.4 4.8 %copy-start.66 = (bf16[8,128,1024]{2,1,0:T(8,128)(2,1)S(1)}, bf16[8,128,1024]{2,1,0:T(8,128)(2,1)}, u32[]{:S(2)}) copy-start(bf16[8,128,1024]{2,1,0:T(8,128)(2,1)} %get-tuple-element.46) | copy-start | bytes 6291460
  173.2 269.8 %all-gather.8.cloned.1.call-start = ((), (), s32[]{:S(2)}) async-start(), calls=%async_computation.4 | async-start | bytes 7077888 | tf_op jit(solution)/shard_map/all_gather | solution.py:381
  173.3 4.3 copy-start.64
  173.3 4.3 copy-start.70
  173.4 4.3 copy-start.72
  254.7 12.8 %copy-start.53 = (f32[256]{0:T(256)S(1)}, f32[256]{0:T(256)}, u32[]{:S(2)}) copy-start(f32[256]{0:T(256)} %copy-done.52) | copy-start | bytes 3076
  254.7 13.5 %copy-start.60 = (s32[8]{0:T(128)S(1)}, s32[8]{0:T(128)}, u32[]{:S(2)}) copy-start(s32[8]{0:T(128)} %get-tuple-element.118) | copy-start | bytes 100
  254.7 13.5 %copy-start.45 = (f32[2,2,256]{2,1,0:T(2,128)S(1)}, f32[2,2,256]{2,1,0:T(2,128)}, u32[]{:S(2)}) copy-start(f32[2,2,256]{2,1,0:T(2,128)} %copy-done.44) | copy-start | bytes 12292
  254.7 13.5 %copy-start.47 = (f32[2,2,256]{2,1,0:T(2,128)S(1)}, f32[2,2,256]{2,1,0:T(2,128)}, u32[]{:S(2)}) copy-start(f32[2,2,256]{2,1,0:T(2,128)} %copy-done.46) | copy-start | bytes 12292
  254.7 14.1 %copy-start.56 = (f32[256]{0:T(256)S(1)}, f32[256]{0:T(256)}, u32[]{:S(2)}) copy-start(f32[256]{0:T(256)} %copy-done.55) | copy-start | bytes 3076
  254.7 14.7 %copy-start.39 = (f32[4,8,256]{2,1,0:T(8,128)S(1)}, f32[4,8,256]{2,1,0:T(8,128)}, u32[]{:S(2)}) copy-start(f32[4,8,256]{2,1,0:T(8,128)} %get-tuple-element.52) | copy-start | bytes 98308
  254.7 15.2 %copy-start.59 = (pred[8]{0:T(512)(128)(4,1)S(1)}, pred[8]{0:T(512)(128)(4,1)}, u32[]{:S(2)}) copy-start(pred[8]{0:T(512)(128)(4,1)} %get-tuple-element.115) | copy-start | bytes 28
  254.8 7.6 %collective-permute-start.2 = (bf16[3,256,128]{2,1,0:T(8,128)(2,1)S(1)}, bf16[3,256,128]{2,1,0:T(8,128)(2,1)S(1)}, u32[]{:S(2)}, u32[]{:S(2)}) collective-permute-start(bf16[3,256,128]{2,1,0:T(8,128)(2,1)S(1)} %get-tuple-element.89), channel_id=1, source_target_pairs={{0,3},{1,0},{2,1},{3,2},{4,7},{5,4},{6,5},{7,6},{8,11},{9,8},{10,9... | collective-permute-start | bytes 589832 | tf_op jit(solution)/shard_map/ppermute | solution.py:226
  255.2 7.1 %collective-permute-start.1 = (bf16[3,256,128]{2,1,0:T(8,128)(2,1)S(1)}, bf16[3,256,128]{2,1,0:T(8,128)(2,1)S(1)}, u32[]{:S(2)}, u32[]{:S(2)}) collective-permute-start(bf16[3,256,128]{2,1,0:T(8,128)(2,1)S(1)} %get-tuple-element.90), channel_id=1, source_target_pairs={{0,2},{1,3},{2,0},{3,1},{4,6},{5,7},{6,4},{7,5},{8,10},{9,11},{10,... | collective-permute-start | bytes 589832 | tf_op jit(solution)/shard_map/ppermute | solution.py:226
  256.6 8.8 %collective-permute-start = (bf16[3,256,128]{2,1,0:T(8,128)(2,1)S(1)}, bf16[3,256,128]{2,1,0:T(8,128)(2,1)S(1)}, u32[]{:S(2)}, u32[]{:S(2)}) collective-permute-start(bf16[3,256,128]{2,1,0:T(8,128)(2,1)S(1)} %get-tuple-element.91), channel_id=1, source_target_pairs={{0,1},{1,2},{2,3},{3,0},{4,5},{5,6},{6,7},{7,4},{8,9},{9,10},{10,1... | collective-permute-start | bytes 589832 | tf_op jit(solution)/shard_map/ppermute | solution.py:226
  265.4 4.7 %copy-start.43 = (f32[256]{0:T(256)S(1)}, f32[256]{0:T(256)}, u32[]{:S(2)}) copy-start(f32[256]{0:T(256)} %copy-done.42) | copy-start | bytes 3076
  265.4 4.7 %copy-start.49 = (f32[256]{0:T(256)S(1)}, f32[256]{0:T(256)}, u32[]{:S(2)}) copy-start(f32[256]{0:T(256)} %copy-done.48) | copy-start | bytes 3076
  267.5 24.4 %copy-start.14 = (bf16[4,256,256]{2,1,0:T(8,128)(2,1)S(1)}, bf16[4,256,256]{2,1,0:T(8,128)(2,1)}, u32[]{:S(2)}) copy-start(bf16[4,256,256]{2,1,0:T(8,128)(2,1)} %get-tuple-element.43) | copy-start | bytes 1572868
  272.0 21.3 %copy-start.35 = (f32[2,2,256]{2,1,0:T(2,128)S(1)}, f32[2,2,256]{2,1,0:T(2,128)}, u32[]{:S(2)}) copy-start(f32[2,2,256]{2,1,0:T(2,128)} %log_add_fusion) | copy-start | bytes 12292
  304.8 4.7 copy-start.27
  313.7 29.2 %copy-start.11 = (bf16[2048,128]{0,1:T(8,128)(2,1)S(1)}, bf16[2048,128]{0,1:T(8,128)(2,1)}, u32[]{:S(2)}) copy-start(bf16[2048,128]{0,1:T(8,128)(2,1)} %copy-done.10) | copy-start | bytes 1572868
  403.4 5.2 %copy-start.8 = (f32[256,1024]{1,0:T(8,128)S(1)}, f32[256,1024]{1,0:T(8,128)}, u32[]{:S(2)}) copy-start(f32[256,1024]{1,0:T(8,128)} %convert_element_type.174) | copy-start | bytes 3145732
  403.4 5.4 %copy-start.28 = (bf16[4,64,1024]{2,1,0:T(8,128)(2,1)S(1)}, bf16[4,64,1024]{2,1,0:T(8,128)(2,1)}, u32[]{:S(2)}) copy-start(bf16[4,64,1024]{2,1,0:T(8,128)(2,1)} %get-tuple-element.56) | copy-start | bytes 1572868
  403.4 7.1 %copy-start.16 = (f32[64,1024]{1,0:T(8,128)S(1)}, f32[64,1024]{1,0:T(8,128)}, u32[]{:S(2)}) copy-start(f32[64,1024]{1,0:T(8,128)} %get-tuple-element.73) | copy-start | bytes 786436
  403.4 7.1 %copy-start.57 = (f32[64]{0:T(128)S(1)}, f32[64]{0:T(128)}, u32[]{:S(2)}) copy-start(f32[64]{0:T(128)} %get-tuple-element.70) | copy-start | bytes 772
  403.4 7.1 %copy-start.58 = (f32[64]{0:T(128)S(1)}, f32[64]{0:T(128)}, u32[]{:S(2)}) copy-start(f32[64]{0:T(128)} %get-tuple-element.71) | copy-start | bytes 772
  445.8 14.5 %copy-start.30 = (bf16[4,64,1024]{2,1,0:T(8,128)(2,1)S(1)}, bf16[4,64,1024]{2,1,0:T(8,128)(2,1)}, u32[]{:S(2)}) copy-start(bf16[4,64,1024]{2,1,0:T(8,128)(2,1)} %get-tuple-element.58) | copy-start | bytes 1572868
  445.8 15.3 %copy-start.29 = (bf16[4,64,1024]{2,1,0:T(8,128)(2,1)S(1)}, bf16[4,64,1024]{2,1,0:T(8,128)(2,1)}, u32[]{:S(2)}) copy-start(bf16[4,64,1024]{2,1,0:T(8,128)(2,1)} %get-tuple-element.59) | copy-start | bytes 1572868
  445.8 16.1 %copy-start.1 = (bf16[256,32,128]{2,1,0:T(8,128)(2,1)S(1)}, bf16[256,32,128]{2,1,0:T(8,128)(2,1)}, u32[]{:S(2)}) copy-start(bf16[256,32,128]{2,1,0:T(8,128)(2,1)} %param.25) | copy-start | bytes 6291460
  (32 other events, 78.8 us)
Sparse Core Ops, SparseCore 0:
  56.0 40.2 all-gather.3
  98.5 41.3 all-gather.5
  173.3 38.9 reduce-scatter.1
  266.5 107.7 all-gather.7

commit v3 on v2

--- a/solution.py
+++ b/solution.py
@@ -142,6 +142,180 @@
     return [out.reshape(depth, experts, ff) for out in outs]
 
 
+def expert_kernel(
+    n,
+    rows_ref,
+    probs_ref,
+    grads_ref,
+    w_ref,
+    norm_got,
+    mixed_got,
+    gate_got,
+    wgrad_ref,
+    norm_buf,
+    probs_buf,
+    both_buf,
+    weighted_buf,
+    back_buf,
+    mixed_buf,
+    gate_buf,
+    send_sems,
+    recv_sems,
+):
+    me = lax.axis_index("ctx")
+    hidden = w_ref.shape[1] // 3
+
+    def chunk(ref, k):
+        return ref.at[pl.ds(pl.multiple_of(k * CAP, CAP), CAP)]
+
+    def copy(which, k, source, target, place):
+        return pltpu.make_async_remote_copy(
+            src_ref=source,
+            dst_ref=target,
+            send_sem=send_sems.at[which, k],
+            recv_sem=recv_sems.at[which, k],
+            device_id={"ctx": lax.rem(place, n)},
+            device_id_type=MESH,
+        )
+
+    def out_copies(k):
+        return (
+            copy(0, k, chunk(rows_ref, k), chunk(norm_buf, k), me + k),
+            copy(1, k, probs_ref.at[k], probs_buf.at[k], me + k),
+        )
+
+    def back_copies(k):
+        place = me + n - k
+        return (
+            copy(2, k, chunk(back_buf, k), chunk(norm_got, k), place),
+            copy(3, k, gate_buf.at[k], gate_got.at[k], place),
+            copy(4, k, chunk(mixed_buf, k), chunk(mixed_got, k), place),
+        )
+
+    barrier = pltpu.get_barrier_semaphore()
+    for k in range(1, n):
+        pl.semaphore_signal(
+            barrier, inc=1, device_id={"ctx": lax.rem(me + k, n)}, device_id_type=MESH
+        )
+    pl.semaphore_wait(barrier, n - 1)
+    for k in range(1, n):
+        for item in out_copies(k):
+            item.start()
+    norm_buf[:CAP] = rows_ref[:CAP]
+    probs_buf[0] = probs_ref[0]
+    same = lax.broadcasted_iota(jnp.int32, (CAP, CAP), 0) == lax.broadcasted_iota(
+        jnp.int32, (CAP, CAP), 1
+    )
+
+    def pair(j, carry):
+        for k in (2 * j, 2 * j + 1):
+
+            @pl.when(k > 0)
+            def _():
+                for item in out_copies(k):
+                    item.wait_recv()
+
+        here = pl.ds(pl.multiple_of(j * 2 * CAP, 2 * CAP), 2 * CAP)
+        gate_up = mm(norm_buf[here, :], w_ref[:, : 2 * hidden])
+        down_back = mm(grads_ref[here, :], w_ref[:, 2 * hidden :])
+        probs = jnp.concatenate(
+            [
+                jnp.sum(jnp.where(same, probs_buf[k][:1, :], 0.0), axis=1, keepdims=True)
+                for k in (2 * j, 2 * j + 1)
+            ],
+            axis=0,
+        )
+        gate_pre, up_pre = gate_up[:, :hidden], gate_up[:, hidden:]
+        sig = jax.nn.sigmoid(gate_pre)
+        silu = gate_pre * sig
+        activation = silu * up_pre
+        gate_grad = branch_scale * jnp.sum(activation * down_back, axis=1, keepdims=True)
+        act_grad = (branch_scale * probs) * down_back
+        both_buf[here, :hidden] = (
+            act_grad * up_pre * sig * (1.0 + gate_pre * (1.0 - sig))
+        ).astype(bf16)
+        both_buf[here, hidden:] = (act_grad * silu).astype(bf16)
+        weighted_buf[here, :] = (probs * activation).astype(bf16)
+        back_buf[here, :] = contract_cols(both_buf[here, :], w_ref[:, : 2 * hidden]).astype(bf16)
+        for i in range(2):
+            line = jnp.sum(
+                jnp.where(same, gate_grad[i * CAP : (i + 1) * CAP], 0.0), axis=0, keepdims=True
+            )
+            gate_buf[2 * j + i] = jnp.broadcast_to(line, (8, CAP))
+        mixed_buf[here, :] = contract_cols(weighted_buf[here, :], w_ref[:, 2 * hidden :]).astype(
+            bf16
+        )
+        for k in (2 * j, 2 * j + 1):
+
+            @pl.when(k > 0)
+            def _():
+                for item in back_copies(k):
+                    item.start()
+
+        return carry
+
+    lax.fori_loop(0, n // 2, pair, 0)
+    norm_got[:CAP] = back_buf[:CAP]
+    mixed_got[:CAP] = mixed_buf[:CAP]
+    gate_got[0] = gate_buf[0]
+
+    width = w_ref.shape[0]
+    part = 256
+
+    def weight_grads(j, carry):
+        here = pl.ds(pl.multiple_of(j * part, part), part)
+        wgrad_ref[here, : 2 * hidden] = contract_rows(norm_buf[:, here], both_buf[...]).astype(bf16)
+        wgrad_ref[here, 2 * hidden :] = (
+            contract_rows(grads_ref[:, here], weighted_buf[...]) * branch_scale
+        ).astype(bf16)
+        return carry
+
+    lax.fori_loop(0, width // part, weight_grads, 0)
+    for k in range(1, n):
+        for item in out_copies(k):
+            item.wait_send()
+        for item in back_copies(k):
+            item.wait()
+
+
+def expert_of_place(sizes, rows_sent, probs_sent, grad_rows, expert_w):
+    n = sizes["ctx"]
+    total, width = rows_sent.shape
+    columns = expert_w.shape[1]
+    hidden = columns // 3
+    like = jax.ShapeDtypeStruct
+    vmem = pl.BlockSpec(memory_space=pltpu.VMEM)
+    return pl.pallas_call(
+        functools.partial(expert_kernel, n),
+        out_shape=[
+            like((total, width), bf16),
+            like((total, width), bf16),
+            like(probs_sent.shape, f32),
+            like((width, columns), bf16),
+        ],
+        in_specs=[vmem] * 4,
+        out_specs=[vmem] * 4,
+        scratch_shapes=[
+            pltpu.VMEM((total, width), bf16),
+            pltpu.VMEM(probs_sent.shape, f32),
+            pltpu.VMEM((total, 2 * hidden), bf16),
+            pltpu.VMEM((total, hidden), bf16),
+            pltpu.VMEM((total, width), bf16),
+            pltpu.VMEM((total, width), bf16),
+            pltpu.VMEM(probs_sent.shape, f32),
+            pltpu.SemaphoreType.DMA((5, n)),
+            pltpu.SemaphoreType.DMA((5, n)),
+        ],
+        compiler_params=pltpu.CompilerParams(
+            collective_id=3, has_side_effects=True, vmem_limit_bytes=48 * 1024 * 1024
+        ),
+        cost_estimate=pl.CostEstimate(
+            flops=6 * 2 * total * width * hidden * 3, bytes_accessed=100 << 20, transcendentals=0
+        ),
+        name="expert_of_place",
+    )(rows_sent, probs_sent, grad_rows, expert_w)
+
+
 def rope_tables(places):
     frequencies = jnp.exp(
         jnp.arange(HEAD_SIZE // 2, dtype=jnp.float32) * (-2.0 * math.log(rope_base) / HEAD_SIZE)
@@ -272,8 +446,6 @@
     output_full = lax.all_gather(output_w, "tp", axis=1, tiled=True)
     expert_cat = expert_slices.transpose(2, 1, 0, 3).reshape(depth, 3 * n_tp * ff)
     expert_w = lax.all_gather(expert_cat, "fsdp", axis=0, tiled=True)
-    hidden_units = n_tp * ff
-    gate_up_w, down_w = expert_w[:, : 2 * hidden_units], expert_w[:, 2 * hidden_units :]
 
     lengths_row = lengths[0]
     query_rows = ctx_at * rows + jnp.arange(rows, dtype=jnp.int32)
@@ -331,54 +503,21 @@
     )
     probs_mine = jnp.take(probs_mine, ctx_order, axis=0)
     probs_sent = jnp.sum(picks.astype(f32) * probs_mine[:, None, :], axis=2)
-    rows_sent = mm(picks_flat, normed_two).astype(bf16).reshape(n_ctx, CAP, width)
-    rows_got, probs_got = send(
-        3,
-        (("ctx",), "f", rows_sent),
-        (("ctx",), "f", jnp.broadcast_to(probs_sent[:, None, :], (n_ctx, 8, CAP))),
-    )
-
-    norm_rows = rows_got.reshape(n_ctx * CAP, width)
-    probs_col = probs_got[:, 0, :].reshape(n_ctx * CAP, 1)
-    gate_up = mm(norm_rows, gate_up_w)
-    gate_pre, up_pre = gate_up[:, :hidden_units], gate_up[:, hidden_units:]
-    down_back = mm(grad_rows, down_w)
-    sigmoid_gate = jax.nn.sigmoid(gate_pre)
-    silu_gate = gate_pre * sigmoid_gate
-    activation = silu_gate * up_pre
-    gate_grad_rows = branch_scale * jnp.sum(activation * down_back, axis=1)
-    act_grad = (branch_scale * probs_col) * down_back
-    gate_in = act_grad * up_pre * sigmoid_gate * (1.0 + gate_pre * (1.0 - sigmoid_gate))
-    both_in = jnp.concatenate([gate_in, act_grad * silu_gate], axis=1).astype(bf16)
-    weighted = (probs_col * activation).astype(bf16)
-    mixed = contract_cols(weighted, down_w).astype(bf16).reshape(n_ctx, CAP, width)
-    norm_grad = contract_cols(both_in, gate_up_w).astype(bf16)
-    gate_grad_rows = jnp.broadcast_to(gate_grad_rows.reshape(n_ctx, 1, CAP), (n_ctx, 8, CAP))
-    grad_gate_up = contract_rows(norm_rows, both_in)
-    grad_down = contract_rows(grad_rows, weighted) * branch_scale
-    expert_grad = jnp.concatenate([grad_gate_up, grad_down], axis=1).astype(bf16)
+    rows_sent = mm(picks_flat, normed_two).astype(bf16)
+    probs_sent = jnp.broadcast_to(probs_sent[:, None, :], (n_ctx, 8, CAP))
+    norm_grad_got, mixed_got, gate_grad_got, expert_grad = expert_of_place(
+        sizes, rows_sent, probs_sent, grad_rows, expert_w
+    )
     expert_grad = lax.psum_scatter(expert_grad, "fsdp", scatter_dimension=0, tiled=True)
 
-    norm_grad_got, gate_grad_got, mixed_got = send(
-        4,
-        (("ctx",), "b", norm_grad.reshape(n_ctx, CAP, width)),
-        (("ctx",), "b", gate_grad_rows),
-        (("ctx",), "b", mixed),
-    )
-
     quarter = rows // n_tp
-    norm_grad_part = contract_rows(picks_flat, norm_grad_got.reshape(n_ctx * CAP, width))
+    norm_grad_part = contract_rows(picks_flat, norm_grad_got)
     gate_grad_part = jnp.sum(picks.astype(f32) * gate_grad_got[:, 0, :, None], axis=1)
     norm_grad_parts, gate_grad_parts = send(
         5,
         (("tp",), "a", norm_grad_part.astype(bf16).reshape(n_tp, quarter, width)),
         (("tp",), "g", gate_grad_part),
     )
-
-    expert_grad, _ = lax.optimization_barrier((expert_grad, gate_grad_parts))
-    expert_grad = expert_grad.reshape(depth, 3, n_tp, ff).transpose(2, 1, 0, 3)
-    pieces = shifted(jnp.take(expert_grad, tp_order, axis=0), "tp", 1)
-    expert_all = lax.all_gather(pieces, "ctx", axis=0, tiled=True)
 
     def quarter_of(array):
         return lax.dynamic_slice_in_dim(array, tp_at * quarter, quarter, 0)
@@ -404,6 +543,12 @@
     )
     (attn_in,) = send(6, (("tp",), "g", (branch_scale * residual_grad).astype(bf16)))
     attn_in = attn_in.reshape(rows, width)
+
+    expert_grad, _ = lax.optimization_barrier((expert_grad, attn_in))
+    expert_grad = expert_grad.reshape(depth, 3, n_tp, ff).transpose(2, 1, 0, 3)
+    pieces = shifted(jnp.take(expert_grad, tp_order, axis=0), "tp", 1)
+    expert_all = lax.all_gather(pieces, "ctx", axis=0, tiled=True)
+
     grad_output = contract_rows(attn_in, attended)
     attended_grad = mm(attn_in, output_w).astype(bf16)
 
@@ -443,7 +588,7 @@
     grad_query = contract_rows(normed_one, query_grad)
     grad_key = contract_rows(normed_one, key_grad)
     grad_value = contract_rows(normed_one, value_grad)
-    mixed_part = contract_rows(picks_flat, mixed_got.reshape(n_ctx * CAP, width)).astype(bf16)
+    mixed_part = contract_rows(picks_flat, mixed_got).astype(bf16)
 
     n_rows = n_fsdp * n_ctx
     share = width // n_rows

time: 478 us -> 480 us (level)
  matrix products: 64 us -> 44.1 us
  local copies, waits for them, and re-layouts: 39.7 us -> 58.6 us
  waiting for transfers between devices: 7.27 us -> 23.4 us
  Pallas kernels: 300 us -> 290 us
    pallas_call x10 -> x8, Pallas kernels: 286 us -> 190 us  [exchange(): pl.pallas_call(functools.partial(exchange_kernel, plan, sizes), out_shape...]
    pallas_call x0 -> x1, Pallas kernels: none -> 85.6 us  [expert_of_place(): pl.pallas_call(functools.partial(expert_kernel, n), out_shape=[like((tota...]
    all_gather x1, waiting for transfers between devices: 0.01 us -> 16.7 us  [local(): expert_w = lax.all_gather(expert_cat, 'fsdp', axis=0, tiled=True)]
    dot_general x7 -> x5, matrix products: 15 us -> 6.84 us  [contract_cols(): lax.dot_general(left, right, (((1,), (1,)), ((), ())), precision=precisio...]
    dot_general x10 -> x8, matrix products: 15.8 us -> 8.24 us  [mm(): return jnp.dot(left, right, preferred_element_type=f32)]
    unnamed x158 -> x122, local copies, waits for them, and re-layouts: 12.8 us -> 19.7 us
    dot_general x9 -> x7, matrix products: 12.4 us -> 11.1 us  [contract_rows(): lax.dot_general(left, right, (((0,), (0,)), ((), ())), precision=precisio...]
  transfers between devices with their start and end apart: 7 -> 7, of which waited for: 2 -> 3; matrix products, arithmetic and copies ran while one was open for 22% -> 23% of each run, Pallas kernels for 52% -> 31%
where the time goes in v3:
time: 480 us; the launch traced here: 475 us
  Pallas kernels  290 us (60%)
  local copies, waits for them, and re-layouts  58.6 us (12%)
  matrix products  44.1 us (9%)
  other arithmetic  41.5 us (9%)
  waiting for transfers between devices  23.4 us (5%)
  between operations  15.3 us (3%)
    pallas_call x8, Pallas kernels, exchange(): pl.pallas_call(functools.partial(exchange_kernel, plan, sizes), out_shape...  190 us
    pallas_call x1, Pallas kernels, expert_of_place(): pl.pallas_call(functools.partial(expert_kernel, n), out_shape=[like((tota...  85.6 us
    unnamed x122, local copies, waits for them, and re-layouts  19.7 us
    all_gather x1, waiting for transfers between devices, local(): expert_w = lax.all_gather(expert_cat, 'fsdp', axis=0, tiled=True)  16.7 us
    pallas_call x1, Pallas kernels, spread(): pl.pallas_call(functools.partial(spread_kernel, n_ctx, n_tp), grid=(depth...  14.5 us
    dot_general x7, matrix products, contract_rows(): lax.dot_general(left, right, (((0,), (0,)), ((), ())), precision=precisio...  11.1 us
  transfers between devices with their start and end apart: 7, of which 3 were waited for; matrix products, arithmetic and copies ran while one was open for 23% of the time, Pallas kernels for 31%

profile of v3, /device:TPU:1, one launch (start us, length us, event | category | flops | bytes accessed | tf_op | source)
XLA Modules:
  0.0 475.4 jit_solution(16074390660891547421)
XLA Ops:
  8.2 1.5 constant_dynamic-slice_fusion.1
  12.0 3.1 convolution_convert_fusion.1
  16.7 40.8 %exchange_0.1 = (bf16[4,256,256]{2,1,0:T(8,128)(2,1)}, bf16[4,256,128]{2,1,0:T(8,128)(2,1)}, bf16[4,256,128]{2,1,0:T(8,128)(2,1)}, bf16[4,256,256]{2,1,0:T(8,128...) custom-call(bf16[256,256]{1,0:T(8,128)(2,1)} %refs_0_.1, ...), custom_call_target="tpu_custom_call" | custom-call | bytes 94699520 | tf_op jit(solution)/shard_map/exchange_0/pallas_call | solution.py:103
  57.6 1.8 copy.125
  65.2 26.4 %exchange_1.1 = bf16[8,256,256]{2,1,0:T(8,128)(2,1)} custom-call(bf16[256,256]{1,0:T(8,128)(2,1)} %pad_maximum_fusion.3.refs_0_), custom_call_target="tpu_custom_call" | custom-call | bytes 20971520 | tf_op jit(solution)/shard_map/exchange_1/pallas_call | solution.py:103
  94.1 1.5 fusion.61
  96.8 2.1 copy-done.4
  101.3 11.9 %exchange_2.1 = bf16[4,256,256]{2,1,0:T(8,128)(2,1)} custom-call(bf16[256,256]{1,0:T(8,128)(2,1)} %copy.123.refs_0_), custom_call_target="tpu_custom_call" | custom-call | bytes 10485760 | tf_op jit(solution)/shard_map/exchange_2/pallas_call | solution.py:103
  115.7 2.5 multiply_reduce_fusion.1
  120.8 2.0 convolution_convert_fusion.rows_ref
  122.8 16.7 %all-gather.6.cloned.1.call-done.w_ref = bf16[1024,1536]{1,0:T(8,128)(2,1)} async-done(((bf16[256,1536]{1,0:T(8,128)(2,1)}), bf16[1024,1536]{1,0:T(8,128)(2,1)}) %all-gather.6.cloned.1.call-update) | async-done | bytes 3145744 | tf_op jit(solution)/shard_map/all_gather | solution.py:448
  139.5 85.6 %expert_of_place.1 = (bf16[1024,1024]{1,0:T(8,128)(2,1)S(1)}, bf16[1024,1024]{1,0:T(8,128)(2,1)S(1)}, f32[8,8,128]{2,1,0:T(8,128)S(1)}, bf16[1024,1536]{1,0:T(8,128)(2,1)}) custom-call(bf16[1024,1024]{1,0:T(8,128)(2,1)} %convolution_convert_fusion.rows_ref, f32[8,8,128]{2,1,0:T(8,128)S(1)} %broadcast_in_dim.51.probs_ref, bf16[1024,1024]{1,0:T(8,128)(2,1)} %bitcast.288, ...), custom_call_target="tpu_custom_call" | custom-call | flops 19327352832 | bytes 104857600 | tf_op jit(solution)/shard_map/expert_of_place/pallas_call | solution.py:288
  230.2 1.5 fusion.25.refs_1_
  231.8 3.2 convolution_convert_fusion.5
  234.9 9.8 %exchange_5.1 = (bf16[4,64,1024]{2,1,0:T(8,128)(2,1)}, f32[4,8,256]{2,1,0:T(8,128)}) custom-call(bf16[4,64,1024]{2,1,0:T(8,128)(2,1)} %bitcast.264, f32[8,256]{1,0:T(8,128)} %fusion.25.refs_1_), custom_call_target="tpu_custom_call" | custom-call | bytes 11141120 | tf_op jit(solution)/shard_map/exchange_5/pallas_call | solution.py:103
  251.0 2.2 multiply_reduce_fusion.4
  253.2 1.9 multiply_convert_fusion.2
  255.1 8.6 %exchange_6.1 = bf16[4,64,1024]{2,1,0:T(8,128)(2,1)} custom-call(bf16[64,1024]{1,0:T(8,128)(2,1)} %get-tuple-element.70.refs_0_), custom_call_target="tpu_custom_call" | custom-call | bytes 10485760 | tf_op jit(solution)/shard_map/exchange_6/pallas_call | solution.py:103
  263.8 2.4 reshape.560
  266.2 2.2 copy.166
  268.4 2.8 gather_fusion.2
  272.9 1.9 collective-permute-start
  274.8 5.2 %collective-permute-done.2 = bf16[3,256,128]{2,1,0:T(8,128)(2,1)S(1)} collective-permute-done((bf16[3,256,128]{2,1,0:T(8,128)(2,1)S(1)}, bf16[3,256,128]{2,1,0:T(8,128)(2,1)S(1)}, u32[]{:S(2)}, u32[]{:S(2)}) %collective-permute-start.2) | collective-permute-done | bytes 196640 | tf_op jit(solution)/shard_map/ppermute | solution.py:400
  284.2 1.5 convolution_convert_fusion.8
  285.7 4.8 %fusion.14 = bf16[2,64,2048]{2,1,0:T(8,128)(2,1)S(1)} fusion(bf16[256,2,2,64]{0,3,2,1:T(8,128)(2,1)S(1)} %bitcast.240, f32[2,2,256,2048]{2,3,1,0:T(8,128)} %copy-done.4, f32[2,2,256]{2,1,0:T(2,128)S(1)} %log_add_fusion), kind=kOutput, calls=%fused_computation.21 | convolution fusion | flops 272891904 | bytes 9048064 | tf_op jit(solution)/shard_map/kgrs,rkgd->skd/dot_general | solution.py:557
  291.5 2.3 copy.131
  293.8 5.5 %fusion = (f32[2,2,256]{2,1,0:T(2,128)S(1)}, f32[2,2048,256,2]{2,1,3,0:T(8,128)S(1)}) fusion(f32[2,2,256,2048]{2,3,1,0:T(8,128)} %copy-done.4, f32[2,2,256]{2,1,0:T(2,128)S(1)} %log_add_fusion, bf16[2048,2,64,1]{0,2,3,1:T(8,128)(2,1)} %bitcast.228, bf16[256,2,2,64]{0,3,2,1:T(8,128)(2,1)} %bitcast.241), kind=kOutput, calls=%fused_computation.5 | convolution fusion | flops 274725888 | bytes 17440768 | tf_op jit(solution)/shard_map/rkgd,skd->kgrs/dot_general | solution.py:560
  299.3 4.8 fusion.2
  304.1 2.0 copy-done.5
  308.4 2.2 copy.130
  310.6 2.3 pad_maximum_fusion.refs_0_
  312.9 20.9 %exchange_7.1 = bf16[8,256,256]{2,1,0:T(8,128)(2,1)} custom-call(bf16[8,256,256]{2,1,0:T(8,128)(2,1)} %pad_maximum_fusion.refs_0_), custom_call_target="tpu_custom_call" | custom-call | bytes 20971520 | tf_op jit(solution)/shard_map/exchange_7/pallas_call | solution.py:103
  336.6 1.7 copy.132
  339.3 3.3 convolution_multiply_fusion.1
  343.4 1.5 multiply_reduce_fusion
  344.9 2.0 copy.133
  346.9 2.0 copy.136
  350.0 1.7 copy.158
  351.7 1.7 pad.14.clone
  361.1 1.6 convolution_convert_fusion.4
  362.7 46.5 %exchange_8.1 = (bf16[4,64,1024]{2,1,0:T(8,128)(2,1)}, bf16[4,64,1024]{2,1,0:T(8,128)(2,1)}, bf16[32,32,896]{2,1,0:T(8,128)(2,1)}, f32[32,8,128]{2,1,0:T(8,128)}) custom-call(bf16[4,64,1024]{2,1,0:T(8,128)(2,1)} %bitcast.234, bf16[4,64,1024]{2,1,0:T(8,128)(2,1)} %bitcast.267, bf16[32,32,896]{2,1,0:T(8,128)(2,1)} %copy-done.14, f32[32,8,128]{2,1,0:T(8,128)} %pad.15.refs_3_), custom_call_target="tpu_custom_call" | custom-call | bytes 60293120 | tf_op jit(solution)/shard_map/exchange_8/pallas_call | solution.py:103
  409.1 2.4 reduce_sum.197.refs_0_
  411.5 1.5 reduce_sum.198.refs_1_
  415.5 1.6 add_convert_fusion.refs_2_
  417.9 24.8 %exchange_9.1 = (bf16[8,32,896]{2,1,0:T(8,128)(2,1)}, f32[32,8,128]{2,1,0:T(8,128)}, bf16[4,64,1024]{2,1,0:T(8,128)(2,1)}, bf16[4,64,1024]{2,1,0:T(8,128)(2,1)}) custom-call(bf16[32,896]{1,0:T(8,128)(2,1)} %reduce_sum.197.refs_0_, f32[8,128]{1,0:T(8,128)} %reduce_sum.198.refs_1_, bf16[64,1024]{1,0:T(8,128)(2,1)} %add_convert_fusion.refs_2_, ...), custom_call_target="tpu_custom_call" | custom-call | bytes 32768000 | tf_op jit(solution)/shard_map/exchange_9/pallas_call | solution.py:103
  448.4 2.9 copy-done.2
  451.3 14.5 %spread.1 = (f32[8192,128]{1,0:T(8,128)}, f32[8192,128]{1,0:T(8,128)}, f32[8192,128]{1,0:T(8,128)}) custom-call(bf16[32,3,256,128]{3,2,1,0:T(8,128)(2,1)S(1)} %copy-done.2), custom_call_target="tpu_custom_call" | custom-call | tf_op jit(solution)/shard_map/spread/pallas_call | solution.py:133
  465.8 1.9 copy.182
  (241 shorter events, 64.3 us)
Async XLA Ops:
  7.2 7.9 %copy-start.53 = (bf16[256]{0:T(256)(128)(2,1)S(1)}, bf16[256]{0:T(256)(128)(2,1)}, u32[]{:S(2)}) copy-start(bf16[256]{0:T(256)(128)(2,1)} %param.23) | copy-start | bytes 1540
  7.2 7.9 %copy-start.54 = (bf16[256]{0:T(256)(128)(2,1)S(1)}, bf16[256]{0:T(256)(128)(2,1)}, u32[]{:S(2)}) copy-start(bf16[256]{0:T(256)(128)(2,1)} %param.18) | copy-start | bytes 1540
  7.2 108.5 %all-gather.4.cloned.1.call-start = ((), (), s32[]{:S(2)}) async-start(), calls=%async_computation.1 | async-start | bytes 2621440 | tf_op jit(solution)/shard_map/all_gather | solution.py:446
  10.9 46.7 %copy-start.34 = (pred[8,256]{1,0:T(8,128)(4,1)}, pred[8,256]{1,0:T(8,128)(4,1)S(1)}, u32[]{:S(2)}) copy-start(pred[8,256]{1,0:T(8,128)(4,1)S(1)} %compare_reduce_fusion) | copy-start | bytes 6148
  16.7 44.1 %copy-start.52 = (s32[1,4]{1,0:T(1,128)S(1)}, s32[1,4]{1,0:T(1,128)}, u32[]{:S(2)}) copy-start(s32[1,4]{1,0:T(1,128)} %param.16) | copy-start | bytes 52
  16.7 44.9 %copy-start.6 = (bf16[256,1024]{1,0:T(8,128)(2,1)S(1)}, bf16[256,1024]{1,0:T(8,128)(2,1)}, u32[]{:S(2)}) copy-start(bf16[256,1024]{1,0:T(8,128)(2,1)} %param.14) | copy-start | bytes 1572868
  57.5 5.7 %copy-start.20 = (bf16[4,256,128]{2,1,0:T(8,128)(2,1)S(1)}, bf16[4,256,128]{2,1,0:T(8,128)(2,1)}, u32[]{:S(2)}) copy-start(bf16[4,256,128]{2,1,0:T(8,128)(2,1)} %get-tuple-element.39) | copy-start | bytes 786436
  57.5 5.9 %copy-start.30 = (bf16[4,256,128]{2,1,0:T(8,128)(2,1)S(1)}, bf16[4,256,128]{2,1,0:T(8,128)(2,1)}, u32[]{:S(2)}) copy-start(bf16[4,256,128]{2,1,0:T(8,128)(2,1)} %get-tuple-element.40) | copy-start | bytes 786436
  57.6 81.9 %all-gather.6.cloned.1.call-start = ((), (), s32[]{:S(2)}) async-start(), calls=%async_computation.2 | async-start | bytes 3932160 | tf_op jit(solution)/shard_map/all_gather | solution.py:448
  60.6 203.2 %reduce-scatter.2.cloned.1.call-start = ((), (), s32[]{:S(2)}) async-start(), calls=%async_computation.3 | async-start | bytes 3932160 | tf_op jit(solution)/shard_map/reduce_scatter | solution.py:511
  61.8 31.7 %copy-start.47 = (f32[256]{0:T(256)}, f32[256]{0:T(256)S(1)}, u32[]{:S(2)}) copy-start(f32[256]{0:T(256)S(1)} %add_rsqrt_fusion.1) | copy-start | bytes 3076
  63.4 30.0 %copy-start.9 = (bf16[4,256,256]{2,1,0:T(8,128)(2,1)S(1)}, bf16[4,256,256]{2,1,0:T(8,128)(2,1)}, u32[]{:S(2)}) copy-start(bf16[4,256,256]{2,1,0:T(8,128)(2,1)} %get-tuple-element.41) | copy-start | bytes 1572868
  64.3 273.9 %copy-start.28 = (f32[256,32]{0,1:T(8,128)}, f32[256,32]{0,1:T(8,128)S(1)}, u32[]{:S(2)}) copy-start(f32[256,32]{0,1:T(8,128)S(1)} %get-tuple-element.97) | copy-start | bytes 98308
  93.1 3.7 copy-start.12
  96.8 3.7 copy-start.41
  99.0 15.5 %copy-start.46 = (bf16[4,2,128]{2,1,0:T(2,128)(2,1)S(1)}, bf16[4,2,128]{2,1,0:T(2,128)(2,1)}, u32[]{:S(2)}) copy-start(bf16[4,2,128]{2,1,0:T(2,128)(2,1)} %get-tuple-element.95) | copy-start | bytes 6148
  99.0 16.6 %copy-start.36 = (s32[256,8]{0,1:T(8,128)S(1)}, s32[256,8]{0,1:T(8,128)}, u32[]{:S(2)}) copy-start(s32[256,8]{0,1:T(8,128)} %param.17) | copy-start | bytes 24580
  100.5 15.2 %copy-start.23 = (bf16[2,64,2,256]{3,1,2,0:T(8,128)(2,1)}, bf16[2,64,2,256]{3,1,2,0:T(8,128)(2,1)S(1)}, u32[]{:S(2)}) copy-start(bf16[2,64,2,256]{3,1,2,0:T(8,128)(2,1)S(1)} %fusion.23) | copy-start | bytes 393220
  100.5 18.4 %copy-start.22 = (bf16[4,256,128]{2,1,0:T(8,128)(2,1)S(1)}, bf16[4,256,128]{2,1,0:T(8,128)(2,1)}, u32[]{:S(2)}) copy-start(bf16[4,256,128]{2,1,0:T(8,128)(2,1)} %get-tuple-element.43) | copy-start | bytes 786436
  113.2 7.3 %copy-start.35 = (pred[8,256]{1,0:T(8,128)(4,1)S(1)}, pred[8,256]{1,0:T(8,128)(4,1)}, u32[]{:S(2)}) copy-start(pred[8,256]{1,0:T(8,128)(4,1)} %copy-done.34) | copy-start | bytes 6148
  118.2 21.2 %copy-start.7 = (f32[256,1024]{1,0:T(8,128)}, f32[256,1024]{1,0:T(8,128)S(1)}, u32[]{:S(2)}) copy-start(f32[256,1024]{1,0:T(8,128)S(1)} %get-tuple-element.103) | copy-start | bytes 3145732
  119.1 20.3 %copy-start.37 = (f32[256]{0:T(256)}, f32[256]{0:T(256)S(1)}, u32[]{:S(2)}) copy-start(f32[256]{0:T(256)S(1)} %get-tuple-element.104) | copy-start | bytes 3076
  226.4 221.9 %all-gather.8.cloned.1.call-start = ((), (), s32[]{:S(2)}) async-start(), calls=%async_computation.4 | async-start | bytes 7077888 | tf_op jit(solution)/shard_map/all_gather | solution.py:550
  231.8 18.0 %copy-start.38 = (f32[256]{0:T(256)S(1)}, f32[256]{0:T(256)}, u32[]{:S(2)}) copy-start(f32[256]{0:T(256)} %copy-done.37) | copy-start | bytes 3076
  231.8 18.0 %copy-start.44 = (f32[256]{0:T(256)S(1)}, f32[256]{0:T(256)}, u32[]{:S(2)}) copy-start(f32[256]{0:T(256)} %copy-done.43) | copy-start | bytes 3076
  251.0 4.1 copy-start.32
  268.4 15.2 %copy-start.48 = (f32[256]{0:T(256)S(1)}, f32[256]{0:T(256)}, u32[]{:S(2)}) copy-start(f32[256]{0:T(256)} %copy-done.47) | copy-start | bytes 3076
  268.4 15.8 %copy-start.40 = (f32[2,2,256]{2,1,0:T(2,128)S(1)}, f32[2,2,256]{2,1,0:T(2,128)}, u32[]{:S(2)}) copy-start(f32[2,2,256]{2,1,0:T(2,128)} %copy-done.39) | copy-start | bytes 12292
  268.4 15.8 %copy-start.42 = (f32[2,2,256]{2,1,0:T(2,128)S(1)}, f32[2,2,256]{2,1,0:T(2,128)}, u32[]{:S(2)}) copy-start(f32[2,2,256]{2,1,0:T(2,128)} %copy-done.41) | copy-start | bytes 12292
  272.6 7.5 %collective-permute-start.2 = (bf16[3,256,128]{2,1,0:T(8,128)(2,1)S(1)}, bf16[3,256,128]{2,1,0:T(8,128)(2,1)S(1)}, u32[]{:S(2)}, u32[]{:S(2)}) collective-permute-start(bf16[3,256,128]{2,1,0:T(8,128)(2,1)S(1)} %get-tuple-element.83), channel_id=1, source_target_pairs={{0,3},{1,0},{2,1},{3,2},{4,7},{5,4},{6,5},{7,6},{8,11},{9,8},{10,9... | collective-permute-start | bytes 589832 | tf_op jit(solution)/shard_map/ppermute | solution.py:400
  272.6 7.4 %collective-permute-start.1 = (bf16[3,256,128]{2,1,0:T(8,128)(2,1)S(1)}, bf16[3,256,128]{2,1,0:T(8,128)(2,1)S(1)}, u32[]{:S(2)}, u32[]{:S(2)}) collective-permute-start(bf16[3,256,128]{2,1,0:T(8,128)(2,1)S(1)} %get-tuple-element.84), channel_id=1, source_target_pairs={{0,2},{1,3},{2,0},{3,1},{4,6},{5,7},{6,4},{7,5},{8,10},{9,11},{10,... | collective-permute-start | bytes 589832 | tf_op jit(solution)/shard_map/ppermute | solution.py:400
  272.9 8.5 %collective-permute-start = (bf16[3,256,128]{2,1,0:T(8,128)(2,1)S(1)}, bf16[3,256,128]{2,1,0:T(8,128)(2,1)S(1)}, u32[]{:S(2)}, u32[]{:S(2)}) collective-permute-start(bf16[3,256,128]{2,1,0:T(8,128)(2,1)S(1)} %get-tuple-element.85), channel_id=1, source_target_pairs={{0,1},{1,2},{2,3},{3,0},{4,5},{5,6},{6,7},{7,4},{8,9},{9,10},{10,1... | collective-permute-start | bytes 589832 | tf_op jit(solution)/shard_map/ppermute | solution.py:400
  285.7 4.8 %copy-start.15 = (bf16[256,256]{0,1:T(8,128)(2,1)}, bf16[256,256]{0,1:T(8,128)(2,1)S(1)}, u32[]{:S(2)}) copy-start(bf16[256,256]{0,1:T(8,128)(2,1)S(1)} %convolution_convert_fusion.8) | copy-start | bytes 393220
  299.3 6.8 %copy-start.25 = (bf16[256,4,64]{0,2,1:T(8,128)(2,1)S(1)}, bf16[256,4,64]{0,2,1:T(8,128)(2,1)}, u32[]{:S(2)}) copy-start(bf16[256,4,64]{0,2,1:T(8,128)(2,1)} %copy-done.24) | copy-start | bytes 393220
  338.3 4.4 copy-start.21
  338.3 4.7 copy-start.19
  338.3 4.7 copy-start.31
  339.3 4.1 copy-start.10
  343.0 6.0 %copy-start.33 = (f32[256,32]{0,1:T(8,128)S(1)}, f32[256,32]{0,1:T(8,128)}, u32[]{:S(2)}) copy-start(f32[256,32]{0,1:T(8,128)} %copy-done.32) | copy-start | bytes 98308
  343.3 10.1 %copy-start.45 = (f32[1024]{0:T(1024)S(1)}, f32[1024]{0:T(1024)}, u32[]{:S(2)}) copy-start(f32[1024]{0:T(1024)} %get-tuple-element.64) | copy-start | bytes 12292
  350.0 8.6 %copy-start.13 = (bf16[1024,256]{1,0:T(8,128)(2,1)S(1)}, bf16[1024,256]{1,0:T(8,128)(2,1)}, u32[]{:S(2)}) copy-start(bf16[1024,256]{1,0:T(8,128)(2,1)} %copy.136) | copy-start | bytes 1572868
  353.6 6.2 %copy-start.16 = (bf16[1024,128]{1,0:T(8,128)(2,1)S(1)}, bf16[1024,128]{1,0:T(8,128)(2,1)}, u32[]{:S(2)}) copy-start(bf16[1024,128]{1,0:T(8,128)(2,1)} %pad.14.clone) | copy-start | bytes 786436
  361.1 53.1 %copy-start.8 = (f32[256,1024]{1,0:T(8,128)S(1)}, f32[256,1024]{1,0:T(8,128)}, u32[]{:S(2)}) copy-start(f32[256,1024]{1,0:T(8,128)} %convert_element_type.163) | copy-start | bytes 3145732
  362.7 54.5 %copy-start.17 = (f32[64,1024]{1,0:T(8,128)S(1)}, f32[64,1024]{1,0:T(8,128)}, u32[]{:S(2)}) copy-start(f32[64,1024]{1,0:T(8,128)} %get-tuple-element.71) | copy-start | bytes 786436
  362.7 54.5 %copy-start.50 = (f32[64]{0:T(128)S(1)}, f32[64]{0:T(128)}, u32[]{:S(2)}) copy-start(f32[64]{0:T(128)} %get-tuple-element.68) | copy-start | bytes 772
  362.7 54.5 %copy-start.51 = (f32[64]{0:T(128)S(1)}, f32[64]{0:T(128)}, u32[]{:S(2)}) copy-start(f32[64]{0:T(128)} %get-tuple-element.69) | copy-start | bytes 772
  447.5 20.1 %copy-start.27 = (bf16[4,64,1024]{2,1,0:T(8,128)(2,1)S(1)}, bf16[4,64,1024]{2,1,0:T(8,128)(2,1)}, u32[]{:S(2)}) copy-start(bf16[4,64,1024]{2,1,0:T(8,128)(2,1)} %get-tuple-element.56) | copy-start | bytes 1572868
  447.5 20.9 %copy-start.1 = (bf16[256,32,128]{2,1,0:T(8,128)(2,1)S(1)}, bf16[256,32,128]{2,1,0:T(8,128)(2,1)}, u32[]{:S(2)}) copy-start(bf16[256,32,128]{2,1,0:T(8,128)(2,1)} %param.25) | copy-start | bytes 6291460
  (14 other events, 28.0 us)
Sparse Core Ops, SparseCore 0:
  57.7 40.8 all-gather.3
  100.8 38.6 all-gather.5
  226.5 34.2 reduce-scatter.1
  282.6 95.6 all-gather.7

commit v4 on v3

--- a/solution.py
+++ b/solution.py
@@ -116,22 +116,19 @@
     )(*arrays)
 
 
-def spread_kernel(n_ctx, n_tp, pieces_ref, *out_refs):
-    experts = n_ctx * n_tp
-    tp_at = lax.axis_index("tp")
+def spread_kernel(pieces_ref, *out_refs):
+    experts = pieces_ref.shape[0]
     depth = pieces_ref.shape[2]
     for which, out_ref in enumerate(out_refs):
-        for place in range(experts):
-            step = place % n_tp
-            expert = place - step + lax.rem(tp_at + n_tp - step, n_tp)
-            out_ref[pl.ds(expert, depth, stride=experts), :] = pieces_ref[place, which].astype(f32)
-
-
-def spread(pieces, n_ctx, n_tp):
+        for expert in range(experts):
+            out_ref[pl.ds(expert, depth, stride=experts), :] = pieces_ref[expert, which].astype(f32)
+
+
+def spread(pieces):
     experts, count, depth, ff = pieces.shape
     block = 64
     outs = pl.pallas_call(
-        functools.partial(spread_kernel, n_ctx, n_tp),
+        spread_kernel,
         grid=(depth // block,),
         out_shape=[jax.ShapeDtypeStruct((depth * experts, ff), f32)] * count,
         in_specs=[pl.BlockSpec((experts, count, block, ff), lambda i: (0, 0, i, 0))],
@@ -144,6 +141,7 @@
 
 def expert_kernel(
     n,
+    part,
     rows_ref,
     probs_ref,
     grads_ref,
@@ -198,7 +196,7 @@
             barrier, inc=1, device_id={"ctx": lax.rem(me + k, n)}, device_id_type=MESH
         )
     pl.semaphore_wait(barrier, n - 1)
-    for k in range(1, n):
+    for k in range(1, 4):
         for item in out_copies(k):
             item.start()
     norm_buf[:CAP] = rows_ref[:CAP]
@@ -208,6 +206,12 @@
     )
 
     def pair(j, carry):
+        @pl.when(j < n // 2 - 2)
+        def _():
+            for k in (2 * j + 4, 2 * j + 5):
+                for item in out_copies(k):
+                    item.start()
+
         for k in (2 * j, 2 * j + 1):
 
             @pl.when(k > 0)
@@ -259,15 +263,21 @@
     mixed_got[:CAP] = mixed_buf[:CAP]
     gate_got[0] = gate_buf[0]
 
-    width = w_ref.shape[0]
-    part = 256
+    width, slim = w_ref.shape[0], wgrad_ref.shape[1]
 
     def weight_grads(j, carry):
         here = pl.ds(pl.multiple_of(j * part, part), part)
-        wgrad_ref[here, : 2 * hidden] = contract_rows(norm_buf[:, here], both_buf[...]).astype(bf16)
-        wgrad_ref[here, 2 * hidden :] = (
-            contract_rows(grads_ref[:, here], weighted_buf[...]) * branch_scale
-        ).astype(bf16)
+        gate_up = contract_rows(norm_buf[:, here], both_buf[...]).astype(bf16)
+        down = (contract_rows(grads_ref[:, here], weighted_buf[...]) * branch_scale).astype(bf16)
+        for piece in range(hidden // slim):
+            for which in range(3):
+                row = (j * (hidden // slim) + piece) * 3 + which
+                at = pl.ds(pl.multiple_of(row * part, part), part)
+                if which < 2:
+                    start = which * hidden + piece * slim
+                    wgrad_ref[at, :] = gate_up[:, start : start + slim]
+                else:
+                    wgrad_ref[at, :] = down[:, piece * slim : (piece + 1) * slim]
         return carry
 
     lax.fori_loop(0, width // part, weight_grads, 0)
@@ -286,12 +296,12 @@
     like = jax.ShapeDtypeStruct
     vmem = pl.BlockSpec(memory_space=pltpu.VMEM)
     return pl.pallas_call(
-        functools.partial(expert_kernel, n),
+        functools.partial(expert_kernel, n, width // sizes["fsdp"]),
         out_shape=[
             like((total, width), bf16),
             like((total, width), bf16),
             like(probs_sent.shape, f32),
-            like((width, columns), bf16),
+            like((width * sizes["tp"] * 3, hidden // sizes["tp"]), bf16),
         ],
         in_specs=[vmem] * 4,
         out_specs=[vmem] * 4,
@@ -316,27 +326,20 @@
     )(rows_sent, probs_sent, grad_rows, expert_w)
 
 
-def rope_tables(places):
-    frequencies = jnp.exp(
-        jnp.arange(HEAD_SIZE // 2, dtype=jnp.float32) * (-2.0 * math.log(rope_base) / HEAD_SIZE)
-    )
-    angles = places.astype(jnp.float32)[:, None] * frequencies[None, :]
-    return (jnp.cos(angles)[:, None, :], jnp.sin(angles)[:, None, :])
-
-
-def turn(values, cosine_table, sine_table):
-    row_count = values.shape[0]
-    head_view = values.reshape(row_count, -1, HEAD_SIZE)
-    first_half = head_view[..., : HEAD_SIZE // 2]
-    second_half = head_view[..., HEAD_SIZE // 2 :]
-    turned = jnp.concatenate(
-        [
-            first_half * cosine_table - second_half * sine_table,
-            second_half * cosine_table + first_half * sine_table,
-        ],
-        axis=-1,
-    )
-    return turned.reshape(row_count, -1)
+def rope_tables(places, columns):
+    column = jnp.arange(columns, dtype=jnp.int32)
+    steps = (column % (HEAD_SIZE // 2)).astype(f32)
+    frequencies = jnp.exp(steps * (-2.0 * math.log(rope_base) / HEAD_SIZE))
+    angles = places.astype(f32)[:, None] * frequencies[None, :]
+    first = (column % HEAD_SIZE < HEAD_SIZE // 2)[None, :]
+    sine = jnp.sin(angles)
+    return jnp.cos(angles), jnp.where(first, -sine, sine), first
+
+
+def turn(values, cosine, sine, first):
+    half = HEAD_SIZE // 2
+    other = jnp.where(first, jnp.roll(values, -half, axis=1), jnp.roll(values, half, axis=1))
+    return values * cosine + other * sine
 
 
 def contract_rows(left, right, precision=None):
@@ -392,18 +395,7 @@
     picks = (chosen_mine[:, None, :] & (rank[:, None, :] == slots[None, :, None])).astype(bf16)
     picks_flat = picks.reshape(n_ctx * CAP, rows)
 
-    def shifted(chunks, axis, direction):
-        n = chunks.shape[0]
-        return jnp.stack(
-            [chunks[0]]
-            + [
-                lax.ppermute(chunks[k], axis, [(s, (s + direction * k) % n) for s in range(n)])
-                for k in range(1, n)
-            ]
-        )
-
     first = ctx_at * per_ctx
-    tp_order = lax.rem(tp_at + jnp.arange(n_tp, dtype=jnp.int32), n_tp)
     own_slices = jnp.stack(
         [
             lax.dynamic_slice_in_dim(w, first, per_ctx, 1).transpose(1, 0, 2)
@@ -421,20 +413,16 @@
     )
     router_pad = jnp.pad(w_router, ((0, 0), (0, 128 - experts)))
     grads_sent = mm(picks_flat, cotangent).astype(bf16).reshape(n_ctx, CAP, width)
-    query_w, key_w, value_w, output_w, gains_all, router_all, expert_slices, grad_rows = send(
+    qkv_w, output_w, gains_all, router_all, expert_slices, grad_rows = send(
         0,
-        (("fsdp",), "g", w_query),
-        (("fsdp",), "g", key_weight),
-        (("fsdp",), "g", value_weight),
+        (("fsdp",), "g", jnp.concatenate([w_query, key_weight, value_weight], axis=1)),
         (("fsdp",), "g", w_output),
         (("fsdp",), "g", gains),
         (("fsdp",), "g", router_pad),
         (("tp",), "a", own_slices),
         (("ctx",), "f", grads_sent),
     )
-    query_w = query_w.reshape(width, -1)
-    key_w = key_w.reshape(width, -1)
-    value_w = value_w.reshape(width, -1)
+    qkv_w = qkv_w.reshape(width, -1)
     output_w = output_w.reshape(width, -1)
     lines = depth // 128
     gain_one = gains_all[:, :lines].reshape(width).astype(f32)
@@ -443,7 +431,6 @@
 
     grad_rows = grad_rows.reshape(n_ctx * CAP, width)
 
-    output_full = lax.all_gather(output_w, "tp", axis=1, tiled=True)
     expert_cat = expert_slices.transpose(2, 1, 0, 3).reshape(depth, 3 * n_tp * ff)
     expert_w = lax.all_gather(expert_cat, "fsdp", axis=0, tiled=True)
 
@@ -452,16 +439,21 @@
     seq_ends = jnp.cumsum(lengths_row)
     passed = (query_rows[:, None] >= seq_ends[None, :]).astype(jnp.int32)
     starts = jnp.sum(passed * lengths_row[None, :], axis=1)
-    cosine_table, sine_table = rope_tables(query_rows - starts)
+    q_end, pair_width = w_query.shape[1], key_weight.shape[1]
+    turned = q_end + pair_width
+    cosine, sine, first_half = rope_tables(query_rows - starts, turned)
     hidden_in = inputs.astype(f32)
     scale_one = lax.rsqrt(jnp.mean(hidden_in * hidden_in, axis=-1, keepdims=True) + norm_eps)
     normed_one = (hidden_in * scale_one * gain_one).astype(bf16)
-    queries = turn(mm(normed_one, query_w), cosine_table, sine_table).astype(bf16)
-    keys_local = turn(mm(normed_one, key_w), cosine_table, sine_table).astype(bf16)
-    values_local = mm(normed_one, value_w).astype(bf16)
-    pairs_local = jnp.concatenate([keys_local, values_local], axis=1)
-    pair_width = keys_local.shape[1]
-    (pairs_all,) = send(1, (("ctx",), "g", pairs_local))
+    qkv = mm(normed_one, qkv_w)
+    queries_keys = turn(qkv[:, :turned], cosine, sine, first_half).astype(bf16)
+    queries = queries_keys[:, :q_end]
+    pairs_local = jnp.concatenate(
+        [queries_keys[:, q_end:], qkv[:, turned:].astype(bf16)], axis=1
+    )
+    pairs_all, output_all = send(
+        1, (("ctx",), "g", pairs_local), (("tp",), "g", output_w)
+    )
     total_rows = n_ctx * rows
     pairs_all = pairs_all.reshape(total_rows, 2 * pair_width)
     key_heads = pair_width // HEAD_SIZE
@@ -490,6 +482,7 @@
     attended = attended.reshape(rows, -1).astype(bf16)
     (attended_all,) = send(2, (("tp",), "g", attended))
     attended_all = attended_all.transpose(1, 0, 2).reshape(rows, -1)
+    output_full = output_all.transpose(1, 0, 2).reshape(width, -1)
     residual = hidden_in + branch_scale * contract_cols(attended_all, output_full)
 
     scale_two = lax.rsqrt(jnp.mean(residual * residual, axis=-1, keepdims=True) + norm_eps)
@@ -541,15 +534,18 @@
         * scale_two_own**3
         * jnp.mean(weighted_two * residual_own, axis=-1, keepdims=True)
     )
-    (attn_in,) = send(6, (("tp",), "g", (branch_scale * residual_grad).astype(bf16)))
+    attn_in, pieces = send(
+        6,
+        (("tp",), "g", (branch_scale * residual_grad).astype(bf16)),
+        (("tp",), "a", expert_grad.reshape(n_tp, 3, depth, ff)),
+    )
     attn_in = attn_in.reshape(rows, width)
 
-    expert_grad, _ = lax.optimization_barrier((expert_grad, attn_in))
-    expert_grad = expert_grad.reshape(depth, 3, n_tp, ff).transpose(2, 1, 0, 3)
-    pieces = shifted(jnp.take(expert_grad, tp_order, axis=0), "tp", 1)
     expert_all = lax.all_gather(pieces, "ctx", axis=0, tiled=True)
 
-    grad_output = contract_rows(attn_in, attended)
+    side = jnp.pad(grad_router, ((0, 0), (0, 128 - experts)))
+    early = jnp.concatenate([contract_rows(attn_in, attended), side], axis=1).astype(bf16)
+    mixed_part = contract_rows(picks_flat, mixed_got).astype(bf16)
     attended_grad = mm(attn_in, output_w).astype(bf16)
 
     grad_heads = attended_grad.reshape(rows, key_heads, groups, HEAD_SIZE)
@@ -574,39 +570,42 @@
         ],
         axis=1,
     ).astype(bf16)
-    (pair_got,) = send(7, (("ctx",), "a", pair_grads.reshape(n_ctx, rows, 2 * pair_width)))
+    pair_got, mixed_parts, early_got = send(
+        7,
+        (("ctx",), "a", pair_grads.reshape(n_ctx, rows, 2 * pair_width)),
+        (("tp",), "a", mixed_part.reshape(n_tp, quarter, width)),
+        (("fsdp",), "a", early.reshape(n_fsdp, depth, -1)),
+    )
     pair_owned = jnp.sum(pair_got.astype(f32), axis=0)
-    query_grad = turn(query_grad_rot, cosine_table, -sine_table).astype(bf16)
-    key_grad = turn(pair_owned[:, :pair_width], cosine_table, -sine_table).astype(bf16)
-    value_grad = pair_owned[:, pair_width:].astype(bf16)
-    normed_one_part = (
-        contract_cols(query_grad, query_w)
-        + contract_cols(key_grad, key_w)
-        + contract_cols(value_grad, value_w)
-    )
+    turned_back = turn(
+        jnp.concatenate([query_grad_rot, pair_owned[:, :pair_width]], axis=1),
+        cosine,
+        -sine,
+        first_half,
+    )
+    qkv_grad = jnp.concatenate([turned_back, pair_owned[:, pair_width:]], axis=1).astype(bf16)
+    normed_one_part = contract_cols(qkv_grad, qkv_w)
     grad_gain_part = jnp.sum(normed_one_part * hidden_in * scale_one, axis=0)
-    grad_query = contract_rows(normed_one, query_grad)
-    grad_key = contract_rows(normed_one, key_grad)
-    grad_value = contract_rows(normed_one, value_grad)
-    mixed_part = contract_rows(picks_flat, mixed_got).astype(bf16)
-
-    n_rows = n_fsdp * n_ctx
-    share = width // n_rows
-    side = jnp.pad(grad_router, ((0, 0), (0, 128 - experts)))
-    small = jnp.concatenate([grad_query, grad_key, grad_value, grad_output, side], axis=1)
-    small = small.astype(bf16).reshape(n_rows, share, -1)
-    gain_parts = jnp.stack([grad_gain_part, grad_ffn_part]).reshape(2, n_rows, share)
-    gain_chunks = jnp.pad(gain_parts.transpose(1, 0, 2), ((0, 0), (0, 6), (0, 128 - share)))
-    one_parts, mixed_parts, small_got, gain_got = send(
+    grad_qkv = contract_rows(normed_one, qkv_grad).astype(bf16)
+    output = residual_own + branch_scale * jnp.sum(mixed_parts.astype(f32), axis=0)
+
+    gain_parts = jnp.stack([grad_gain_part, grad_ffn_part]).reshape(2, n_fsdp, depth)
+    gain_chunks = jnp.pad(gain_parts.transpose(1, 0, 2), ((0, 0), (0, 6), (0, 0)))
+    one_parts, qkv_got, gain_got, output = send(
         8,
         (("tp",), "a", normed_one_part.astype(bf16).reshape(n_tp, quarter, width)),
-        (("tp",), "a", mixed_part.reshape(n_tp, quarter, width)),
-        (("fsdp", "ctx"), "a", small),
-        (("fsdp", "ctx"), "a", gain_chunks),
-    )
-    small_sum = jnp.sum(small_got.astype(f32), axis=0).astype(bf16)
+        (("fsdp",), "a", grad_qkv.reshape(n_fsdp, depth, -1)),
+        (("fsdp",), "a", gain_chunks),
+        (("tp",), "g", output.astype(bf16)),
+    )
+    small = jnp.concatenate(
+        [
+            jnp.sum(qkv_got.astype(f32), axis=0).astype(bf16),
+            jnp.sum(early_got.astype(f32), axis=0).astype(bf16),
+        ],
+        axis=1,
+    )
     gain_sum = jnp.sum(gain_got, axis=0)
-    output = residual_own + branch_scale * jnp.sum(mixed_parts.astype(f32), axis=0)
     normed_one_grad = jnp.sum(one_parts.astype(f32), axis=0)
     weighted_one = normed_one_grad * gain_one
     hidden_own, scale_one_own = quarter_of(hidden_in), quarter_of(scale_one)
@@ -617,18 +616,16 @@
         * scale_one_own**3
         * jnp.mean(weighted_one * hidden_own, axis=-1, keepdims=True)
     )
-    small_all, gain_all, output, input_grad = send(
+    small_got, gain_all, input_grad = send(
         9,
-        (("ctx",), "g", small_sum),
+        (("ctx",), "a", small.reshape(n_ctx, depth // n_ctx, -1)),
         (("ctx", "tp"), "g", gain_sum),
-        (("tp",), "g", output.astype(bf16)),
         (("tp",), "g", input_grad.astype(bf16)),
     )
+    (small_all,) = send(10, (("ctx",), "g", jnp.sum(small_got.astype(f32), axis=0).astype(bf16)))
     small_all = small_all.reshape(depth, -1).astype(f32)
-    gain_all = jnp.sum(gain_all[:, :2, :share].reshape(n_ctx, n_tp, 2, share), axis=1)
-    gain_all = gain_all.transpose(1, 0, 2).reshape(2, depth)
-    grad_gate, grad_up, grad_down = spread(expert_all, n_ctx, n_tp)
-    q_end = queries.shape[1]
+    gain_all = jnp.sum(gain_all, axis=0)
+    grad_gate, grad_up, grad_down = spread(expert_all)
     k_end, v_end = q_end + pair_width, q_end + 2 * pair_width
     o_end = v_end + attended.shape[1]
     return (

time: 480 us -> 443 us (0.923)
  local copies, waits for them, and re-layouts: 58.6 us -> 32.4 us
  Pallas kernels: 290 us -> 301 us
  waiting for transfers between devices: 23.4 us -> 16.6 us
  matrix products: 44.1 us -> 39.3 us
    all_gather x1, waiting for transfers between devices: 16.7 us -> 0.01 us  [local(): expert_w = lax.all_gather(expert_cat, 'fsdp', axis=0, tiled=True)]
    reduce_scatter x1, waiting for transfers between devices: 0.02 us -> 16.6 us  [local(): lax.psum_scatter(expert_grad, 'fsdp', scatter_dimension=0, tiled=True)]
    pallas_call x8 -> x9, Pallas kernels: 190 us -> 204 us  [exchange(): pl.pallas_call(functools.partial(exchange_kernel, plan, sizes), out_shape...]
    ppermute x3 -> x0, waiting for transfers between devices: 6.59 us -> none  [shifted(): lax.ppermute(chunks[k], axis, [(s, (s + direction * k) % n) for s in rang...]
    unnamed x122 -> x103, local copies, waits for them, and re-layouts: 19.7 us -> 14.5 us
    dot_general x7 -> x5, matrix products: 11.1 us -> 6.9 us  [contract_rows(): lax.dot_general(left, right, (((0,), (0,)), ((), ())), precision=precisio...]
  transfers between devices with their start and end apart: 7 -> 3, of which waited for: 3 -> 1; matrix products, arithmetic and copies ran while one was open for 23% -> 19% of each run, Pallas kernels for 31% -> 33%
where the time goes in v4:
time: 443 us; the launch traced here: 442 us
  Pallas kernels  301 us (68%)
  matrix products  39.3 us (9%)
  other arithmetic  36.8 us (8%)
  local copies, waits for them, and re-layouts  32.4 us (7%)
  waiting for transfers between devices  16.6 us (4%)
  between operations  14.8 us (3%)
    pallas_call x9, Pallas kernels, exchange(): pl.pallas_call(functools.partial(exchange_kernel, plan, sizes), out_shape...  204 us
    pallas_call x1, Pallas kernels, expert_of_place(): pl.pallas_call(functools.partial(expert_kernel, n, width // sizes['fsdp']...  83.4 us
    reduce_scatter x1, waiting for transfers between devices, local(): lax.psum_scatter(expert_grad, 'fsdp', scatter_dimension=0, tiled=True)  16.6 us
    unnamed x103, local copies, waits for them, and re-layouts  14.5 us
    pallas_call x1, Pallas kernels, spread(): pl.pallas_call(spread_kernel, grid=(depth // block,), out_shape=[jax.Shap...  13.9 us
  transfers between devices with their start and end apart: 3, of which 1 were waited for; matrix products, arithmetic and copies ran while one was open for 19% of the time, Pallas kernels for 33%

profile of v4, /device:TPU:1, one launch (start us, length us, event | category | flops | bytes accessed | tf_op | source)
XLA Modules:
  0.0 441.6 jit_solution(10674268949598176014)
XLA Ops:
  7.3 1.6 constant_dynamic-slice_fusion.1
  11.4 3.1 convolution_convert_fusion.1
  17.6 40.5 %exchange_0.1 = (bf16[4,256,512]{2,1,0:T(8,128)(2,1)}, bf16[4,256,256]{2,1,0:T(8,128)(2,1)}, bf16[4,16,128]{2,1,0:T(8,128)(2,1)}, bf16[4,256,128]{2,1,0:T(8,128)...) custom-call(bf16[256,512]{1,0:T(8,128)(2,1)} %pad_maximum_fusion.5.refs_0_, ...), custom_call_target="tpu_custom_call" | custom-call | bytes 94699520 | tf_op jit(solution)/shard_map/exchange_0/pallas_call | solution.py:103
  58.1 1.8 copy.106
  63.3 1.9 fusion.41
  66.5 39.2 %exchange_1.1 = (bf16[8,256,256]{2,1,0:T(8,128)(2,1)}, bf16[4,1024,256]{2,1,0:T(8,128)(2,1)}) custom-call(bf16[256,256]{1,0:T(8,128)(2,1)} %pad_maximum_fusion.9.refs_0_, bf16[1024,256]{1,0:T(8,128)(2,1)} %bitcast.200), custom_call_target="tpu_custom_call" | custom-call | bytes 62914560 | tf_op jit(solution)/shard_map/exchange_1/pallas_call | solution.py:103
  105.6 1.3 fusion.78
  107.5 1.5 fusion.85
  110.2 2.1 copy-done.4
  112.4 1.5 fusion.29
  114.7 8.5 %exchange_2.1 = bf16[4,256,256]{2,1,0:T(8,128)(2,1)} custom-call(bf16[256,256]{1,0:T(8,128)(2,1)} %copy.105.refs_0_), custom_call_target="tpu_custom_call" | custom-call | bytes 10485760 | tf_op jit(solution)/shard_map/exchange_2/pallas_call | solution.py:103
  123.2 2.6 multiply_reduce_fusion.1
  127.5 2.0 convolution_convert_fusion.rows_ref
  129.5 83.4 %expert_of_place.1 = (bf16[1024,1024]{1,0:T(8,128)(2,1)S(1)}, bf16[1024,1024]{1,0:T(8,128)(2,1)S(1)}, f32[8,8,128]{2,1,0:T(8,128)S(1)}, bf16[12288,128]{1,0:T(8,128)(2,1)}) custom-call(bf16[1024,1024]{1,0:T(8,128)(2,1)} %convolution_convert_fusion.rows_ref, f32[8,8,128]{2,1,0:T(8,128)S(1)} %broadcast_in_dim.101.probs_ref, bf16[1024,1024]{1,0:T(8,128)(2,1)} %bitcast.246, ...), custom_call_target="tpu_custom_call" | custom-call | flops 19327352832 | bytes 104857600 | tf_op jit(solution)/shard_map/expert_of_place/pallas_call | solution.py:298
  212.9 1.3 copy-done.3
  216.0 3.1 convolution_convert_fusion.5
  219.2 9.8 %exchange_5.1 = (bf16[4,64,1024]{2,1,0:T(8,128)(2,1)}, f32[4,8,256]{2,1,0:T(8,128)}) custom-call(bf16[4,64,1024]{2,1,0:T(8,128)(2,1)} %bitcast.229, f32[8,256]{1,0:T(8,128)} %fusion.31.refs_1_), custom_call_target="tpu_custom_call" | custom-call | bytes 11141120 | tf_op jit(solution)/shard_map/exchange_5/pallas_call | solution.py:103
  232.3 1.7 multiply_reduce_fusion.4
  234.0 1.9 multiply_convert_fusion.2
  235.9 16.6 %reduce-scatter.2.cloned.1.call-done = bf16[3072,128]{1,0:T(8,128)(2,1)} async-done(((bf16[12288,128]{1,0:T(8,128)(2,1)}), bf16[3072,128]{1,0:T(8,128)(2,1)}) %reduce-scatter.2.cloned.1.call-update) | async-done | bytes 786448 | tf_op jit(solution)/shard_map/reduce_scatter | solution.py:504
  252.5 17.5 %exchange_6.1 = (bf16[4,64,1024]{2,1,0:T(8,128)(2,1)}, bf16[4,3,256,128]{3,2,1,0:T(8,128)(2,1)}) custom-call(bf16[64,1024]{1,0:T(8,128)(2,1)} %get-tuple-element.74.refs_0_, bf16[4,3,256,128]{3,2,1,0:T(8,128)(2,1)} %bitcast.219), custom_call_target="tpu_custom_call" | custom-call | bytes 26214400 | tf_op jit(solution)/shard_map/exchange_6/pallas_call | solution.py:103
  271.1 1.3 fusion.68
  274.4 1.7 pad.14.clone
  276.1 1.6 convolution_convert_fusion.4
  277.6 1.3 copy.113
  278.9 1.7 convolution_convert_fusion.6
  280.6 5.5 %fusion = (f32[2,2,256]{2,1,0:T(2,128)S(1)}, f32[2,2048,256,2]{2,1,3,0:T(8,128)S(1)}) fusion(f32[2,2,256,2048]{2,3,1,0:T(8,128)} %copy-done.4, f32[2,2,256]{2,1,0:T(2,128)S(1)} %log_add_fusion, bf16[2048,2,64,1]{0,2,3,1:T(8,128)(2,1)S(1)} %bitcast.197, bf16[256,2,2,64]{0,3,2,1:T(8,128)(2,1)S(1)} %bitcast.208), kind=kOutput, calls=%fused_computation.4 | convolution fusion | flops 274725888 | bytes 17440768 | tf_op jit(solution)/shard_map/rkgd,skd->kgrs/dot_general | solution.py:556
  286.6 1.6 fusion.2
  288.3 2.0 copy-done.5
  290.3 1.4 fusion.13
  292.2 4.9 %fusion.14 = bf16[2,64,2048]{2,1,0:T(8,128)(2,1)S(1)} fusion(bf16[256,2,2,64]{0,3,2,1:T(8,128)(2,1)S(1)} %bitcast.209, f32[2,2,256,2048]{2,3,1,0:T(8,128)} %copy-done.4, f32[2,2,256]{2,1,0:T(2,128)S(1)} %log_add_fusion), kind=kOutput, calls=%fused_computation.20 | convolution fusion | flops 272891904 | bytes 9048064 | tf_op jit(solution)/shard_map/kgrs,rkgd->skd/dot_general | solution.py:553
  298.1 2.0 pad_maximum_fusion.2.refs_2_
  301.1 38.9 %exchange_7.1 = (bf16[8,256,256]{2,1,0:T(8,128)(2,1)}, bf16[4,64,1024]{2,1,0:T(8,128)(2,1)}, bf16[4,256,384]{2,1,0:T(8,128)(2,1)}) custom-call(bf16[8,256,256]{2,1,0:T(8,128)(2,1)} %pad_maximum_fusion.refs_0_, bf16[4,64,1024]{2,1,0:T(8,128)(2,1)} %bitcast.230, bf16[4,256,384]{2,1,0:T(8,128)(2,1)} %pad_maximum_fusion.2.refs_2_), custom_call_target="tpu_custom_call" | custom-call | bytes 47185920 | tf_op jit(solution)/shard_map/exchange_7/pallas_call | solution.py:103
  340.1 1.4 convert_reduce_fusion
  341.6 3.1 convolution_multiply_fusion
  345.1 1.8 fusion.43
  346.9 2.6 multiply_reduce_fusion
  350.2 1.7 add_convert_fusion.refs_3_
  352.0 1.5 convolution_convert_fusion.2
  353.5 19.7 %exchange_8.1 = (bf16[4,64,1024]{2,1,0:T(8,128)(2,1)}, bf16[4,256,512]{2,1,0:T(8,128)(2,1)}, f32[4,8,256]{2,1,0:T(8,128)}, bf16[4,64,1024]{2,1,0:T(8,128)(2,1)}) custom-call(bf16[4,64,1024]{2,1,0:T(8,128)(2,1)} %bitcast.228, bf16[4,256,512]{2,1,0:T(8,128)(2,1)} %bitcast.211, f32[4,8,256]{2,1,0:T(8,128)} %pad.15.refs_2_, bf16[64,1024]{1,0:T(8,128)(2,1)} %add_convert_fusion.refs_3_), custom_call_target="tpu_custom_call" | custom-call | bytes 42598400 | tf_op jit(solution)/shard_map/exchange_8/pallas_call | solution.py:103
  373.2 1.5 reduce_sum.222
  374.8 1.4 reduce_sum.224.refs_1_
  379.1 18.1 %exchange_9.1 = (bf16[8,32,896]{2,1,0:T(8,128)(2,1)}, f32[32,8,256]{2,1,0:T(8,128)}, bf16[4,64,1024]{2,1,0:T(8,128)(2,1)}) custom-call(bf16[8,32,896]{2,1,0:T(8,128)(2,1)} %bitcast.207, f32[8,256]{1,0:T(8,128)} %reduce_sum.224.refs_1_, bf16[64,1024]{1,0:T(8,128)(2,1)} %subtract_convert_fusion.refs_2_), custom_call_target="tpu_custom_call" | custom-call | bytes 24903680 | tf_op jit(solution)/shard_map/exchange_9/pallas_call | solution.py:103
  397.3 1.7 reduce_sum.228.refs_0_
  399.0 11.8 %exchange_10.1 = bf16[8,32,896]{2,1,0:T(8,128)(2,1)} custom-call(bf16[32,896]{1,0:T(8,128)(2,1)} %reduce_sum.228.refs_0_), custom_call_target="tpu_custom_call" | custom-call | bytes 9175040 | tf_op jit(solution)/shard_map/exchange_10/pallas_call | solution.py:103
  415.7 2.8 copy-done.2
  418.5 13.9 %spread.1 = (f32[8192,128]{1,0:T(8,128)}, f32[8192,128]{1,0:T(8,128)}, f32[8192,128]{1,0:T(8,128)}) custom-call(bf16[32,3,256,128]{3,2,1,0:T(8,128)(2,1)S(1)} %copy-done.2), custom_call_target="tpu_custom_call" | custom-call | tf_op jit(solution)/shard_map/spread/pallas_call | solution.py:130
  433.2 1.9 copy.152
  (199 shorter events, 35.2 us)
Async XLA Ops:
  7.2 1.9 copy-start
  7.2 9.0 %copy-start.23 = (bf16[256,128]{1,0:T(8,128)(2,1)S(1)}, bf16[256,128]{1,0:T(8,128)(2,1)}, u32[]{:S(2)}) copy-start(bf16[256,128]{1,0:T(8,128)(2,1)} %param.21) | copy-start | bytes 196612
  7.2 122.3 %all-gather.3.cloned.1.call-start = ((), (), s32[]{:S(2)}) async-start(), calls=%async_computation.1 | async-start | bytes 3932160 | tf_op jit(solution)/shard_map/all_gather | solution.py:435
  7.3 9.7 %copy-start.41 = (bf16[256]{0:T(256)(128)(2,1)S(1)}, bf16[256]{0:T(256)(128)(2,1)}, u32[]{:S(2)}) copy-start(bf16[256]{0:T(256)(128)(2,1)} %param.23) | copy-start | bytes 1540
  7.3 9.7 %copy-start.42 = (bf16[256]{0:T(256)(128)(2,1)S(1)}, bf16[256]{0:T(256)(128)(2,1)}, u32[]{:S(2)}) copy-start(bf16[256]{0:T(256)(128)(2,1)} %param.18) | copy-start | bytes 1540
  9.3 6.9 %copy-start.22 = (bf16[256,256]{1,0:T(8,128)(2,1)S(1)}, bf16[256,256]{1,0:T(8,128)(2,1)}, u32[]{:S(2)}) copy-start(bf16[256,256]{1,0:T(8,128)(2,1)} %param.19) | copy-start | bytes 393220
  9.3 6.9 %copy-start.24 = (bf16[256,128]{1,0:T(8,128)(2,1)S(1)}, bf16[256,128]{1,0:T(8,128)(2,1)}, u32[]{:S(2)}) copy-start(bf16[256,128]{1,0:T(8,128)(2,1)} %param.20) | copy-start | bytes 196612
  16.2 45.8 %copy-start.8 = (bf16[256,1024]{1,0:T(8,128)(2,1)S(1)}, bf16[256,1024]{1,0:T(8,128)(2,1)}, u32[]{:S(2)}) copy-start(bf16[256,1024]{1,0:T(8,128)(2,1)} %param.14) | copy-start | bytes 1572868
  58.1 4.1 copy-start.43
  58.1 4.9 %copy-start.40 = (s32[1,4]{1,0:T(1,128)S(1)}, s32[1,4]{1,0:T(1,128)}, u32[]{:S(2)}) copy-start(s32[1,4]{1,0:T(1,128)} %param.16) | copy-start | bytes 52
  61.1 191.4 %reduce-scatter.2.cloned.1.call-start = ((), (), s32[]{:S(2)}) async-start(), calls=%async_computation.2 | async-start | bytes 3932160 | tf_op jit(solution)/shard_map/reduce_scatter | solution.py:504
  62.2 44.8 %copy-start.34 = (f32[256]{0:T(256)}, f32[256]{0:T(256)S(1)}, u32[]{:S(2)}) copy-start(f32[256]{0:T(256)S(1)} %add_rsqrt_fusion.1) | copy-start | bytes 3076
  63.0 46.1 %copy-start.26 = (f32[384]{0:T(512)}, f32[384]{0:T(512)S(1)}, u32[]{:S(2)}) copy-start(f32[384]{0:T(512)S(1)} %fusion.58) | copy-start | bytes 4612
  63.0 46.1 %copy-start.38 = (pred[384]{0:T(512)(128)(4,1)}, pred[384]{0:T(512)(128)(4,1)S(1)}, u32[]{:S(2)}) copy-start(pred[384]{0:T(512)(128)(4,1)S(1)} %fusion.59) | copy-start | bytes 1156
  63.3 45.7 %copy-start.32 = (f32[256]{0:T(256)}, f32[256]{0:T(256)S(1)}, u32[]{:S(2)}) copy-start(f32[256]{0:T(256)S(1)} %subtract_convert_fusion.1) | copy-start | bytes 3076
  107.1 1.9 copy-start.9
  107.3 1.8 copy-start.18
  107.5 2.7 copy-start.11
  109.1 3.2 copy-start.4
  109.1 3.3 copy-start.28
  110.2 3.7 copy-start.30
  112.4 10.8 %copy-start.25 = (s32[256,8]{0,1:T(8,128)S(1)}, s32[256,8]{0,1:T(8,128)}, u32[]{:S(2)}) copy-start(s32[256,8]{0,1:T(8,128)} %param.17) | copy-start | bytes 24580
  113.9 9.3 %copy-start.16 = (bf16[2,64,2,256]{3,1,2,0:T(8,128)(2,1)}, bf16[2,64,2,256]{3,1,2,0:T(8,128)(2,1)S(1)}, u32[]{:S(2)}) copy-start(bf16[2,64,2,256]{3,1,2,0:T(8,128)(2,1)S(1)} %fusion.29) | copy-start | bytes 393220
  113.9 12.1 %copy-start.14 = (bf16[4,256,128]{2,1,0:T(8,128)(2,1)S(1)}, bf16[4,256,128]{2,1,0:T(8,128)(2,1)}, u32[]{:S(2)}) copy-start(bf16[4,256,128]{2,1,0:T(8,128)(2,1)} %get-tuple-element.46) | copy-start | bytes 786436
  125.9 3.6 copy-start.6
  126.4 104.1 %copy-start.31 = (f32[256]{0:T(256)}, f32[256]{0:T(256)S(1)}, u32[]{:S(2)}) copy-start(f32[256]{0:T(256)S(1)} %fusion.54) | copy-start | bytes 3076
  214.3 201.5 %all-gather.5.cloned.1.call-start = ((), (), s32[]{:S(2)}) async-start(), calls=%async_computation.3 | async-start | bytes 7077888 | tf_op jit(solution)/shard_map/all_gather | solution.py:544
  219.1 53.3 %copy-start.29 = (f32[2,2,256]{2,1,0:T(2,128)S(1)}, f32[2,2,256]{2,1,0:T(2,128)}, u32[]{:S(2)}) copy-start(f32[2,2,256]{2,1,0:T(2,128)} %copy-done.28) | copy-start | bytes 12292
  273.5 7.1 %copy-start.12 = (bf16[2048,128]{0,1:T(8,128)(2,1)S(1)}, bf16[2048,128]{0,1:T(8,128)(2,1)}, u32[]{:S(2)}) copy-start(bf16[2048,128]{0,1:T(8,128)(2,1)} %copy-done.11) | copy-start | bytes 1572868
  280.6 5.5 %slice-start = ((s8[8388608]{0:T(1024)(128)(4,1)}), s8[4194304]{0:T(1024)(128)(4,1)S(1)}, s32[]{:S(2)}) async-start(s8[8388608]{0:T(1024)(128)(4,1)} %bitcast.191), calls=%async_computation.4 | async-start | bytes 8388608
  280.6 6.0 %slice-start.1 = ((s8[8388608]{0:T(1024)(128)(4,1)}), s8[4194304]{0:T(1024)(128)(4,1)S(1)}, s32[]{:S(2)}) async-start(s8[8388608]{0:T(1024)(128)(4,1)} %bitcast.191), calls=%async_computation.5 | async-start | bytes 8388608
  286.6 3.7 copy-start.19
  288.3 2.0 copy-start.5
  292.2 5.5 %copy-start.17 = (bf16[2,64,2,256]{3,1,2,0:T(8,128)(2,1)S(1)}, bf16[2,64,2,256]{3,1,2,0:T(8,128)(2,1)}, u32[]{:S(2)}) copy-start(bf16[2,64,2,256]{3,1,2,0:T(8,128)(2,1)} %copy-done.16) | copy-start | bytes 393220
  298.0 43.6 %copy-start.10 = (bf16[2048,128]{0,1:T(8,128)(2,1)S(1)}, bf16[2048,128]{0,1:T(8,128)(2,1)}, u32[]{:S(2)}) copy-start(bf16[2048,128]{0,1:T(8,128)(2,1)} %copy-done.9) | copy-start | bytes 1572868
  340.1 5.0 %copy-start.27 = (f32[384]{0:T(512)S(1)}, f32[384]{0:T(512)}, u32[]{:S(2)}) copy-start(f32[384]{0:T(512)} %copy-done.26) | copy-start | bytes 4612
  340.1 5.0 %copy-start.33 = (f32[256]{0:T(256)S(1)}, f32[256]{0:T(256)}, u32[]{:S(2)}) copy-start(f32[256]{0:T(256)} %copy-done.32) | copy-start | bytes 3076
  340.1 5.0 %copy-start.39 = (pred[384]{0:T(512)(128)(4,1)S(1)}, pred[384]{0:T(512)(128)(4,1)}, u32[]{:S(2)}) copy-start(pred[384]{0:T(512)(128)(4,1)} %copy-done.38) | copy-start | bytes 1156
  341.6 5.3 %copy-start.35 = (f32[256]{0:T(256)S(1)}, f32[256]{0:T(256)}, u32[]{:S(2)}) copy-start(f32[256]{0:T(256)} %copy-done.34) | copy-start | bytes 3076
  344.7 5.4 %copy-start.20 = (bf16[4,64,1024]{2,1,0:T(8,128)(2,1)S(1)}, bf16[4,64,1024]{2,1,0:T(8,128)(2,1)}, u32[]{:S(2)}) copy-start(bf16[4,64,1024]{2,1,0:T(8,128)(2,1)} %get-tuple-element.57) | copy-start | bytes 1572868
  346.9 27.8 %copy-start.15 = (bf16[4,256,384]{2,1,0:T(8,128)(2,1)S(1)}, bf16[4,256,384]{2,1,0:T(8,128)(2,1)}, u32[]{:S(2)}) copy-start(bf16[4,256,384]{2,1,0:T(8,128)(2,1)} %get-tuple-element.60) | copy-start | bytes 2359300
  350.2 27.9 %copy-start.7 = (f32[256,1024]{1,0:T(8,128)S(1)}, f32[256,1024]{1,0:T(8,128)}, u32[]{:S(2)}) copy-start(f32[256,1024]{1,0:T(8,128)} %convert_element_type.143) | copy-start | bytes 3145732
  352.0 26.3 %copy-start.13 = (f32[64,1024]{1,0:T(8,128)S(1)}, f32[64,1024]{1,0:T(8,128)}, u32[]{:S(2)}) copy-start(f32[64,1024]{1,0:T(8,128)} %get-tuple-element.75) | copy-start | bytes 786436
  352.0 26.3 %copy-start.36 = (f32[64]{0:T(128)S(1)}, f32[64]{0:T(128)}, u32[]{:S(2)}) copy-start(f32[64]{0:T(128)} %get-tuple-element.72) | copy-start | bytes 772
  352.0 26.4 %copy-start.37 = (f32[64]{0:T(128)S(1)}, f32[64]{0:T(128)}, u32[]{:S(2)}) copy-start(f32[64]{0:T(128)} %get-tuple-element.73) | copy-start | bytes 772
  411.9 20.5 %copy-start.21 = (bf16[4,64,1024]{2,1,0:T(8,128)(2,1)S(1)}, bf16[4,64,1024]{2,1,0:T(8,128)(2,1)}, u32[]{:S(2)}) copy-start(bf16[4,64,1024]{2,1,0:T(8,128)(2,1)} %get-tuple-element.58) | copy-start | bytes 1572868
  414.9 20.2 %copy-start.1 = (bf16[256,32,128]{2,1,0:T(8,128)(2,1)S(1)}, bf16[256,32,128]{2,1,0:T(8,128)(2,1)}, u32[]{:S(2)}) copy-start(bf16[256,32,128]{2,1,0:T(8,128)(2,1)} %param.25) | copy-start | bytes 6291460
  415.7 2.8 copy-start.2
  (1 other events, 1.3 us)
Sparse Core Ops, SparseCore 0:
  61.2 40.8 all-gather.2
  214.4 38.0 reduce-scatter.1
  270.1 104.5 all-gather.4

commit v5 on v4

--- a/solution.py
+++ b/solution.py
@@ -141,6 +141,7 @@
 
 def expert_kernel(
     n,
+    n_fsdp,
     part,
     rows_ref,
     probs_ref,
@@ -150,6 +151,8 @@
     mixed_got,
     gate_got,
     wgrad_ref,
+    wgrad_buf,
+    wgrad_got,
     norm_buf,
     probs_buf,
     both_buf,
@@ -159,8 +162,10 @@
     gate_buf,
     send_sems,
     recv_sems,
+    wgrad_send,
+    wgrad_recv,
 ):
-    me = lax.axis_index("ctx")
+    me, fsdp_at = lax.axis_index("ctx"), lax.axis_index("fsdp")
     hidden = w_ref.shape[1] // 3
 
     def chunk(ref, k):
@@ -195,7 +200,14 @@
         pl.semaphore_signal(
             barrier, inc=1, device_id={"ctx": lax.rem(me + k, n)}, device_id_type=MESH
         )
-    pl.semaphore_wait(barrier, n - 1)
+    for k in range(1, n_fsdp):
+        pl.semaphore_signal(
+            barrier,
+            inc=1,
+            device_id={"fsdp": lax.rem(fsdp_at + k, n_fsdp)},
+            device_id_type=MESH,
+        )
+    pl.semaphore_wait(barrier, n - 1 + n_fsdp - 1)
     for k in range(1, 4):
         for item in out_copies(k):
             item.start()
@@ -263,24 +275,51 @@
     mixed_got[:CAP] = mixed_buf[:CAP]
     gate_got[0] = gate_buf[0]
 
-    width, slim = w_ref.shape[0], wgrad_ref.shape[1]
+    slim = wgrad_ref.shape[1]
+
+    def wgrad_copy(k):
+        return pltpu.make_async_remote_copy(
+            src_ref=wgrad_buf.at[k],
+            dst_ref=wgrad_got.at[k],
+            send_sem=wgrad_send.at[k],
+            recv_sem=wgrad_recv.at[k],
+            device_id={"fsdp": lax.rem(fsdp_at + k, n_fsdp)},
+            device_id_type=MESH,
+        )
 
     def weight_grads(j, carry):
-        here = pl.ds(pl.multiple_of(j * part, part), part)
+        k = lax.rem(j + 1, n_fsdp)
+        here = pl.ds(pl.multiple_of(lax.rem(fsdp_at + k, n_fsdp) * part, part), part)
         gate_up = contract_rows(norm_buf[:, here], both_buf[...]).astype(bf16)
         down = (contract_rows(grads_ref[:, here], weighted_buf[...]) * branch_scale).astype(bf16)
         for piece in range(hidden // slim):
             for which in range(3):
-                row = (j * (hidden // slim) + piece) * 3 + which
-                at = pl.ds(pl.multiple_of(row * part, part), part)
+                row = (piece * 3 + which) * part
                 if which < 2:
                     start = which * hidden + piece * slim
-                    wgrad_ref[at, :] = gate_up[:, start : start + slim]
+                    wgrad_buf[k, row : row + part, :] = gate_up[:, start : start + slim]
                 else:
-                    wgrad_ref[at, :] = down[:, piece * slim : (piece + 1) * slim]
+                    wgrad_buf[k, row : row + part, :] = down[:, piece * slim : (piece + 1) * slim]
+
+        @pl.when(k > 0)
+        def _():
+            wgrad_copy(k).start()
+
         return carry
 
-    lax.fori_loop(0, width // part, weight_grads, 0)
+    lax.fori_loop(0, n_fsdp, weight_grads, 0)
+    for k in range(1, n_fsdp):
+        wgrad_copy(k).wait()
+
+    def summed(j, carry):
+        at = pl.ds(pl.multiple_of(j * part, part), part)
+        total = wgrad_buf[0, at, :].astype(f32)
+        for k in range(1, n_fsdp):
+            total += wgrad_got[k, at, :].astype(f32)
+        wgrad_ref[at, :] = total.astype(bf16)
+        return carry
+
+    lax.fori_loop(0, wgrad_ref.shape[0] // part, summed, 0)
     for k in range(1, n):
         for item in out_copies(k):
             item.wait_send()
@@ -291,21 +330,24 @@
 def expert_of_place(sizes, rows_sent, probs_sent, grad_rows, expert_w):
     n = sizes["ctx"]
     total, width = rows_sent.shape
-    columns = expert_w.shape[1]
-    hidden = columns // 3
+    n_fsdp, n_tp = sizes["fsdp"], sizes["tp"]
+    hidden, part = expert_w.shape[1] // 3, width // n_fsdp
+    owned = (n_tp * 3 * part, hidden // n_tp)
     like = jax.ShapeDtypeStruct
     vmem = pl.BlockSpec(memory_space=pltpu.VMEM)
     return pl.pallas_call(
-        functools.partial(expert_kernel, n, width // sizes["fsdp"]),
+        functools.partial(expert_kernel, n, n_fsdp, part),
         out_shape=[
             like((total, width), bf16),
             like((total, width), bf16),
             like(probs_sent.shape, f32),
-            like((width * sizes["tp"] * 3, hidden // sizes["tp"]), bf16),
+            like(owned, bf16),
         ],
         in_specs=[vmem] * 4,
         out_specs=[vmem] * 4,
         scratch_shapes=[
+            pltpu.VMEM((n_fsdp,) + owned, bf16),
+            pltpu.VMEM((n_fsdp,) + owned, bf16),
             pltpu.VMEM((total, width), bf16),
             pltpu.VMEM(probs_sent.shape, f32),
             pltpu.VMEM((total, 2 * hidden), bf16),
@@ -315,6 +357,8 @@
             pltpu.VMEM(probs_sent.shape, f32),
             pltpu.SemaphoreType.DMA((5, n)),
             pltpu.SemaphoreType.DMA((5, n)),
+            pltpu.SemaphoreType.DMA((n_fsdp,)),
+            pltpu.SemaphoreType.DMA((n_fsdp,)),
         ],
         compiler_params=pltpu.CompilerParams(
             collective_id=3, has_side_effects=True, vmem_limit_bytes=48 * 1024 * 1024
@@ -413,17 +457,15 @@
     )
     router_pad = jnp.pad(w_router, ((0, 0), (0, 128 - experts)))
     grads_sent = mm(picks_flat, cotangent).astype(bf16).reshape(n_ctx, CAP, width)
-    qkv_w, output_w, gains_all, router_all, expert_slices, grad_rows = send(
+    qkv_w, gains_all, router_all, expert_slices, grad_rows = send(
         0,
         (("fsdp",), "g", jnp.concatenate([w_query, key_weight, value_weight], axis=1)),
-        (("fsdp",), "g", w_output),
         (("fsdp",), "g", gains),
         (("fsdp",), "g", router_pad),
         (("tp",), "a", own_slices),
         (("ctx",), "f", grads_sent),
     )
     qkv_w = qkv_w.reshape(width, -1)
-    output_w = output_w.reshape(width, -1)
     lines = depth // 128
     gain_one = gains_all[:, :lines].reshape(width).astype(f32)
     gain_two = gains_all[:, lines : 2 * lines].reshape(width).astype(f32)
@@ -451,9 +493,8 @@
     pairs_local = jnp.concatenate(
         [queries_keys[:, q_end:], qkv[:, turned:].astype(bf16)], axis=1
     )
-    pairs_all, output_all = send(
-        1, (("ctx",), "g", pairs_local), (("tp",), "g", output_w)
-    )
+    pairs_all, output_w = send(1, (("ctx",), "g", pairs_local), (("fsdp",), "g", w_output))
+    output_w = output_w.reshape(width, -1)
     total_rows = n_ctx * rows
     pairs_all = pairs_all.reshape(total_rows, 2 * pair_width)
     key_heads = pair_width // HEAD_SIZE
@@ -480,13 +521,20 @@
         "kgrs,skd->rkgd", attn_probs.astype(bf16), values_all, preferred_element_type=f32
     )
     attended = attended.reshape(rows, -1).astype(bf16)
-    (attended_all,) = send(2, (("tp",), "g", attended))
-    attended_all = attended_all.transpose(1, 0, 2).reshape(rows, -1)
-    output_full = output_all.transpose(1, 0, 2).reshape(width, -1)
-    residual = hidden_in + branch_scale * contract_cols(attended_all, output_full)
-
-    scale_two = lax.rsqrt(jnp.mean(residual * residual, axis=-1, keepdims=True) + norm_eps)
-    normed_two = (residual * scale_two * gain_two).astype(bf16)
+    quarter = rows // n_tp
+
+    def quarter_of(array):
+        return lax.dynamic_slice_in_dim(array, tp_at * quarter, quarter, 0)
+
+    attn_part = contract_cols(attended, output_w).astype(bf16)
+    (attn_parts,) = send(2, (("tp",), "a", attn_part.reshape(n_tp, quarter, width)))
+    hidden_own, scale_one_own = quarter_of(hidden_in), quarter_of(scale_one)
+    residual_own = hidden_own + branch_scale * jnp.sum(attn_parts.astype(f32), axis=0)
+
+    scale_two_own = lax.rsqrt(jnp.mean(residual_own * residual_own, axis=-1, keepdims=True) + norm_eps)
+    normed_two_own = (residual_own * scale_two_own * gain_two).astype(bf16)
+    (normed_two,) = send(11, (("tp",), "g", normed_two_own))
+    normed_two = normed_two.reshape(rows, width)
     logits = mm(normed_two, router_w)
     route_masked = jnp.where(chosen, logits, -1e30)
     route_exp = jnp.exp(route_masked - jnp.max(route_masked, axis=-1, keepdims=True))
@@ -501,19 +549,16 @@
     norm_grad_got, mixed_got, gate_grad_got, expert_grad = expert_of_place(
         sizes, rows_sent, probs_sent, grad_rows, expert_w
     )
-    expert_grad = lax.psum_scatter(expert_grad, "fsdp", scatter_dimension=0, tiled=True)
-
-    quarter = rows // n_tp
+
     norm_grad_part = contract_rows(picks_flat, norm_grad_got)
     gate_grad_part = jnp.sum(picks.astype(f32) * gate_grad_got[:, 0, :, None], axis=1)
-    norm_grad_parts, gate_grad_parts = send(
+    norm_grad_parts, gate_grad_parts, pieces = send(
         5,
         (("tp",), "a", norm_grad_part.astype(bf16).reshape(n_tp, quarter, width)),
         (("tp",), "g", gate_grad_part),
-    )
-
-    def quarter_of(array):
-        return lax.dynamic_slice_in_dim(array, tp_at * quarter, quarter, 0)
+        (("tp",), "a", expert_grad.reshape(n_tp, 3, depth, ff)),
+    )
+    expert_all = lax.all_gather(pieces, "ctx", axis=0, tiled=True)
 
     back_order = lax.rem(jnp.arange(n_ctx, dtype=jnp.int32) + n_ctx - ctx_at, n_ctx)
     gate_grads = jnp.take(gate_grad_parts, back_order, axis=1)
@@ -525,7 +570,6 @@
     router_back = contract_cols(quarter_of(route_grad), router_w.astype(f32), highest)
     normed_grad = jnp.sum(norm_grad_parts.astype(f32), axis=0) + router_back
     weighted_two = normed_grad * gain_two
-    residual_own, scale_two_own = quarter_of(residual), quarter_of(scale_two)
     grad_ffn_part = jnp.sum(normed_grad * residual_own * scale_two_own, axis=0)
     residual_grad = (
         quarter_of(cotangent).astype(f32)
@@ -534,14 +578,8 @@
         * scale_two_own**3
         * jnp.mean(weighted_two * residual_own, axis=-1, keepdims=True)
     )
-    attn_in, pieces = send(
-        6,
-        (("tp",), "g", (branch_scale * residual_grad).astype(bf16)),
-        (("tp",), "a", expert_grad.reshape(n_tp, 3, depth, ff)),
-    )
+    (attn_in,) = send(6, (("tp",), "g", (branch_scale * residual_grad).astype(bf16)))
     attn_in = attn_in.reshape(rows, width)
-
-    expert_all = lax.all_gather(pieces, "ctx", axis=0, tiled=True)
 
     side = jnp.pad(grad_router, ((0, 0), (0, 128 - experts)))
     early = jnp.concatenate([contract_rows(attn_in, attended), side], axis=1).astype(bf16)
@@ -608,7 +646,6 @@
     gain_sum = jnp.sum(gain_got, axis=0)
     normed_one_grad = jnp.sum(one_parts.astype(f32), axis=0)
     weighted_one = normed_one_grad * gain_one
-    hidden_own, scale_one_own = quarter_of(hidden_in), quarter_of(scale_one)
     input_grad = (
         residual_grad
         + scale_one_own * weighted_one

time: 443 us -> 439 us (level)
  waiting for transfers between devices: 16.6 us -> 0.04 us
  Pallas kernels: 301 us -> 309 us
    reduce_scatter x1 -> x0, waiting for transfers between devices: 16.6 us -> none  [local(): lax.psum_scatter(expert_grad, 'fsdp', scatter_dimension=0, tiled=True)]
    pallas_call x9 -> x10, Pallas kernels: 204 us -> 211 us  [exchange(): pl.pallas_call(functools.partial(exchange_kernel, plan, sizes), out_shape...]
    unnamed x103 -> x107, local copies, waits for them, and re-layouts: 14.5 us -> 14.7 us
  transfers between devices with their start and end apart: 3 -> 2, of which waited for: 1 -> 0; matrix products, arithmetic and copies ran while one was open for 19% -> 20% of each run, Pallas kernels for 33% -> 35%
where the time goes in v5:
time: 439 us; the launch traced here: 437 us
  Pallas kernels  309 us (70%)
  matrix products  40.4 us (9%)
  other arithmetic  38.4 us (9%)
  local copies, waits for them, and re-layouts  34.3 us (8%)
  between operations  15.1 us (3%)
    pallas_call x10, Pallas kernels, exchange(): pl.pallas_call(functools.partial(exchange_kernel, plan, sizes), out_shape...  211 us
    pallas_call x1, Pallas kernels, expert_of_place(): pl.pallas_call(functools.partial(expert_kernel, n, n_fsdp, part), out_sha...  83.7 us
    unnamed x107, local copies, waits for them, and re-layouts  14.7 us
    pallas_call x1, Pallas kernels, spread(): pl.pallas_call(spread_kernel, grid=(depth // block,), out_shape=[jax.Shap...  13.9 us
    dot_general x6, matrix products, mm(): return jnp.dot(left, right, preferred_element_type=f32)  9.73 us
  transfers between devices with their start and end apart: 2, of which 0 were waited for; matrix products, arithmetic and copies ran while one was open for 20% of the time, Pallas kernels for 35%

profile of v5, /device:TPU:1, one launch (start us, length us, event | category | flops | bytes accessed | tf_op | source)
XLA Modules:
  0.0 437.4 jit_solution(7100710364283279501)
XLA Ops:
  7.3 1.6 constant_dynamic-slice_fusion.1
  11.4 3.2 convolution_convert_fusion.1
  17.7 40.3 %exchange_0.1 = (bf16[4,256,512]{2,1,0:T(8,128)(2,1)}, bf16[4,16,128]{2,1,0:T(8,128)(2,1)}, bf16[4,256,128]{2,1,0:T(8,128)(2,1)}, bf16[4,3,256,128]{3,2,1,0:T(8,128)(2,1)}, bf16[8,128,1024]{2,1,0:T(8,128)(2,1)}) custom-call(bf16[256,512]{1,0:T(8,128)(2,1)} %pad_maximum_fusion.5.refs_0_, bf16[16,128]{1,0:T(8,128)(2,1)} %maximum_maximum_fusion.refs_1_, ...), custom_call_target="tpu_custom_call" | custom-call | bytes 84213760 | tf_op jit(solution)/shard_map/exchange_0/pallas_call | solution.py:103
  58.0 1.8 copy.102
  63.2 1.9 fusion.28
  65.2 1.3 fusion.17
  67.3 16.8 %exchange_1.1 = (bf16[8,256,256]{2,1,0:T(8,128)(2,1)}, bf16[4,256,256]{2,1,0:T(8,128)(2,1)}) custom-call(bf16[256,256]{1,0:T(8,128)(2,1)} %pad_maximum_fusion.9.refs_0_, bf16[256,256]{1,0:T(8,128)(2,1)} %refs_1_.1), custom_call_target="tpu_custom_call" | custom-call | bytes 31457280 | tf_op jit(solution)/shard_map/exchange_1/pallas_call | solution.py:103
  86.0 2.7 fusion.71
  89.9 2.1 copy-done.4
  92.0 1.5 fusion.18
  94.7 12.1 %exchange_2.1 = bf16[4,64,1024]{2,1,0:T(8,128)(2,1)} custom-call(bf16[4,64,1024]{2,1,0:T(8,128)(2,1)} %bitcast.190), custom_call_target="tpu_custom_call" | custom-call | bytes 10485760 | tf_op jit(solution)/shard_map/exchange_2/pallas_call | solution.py:103
  109.4 8.5 %exchange_11.1 = bf16[4,64,1024]{2,1,0:T(8,128)(2,1)} custom-call(bf16[64,1024]{1,0:T(8,128)(2,1)} %multiply_convert_fusion.2.refs_0_), custom_call_target="tpu_custom_call" | custom-call | bytes 10485760 | tf_op jit(solution)/shard_map/exchange_11/pallas_call | solution.py:103
  117.9 1.3 fusion.72
  121.1 3.1 convolution_convert_fusion.rows_ref
  124.2 83.7 %expert_of_place.1 = (bf16[1024,1024]{1,0:T(8,128)(2,1)S(1)}, bf16[1024,1024]{1,0:T(8,128)(2,1)S(1)}, f32[8,8,128]{2,1,0:T(8,128)S(1)}, bf16[3072,128]{1,0:T(8,128)(2,1)S(1)}) custom-call(bf16[1024,1024]{1,0:T(8,128)(2,1)} %convolution_convert_fusion.rows_ref, f32[8,8,128]{2,1,0:T(8,128)S(1)} %broadcast_in_dim.101.probs_ref, bf16[1024,1024]{1,0:T(8,128)(2,1)} %bitcast.230, ...), custom_call_target="tpu_custom_call" | custom-call | flops 19327352832 | bytes 104857600 | tf_op jit(solution)/shard_map/expert_of_place/pallas_call | solution.py:338
  208.8 1.6 convolution_convert_fusion.6
  211.2 18.0 %exchange_5.1 = (bf16[4,64,1024]{2,1,0:T(8,128)(2,1)}, f32[4,8,256]{2,1,0:T(8,128)}, bf16[4,3,256,128]{3,2,1,0:T(8,128)(2,1)}) custom-call(bf16[4,64,1024]{2,1,0:T(8,128)(2,1)} %bitcast.213, f32[8,256]{1,0:T(8,128)} %fusion.20.refs_1_, bf16[4,3,256,128]{3,2,1,0:T(8,128)(2,1)} %bitcast.170), custom_call_target="tpu_custom_call" | custom-call | bytes 26869760 | tf_op jit(solution)/shard_map/exchange_5/pallas_call | solution.py:103
  232.6 1.6 multiply_reduce_fusion.3
  234.2 1.8 multiply_convert_fusion.1
  236.0 8.5 %exchange_6.1 = bf16[4,64,1024]{2,1,0:T(8,128)(2,1)} custom-call(bf16[64,1024]{1,0:T(8,128)(2,1)} %get-tuple-element.70.refs_0_), custom_call_target="tpu_custom_call" | custom-call | bytes 10485760 | tf_op jit(solution)/shard_map/exchange_6/pallas_call | solution.py:103
  244.5 2.0 copy.109
  247.8 1.5 convolution_convert_fusion.7
  249.4 5.6 %fusion = (f32[2,2,256]{2,1,0:T(2,128)S(1)}, f32[2,2048,256,2]{2,1,3,0:T(8,128)S(1)}) fusion(f32[2,2,256,2048]{2,3,1,0:T(8,128)} %copy-done.4, f32[2,2,256]{2,1,0:T(2,128)S(1)} %log_add_fusion, bf16[2048,2,64,1]{0,2,3,1:T(8,128)(2,1)} %bitcast.182, bf16[256,2,2,64]{0,3,2,1:T(8,128)(2,1)S(1)} %bitcast.192), kind=kOutput, calls=%fused_computation.4 | convolution fusion | flops 274725888 | bytes 17440768 | tf_op jit(solution)/shard_map/rkgd,skd->kgrs/dot_general | solution.py:594
  256.1 1.6 fusion.2
  257.8 2.0 copy-done.5
  259.8 1.4 fusion.13
  262.5 4.9 %fusion.14 = bf16[2,64,2048]{2,1,0:T(8,128)(2,1)S(1)} fusion(bf16[256,2,2,64]{0,3,2,1:T(8,128)(2,1)S(1)} %bitcast.193, f32[2,2,256,2048]{2,3,1,0:T(8,128)} %copy-done.4, f32[2,2,256]{2,1,0:T(2,128)S(1)} %log_add_fusion), kind=kOutput, calls=%fused_computation.20 | convolution fusion | flops 272891904 | bytes 9048064 | tf_op jit(solution)/shard_map/kgrs,rkgd->skd/dot_general | solution.py:591
  268.3 2.2 copy.108
  270.6 1.3 convolution_convert_fusion.3
  271.9 1.9 pad_maximum_fusion.2.refs_2_
  273.8 2.3 pad_maximum_fusion.refs_0_
  276.1 1.6 convolution_convert_fusion.5
  277.6 57.7 %exchange_7.1 = (bf16[8,256,256]{2,1,0:T(8,128)(2,1)}, bf16[4,64,1024]{2,1,0:T(8,128)(2,1)}, bf16[4,256,384]{2,1,0:T(8,128)(2,1)}) custom-call(bf16[8,256,256]{2,1,0:T(8,128)(2,1)} %pad_maximum_fusion.refs_0_, bf16[4,64,1024]{2,1,0:T(8,128)(2,1)} %bitcast.214, bf16[4,256,384]{2,1,0:T(8,128)(2,1)} %pad_maximum_fusion.2.refs_2_), custom_call_target="tpu_custom_call" | custom-call | bytes 47185920 | tf_op jit(solution)/shard_map/exchange_7/pallas_call | solution.py:103
  335.4 1.4 convert_reduce_fusion
  336.9 3.0 convolution_multiply_fusion
  340.3 2.0 fusion.30
  342.4 2.5 multiply_reduce_fusion
  346.3 1.5 convolution_convert_fusion.2
  347.8 19.6 %exchange_8.1 = (bf16[4,64,1024]{2,1,0:T(8,128)(2,1)}, bf16[4,256,512]{2,1,0:T(8,128)(2,1)}, f32[4,8,256]{2,1,0:T(8,128)}, bf16[4,64,1024]{2,1,0:T(8,128)(2,1)}) custom-call(bf16[4,64,1024]{2,1,0:T(8,128)(2,1)} %bitcast.212, bf16[4,256,512]{2,1,0:T(8,128)(2,1)} %bitcast.197, f32[4,8,256]{2,1,0:T(8,128)} %pad.15.refs_2_, bf16[64,1024]{1,0:T(8,128)(2,1)} %add_convert_fusion.refs_3_), custom_call_target="tpu_custom_call" | custom-call | bytes 42598400 | tf_op jit(solution)/shard_map/exchange_8/pallas_call | solution.py:103
  367.5 1.5 reduce_sum.232
  368.9 1.3 reduce_sum.233
  370.2 1.4 reduce_sum.234.refs_1_
  374.5 19.2 %exchange_9.1 = (bf16[8,32,896]{2,1,0:T(8,128)(2,1)}, f32[32,8,256]{2,1,0:T(8,128)}, bf16[4,64,1024]{2,1,0:T(8,128)(2,1)}) custom-call(bf16[8,32,896]{2,1,0:T(8,128)(2,1)} %bitcast.191, f32[8,256]{1,0:T(8,128)} %reduce_sum.234.refs_1_, bf16[64,1024]{1,0:T(8,128)(2,1)} %subtract_convert_fusion.refs_2_), custom_call_target="tpu_custom_call" | custom-call | bytes 24903680 | tf_op jit(solution)/shard_map/exchange_9/pallas_call | solution.py:103
  393.7 1.7 reduce_sum.238.refs_0_
  395.4 10.9 %exchange_10.1 = bf16[8,32,896]{2,1,0:T(8,128)(2,1)} custom-call(bf16[32,896]{1,0:T(8,128)(2,1)} %reduce_sum.238.refs_0_), custom_call_target="tpu_custom_call" | custom-call | bytes 9175040 | tf_op jit(solution)/shard_map/exchange_10/pallas_call | solution.py:103
  411.2 2.8 copy-done.2
  414.0 13.9 %spread.1 = (f32[8192,128]{1,0:T(8,128)}, f32[8192,128]{1,0:T(8,128)}, f32[8192,128]{1,0:T(8,128)}) custom-call(bf16[32,3,256,128]{3,2,1,0:T(8,128)(2,1)S(1)} %copy-done.2), custom_call_target="tpu_custom_call" | custom-call | tf_op jit(solution)/shard_map/spread/pallas_call | solution.py:130
  428.7 1.9 copy.149
  (203 shorter events, 38.3 us)
Async XLA Ops:
  7.2 1.9 copy-start
  7.2 9.1 %copy-start.26 = (bf16[256,256]{1,0:T(8,128)(2,1)S(1)}, bf16[256,256]{1,0:T(8,128)(2,1)}, u32[]{:S(2)}) copy-start(bf16[256,256]{1,0:T(8,128)(2,1)} %param.19) | copy-start | bytes 393220
  7.2 9.1 %copy-start.28 = (bf16[256,128]{1,0:T(8,128)(2,1)S(1)}, bf16[256,128]{1,0:T(8,128)(2,1)}, u32[]{:S(2)}) copy-start(bf16[256,128]{1,0:T(8,128)(2,1)} %param.20) | copy-start | bytes 196612
  7.2 9.0 %copy-start.27 = (bf16[256,128]{1,0:T(8,128)(2,1)S(1)}, bf16[256,128]{1,0:T(8,128)(2,1)}, u32[]{:S(2)}) copy-start(bf16[256,128]{1,0:T(8,128)(2,1)} %param.21) | copy-start | bytes 196612
  7.2 116.9 %all-gather.3.cloned.1.call-start = ((), (), s32[]{:S(2)}) async-start(), calls=%async_computation | async-start | bytes 3932160 | tf_op jit(solution)/shard_map/all_gather | solution.py:477
  7.3 9.7 %copy-start.43 = (bf16[256]{0:T(256)(128)(2,1)S(1)}, bf16[256]{0:T(256)(128)(2,1)}, u32[]{:S(2)}) copy-start(bf16[256]{0:T(256)(128)(2,1)} %param.23) | copy-start | bytes 1540
  7.3 9.7 %copy-start.44 = (bf16[256]{0:T(256)(128)(2,1)S(1)}, bf16[256]{0:T(256)(128)(2,1)}, u32[]{:S(2)}) copy-start(bf16[256]{0:T(256)(128)(2,1)} %param.18) | copy-start | bytes 1540
  11.4 46.6 %copy-start.17 = (pred[1024,256]{1,0:T(32,128)(4,1)}, pred[1024,256]{1,0:T(32,128)(4,1)S(1)}, u32[]{:S(2)}) copy-start(pred[1024,256]{1,0:T(32,128)(4,1)S(1)} %fusion.22) | copy-start | bytes 786436
  16.3 45.6 %copy-start.9 = (bf16[256,1024]{1,0:T(8,128)(2,1)S(1)}, bf16[256,1024]{1,0:T(8,128)(2,1)}, u32[]{:S(2)}) copy-start(bf16[256,1024]{1,0:T(8,128)(2,1)} %param.14) | copy-start | bytes 1572868
  58.0 4.1 copy-start.45
  58.0 4.9 %copy-start.42 = (s32[1,4]{1,0:T(1,128)S(1)}, s32[1,4]{1,0:T(1,128)}, u32[]{:S(2)}) copy-start(s32[1,4]{1,0:T(1,128)} %param.16) | copy-start | bytes 52
  61.0 350.2 %all-gather.5.cloned.1.call-start = ((), (), s32[]{:S(2)}) async-start(), calls=%async_computation.1 | async-start | bytes 7077888 | tf_op jit(solution)/shard_map/all_gather | solution.py:561
  62.1 167.2 %copy-start.34 = (f32[256]{0:T(256)}, f32[256]{0:T(256)S(1)}, u32[]{:S(2)}) copy-start(f32[256]{0:T(256)S(1)} %add_rsqrt_fusion) | copy-start | bytes 3076
  62.9 23.1 %copy-start.38 = (pred[384]{0:T(512)(128)(4,1)}, pred[384]{0:T(512)(128)(4,1)S(1)}, u32[]{:S(2)}) copy-start(pred[384]{0:T(512)(128)(4,1)S(1)} %fusion.46) | copy-start | bytes 1156
  63.2 22.8 %copy-start.30 = (f32[256]{0:T(256)}, f32[256]{0:T(256)S(1)}, u32[]{:S(2)}) copy-start(f32[256]{0:T(256)S(1)} %subtract_convert_fusion.1) | copy-start | bytes 3076
  66.5 19.2 %slice-start.2 = ((bf16[256,384]{1,0:T(8,128)(2,1)}), bf16[256,256]{1,0:T(8,128)(2,1)S(1)}, s32[]{:S(2)}) async-start(bf16[256,384]{1,0:T(8,128)(2,1)} %copy-done.20), calls=%async_computation.4 | async-start | bytes 262144 | tf_op jit(solution)/shard_map/slice | solution.py:492
  66.6 41.4 %copy-start.7 = (f32[256,1024]{1,0:T(8,128)}, f32[256,1024]{1,0:T(8,128)S(1)}, u32[]{:S(2)}) copy-start(f32[256,1024]{1,0:T(8,128)S(1)} %convert_element_type.152) | copy-start | bytes 3145732
  85.6 3.1 copy-start.10
  85.8 3.0 copy-start.22
  86.0 7.5 %copy-start.12 = (bf16[2048,128]{0,1:T(8,128)(2,1)}, bf16[2048,128]{0,1:T(8,128)(2,1)S(1)}, u32[]{:S(2)}) copy-start(bf16[2048,128]{0,1:T(8,128)(2,1)S(1)} %copy.100) | copy-start | bytes 1572868
  88.8 3.2 copy-start.4
  93.5 13.3 %copy-start.21 = (bf16[2,64,2,256]{3,1,2,0:T(8,128)(2,1)}, bf16[2,64,2,256]{3,1,2,0:T(8,128)(2,1)S(1)}, u32[]{:S(2)}) copy-start(bf16[2,64,2,256]{3,1,2,0:T(8,128)(2,1)S(1)} %fusion.18) | copy-start | bytes 393220
  93.5 24.4 %copy-start.29 = (s32[256,8]{0,1:T(8,128)S(1)}, s32[256,8]{0,1:T(8,128)}, u32[]{:S(2)}) copy-start(s32[256,8]{0,1:T(8,128)} %param.17) | copy-start | bytes 24580
  93.5 24.4 %copy-start.15 = (bf16[4,256,128]{2,1,0:T(8,128)(2,1)S(1)}, bf16[4,256,128]{2,1,0:T(8,128)(2,1)}, u32[]{:S(2)}) copy-start(bf16[4,256,128]{2,1,0:T(8,128)(2,1)} %get-tuple-element.43) | copy-start | bytes 786436
  108.7 9.3 %copy-start.32 = (f32[64]{0:T(128)}, f32[64]{0:T(128)S(1)}, u32[]{:S(2)}) copy-start(f32[64]{0:T(128)S(1)} %get-tuple-element.93) | copy-start | bytes 772
  124.2 84.6 %copy-start.18 = (pred[1024,256]{1,0:T(32,128)(4,1)S(1)}, pred[1024,256]{1,0:T(32,128)(4,1)}, u32[]{:S(2)}) copy-start(pred[1024,256]{1,0:T(32,128)(4,1)} %copy-done.17) | copy-start | bytes 786436
  208.8 22.5 %copy-start.41 = (pred[8]{0:T(512)(128)(4,1)S(1)}, pred[8]{0:T(512)(128)(4,1)}, u32[]{:S(2)}) copy-start(pred[8]{0:T(512)(128)(4,1)} %get-tuple-element.102) | copy-start | bytes 28
  208.8 23.8 %copy-start.33 = (f32[64]{0:T(128)S(1)}, f32[64]{0:T(128)}, u32[]{:S(2)}) copy-start(f32[64]{0:T(128)} %copy-done.32) | copy-start | bytes 772
  208.8 25.5 %copy-start.40 = (f32[64]{0:T(128)S(1)}, f32[64]{0:T(128)}, u32[]{:S(2)}) copy-start(f32[64]{0:T(128)} %get-tuple-element.92) | copy-start | bytes 772
  210.3 36.2 %copy-start.6 = (bf16[4,64,1024]{2,1,0:T(8,128)(2,1)S(1)}, bf16[4,64,1024]{2,1,0:T(8,128)(2,1)}, u32[]{:S(2)}) copy-start(bf16[4,64,1024]{2,1,0:T(8,128)(2,1)} %exchange_11.1) | copy-start | bytes 1572868
  249.4 5.7 %slice-start = ((s8[8388608]{0:T(1024)(128)(4,1)}), s8[4194304]{0:T(1024)(128)(4,1)S(1)}, s32[]{:S(2)}) async-start(s8[8388608]{0:T(1024)(128)(4,1)} %bitcast.171), calls=%async_computation.2 | async-start | bytes 8388608
  249.4 6.8 %slice-start.1 = ((s8[8388608]{0:T(1024)(128)(4,1)}), s8[4194304]{0:T(1024)(128)(4,1)S(1)}, s32[]{:S(2)}) async-start(s8[8388608]{0:T(1024)(128)(4,1)} %bitcast.171), calls=%async_computation.3 | async-start | bytes 8388608
  256.1 3.7 copy-start.23
  257.8 2.0 copy-start.5
  262.5 8.0 %copy-start.14 = (bf16[1024,256]{1,0:T(8,128)(2,1)S(1)}, bf16[1024,256]{1,0:T(8,128)(2,1)}, u32[]{:S(2)}) copy-start(bf16[1024,256]{1,0:T(8,128)(2,1)} %copy.109) | copy-start | bytes 1572868
  270.6 5.5 %copy-start.19 = (pred[1024,256]{1,0:T(32,128)(4,1)S(1)}, pred[1024,256]{1,0:T(32,128)(4,1)}, u32[]{:S(2)}) copy-start(pred[1024,256]{1,0:T(32,128)(4,1)} %copy-done.17) | copy-start | bytes 786436
  276.1 60.8 %copy-start.11 = (bf16[2048,128]{0,1:T(8,128)(2,1)S(1)}, bf16[2048,128]{0,1:T(8,128)(2,1)}, u32[]{:S(2)}) copy-start(bf16[2048,128]{0,1:T(8,128)(2,1)} %copy-done.10) | copy-start | bytes 1572868
  335.3 5.0 %copy-start.31 = (f32[256]{0:T(256)S(1)}, f32[256]{0:T(256)}, u32[]{:S(2)}) copy-start(f32[256]{0:T(256)} %copy-done.30) | copy-start | bytes 3076
  335.3 5.0 %copy-start.39 = (pred[384]{0:T(512)(128)(4,1)S(1)}, pred[384]{0:T(512)(128)(4,1)}, u32[]{:S(2)}) copy-start(pred[384]{0:T(512)(128)(4,1)} %copy-done.38) | copy-start | bytes 1156
  336.9 5.5 %copy-start.35 = (f32[256]{0:T(256)S(1)}, f32[256]{0:T(256)}, u32[]{:S(2)}) copy-start(f32[256]{0:T(256)} %copy-done.34) | copy-start | bytes 3076
  339.9 5.6 %copy-start.24 = (bf16[4,64,1024]{2,1,0:T(8,128)(2,1)S(1)}, bf16[4,64,1024]{2,1,0:T(8,128)(2,1)}, u32[]{:S(2)}) copy-start(bf16[4,64,1024]{2,1,0:T(8,128)(2,1)} %get-tuple-element.53) | copy-start | bytes 1572868
  345.6 27.9 %copy-start.8 = (f32[256,1024]{1,0:T(8,128)S(1)}, f32[256,1024]{1,0:T(8,128)}, u32[]{:S(2)}) copy-start(f32[256,1024]{1,0:T(8,128)} %copy-done.7) | copy-start | bytes 3145732
  346.3 27.4 %copy-start.16 = (f32[64,1024]{1,0:T(8,128)S(1)}, f32[64,1024]{1,0:T(8,128)}, u32[]{:S(2)}) copy-start(f32[64,1024]{1,0:T(8,128)} %get-tuple-element.71) | copy-start | bytes 786436
  346.3 27.4 %copy-start.36 = (f32[64]{0:T(128)S(1)}, f32[64]{0:T(128)}, u32[]{:S(2)}) copy-start(f32[64]{0:T(128)} %get-tuple-element.68) | copy-start | bytes 772
  346.3 27.4 %copy-start.37 = (f32[64]{0:T(128)S(1)}, f32[64]{0:T(128)}, u32[]{:S(2)}) copy-start(f32[64]{0:T(128)} %get-tuple-element.69) | copy-start | bytes 772
  407.4 20.5 %copy-start.25 = (bf16[4,64,1024]{2,1,0:T(8,128)(2,1)S(1)}, bf16[4,64,1024]{2,1,0:T(8,128)(2,1)}, u32[]{:S(2)}) copy-start(bf16[4,64,1024]{2,1,0:T(8,128)(2,1)} %get-tuple-element.54) | copy-start | bytes 1572868
  410.4 20.2 %copy-start.1 = (bf16[256,32,128]{2,1,0:T(8,128)(2,1)S(1)}, bf16[256,32,128]{2,1,0:T(8,128)(2,1)}, u32[]{:S(2)}) copy-start(bf16[256,32,128]{2,1,0:T(8,128)(2,1)} %param.25) | copy-start | bytes 6291460
  411.2 2.8 copy-start.2
  (3 other events, 3.7 us)
Sparse Core Ops, SparseCore 0:
  61.2 45.6 all-gather.2
  229.4 121.2 all-gather.4

commit v6 on v5

--- a/solution.py
+++ b/solution.py
@@ -18,6 +18,10 @@
 highest = lax.Precision.HIGHEST
 bf16 = jnp.bfloat16
 f32 = jnp.float32
+
+
+def offset(slot, n):
+    return slot // 2 + slot % 2 * (n // 2)
 
 
 def exchange_kernel(plan, sizes, *refs):
@@ -60,8 +64,8 @@
     for at, (axes, mode) in enumerate(plan):
         mine = flat(axes, place(axes, 0))
         for step in range(1, math.prod(sizes[a] for a in axes)):
-            if mode in "fb":
-                peer = place(axes, step if mode == "f" else sizes[axes[0]] - step)
+            if mode == "f":
+                peer = place(axes, offset(step, sizes[axes[0]]))
                 source, slot = ins[at].at[step], step
             else:
                 peer = place(axes, step)
@@ -77,7 +81,7 @@
             )
             copy.start()
             copies.append(copy)
-        if mode in "fb":
+        if mode == "f":
             mine = 0
         own = pltpu.make_async_copy(
             ins[at] if mode == "g" else ins[at].at[mine], outs[at].at[mine], self_sem.at[at]
@@ -116,27 +120,121 @@
     )(*arrays)
 
 
-def spread_kernel(pieces_ref, *out_refs):
-    experts = pieces_ref.shape[0]
-    depth = pieces_ref.shape[2]
-    for which, out_ref in enumerate(out_refs):
-        for expert in range(experts):
-            out_ref[pl.ds(expert, depth, stride=experts), :] = pieces_ref[expert, which].astype(f32)
-
-
-def spread(pieces):
-    experts, count, depth, ff = pieces.shape
+def spread_kernel(steps, early_ref, late_ref, *out_refs):
+    experts, _, depth, _ = early_ref.shape
+
+    def write(pieces_ref):
+        for which, out_ref in enumerate(out_refs):
+            for expert in range(experts):
+                out_ref[pl.ds(expert, depth, stride=experts), :] = pieces_ref[
+                    expert, which
+                ].astype(f32)
+
+    @pl.when(pl.program_id(0) < steps)
+    def _():
+        write(early_ref)
+
+    @pl.when(pl.program_id(0) >= steps)
+    def _():
+        write(late_ref)
+
+
+def spread(early, late):
+    experts, count, depth, ff = early.shape
     block = 64
+    steps = depth // block
+    shape = (experts, count, block, ff)
     outs = pl.pallas_call(
-        spread_kernel,
-        grid=(depth // block,),
-        out_shape=[jax.ShapeDtypeStruct((depth * experts, ff), f32)] * count,
-        in_specs=[pl.BlockSpec((experts, count, block, ff), lambda i: (0, 0, i, 0))],
+        functools.partial(spread_kernel, steps),
+        grid=(2 * steps,),
+        out_shape=[jax.ShapeDtypeStruct((2 * depth * experts, ff), f32)] * count,
+        in_specs=[
+            pl.BlockSpec(shape, lambda i: (0, 0, jnp.minimum(i, steps - 1), 0)),
+            pl.BlockSpec(shape, lambda i: (0, 0, jnp.maximum(i - steps, 0), 0)),
+        ],
         out_specs=[pl.BlockSpec((block * experts, ff), lambda i: (i, 0))] * count,
-        compiler_params=pltpu.CompilerParams(vmem_limit_bytes=32 * 1024 * 1024),
+        compiler_params=pltpu.CompilerParams(vmem_limit_bytes=40 * 1024 * 1024),
         name="spread",
-    )(pieces)
-    return [out.reshape(depth, experts, ff) for out in outs]
+    )(early, late)
+    return [out.reshape(2 * depth, experts, ff) for out in outs]
+
+
+def attention_back_kernel(groups, starts_ref, first_ref, queries_ref, grads_ref, pairs_ref, query_out, pair_out, probs, back):
+    rows = queries_ref.shape[0]
+    total, both = pairs_ref.shape
+    pair_width = both // 2
+    block = 512
+    blocks = [slice(at, at + block) for at in range(0, total, block)]
+    scale = HEAD_SIZE ** (-0.5)
+    places = jnp.concatenate([first_ref[0, 0] + lax.broadcasted_iota(jnp.int32, (rows, 1), 0)] * groups, axis=0)
+    starts = jnp.concatenate([starts_ref[...]] * groups, axis=0)
+    query_parts, key_parts, value_parts = [], [], []
+    for head in range(pair_width // HEAD_SIZE):
+
+        def heads_of(ref):
+            at = [(head * groups + g) * HEAD_SIZE for g in range(groups)]
+            return jnp.concatenate([ref[:, a : a + HEAD_SIZE] for a in at], axis=0)
+
+        queries, grads = heads_of(queries_ref), heads_of(grads_ref)
+        own = slice(head * HEAD_SIZE, (head + 1) * HEAD_SIZE)
+        own_values = slice(pair_width + own.start, pair_width + own.stop)
+        top = jnp.full((rows * groups, 1), -1e30, f32)
+        for part in blocks:
+            key_rows = part.start + lax.broadcasted_iota(jnp.int32, (1, block), 1)
+            allowed = (key_rows >= starts) & (key_rows <= places)
+            scores = contract_cols(queries, pairs_ref[part, own]) * scale
+            scores = jnp.where(allowed, scores, -1e30)
+            probs[:, part] = scores
+            top = jnp.maximum(top, jnp.max(scores, axis=1, keepdims=True))
+        count = jnp.zeros((rows * groups, 1), f32)
+        for part in blocks:
+            raised = jnp.exp(probs[:, part] - top)
+            probs[:, part] = raised
+            count += jnp.sum(raised, axis=1, keepdims=True)
+        share = 1.0 / count
+        mean = jnp.zeros((rows * groups, 1), f32)
+        for part in blocks:
+            weights = probs[:, part] * share
+            probs[:, part] = weights
+            prob_grad = contract_cols(grads, pairs_ref[part, own_values])
+            back[:, part] = prob_grad
+            mean += jnp.sum(weights * prob_grad, axis=1, keepdims=True)
+        query_grad = jnp.zeros((rows * groups, HEAD_SIZE), f32)
+        keys_here, values_here = [], []
+        for part in blocks:
+            weights = probs[:, part]
+            score_grad = (weights * (back[:, part] - mean)).astype(bf16)
+            query_grad += mm(score_grad, pairs_ref[part, own])
+            keys_here.append((contract_rows(score_grad, queries) * scale).astype(bf16))
+            values_here.append(contract_rows(weights.astype(bf16), grads).astype(bf16))
+        query_grad = query_grad * scale
+        query_parts += [query_grad[g * rows : (g + 1) * rows] for g in range(groups)]
+        key_parts.append(jnp.concatenate(keys_here, axis=0))
+        value_parts.append(jnp.concatenate(values_here, axis=0))
+    query_out[...] = jnp.concatenate(query_parts, axis=1)
+    pair_out[...] = jnp.concatenate(key_parts + value_parts, axis=1)
+
+
+def attention_back(starts, first_row, queries, grads, pairs, pair_width):
+    rows, q_width = queries.shape
+    total = pairs.shape[0]
+    groups = q_width // pair_width
+    vmem = pl.BlockSpec(memory_space=pltpu.VMEM)
+    return pl.pallas_call(
+        functools.partial(attention_back_kernel, groups),
+        out_shape=[
+            jax.ShapeDtypeStruct((rows, q_width), f32),
+            jax.ShapeDtypeStruct((total, 2 * pair_width), bf16),
+        ],
+        in_specs=[vmem, pl.BlockSpec(memory_space=pltpu.SMEM), vmem, vmem, vmem],
+        out_specs=[vmem, vmem],
+        scratch_shapes=[pltpu.VMEM((rows * groups, total), f32)] * 2,
+        compiler_params=pltpu.CompilerParams(vmem_limit_bytes=48 * 1024 * 1024),
+        cost_estimate=pl.CostEstimate(
+            flops=10 * rows * q_width * total, bytes_accessed=8 << 20, transcendentals=rows * total * 4
+        ),
+        name="attention_back",
+    )(starts.reshape(rows, 1), first_row.reshape(1, 1), queries, grads, pairs)
 
 
 def expert_kernel(
@@ -151,6 +249,7 @@
     mixed_got,
     gate_got,
     wgrad_ref,
+    wgrad_late_ref,
     wgrad_buf,
     wgrad_got,
     norm_buf,
@@ -182,13 +281,14 @@
         )
 
     def out_copies(k):
+        place = me + offset(k, n)
         return (
-            copy(0, k, chunk(rows_ref, k), chunk(norm_buf, k), me + k),
-            copy(1, k, probs_ref.at[k], probs_buf.at[k], me + k),
+            copy(0, k, chunk(rows_ref, k), chunk(norm_buf, k), place),
+            copy(1, k, probs_ref.at[k], probs_buf.at[k], place),
         )
 
     def back_copies(k):
-        place = me + n - k
+        place = me + n - offset(k, n)
         return (
             copy(2, k, chunk(back_buf, k), chunk(norm_got, k), place),
             copy(3, k, gate_buf.at[k], gate_got.at[k], place),
@@ -316,10 +416,13 @@
         total = wgrad_buf[0, at, :].astype(f32)
         for k in range(1, n_fsdp):
             total += wgrad_got[k, at, :].astype(f32)
-        wgrad_ref[at, :] = total.astype(bf16)
+        half = part // 2
+        to = pl.ds(pl.multiple_of(j * half, half), half)
+        wgrad_ref[to, :] = total[:half].astype(bf16)
+        wgrad_late_ref[to, :] = total[half:].astype(bf16)
         return carry
 
-    lax.fori_loop(0, wgrad_ref.shape[0] // part, summed, 0)
+    lax.fori_loop(0, wgrad_buf.shape[1] // part, summed, 0)
     for k in range(1, n):
         for item in out_copies(k):
             item.wait_send()
@@ -341,10 +444,11 @@
             like((total, width), bf16),
             like((total, width), bf16),
             like(probs_sent.shape, f32),
-            like(owned, bf16),
+            like((owned[0] // 2, owned[1]), bf16),
+            like((owned[0] // 2, owned[1]), bf16),
         ],
         in_specs=[vmem] * 4,
-        out_specs=[vmem] * 4,
+        out_specs=[vmem] * 5,
         scratch_shapes=[
             pltpu.VMEM((n_fsdp,) + owned, bf16),
             pltpu.VMEM((n_fsdp,) + owned, bf16),
@@ -430,7 +534,8 @@
     chosen = jnp.any(
         expert_ids[:, :, None] == jnp.arange(experts, dtype=jnp.int32)[None, None, :], axis=1
     )
-    ctx_order = lax.rem(ctx_at + jnp.arange(n_ctx, dtype=jnp.int32), n_ctx)
+    offsets = [offset(slot, n_ctx) for slot in range(n_ctx)]
+    ctx_order = lax.rem(ctx_at + jnp.array(offsets, dtype=jnp.int32), n_ctx)
     mine = ctx_order * per_ctx + tp_at
     chosen_mine = jnp.any(expert_ids[None, :, :] == mine[:, None, None], axis=2)
     earlier = jnp.arange(rows)[:, None] < jnp.arange(rows)[None, :]
@@ -505,18 +610,11 @@
     key_rows = jnp.arange(total_rows, dtype=jnp.int32)
     allowed = (key_rows[None, :] >= starts[:, None]) & (key_rows[None, :] <= query_rows[:, None])
 
-    def masked_scores():
-        raw_scores = jnp.einsum(
-            "rkgd,skd->kgrs", query_head_rows, keys_all, preferred_element_type=f32
-        )
-        return jnp.where(allowed, raw_scores * HEAD_SIZE ** (-0.5), -1e30)
-
-    masked = masked_scores()
+    raw_scores = jnp.einsum("rkgd,skd->kgrs", query_head_rows, keys_all, preferred_element_type=f32)
+    masked = jnp.where(allowed, raw_scores * HEAD_SIZE ** (-0.5), -1e30)
     row_top = jnp.max(masked, axis=-1, keepdims=True)
     shifted_exp = jnp.exp(masked - row_top)
-    row_total = jnp.sum(shifted_exp, axis=-1, keepdims=True)
-    attn_probs = shifted_exp / row_total
-    log_total = row_top + jnp.log(row_total)
+    attn_probs = shifted_exp / jnp.sum(shifted_exp, axis=-1, keepdims=True)
     attended = jnp.einsum(
         "kgrs,skd->rkgd", attn_probs.astype(bf16), values_all, preferred_element_type=f32
     )
@@ -546,21 +644,22 @@
     probs_sent = jnp.sum(picks.astype(f32) * probs_mine[:, None, :], axis=2)
     rows_sent = mm(picks_flat, normed_two).astype(bf16)
     probs_sent = jnp.broadcast_to(probs_sent[:, None, :], (n_ctx, 8, CAP))
-    norm_grad_got, mixed_got, gate_grad_got, expert_grad = expert_of_place(
+    norm_grad_got, mixed_got, gate_grad_got, *expert_grads = expert_of_place(
         sizes, rows_sent, probs_sent, grad_rows, expert_w
     )
 
     norm_grad_part = contract_rows(picks_flat, norm_grad_got)
     gate_grad_part = jnp.sum(picks.astype(f32) * gate_grad_got[:, 0, :, None], axis=1)
-    norm_grad_parts, gate_grad_parts, pieces = send(
+    norm_grad_parts, gate_grad_parts, pieces, late_pieces = send(
         5,
         (("tp",), "a", norm_grad_part.astype(bf16).reshape(n_tp, quarter, width)),
         (("tp",), "g", gate_grad_part),
-        (("tp",), "a", expert_grad.reshape(n_tp, 3, depth, ff)),
+        *[(("tp",), "a", grad.reshape(n_tp, 3, depth // 2, ff)) for grad in expert_grads],
     )
     expert_all = lax.all_gather(pieces, "ctx", axis=0, tiled=True)
 
-    back_order = lax.rem(jnp.arange(n_ctx, dtype=jnp.int32) + n_ctx - ctx_at, n_ctx)
+    slot_of = jnp.array([offsets.index(k) for k in range(n_ctx)], dtype=jnp.int32)
+    back_order = slot_of[lax.rem(jnp.arange(n_ctx, dtype=jnp.int32) + n_ctx - ctx_at, n_ctx)]
     gate_grads = jnp.take(gate_grad_parts, back_order, axis=1)
     gate_grads = gate_grads.transpose(2, 1, 0).reshape(rows, experts)
     route_grad = gate_probs * (
@@ -586,34 +685,17 @@
     mixed_part = contract_rows(picks_flat, mixed_got).astype(bf16)
     attended_grad = mm(attn_in, output_w).astype(bf16)
 
-    grad_heads = attended_grad.reshape(rows, key_heads, groups, HEAD_SIZE)
-    attn_probs = jnp.exp(masked_scores() - log_total)
-    value_grad_all = jnp.einsum(
-        "kgrs,rkgd->skd", attn_probs.astype(bf16), grad_heads, preferred_element_type=f32
-    )
-    prob_grad = jnp.einsum("rkgd,skd->kgrs", grad_heads, values_all, preferred_element_type=f32)
-    score_grad = (
-        attn_probs * (prob_grad - jnp.sum(attn_probs * prob_grad, axis=-1, keepdims=True))
-    ).astype(bf16)
-    query_grad_rot = jnp.einsum(
-        "kgrs,skd->rkgd", score_grad, keys_all, preferred_element_type=f32
-    ).reshape(rows, -1) * HEAD_SIZE ** (-0.5)
-    key_grad_all = jnp.einsum(
-        "kgrs,rkgd->skd", score_grad, query_head_rows, preferred_element_type=f32
-    ) * HEAD_SIZE ** (-0.5)
-    pair_grads = jnp.concatenate(
-        [
-            key_grad_all.reshape(total_rows, pair_width),
-            value_grad_all.reshape(total_rows, pair_width),
-        ],
-        axis=1,
-    ).astype(bf16)
+    query_grad_rot, pair_grads = attention_back(
+        starts, ctx_at * rows, queries, attended_grad, pairs_all, pair_width
+    )
     pair_got, mixed_parts, early_got = send(
         7,
         (("ctx",), "a", pair_grads.reshape(n_ctx, rows, 2 * pair_width)),
         (("tp",), "a", mixed_part.reshape(n_tp, quarter, width)),
         (("fsdp",), "a", early.reshape(n_fsdp, depth, -1)),
     )
+    late_pieces, pair_got = lax.optimization_barrier((late_pieces, pair_got))
+    late_all = lax.all_gather(late_pieces, "ctx", axis=0, tiled=True)
     pair_owned = jnp.sum(pair_got.astype(f32), axis=0)
     turned_back = turn(
         jnp.concatenate([query_grad_rot, pair_owned[:, :pair_width]], axis=1),
@@ -662,7 +744,7 @@
     (small_all,) = send(10, (("ctx",), "g", jnp.sum(small_got.astype(f32), axis=0).astype(bf16)))
     small_all = small_all.reshape(depth, -1).astype(f32)
     gain_all = jnp.sum(gain_all, axis=0)
-    grad_gate, grad_up, grad_down = spread(expert_all)
+    grad_gate, grad_up, grad_down = spread(expert_all, late_all)
     k_end, v_end = q_end + pair_width, q_end + 2 * pair_width
     o_end = v_end + attended.shape[1]
     return (

time: 439 us -> 427 us (0.973); the launches traced: 437 us -> 420 us
  matrix products: 40.4 us -> 30.5 us
  other arithmetic: 38.4 us -> 32.6 us
    dot_general x5 -> x0, matrix products: 17.7 us -> none  [the longest x1 5.63 us: local(): jnp.einsum('rkgd,skd->kgrs', grad_heads, values_all, preferred_element_ty...]
    pallas_call x1 -> x2, Pallas kernels: 13.9 us -> 22.9 us  [the longest x1 14.7 us: spread(): pl.pallas_call(functools.partial(spread_kernel, steps), grid=(2 * steps,)...]
    sub x0 -> x1, matrix products: none -> 7.31 us  [local(): shifted_exp = jnp.exp(masked - row_top)]
    pallas_call x10, Pallas kernels: 211 us -> 205 us  [exchange(): pl.pallas_call(functools.partial(exchange_kernel, plan, sizes), out_shape...]
    unnamed x107 -> x123, local copies, waits for them, and re-layouts: 14.7 us -> 10.9 us
  transfers between devices with their start and end apart: 2 -> 3, of which waited for: 0 -> 0; matrix products, arithmetic and copies ran while one was open for 20% -> 16% of each run, Pallas kernels for 35% -> 37%
where the time goes in v6:
time: 427 us; the launch traced here: 420 us
  Pallas kernels  310 us (73%)
  other arithmetic  32.6 us (8%)
  local copies, waits for them, and re-layouts  31 us (7%)
  matrix products  30.5 us (7%)
  between operations  15.2 us (4%)
    pallas_call x10, Pallas kernels, exchange(): pl.pallas_call(functools.partial(exchange_kernel, plan, sizes), out_shape...  205 us
    pallas_call x1, Pallas kernels, expert_of_place(): pl.pallas_call(functools.partial(expert_kernel, n, n_fsdp, part), out_sha...  81.6 us
    pallas_call x1, Pallas kernels, spread(): pl.pallas_call(functools.partial(spread_kernel, steps), grid=(2 * steps,)...  14.7 us
    unnamed x123, local copies, waits for them, and re-layouts  10.9 us
    dot_general x6, matrix products, mm(): return jnp.dot(left, right, preferred_element_type=f32)  9.79 us
  transfers between devices with their start and end apart: 3, of which 0 were waited for; matrix products, arithmetic and copies ran while one was open for 16% of the time, Pallas kernels for 37%

profile of v6, /device:TPU:1, one launch (start us, length us, event | category | flops | bytes accessed | tf_op | source)
XLA Modules:
  0.0 419.6 jit_solution(11824371595285756353)
XLA Ops:
  7.3 1.4 gather_fusion.1
  8.8 1.2 compare_and_fusion.1
  12.5 1.5 constant_dynamic-slice_fusion.1
  15.1 2.0 convolution_convert_fusion.1
  18.6 1.0 pad_maximum_fusion.refs_3_
  19.5 39.4 %exchange_0.1 = (bf16[4,256,512]{2,1,0:T(8,128)(2,1)}, bf16[4,16,128]{2,1,0:T(8,128)(2,1)}, bf16[4,256,128]{2,1,0:T(8,128)(2,1)}, bf16[4,3,256,128]{3,2,1,0:T(8,128)(2,1)}, bf16[8,128,1024]{2,1,0:T(8,128)(2,1)}) custom-call(bf16[256,512]{1,0:T(8,128)(2,1)} %pad_maximum_fusion.4.refs_0_, bf16[16,128]{1,0:T(8,128)(2,1)} %maximum_maximum_fusion.refs_1_, ...), custom_call_target="tpu_custom_call" | custom-call | bytes 84213760 | tf_op jit(solution)/shard_map/exchange_0/pallas_call | solution.py:107
  59.0 1.8 copy.85
  60.8 1.2 reshape.394
  63.6 1.4 fusion.60
  64.9 1.7 fusion.30
  68.4 2.6 fusion.19
  72.5 20.0 %exchange_1.1 = (bf16[8,256,256]{2,1,0:T(8,128)(2,1)}, bf16[4,256,256]{2,1,0:T(8,128)(2,1)}) custom-call(bf16[256,256]{1,0:T(8,128)(2,1)} %pad_maximum_fusion.8.refs_0_, bf16[256,256]{1,0:T(8,128)(2,1)} %refs_1_.1), custom_call_target="tpu_custom_call" | custom-call | bytes 31457280 | tf_op jit(solution)/shard_map/exchange_1/pallas_call | solution.py:107
  92.5 1.3 fusion.55
  93.8 1.0 copy.82
  95.5 7.3 %fusion.62 = (f32[2,2,256]{2,1,0:T(2,128)S(1)}, f32[2,2,256,2048]{2,3,1,0:T(8,128)}) fusion(pred[256,2048]{0,1:T(8,128)(4,1)S(1)} %fusion.6, bf16[2048,2,64,1]{0,2,3,1:T(8,128)(2,1)} %bitcast.176, bf16[256,2,2,64]{0,3,2,1:T(8,128)(2,1)S(1)} %bitcast.178), kind=kOutput, calls=%fused_computation.167 | convolution fusion | flops 276826112 | bytes 9572352 | tf_op jit(solution)/shard_map/sub | solution.py:616
  102.8 4.3 %fusion.7 = bf16[2,64,2,256]{3,1,2,0:T(8,128)(2,1)S(1)} fusion(bf16[2048,2,64,1]{0,2,3,1:T(8,128)(2,1)S(1)} %bitcast.175, f32[2,2,256,2048]{2,3,1,0:T(8,128)} %get-tuple-element.111, f32[2,2,256]{2,1,0:T(2,128)S(1)} %get-tuple-element.110), kind=kOutput, calls=%fused_computation.27 | convolution fusion | flops 272695296 | bytes 9048064 | tf_op jit(solution)/shard_map/kgrs,skd->rkgd/dot_general | solution.py:618
  107.2 1.2 convolution_convert_fusion.4
  108.3 10.8 %exchange_2.1 = bf16[4,64,1024]{2,1,0:T(8,128)(2,1)} custom-call(bf16[4,64,1024]{2,1,0:T(8,128)(2,1)} %bitcast.157), custom_call_target="tpu_custom_call" | custom-call | bytes 10485760 | tf_op jit(solution)/shard_map/exchange_2/pallas_call | solution.py:107
  119.1 1.1 convert_reduce_fusion.4
  121.7 8.5 %exchange_11.1 = bf16[4,64,1024]{2,1,0:T(8,128)(2,1)} custom-call(bf16[64,1024]{1,0:T(8,128)(2,1)} %multiply_convert_fusion.2.refs_0_), custom_call_target="tpu_custom_call" | custom-call | bytes 10485760 | tf_op jit(solution)/shard_map/exchange_11/pallas_call | solution.py:107
  130.2 1.3 fusion.63
  132.8 3.1 convolution_convert_fusion.rows_ref
  135.9 81.6 %expert_of_place.1 = (bf16[1024,1024]{1,0:T(8,128)(2,1)S(1)}, bf16[1024,1024]{1,0:T(8,128)(2,1)S(1)}, f32[8,8,128]{2,1,0:T(8,128)S(1)}, bf16[1536,128]{1,0:T(8,128)(2,1)S(1)}, bf16[1536,128]{1,0:T(8,128)(2,1)S(1)}) custom-call(bf16[1024,1024]{1,0:T(8,128)(2,1)} %convolution_convert_fusion.rows_ref, f32[8,8,128]{2,1,0:T(8,128)S(1)} %broadcast_in_dim.102.probs_ref, ...), custom_call_target="tpu_custom_call" | custom-call | flops 19327352832 | bytes 104857600 | tf_op jit(solution)/shard_map/expert_of_place/pallas_call | solution.py:441
  219.0 1.6 convolution_convert_fusion.6
  221.4 18.1 %exchange_5.1 = (bf16[4,64,1024]{2,1,0:T(8,128)(2,1)}, f32[4,8,256]{2,1,0:T(8,128)}, bf16[4,3,128,128]{3,2,1,0:T(8,128)(2,1)}, bf16[4,3,128,128]{3,2,1,0:T(8,128)(2,1)}) custom-call(bf16[4,64,1024]{2,1,0:T(8,128)(2,1)} %bitcast.174, f32[8,256]{1,0:T(8,128)} %fusion.9.refs_1_, bf16[4,3,128,128]{3,2,1,0:T(8,128)(2,1)} %bitcast.146, ...), custom_call_target="tpu_custom_call" | custom-call | bytes 26869760 | tf_op jit(solution)/shard_map/exchange_5/pallas_call | solution.py:107
  243.7 1.9 multiply_convert_fusion.1
  245.6 10.3 %exchange_6.1 = bf16[4,64,1024]{2,1,0:T(8,128)(2,1)} custom-call(bf16[64,1024]{1,0:T(8,128)(2,1)} %get-tuple-element.82.refs_0_), custom_call_target="tpu_custom_call" | custom-call | bytes 10485760 | tf_op jit(solution)/shard_map/exchange_6/pallas_call | solution.py:107
  255.9 2.0 copy.88
  257.9 1.5 convolution_convert_fusion.7.grads_ref
  259.5 8.3 %attention_back.1 = (f32[256,256]{1,0:T(8,128)S(1)}, bf16[2048,256]{1,0:T(8,128)(2,1)S(1)}) custom-call(s32[256,1]{1,0:T(8,128)S(1)} %copy.87.starts_ref, s32[1,1]{1,0:T(1,128)} %bitcast.4.first_ref, bf16[256,256]{1,0:T(8,128)(2,1)S(1)} %slice.132.queries_ref, bf16[256,256]{1,0:T(8,128)(2,1)S(1)} %convolution_convert_fusion.7.grads_ref, ...), custom_call_target="tpu_custom_call" | custom-call | flops 1342177280 | bytes 8388608 | tf_op jit(solution)/shard_map/attention_back/pallas_call | solution.py:223
  268.2 1.0 pad_maximum_fusion.1.refs_2_
  270.0 1.6 convolution_convert_fusion.5
  271.6 38.6 %exchange_7.1 = (bf16[8,256,256]{2,1,0:T(8,128)(2,1)}, bf16[4,64,1024]{2,1,0:T(8,128)(2,1)}, bf16[4,256,384]{2,1,0:T(8,128)(2,1)}) custom-call(bf16[8,256,256]{2,1,0:T(8,128)(2,1)} %bitcast.145, bf16[4,64,1024]{2,1,0:T(8,128)(2,1)} %bitcast.177, bf16[4,256,384]{2,1,0:T(8,128)(2,1)} %pad_maximum_fusion.1.refs_2_), custom_call_target="tpu_custom_call" | custom-call | bytes 47185920 | tf_op jit(solution)/shard_map/exchange_7/pallas_call | solution.py:107
  310.8 1.5 convert_reduce_fusion
  313.9 2.6 fusion.21
  316.6 2.0 multiply_reduce_fusion
  320.0 1.5 convolution_convert_fusion.2
  321.5 20.4 %exchange_8.1 = (bf16[4,64,1024]{2,1,0:T(8,128)(2,1)}, bf16[4,256,512]{2,1,0:T(8,128)(2,1)}, f32[4,8,256]{2,1,0:T(8,128)}, bf16[4,64,1024]{2,1,0:T(8,128)(2,1)}) custom-call(bf16[4,64,1024]{2,1,0:T(8,128)(2,1)} %bitcast.173, bf16[4,256,512]{2,1,0:T(8,128)(2,1)} %bitcast.161, f32[4,8,256]{2,1,0:T(8,128)} %pad.15.refs_2_, bf16[64,1024]{1,0:T(8,128)(2,1)} %add_convert_fusion.refs_3_), custom_call_target="tpu_custom_call" | custom-call | bytes 42598400 | tf_op jit(solution)/shard_map/exchange_8/pallas_call | solution.py:107
  342.0 1.4 reduce_sum.224.refs_1_
  343.4 1.5 reduce_sum.222
  346.7 27.5 %exchange_9.1 = (bf16[8,32,896]{2,1,0:T(8,128)(2,1)}, f32[32,8,256]{2,1,0:T(8,128)}, bf16[4,64,1024]{2,1,0:T(8,128)(2,1)}) custom-call(bf16[8,32,896]{2,1,0:T(8,128)(2,1)} %bitcast.158, f32[8,256]{1,0:T(8,128)} %reduce_sum.224.refs_1_, bf16[64,1024]{1,0:T(8,128)(2,1)} %subtract_convert_fusion.refs_2_), custom_call_target="tpu_custom_call" | custom-call | bytes 24903680 | tf_op jit(solution)/shard_map/exchange_9/pallas_call | solution.py:107
  374.2 1.0 reduce_sum.227
  375.2 1.7 reduce_sum.228.refs_0_
  376.9 11.7 %exchange_10.1 = bf16[8,32,896]{2,1,0:T(8,128)(2,1)} custom-call(bf16[32,896]{1,0:T(8,128)(2,1)} %reduce_sum.228.refs_0_), custom_call_target="tpu_custom_call" | custom-call | bytes 9175040 | tf_op jit(solution)/shard_map/exchange_10/pallas_call | solution.py:107
  388.7 1.1 bitcast_convert_fusion
  392.6 1.9 copy-done.2
  394.5 1.9 copy-done.3
  396.4 14.7 %spread.1 = (f32[8192,128]{1,0:T(8,128)}, f32[8192,128]{1,0:T(8,128)}, f32[8192,128]{1,0:T(8,128)}) custom-call(bf16[32,3,128,128]{3,2,1,0:T(8,128)(2,1)S(1)} %copy-done.2, bf16[32,3,128,128]{3,2,1,0:T(8,128)(2,1)S(1)} %copy-done.3), custom_call_target="tpu_custom_call" | custom-call | tf_op jit(solution)/shard_map/spread/pallas_call | solution.py:147
  (214 shorter events, 30.8 us)
Async XLA Ops:
  7.2 5.1 %copy-start = (bf16[256,32,128]{2,1,0:T(8,128)(2,1)S(1)}, bf16[256,32,128]{2,1,0:T(8,128)(2,1)}, u32[]{:S(2)}) copy-start(bf16[256,32,128]{2,1,0:T(8,128)(2,1)} %param.27) | copy-start | bytes 6291460
  7.2 128.7 %all-gather.4.cloned.1.call-start = ((), (), s32[]{:S(2)}) async-start(), calls=%async_computation | async-start | bytes 3932160 | tf_op jit(solution)/shard_map/all_gather | solution.py:582
  7.3 7.8 %copy-start.19 = (bf16[256,1024]{1,0:T(8,128)(2,1)S(1)}, bf16[256,1024]{1,0:T(8,128)(2,1)}, u32[]{:S(2)}) copy-start(bf16[256,1024]{1,0:T(8,128)(2,1)} %param.17) | copy-start | bytes 1572868
  14.0 3.2 copy-start.54
  14.0 3.2 copy-start.55
  14.0 3.8 copy-start.29
  14.0 3.8 copy-start.30
  14.0 3.8 copy-start.31
  15.1 203.9 %copy-start.17 = (pred[1024,256]{1,0:T(32,128)(4,1)}, pred[1024,256]{1,0:T(32,128)(4,1)S(1)}, u32[]{:S(2)}) copy-start(pred[1024,256]{1,0:T(32,128)(4,1)S(1)} %fusion.11) | copy-start | bytes 786436
  59.0 4.3 %copy-start.11 = (bf16[256,1024]{1,0:T(8,128)(2,1)S(1)}, bf16[256,1024]{1,0:T(8,128)(2,1)}, u32[]{:S(2)}) copy-start(bf16[256,1024]{1,0:T(8,128)(2,1)} %param.16) | copy-start | bytes 1572868
  62.0 330.6 %all-gather.6.cloned.1.call-start = ((), (), s32[]{:S(2)}) async-start(), calls=%async_computation.1 | async-start | bytes 3538944 | tf_op jit(solution)/shard_map/all_gather | solution.py:659
  63.6 3.1 copy-start.42
  64.9 2.6 copy-start.53
  67.8 3.2 copy-start.36
  92.5 2.5 copy-start.35
  92.5 2.5 copy-start.41
  102.8 4.3 %copy-start.12 = (bf16[4,256,256]{2,1,0:T(8,128)(2,1)S(1)}, bf16[4,256,256]{2,1,0:T(8,128)(2,1)}, u32[]{:S(2)}) copy-start(bf16[4,256,256]{2,1,0:T(8,128)(2,1)} %get-tuple-element.48) | copy-start | bytes 1572868
  107.1 14.5 %copy-start.21 = (bf16[2,64,2,256]{3,1,2,0:T(8,128)(2,1)}, bf16[2,64,2,256]{3,1,2,0:T(8,128)(2,1)S(1)}, u32[]{:S(2)}) copy-start(bf16[2,64,2,256]{3,1,2,0:T(8,128)(2,1)S(1)} %fusion.7) | copy-start | bytes 393220
  108.3 21.8 %copy-start.32 = (s32[256,8]{0,1:T(8,128)S(1)}, s32[256,8]{0,1:T(8,128)}, u32[]{:S(2)}) copy-start(s32[256,8]{0,1:T(8,128)} %param.19) | copy-start | bytes 24580
  108.3 21.9 %copy-start.14 = (bf16[4,256,128]{2,1,0:T(8,128)(2,1)S(1)}, bf16[4,256,128]{2,1,0:T(8,128)(2,1)}, u32[]{:S(2)}) copy-start(bf16[4,256,128]{2,1,0:T(8,128)(2,1)} %get-tuple-element.49) | copy-start | bytes 786436
  119.1 12.6 %copy-start.49 = (s32[8]{0:T(128)S(1)}, s32[8]{0:T(128)}, u32[]{:S(2)}) copy-start(s32[8]{0:T(128)} %get-tuple-element.108) | copy-start | bytes 100
  119.1 13.2 %copy-start.48 = (pred[8]{0:T(512)(128)(4,1)S(1)}, pred[8]{0:T(512)(128)(4,1)}, u32[]{:S(2)}) copy-start(pred[8]{0:T(512)(128)(4,1)} %get-tuple-element.84) | copy-start | bytes 28
  219.0 21.0 %copy-start.51 = (s32[8]{0:T(128)S(1)}, s32[8]{0:T(128)}, u32[]{:S(2)}) copy-start(s32[8]{0:T(128)} %copy-done.50) | copy-start | bytes 100
  219.0 22.4 %copy-start.47 = (pred[8]{0:T(512)(128)(4,1)S(1)}, pred[8]{0:T(512)(128)(4,1)}, u32[]{:S(2)}) copy-start(pred[8]{0:T(512)(128)(4,1)} %get-tuple-element.116) | copy-start | bytes 28
  219.0 22.6 %copy-start.10 = (bf16[4,64,1024]{2,1,0:T(8,128)(2,1)S(1)}, bf16[4,64,1024]{2,1,0:T(8,128)(2,1)}, u32[]{:S(2)}) copy-start(bf16[4,64,1024]{2,1,0:T(8,128)(2,1)} %exchange_11.1) | copy-start | bytes 1572868
  221.4 21.6 %copy-start.39 = (f32[64]{0:T(128)S(1)}, f32[64]{0:T(128)}, u32[]{:S(2)}) copy-start(f32[64]{0:T(128)} %copy-done.38) | copy-start | bytes 772
  239.6 3.3 copy-start.24
  239.6 4.1 copy-start.52
  239.6 152.9 %all-gather.8.cloned.1.call-start = ((), (), s32[]{:S(2)}) async-start(), calls=%async_computation.2 | async-start | bytes 3538944 | tf_op jit(solution)/shard_map/all_gather | solution.py:698
  243.6 15.8 %copy-start.4 = (bf16[8,256,256]{2,1,0:T(8,128)(2,1)S(1)}, bf16[8,256,256]{2,1,0:T(8,128)(2,1)}, u32[]{:S(2)}) copy-start(bf16[8,256,256]{2,1,0:T(8,128)(2,1)} %get-tuple-element.47) | copy-start | bytes 3145732
  259.4 8.4 %copy-start.13 = (bf16[1024,256]{1,0:T(8,128)(2,1)S(1)}, bf16[1024,256]{1,0:T(8,128)(2,1)}, u32[]{:S(2)}) copy-start(bf16[1024,256]{1,0:T(8,128)(2,1)} %copy.88) | copy-start | bytes 1572868
  259.5 8.4 %copy-start.22 = (bf16[2,64,2,256]{3,1,2,0:T(8,128)(2,1)S(1)}, bf16[2,64,2,256]{3,1,2,0:T(8,128)(2,1)}, u32[]{:S(2)}) copy-start(bf16[2,64,2,256]{3,1,2,0:T(8,128)(2,1)} %copy-done.21) | copy-start | bytes 393220
  259.5 8.7 %copy-start.16 = (bf16[1024,128]{1,0:T(8,128)(2,1)S(1)}, bf16[1024,128]{1,0:T(8,128)(2,1)}, u32[]{:S(2)}) copy-start(bf16[1024,128]{1,0:T(8,128)(2,1)} %pad.14.clone) | copy-start | bytes 786436
  267.8 3.8 copy-start.5
  271.6 38.6 %copy-start.43 = (f32[256]{0:T(256)S(1)}, f32[256]{0:T(256)}, u32[]{:S(2)}) copy-start(f32[256]{0:T(256)} %copy-done.42) | copy-start | bytes 3076
  310.1 2.9 copy-start.20
  310.8 2.6 copy-start.33
  310.8 2.7 copy-start.37
  313.2 3.3 copy-start.56
  313.9 5.3 %copy-start.23 = (bf16[4,64,1024]{2,1,0:T(8,128)(2,1)S(1)}, bf16[4,64,1024]{2,1,0:T(8,128)(2,1)}, u32[]{:S(2)}) copy-start(bf16[4,64,1024]{2,1,0:T(8,128)(2,1)} %get-tuple-element.64) | copy-start | bytes 1572868
  316.6 3.4 copy-start.44
  341.9 3.8 copy-start.25
  341.9 4.0 copy-start.15
  341.9 4.0 copy-start.45
  341.9 4.0 copy-start.46
  391.7 19.3 %copy-start.26 = (bf16[4,64,1024]{2,1,0:T(8,128)(2,1)S(1)}, bf16[4,64,1024]{2,1,0:T(8,128)(2,1)}, u32[]{:S(2)}) copy-start(bf16[4,64,1024]{2,1,0:T(8,128)(2,1)} %get-tuple-element.65) | copy-start | bytes 1572868
  391.7 20.1 %copy-start.27 = (bf16[4,64,1024]{2,1,0:T(8,128)(2,1)S(1)}, bf16[4,64,1024]{2,1,0:T(8,128)(2,1)}, u32[]{:S(2)}) copy-start(bf16[4,64,1024]{2,1,0:T(8,128)(2,1)} %get-tuple-element.70) | copy-start | bytes 1572868
  396.4 16.3 %copy-start.1 = (bf16[256,32,128]{2,1,0:T(8,128)(2,1)S(1)}, bf16[256,32,128]{2,1,0:T(8,128)(2,1)}, u32[]{:S(2)}) copy-start(bf16[256,32,128]{2,1,0:T(8,128)(2,1)} %param.27) | copy-start | bytes 6291460
  (12 other events, 15.3 us)
Sparse Core Ops, SparseCore 0:
  62.1 47.2 all-gather.3
  239.7 79.5 all-gather.5
  321.6 70.4 all-gather.7

commit v7 on v6

--- a/solution.py
+++ b/solution.py
@@ -120,43 +120,81 @@
     )(*arrays)
 
 
-def spread_kernel(steps, early_ref, late_ref, *out_refs):
-    experts, _, depth, _ = early_ref.shape
-
-    def write(pieces_ref):
-        for which, out_ref in enumerate(out_refs):
-            for expert in range(experts):
-                out_ref[pl.ds(expert, depth, stride=experts), :] = pieces_ref[
-                    expert, which
-                ].astype(f32)
-
-    @pl.when(pl.program_id(0) < steps)
-    def _():
-        write(early_ref)
-
-    @pl.when(pl.program_id(0) >= steps)
-    def _():
-        write(late_ref)
-
-
-def spread(early, late):
-    experts, count, depth, ff = early.shape
+def spread_kernel(pieces_ref, *out_refs):
+    for which, out_ref in enumerate(out_refs):
+        turned = jnp.swapaxes(pieces_ref[:, which].astype(f32), 0, 1)
+        out_ref[...] = turned.reshape(out_ref.shape)
+
+
+def spread(pieces):
+    experts, count, depth, ff = pieces.shape
     block = 64
-    steps = depth // block
-    shape = (experts, count, block, ff)
     outs = pl.pallas_call(
-        functools.partial(spread_kernel, steps),
-        grid=(2 * steps,),
-        out_shape=[jax.ShapeDtypeStruct((2 * depth * experts, ff), f32)] * count,
-        in_specs=[
-            pl.BlockSpec(shape, lambda i: (0, 0, jnp.minimum(i, steps - 1), 0)),
-            pl.BlockSpec(shape, lambda i: (0, 0, jnp.maximum(i - steps, 0), 0)),
-        ],
+        spread_kernel,
+        grid=(depth // block,),
+        out_shape=[jax.ShapeDtypeStruct((depth * experts, ff), f32)] * count,
+        in_specs=[pl.BlockSpec((experts, count, block, ff), lambda i: (0, 0, i, 0))],
         out_specs=[pl.BlockSpec((block * experts, ff), lambda i: (i, 0))] * count,
         compiler_params=pltpu.CompilerParams(vmem_limit_bytes=40 * 1024 * 1024),
         name="spread",
-    )(early, late)
-    return [out.reshape(2 * depth, experts, ff) for out in outs]
+    )(pieces)
+    return [out.reshape(depth, experts, ff) for out in outs]
+
+
+def attention_kernel(groups, starts_ref, first_ref, queries_ref, pairs_ref, out_ref, probs):
+    rows = queries_ref.shape[0]
+    total, both = pairs_ref.shape
+    pair_width = both // 2
+    block = 512
+    blocks = [slice(at, at + block) for at in range(0, total, block)]
+    places = jnp.concatenate(
+        [first_ref[0, 0] + lax.broadcasted_iota(jnp.int32, (rows, 1), 0)] * groups, axis=0
+    )
+    starts = jnp.concatenate([starts_ref[...]] * groups, axis=0)
+    parts = []
+    for head in range(pair_width // HEAD_SIZE):
+        at = [(head * groups + g) * HEAD_SIZE for g in range(groups)]
+        queries = jnp.concatenate([queries_ref[:, a : a + HEAD_SIZE] for a in at], axis=0)
+        own = slice(head * HEAD_SIZE, (head + 1) * HEAD_SIZE)
+        own_values = slice(pair_width + own.start, pair_width + own.stop)
+        top = jnp.full((rows * groups, 1), -1e30, f32)
+        for part in blocks:
+            key_rows = part.start + lax.broadcasted_iota(jnp.int32, (1, block), 1)
+            allowed = (key_rows >= starts) & (key_rows <= places)
+            scores = contract_cols(queries, pairs_ref[part, own]) * HEAD_SIZE ** (-0.5)
+            scores = jnp.where(allowed, scores, -1e30)
+            probs[:, part] = scores
+            top = jnp.maximum(top, jnp.max(scores, axis=1, keepdims=True))
+        count = jnp.zeros((rows * groups, 1), f32)
+        for part in blocks:
+            raised = jnp.exp(probs[:, part] - top)
+            probs[:, part] = raised
+            count += jnp.sum(raised, axis=1, keepdims=True)
+        share = 1.0 / count
+        attended = jnp.zeros((rows * groups, HEAD_SIZE), f32)
+        for part in blocks:
+            attended += mm((probs[:, part] * share).astype(bf16), pairs_ref[part, own_values])
+        parts += [attended[g * rows : (g + 1) * rows] for g in range(groups)]
+    out_ref[...] = jnp.concatenate(parts, axis=1).astype(bf16)
+
+
+def attention(starts, first_row, queries, pairs, pair_width):
+    rows, q_width = queries.shape
+    total = pairs.shape[0]
+    groups = q_width // pair_width
+    vmem = pl.BlockSpec(memory_space=pltpu.VMEM)
+    return pl.pallas_call(
+        functools.partial(attention_kernel, groups),
+        out_shape=jax.ShapeDtypeStruct((rows, q_width), bf16),
+        in_specs=[vmem, pl.BlockSpec(memory_space=pltpu.SMEM), vmem, vmem],
+        out_specs=vmem,
+        scratch_shapes=[pltpu.VMEM((rows * groups, total), f32)],
+        compiler_params=pltpu.CompilerParams(vmem_limit_bytes=40 * 1024 * 1024),
+        cost_estimate=pl.CostEstimate(
+            flops=4 * rows * q_width * total, bytes_accessed=4 << 20, transcendentals=rows * total * 4
+        ),
+        name="attention",
+    )(starts.reshape(rows, 1), first_row.reshape(1, 1), queries, pairs)
 
 
 def attention_back_kernel(groups, starts_ref, first_ref, queries_ref, grads_ref, pairs_ref, query_out, pair_out, probs, back):
@@ -249,7 +287,6 @@
     mixed_got,
     gate_got,
     wgrad_ref,
-    wgrad_late_ref,
     wgrad_buf,
     wgrad_got,
     norm_buf,
@@ -416,10 +453,7 @@
         total = wgrad_buf[0, at, :].astype(f32)
         for k in range(1, n_fsdp):
             total += wgrad_got[k, at, :].astype(f32)
-        half = part // 2
-        to = pl.ds(pl.multiple_of(j * half, half), half)
-        wgrad_ref[to, :] = total[:half].astype(bf16)
-        wgrad_late_ref[to, :] = total[half:].astype(bf16)
+        wgrad_ref[at, :] = total.astype(bf16)
         return carry
 
     lax.fori_loop(0, wgrad_buf.shape[1] // part, summed, 0)
@@ -444,11 +478,10 @@
             like((total, width), bf16),
             like((total, width), bf16),
             like(probs_sent.shape, f32),
-            like((owned[0] // 2, owned[1]), bf16),
-            like((owned[0] // 2, owned[1]), bf16),
+            like(owned, bf16),
         ],
         in_specs=[vmem] * 4,
-        out_specs=[vmem] * 5,
+        out_specs=[vmem] * 4,
         scratch_shapes=[
             pltpu.VMEM((n_fsdp,) + owned, bf16),
             pltpu.VMEM((n_fsdp,) + owned, bf16),
@@ -602,23 +635,7 @@
     output_w = output_w.reshape(width, -1)
     total_rows = n_ctx * rows
     pairs_all = pairs_all.reshape(total_rows, 2 * pair_width)
-    key_heads = pair_width // HEAD_SIZE
-    groups = queries.shape[1] // pair_width
-    keys_all = pairs_all[:, :pair_width].reshape(total_rows, key_heads, HEAD_SIZE)
-    values_all = pairs_all[:, pair_width:].reshape(total_rows, key_heads, HEAD_SIZE)
-    query_head_rows = queries.reshape(rows, key_heads, groups, HEAD_SIZE)
-    key_rows = jnp.arange(total_rows, dtype=jnp.int32)
-    allowed = (key_rows[None, :] >= starts[:, None]) & (key_rows[None, :] <= query_rows[:, None])
-
-    raw_scores = jnp.einsum("rkgd,skd->kgrs", query_head_rows, keys_all, preferred_element_type=f32)
-    masked = jnp.where(allowed, raw_scores * HEAD_SIZE ** (-0.5), -1e30)
-    row_top = jnp.max(masked, axis=-1, keepdims=True)
-    shifted_exp = jnp.exp(masked - row_top)
-    attn_probs = shifted_exp / jnp.sum(shifted_exp, axis=-1, keepdims=True)
-    attended = jnp.einsum(
-        "kgrs,skd->rkgd", attn_probs.astype(bf16), values_all, preferred_element_type=f32
-    )
-    attended = attended.reshape(rows, -1).astype(bf16)
+    attended = attention(starts, ctx_at * rows, queries, pairs_all, pair_width)
     quarter = rows // n_tp
 
     def quarter_of(array):
@@ -644,19 +661,22 @@
     probs_sent = jnp.sum(picks.astype(f32) * probs_mine[:, None, :], axis=2)
     rows_sent = mm(picks_flat, normed_two).astype(bf16)
     probs_sent = jnp.broadcast_to(probs_sent[:, None, :], (n_ctx, 8, CAP))
-    norm_grad_got, mixed_got, gate_grad_got, *expert_grads = expert_of_place(
+    norm_grad_got, mixed_got, gate_grad_got, expert_grad = expert_of_place(
         sizes, rows_sent, probs_sent, grad_rows, expert_w
     )
 
     norm_grad_part = contract_rows(picks_flat, norm_grad_got)
     gate_grad_part = jnp.sum(picks.astype(f32) * gate_grad_got[:, 0, :, None], axis=1)
-    norm_grad_parts, gate_grad_parts, pieces, late_pieces = send(
+    norm_grad_parts, gate_grad_parts, pieces = send(
         5,
         (("tp",), "a", norm_grad_part.astype(bf16).reshape(n_tp, quarter, width)),
         (("tp",), "g", gate_grad_part),
-        *[(("tp",), "a", grad.reshape(n_tp, 3, depth // 2, ff)) for grad in expert_grads],
-    )
-    expert_all = lax.all_gather(pieces, "ctx", axis=0, tiled=True)
+        (("tp",), "a", expert_grad.reshape(n_tp, 3, depth, ff)),
+    )
+
+    pairs = [[2 * i, 2 * i + 1] for i in range(n_ctx // 2)]
+    rings = [list(range(start, n_ctx, 2)) for start in range(2)]
+    pieces = lax.all_gather(pieces, "ctx", axis=0, tiled=True, axis_index_groups=pairs)
 
     slot_of = jnp.array([offsets.index(k) for k in range(n_ctx)], dtype=jnp.int32)
     back_order = slot_of[lax.rem(jnp.arange(n_ctx, dtype=jnp.int32) + n_ctx - ctx_at, n_ctx)]
@@ -688,14 +708,14 @@
     query_grad_rot, pair_grads = attention_back(
         starts, ctx_at * rows, queries, attended_grad, pairs_all, pair_width
     )
+    pieces, pair_grads = lax.optimization_barrier((pieces, pair_grads))
+    expert_all = lax.all_gather(pieces, "ctx", axis=0, tiled=True, axis_index_groups=rings)
     pair_got, mixed_parts, early_got = send(
         7,
         (("ctx",), "a", pair_grads.reshape(n_ctx, rows, 2 * pair_width)),
         (("tp",), "a", mixed_part.reshape(n_tp, quarter, width)),
         (("fsdp",), "a", early.reshape(n_fsdp, depth, -1)),
     )
-    late_pieces, pair_got = lax.optimization_barrier((late_pieces, pair_got))
-    late_all = lax.all_gather(late_pieces, "ctx", axis=0, tiled=True)
     pair_owned = jnp.sum(pair_got.astype(f32), axis=0)
     turned_back = turn(
         jnp.concatenate([query_grad_rot, pair_owned[:, :pair_width]], axis=1),
@@ -744,7 +764,7 @@
     (small_all,) = send(10, (("ctx",), "g", jnp.sum(small_got.astype(f32), axis=0).astype(bf16)))
     small_all = small_all.reshape(depth, -1).astype(f32)
     gain_all = jnp.sum(gain_all, axis=0)
-    grad_gate, grad_up, grad_down = spread(expert_all, late_all)
+    grad_gate, grad_up, grad_down = spread(expert_all)
     k_end, v_end = q_end + pair_width, q_end + 2 * pair_width
     o_end = v_end + attended.shape[1]
     return (

time: 427 us -> 377 us (0.88); the launches traced: 420 us -> 376 us
  Pallas kernels: 310 us -> 279 us
  matrix products: 30.5 us -> 19.8 us
  waiting for transfers between devices: 0.05 us -> 6.89 us
  local copies, waits for them, and re-layouts: 31 us -> 24.7 us
    pallas_call x10, Pallas kernels: 205 us -> 179 us  [exchange(): pl.pallas_call(functools.partial(exchange_kernel, plan, sizes), out_shape...]
    sub x1 -> x0, matrix products: 7.31 us -> none  [local(): shifted_exp = jnp.exp(masked - row_top)]
    all_gather x2, waiting for transfers between devices: 0.01 us -> 6.84 us  [the longest x1 6.84 us: local(): lax.all_gather(pieces, 'ctx', axis=0, tiled=True, axis_index_groups=pairs)]
    pallas_call x1 -> x2, Pallas kernels: 14.7 us -> 10.1 us  [the longest x1 5.08 us: attention(): pl.pallas_call(functools.partial(attention_kernel, groups), out_shape=jax...]
    dot_general x1 -> x0, matrix products: 4.29 us -> none  [local(): jnp.einsum('kgrs,skd->rkgd', attn_probs.astype(bf16), values_all, preferr...]
    unnamed x123 -> x93, local copies, waits for them, and re-layouts: 10.9 us -> 9.45 us
  transfers between devices with their start and end apart: 3 -> 3, of which waited for: 0 -> 1; matrix products, arithmetic and copies ran while one was open for 16% -> 13% of each run, Pallas kernels for 37% -> 36%
where the time goes in v7:
time: 377 us; the launch traced here: 376 us
  Pallas kernels  279 us (74%)
  other arithmetic  29.9 us (8%)
  local copies, waits for them, and re-layouts  24.7 us (7%)
  matrix products  19.8 us (5%)
  between operations  14.7 us (4%)
  waiting for transfers between devices  6.89 us (2%)
    pallas_call x10, Pallas kernels, exchange(): pl.pallas_call(functools.partial(exchange_kernel, plan, sizes), out_shape...  179 us
    pallas_call x1, Pallas kernels, expert_of_place(): pl.pallas_call(functools.partial(expert_kernel, n, n_fsdp, part), out_sha...  81.6 us
    dot_general x6, matrix products, mm(): return jnp.dot(left, right, preferred_element_type=f32)  9.62 us
    unnamed x93, local copies, waits for them, and re-layouts  9.45 us
    pallas_call x1, Pallas kernels, attention_back(): pl.pallas_call(functools.partial(attention_back_kernel, groups), out_shap...  8.3 us
  transfers between devices with their start and end apart: 3, of which 1 were waited for; matrix products, arithmetic and copies ran while one was open for 13% of the time, Pallas kernels for 36%

profile of v7, /device:TPU:1, one launch (start us, length us, event | category | flops | bytes accessed | tf_op | source)
XLA Modules:
  0.0 375.9 jit_solution(5418786781203707595)
XLA Ops:
  7.3 1.4 gather_fusion.1
  11.4 1.5 constant_dynamic-slice_fusion.1
  14.1 2.0 convolution_convert_fusion.1
  17.5 1.0 pad_maximum_fusion.refs_3_
  18.5 39.4 %exchange_0.1 = (bf16[4,256,512]{2,1,0:T(8,128)(2,1)}, bf16[4,16,128]{2,1,0:T(8,128)(2,1)}, bf16[4,256,128]{2,1,0:T(8,128)(2,1)}, bf16[4,3,256,128]{3,2,1,0:T(8,128)(2,1)}, bf16[8,128,1024]{2,1,0:T(8,128)(2,1)}) custom-call(bf16[256,512]{1,0:T(8,128)(2,1)} %pad_maximum_fusion.4.refs_0_, bf16[16,128]{1,0:T(8,128)(2,1)} %maximum_maximum_fusion.refs_1_, ...), custom_call_target="tpu_custom_call" | custom-call | bytes 84213760 | tf_op jit(solution)/shard_map/exchange_0/pallas_call | solution.py:107
  57.9 1.8 copy.75
  59.7 1.2 reshape.375
  62.2 1.7 fusion.20
  64.7 1.8 fusion.9
  67.3 17.4 %exchange_1.1 = (bf16[8,256,256]{2,1,0:T(8,128)(2,1)}, bf16[4,256,256]{2,1,0:T(8,128)(2,1)}) custom-call(bf16[256,256]{1,0:T(8,128)(2,1)} %pad_maximum_fusion.8.refs_0_, bf16[256,256]{1,0:T(8,128)(2,1)} %refs_1_.1), custom_call_target="tpu_custom_call" | custom-call | bytes 31457280 | tf_op jit(solution)/shard_map/exchange_1/pallas_call | solution.py:107
  84.7 1.2 copy-done.5
  85.9 5.1 %attention.1 = bf16[256,256]{1,0:T(8,128)(2,1)S(1)} custom-call(s32[256,1]{1,0:T(8,128)S(1)} %copy.77.starts_ref, s32[1,1]{1,0:T(1,128)} %bitcast.4.first_ref, bf16[256,256]{1,0:T(8,128)(2,1)S(1)} %slice.124.queries_ref, bf16[2048,256]{1,0:T(8,128)(2,1)S(1)} %bitcast.114), custom_call_target="tpu_custom_call" | custom-call | flops 536870912 | bytes 4194304 | tf_op jit(solution)/shard_map/attention/pallas_call | solution.py:186
  91.0 1.1 convolution_convert_fusion.4
  92.1 12.5 %exchange_2.1 = bf16[4,64,1024]{2,1,0:T(8,128)(2,1)} custom-call(bf16[4,64,1024]{2,1,0:T(8,128)(2,1)} %bitcast.125), custom_call_target="tpu_custom_call" | custom-call | bytes 10485760 | tf_op jit(solution)/shard_map/exchange_2/pallas_call | solution.py:107
  104.6 1.1 convert_reduce_fusion.4
  106.7 8.5 %exchange_11.1 = bf16[4,64,1024]{2,1,0:T(8,128)(2,1)} custom-call(bf16[64,1024]{1,0:T(8,128)(2,1)} %multiply_convert_fusion.2.refs_0_), custom_call_target="tpu_custom_call" | custom-call | bytes 10485760 | tf_op jit(solution)/shard_map/exchange_11/pallas_call | solution.py:107
  115.2 1.3 fusion.50
  117.8 3.1 convolution_convert_fusion.rows_ref
  120.9 81.6 %expert_of_place.1 = (bf16[1024,1024]{1,0:T(8,128)(2,1)S(1)}, bf16[1024,1024]{1,0:T(8,128)(2,1)S(1)}, f32[8,8,128]{2,1,0:T(8,128)S(1)}, bf16[3072,128]{1,0:T(8,128)(2,1)S(1)}) custom-call(bf16[1024,1024]{1,0:T(8,128)(2,1)} %convolution_convert_fusion.rows_ref, f32[8,8,128]{2,1,0:T(8,128)S(1)} %broadcast_in_dim.86.probs_ref, bf16[1024,1024]{1,0:T(8,128)(2,1)} %bitcast.158, ...), custom_call_target="tpu_custom_call" | custom-call | flops 19327352832 | bytes 104857600 | tf_op jit(solution)/shard_map/expert_of_place/pallas_call | solution.py:475
  202.5 0.9 copy-done.4
  203.4 1.6 convolution_convert_fusion.6
  205.8 18.2 %exchange_5.1 = (bf16[4,64,1024]{2,1,0:T(8,128)(2,1)}, f32[4,8,256]{2,1,0:T(8,128)}, bf16[4,3,256,128]{3,2,1,0:T(8,128)(2,1)}) custom-call(bf16[4,64,1024]{2,1,0:T(8,128)(2,1)} %bitcast.140, f32[8,256]{1,0:T(8,128)} %fusion.1.refs_1_, bf16[4,3,256,128]{3,2,1,0:T(8,128)(2,1)} %bitcast.113), custom_call_target="tpu_custom_call" | custom-call | bytes 26869760 | tf_op jit(solution)/shard_map/exchange_5/pallas_call | solution.py:107
  225.8 1.1 convert_reduce_fusion.3
  227.6 1.7 multiply_convert_fusion.1
  229.3 10.5 %exchange_6.1 = bf16[4,64,1024]{2,1,0:T(8,128)(2,1)} custom-call(bf16[64,1024]{1,0:T(8,128)(2,1)} %get-tuple-element.78.refs_0_), custom_call_target="tpu_custom_call" | custom-call | bytes 10485760 | tf_op jit(solution)/shard_map/exchange_6/pallas_call | solution.py:107
  239.8 1.3 convolution_convert_fusion.7.grads_ref
  241.2 8.3 %attention_back.1 = (f32[256,256]{1,0:T(8,128)S(1)}, bf16[2048,256]{1,0:T(8,128)(2,1)S(1)}) custom-call(s32[256,1]{1,0:T(8,128)S(1)} %copy.77.starts_ref, s32[1,1]{1,0:T(1,128)} %bitcast.4.first_ref, bf16[256,256]{1,0:T(8,128)(2,1)S(1)} %slice.124.queries_ref, bf16[256,256]{1,0:T(8,128)(2,1)S(1)} %convolution_convert_fusion.7.grads_ref, ...), custom_call_target="tpu_custom_call" | custom-call | flops 1342177280 | bytes 8388608 | tf_op jit(solution)/shard_map/attention_back/pallas_call | solution.py:261
  249.5 1.0 copy-done.3
  250.5 6.8 %all-gather.6.cloned.1.call-done = bf16[8,3,256,128]{3,2,1,0:T(8,128)(2,1)} async-done(((bf16[4,3,256,128]{3,2,1,0:T(8,128)(2,1)}), bf16[8,3,256,128]{3,2,1,0:T(8,128)(2,1)}) %all-gather.6.cloned.1.call-update) | async-done | bytes 1572880 | tf_op jit(solution)/shard_map/all_gather | solution.py:679
  259.9 1.0 copy.78
  260.9 1.4 convolution_convert_fusion.3
  262.3 1.9 pad_maximum_fusion.1.refs_2_
  264.2 1.6 convolution_convert_fusion.5
  265.8 22.5 %exchange_7.1 = (bf16[8,256,256]{2,1,0:T(8,128)(2,1)}, bf16[4,64,1024]{2,1,0:T(8,128)(2,1)}, bf16[4,256,384]{2,1,0:T(8,128)(2,1)}) custom-call(bf16[8,256,256]{2,1,0:T(8,128)(2,1)} %bitcast.112, bf16[4,64,1024]{2,1,0:T(8,128)(2,1)} %bitcast.141, bf16[4,256,384]{2,1,0:T(8,128)(2,1)} %pad_maximum_fusion.1.refs_2_), custom_call_target="tpu_custom_call" | custom-call | bytes 47185920 | tf_op jit(solution)/shard_map/exchange_7/pallas_call | solution.py:107
  288.3 1.5 convert_reduce_fusion
  290.3 2.7 fusion.11
  293.0 2.0 multiply_reduce_fusion
  296.5 1.5 convolution_convert_fusion.2
  298.0 18.6 %exchange_8.1 = (bf16[4,64,1024]{2,1,0:T(8,128)(2,1)}, bf16[4,256,512]{2,1,0:T(8,128)(2,1)}, f32[4,8,256]{2,1,0:T(8,128)}, bf16[4,64,1024]{2,1,0:T(8,128)(2,1)}) custom-call(bf16[4,64,1024]{2,1,0:T(8,128)(2,1)} %bitcast.139, bf16[4,256,512]{2,1,0:T(8,128)(2,1)} %bitcast.129, f32[4,8,256]{2,1,0:T(8,128)} %pad.15.refs_2_, bf16[64,1024]{1,0:T(8,128)(2,1)} %add_convert_fusion.refs_3_), custom_call_target="tpu_custom_call" | custom-call | bytes 42598400 | tf_op jit(solution)/shard_map/exchange_8/pallas_call | solution.py:107
  316.6 1.4 reduce_sum.214.refs_1_
  318.0 1.5 reduce_sum.212
  321.3 21.9 %exchange_9.1 = (bf16[8,32,896]{2,1,0:T(8,128)(2,1)}, f32[32,8,256]{2,1,0:T(8,128)}, bf16[4,64,1024]{2,1,0:T(8,128)(2,1)}) custom-call(bf16[8,32,896]{2,1,0:T(8,128)(2,1)} %bitcast.126, f32[8,256]{1,0:T(8,128)} %reduce_sum.214.refs_1_, bf16[64,1024]{1,0:T(8,128)(2,1)} %subtract_convert_fusion.refs_2_), custom_call_target="tpu_custom_call" | custom-call | bytes 24903680 | tf_op jit(solution)/shard_map/exchange_9/pallas_call | solution.py:107
  343.2 1.0 reduce_sum.217
  344.2 1.7 reduce_sum.218.refs_0_
  345.9 10.1 %exchange_10.1 = bf16[8,32,896]{2,1,0:T(8,128)(2,1)} custom-call(bf16[32,896]{1,0:T(8,128)(2,1)} %reduce_sum.218.refs_0_), custom_call_target="tpu_custom_call" | custom-call | bytes 9175040 | tf_op jit(solution)/shard_map/exchange_10/pallas_call | solution.py:107
  356.1 1.1 bitcast_convert_fusion
  360.0 2.8 copy-done.2
  362.8 5.0 %spread.1 = (f32[8192,128]{1,0:T(8,128)}, f32[8192,128]{1,0:T(8,128)}, f32[8192,128]{1,0:T(8,128)}) custom-call(bf16[32,3,256,128]{3,2,1,0:T(8,128)(2,1)S(1)} %copy-done.2), custom_call_target="tpu_custom_call" | custom-call | tf_op jit(solution)/shard_map/spread/pallas_call | solution.py:132
  (178 shorter events, 24.2 us)
Async XLA Ops:
  7.2 4.1 %copy-start = (bf16[256,32,128]{2,1,0:T(8,128)(2,1)S(1)}, bf16[256,32,128]{2,1,0:T(8,128)(2,1)}, u32[]{:S(2)}) copy-start(bf16[256,32,128]{2,1,0:T(8,128)(2,1)} %param.27) | copy-start | bytes 6291460
  7.2 113.7 %all-gather.4.cloned.1.call-start = ((), (), s32[]{:S(2)}) async-start(), calls=%async_computation | async-start | bytes 3932160 | tf_op jit(solution)/shard_map/all_gather | solution.py:615
  7.3 6.8 %copy-start.19 = (bf16[256,1024]{1,0:T(8,128)(2,1)S(1)}, bf16[256,1024]{1,0:T(8,128)(2,1)}, u32[]{:S(2)}) copy-start(bf16[256,1024]{1,0:T(8,128)(2,1)} %param.17) | copy-start | bytes 1572868
  12.9 3.2 copy-start.39
  13.0 3.2 copy-start.40
  13.0 3.8 %copy-start.28 = (bf16[256,256]{1,0:T(8,128)(2,1)S(1)}, bf16[256,256]{1,0:T(8,128)(2,1)}, u32[]{:S(2)}) copy-start(bf16[256,256]{1,0:T(8,128)(2,1)} %param.21) | copy-start | bytes 393220
  13.0 3.8 %copy-start.29 = (bf16[256,128]{1,0:T(8,128)(2,1)S(1)}, bf16[256,128]{1,0:T(8,128)(2,1)}, u32[]{:S(2)}) copy-start(bf16[256,128]{1,0:T(8,128)(2,1)} %param.23) | copy-start | bytes 196612
  13.0 3.8 %copy-start.30 = (bf16[256,128]{1,0:T(8,128)(2,1)S(1)}, bf16[256,128]{1,0:T(8,128)(2,1)}, u32[]{:S(2)}) copy-start(bf16[256,128]{1,0:T(8,128)(2,1)} %param.22) | copy-start | bytes 196612
  14.1 189.3 %copy-start.17 = (pred[1024,256]{1,0:T(32,128)(4,1)}, pred[1024,256]{1,0:T(32,128)(4,1)S(1)}, u32[]{:S(2)}) copy-start(pred[1024,256]{1,0:T(32,128)(4,1)S(1)} %fusion.3) | copy-start | bytes 786436
  57.9 3.3 copy-start.13
  60.9 3.1 copy-start.38
  60.9 196.4 %all-gather.6.cloned.1.call-start = ((), (), s32[]{:S(2)}) async-start(), calls=%async_computation.1 | async-start | bytes 2359296 | tf_op jit(solution)/shard_map/all_gather | solution.py:679
  61.4 2.9 copy-start.32
  63.9 2.5 copy-start.37
  64.0 41.7 %copy-start.11 = (f32[256,1024]{1,0:T(8,128)}, f32[256,1024]{1,0:T(8,128)S(1)}, u32[]{:S(2)}) copy-start(f32[256,1024]{1,0:T(8,128)S(1)} %convert_element_type.131) | copy-start | bytes 3145732
  84.7 1.2 copy-start.5
  85.9 5.1 %copy-start.15 = (bf16[4,256,256]{2,1,0:T(8,128)(2,1)S(1)}, bf16[4,256,256]{2,1,0:T(8,128)(2,1)}, u32[]{:S(2)}) copy-start(bf16[4,256,256]{2,1,0:T(8,128)(2,1)} %get-tuple-element.46) | copy-start | bytes 1572868
  92.1 23.0 %copy-start.31 = (s32[256,8]{0,1:T(8,128)S(1)}, s32[256,8]{0,1:T(8,128)}, u32[]{:S(2)}) copy-start(s32[256,8]{0,1:T(8,128)} %param.19) | copy-start | bytes 24580
  92.1 23.1 %copy-start.16 = (bf16[4,256,128]{2,1,0:T(8,128)(2,1)S(1)}, bf16[4,256,128]{2,1,0:T(8,128)(2,1)}, u32[]{:S(2)}) copy-start(bf16[4,256,128]{2,1,0:T(8,128)(2,1)} %get-tuple-element.47) | copy-start | bytes 786436
  202.5 0.9 copy-start.4
  203.4 1.6 copy-start.7
  224.0 136.0 %all-gather.8.cloned.1.call-start = ((), (), s32[]{:S(2)}) async-start(), calls=%async_computation.2 | async-start | bytes 7864320 | tf_op jit(solution)/shard_map/all_gather | solution.py:712
  226.9 14.3 %copy-start.6 = (bf16[8,256,256]{2,1,0:T(8,128)(2,1)S(1)}, bf16[8,256,256]{2,1,0:T(8,128)(2,1)}, u32[]{:S(2)}) copy-start(bf16[8,256,256]{2,1,0:T(8,128)(2,1)} %get-tuple-element.45) | copy-start | bytes 3145732
  226.9 2.4 copy-start.26
  241.2 16.2 %copy-start.33 = (f32[256]{0:T(256)S(1)}, f32[256]{0:T(256)}, u32[]{:S(2)}) copy-start(f32[256]{0:T(256)} %copy-done.32) | copy-start | bytes 3076
  241.2 16.8 %copy-start.9 = (bf16[4,64,1024]{2,1,0:T(8,128)(2,1)S(1)}, bf16[4,64,1024]{2,1,0:T(8,128)(2,1)}, u32[]{:S(2)}) copy-start(bf16[4,64,1024]{2,1,0:T(8,128)(2,1)} %exchange_11.1) | copy-start | bytes 1572868
  241.2 16.8 %copy-start.27 = (f32[256,32]{0,1:T(8,128)S(1)}, f32[256,32]{0,1:T(8,128)}, u32[]{:S(2)}) copy-start(f32[256,32]{0,1:T(8,128)} %copy-done.26) | copy-start | bytes 98308
  249.5 1.0 copy-start.3
  250.5 9.4 %copy-start.10 = (bf16[4,64,1024]{2,1,0:T(8,128)(2,1)S(1)}, bf16[4,64,1024]{2,1,0:T(8,128)(2,1)}, u32[]{:S(2)}) copy-start(bf16[4,64,1024]{2,1,0:T(8,128)(2,1)} %exchange_6.1) | copy-start | bytes 1572868
  259.2 5.0 %copy-start.8 = (bf16[1024,1024]{1,0:T(8,128)(2,1)S(1)}, bf16[1024,1024]{1,0:T(8,128)(2,1)}, u32[]{:S(2)}) copy-start(bf16[1024,1024]{1,0:T(8,128)(2,1)} %copy-done.7) | copy-start | bytes 6291460
  260.9 3.3 copy-start.18
  288.3 1.6 copy-start.20
  288.3 2.0 copy-start.25
  289.8 3.2 copy-start.14
  290.1 2.9 copy-start.41
  290.3 5.4 %copy-start.21 = (bf16[4,64,1024]{2,1,0:T(8,128)(2,1)S(1)}, bf16[4,64,1024]{2,1,0:T(8,128)(2,1)}, u32[]{:S(2)}) copy-start(bf16[4,64,1024]{2,1,0:T(8,128)(2,1)} %get-tuple-element.61) | copy-start | bytes 1572868
  293.0 3.4 copy-start.34
  298.0 22.4 %copy-start.12 = (f32[256,1024]{1,0:T(8,128)S(1)}, f32[256,1024]{1,0:T(8,128)}, u32[]{:S(2)}) copy-start(f32[256,1024]{1,0:T(8,128)} %copy-done.11) | copy-start | bytes 3145732
  316.6 3.7 copy-start.22
  316.6 3.9 %copy-start.35 = (f32[64]{0:T(128)S(1)}, f32[64]{0:T(128)}, u32[]{:S(2)}) copy-start(f32[64]{0:T(128)} %get-tuple-element.76) | copy-start | bytes 772
  316.6 3.9 %copy-start.36 = (f32[64]{0:T(128)S(1)}, f32[64]{0:T(128)}, u32[]{:S(2)}) copy-start(f32[64]{0:T(128)} %get-tuple-element.77) | copy-start | bytes 772
  360.0 2.8 copy-start.2
  362.7 5.1 %copy-start.23 = (bf16[4,64,1024]{2,1,0:T(8,128)(2,1)S(1)}, bf16[4,64,1024]{2,1,0:T(8,128)(2,1)}, u32[]{:S(2)}) copy-start(bf16[4,64,1024]{2,1,0:T(8,128)(2,1)} %get-tuple-element.62) | copy-start | bytes 1572868
  362.7 5.8 %copy-start.24 = (bf16[4,64,1024]{2,1,0:T(8,128)(2,1)S(1)}, bf16[4,64,1024]{2,1,0:T(8,128)(2,1)}, u32[]{:S(2)}) copy-start(bf16[4,64,1024]{2,1,0:T(8,128)(2,1)} %get-tuple-element.67) | copy-start | bytes 1572868
  362.7 6.6 %copy-start.1 = (bf16[256,32,128]{2,1,0:T(8,128)(2,1)S(1)}, bf16[256,32,128]{2,1,0:T(8,128)(2,1)}, u32[]{:S(2)}) copy-start(bf16[256,32,128]{2,1,0:T(8,128)(2,1)} %param.27) | copy-start | bytes 6291460
Sparse Core Ops, SparseCore 0:
  61.0 46.5 all-gather.3
  224.1 33.1 all-gather.5
  259.0 80.8 all-gather.7

commit v8 on v7

--- a/solution.py
+++ b/solution.py
@@ -282,11 +282,12 @@
     rows_ref,
     probs_ref,
     grads_ref,
-    w_ref,
+    slices_ref,
     norm_got,
     mixed_got,
     gate_got,
     wgrad_ref,
+    w_ref,
     wgrad_buf,
     wgrad_got,
     norm_buf,
@@ -350,6 +351,13 @@
             item.start()
     norm_buf[:CAP] = rows_ref[:CAP]
     probs_buf[0] = probs_ref[0]
+    slim = wgrad_ref.shape[1]
+    n_tp = hidden // slim
+    for place in range(slices_ref.shape[0]):
+        down = place // n_tp * part
+        for which in range(3):
+            start = which * hidden + place % n_tp * slim
+            w_ref[down : down + part, start : start + slim] = slices_ref[place, which]
     same = lax.broadcasted_iota(jnp.int32, (CAP, CAP), 0) == lax.broadcasted_iota(
         jnp.int32, (CAP, CAP), 1
     )
@@ -412,8 +420,6 @@
     mixed_got[:CAP] = mixed_buf[:CAP]
     gate_got[0] = gate_buf[0]
 
-    slim = wgrad_ref.shape[1]
-
     def wgrad_copy(k):
         return pltpu.make_async_remote_copy(
             src_ref=wgrad_buf.at[k],
@@ -468,7 +474,7 @@
     n = sizes["ctx"]
     total, width = rows_sent.shape
     n_fsdp, n_tp = sizes["fsdp"], sizes["tp"]
-    hidden, part = expert_w.shape[1] // 3, width // n_fsdp
+    hidden, part = expert_w.shape[3] * n_tp, width // n_fsdp
     owned = (n_tp * 3 * part, hidden // n_tp)
     like = jax.ShapeDtypeStruct
     vmem = pl.BlockSpec(memory_space=pltpu.VMEM)
@@ -483,6 +489,7 @@
         in_specs=[vmem] * 4,
         out_specs=[vmem] * 4,
         scratch_shapes=[
+            pltpu.VMEM((width, 3 * hidden), bf16),
             pltpu.VMEM((n_fsdp,) + owned, bf16),
             pltpu.VMEM((n_fsdp,) + owned, bf16),
             pltpu.VMEM((total, width), bf16),
@@ -564,6 +571,29 @@
     send = functools.partial(exchange, sizes)
     ctx_at, tp_at = lax.axis_index("ctx"), lax.axis_index("tp")
 
+    first = ctx_at * per_ctx
+    own_slices = jnp.stack(
+        [
+            lax.dynamic_slice_in_dim(w, first, per_ctx, 1).transpose(1, 0, 2)
+            for w in (w_gate, w_up, w_down)
+        ],
+        axis=1,
+    )
+    lines = depth // 128
+
+    def lined(gain):
+        return jnp.pad(gain.reshape(lines, 128), ((0, 16 - lines), (0, 0)))
+
+    qkv_w, gain_one, expert_slices = send(
+        0,
+        (("fsdp",), "g", jnp.concatenate([w_query, key_weight, value_weight], axis=1)),
+        (("fsdp",), "g", lined(attn_gain)),
+        (("tp",), "a", own_slices),
+    )
+    qkv_w = qkv_w.reshape(width, -1)
+    gain_one = gain_one[:, :lines].reshape(width).astype(f32)
+    expert_w = lax.all_gather(expert_slices, "fsdp", axis=0, tiled=True)
+
     chosen = jnp.any(
         expert_ids[:, :, None] == jnp.arange(experts, dtype=jnp.int32)[None, None, :], axis=1
     )
@@ -576,43 +606,6 @@
     slots = jnp.arange(CAP, dtype=f32)
     picks = (chosen_mine[:, None, :] & (rank[:, None, :] == slots[None, :, None])).astype(bf16)
     picks_flat = picks.reshape(n_ctx * CAP, rows)
-
-    first = ctx_at * per_ctx
-    own_slices = jnp.stack(
-        [
-            lax.dynamic_slice_in_dim(w, first, per_ctx, 1).transpose(1, 0, 2)
-            for w in (w_gate, w_up, w_down)
-        ],
-        axis=1,
-    )
-    gains = jnp.concatenate(
-        [
-            attn_gain.reshape(-1, 128),
-            ffn_gain.reshape(-1, 128),
-            jnp.zeros((16 - 2 * depth // 128, 128), bf16),
-        ],
-        axis=0,
-    )
-    router_pad = jnp.pad(w_router, ((0, 0), (0, 128 - experts)))
-    grads_sent = mm(picks_flat, cotangent).astype(bf16).reshape(n_ctx, CAP, width)
-    qkv_w, gains_all, router_all, expert_slices, grad_rows = send(
-        0,
-        (("fsdp",), "g", jnp.concatenate([w_query, key_weight, value_weight], axis=1)),
-        (("fsdp",), "g", gains),
-        (("fsdp",), "g", router_pad),
-        (("tp",), "a", own_slices),
-        (("ctx",), "f", grads_sent),
-    )
-    qkv_w = qkv_w.reshape(width, -1)
-    lines = depth // 128
-    gain_one = gains_all[:, :lines].reshape(width).astype(f32)
-    gain_two = gains_all[:, lines : 2 * lines].reshape(width).astype(f32)
-    router_w = router_all.reshape(width, 128)[:, :experts]
-
-    grad_rows = grad_rows.reshape(n_ctx * CAP, width)
-
-    expert_cat = expert_slices.transpose(2, 1, 0, 3).reshape(depth, 3 * n_tp * ff)
-    expert_w = lax.all_gather(expert_cat, "fsdp", axis=0, tiled=True)
 
     lengths_row = lengths[0]
     query_rows = ctx_at * rows + jnp.arange(rows, dtype=jnp.int32)
@@ -631,8 +624,19 @@
     pairs_local = jnp.concatenate(
         [queries_keys[:, q_end:], qkv[:, turned:].astype(bf16)], axis=1
     )
-    pairs_all, output_w = send(1, (("ctx",), "g", pairs_local), (("fsdp",), "g", w_output))
+    grads_sent = mm(picks_flat, cotangent).astype(bf16).reshape(n_ctx, CAP, width)
+    pairs_all, output_w, gain_two, router_all, grad_rows = send(
+        1,
+        (("ctx",), "g", pairs_local),
+        (("fsdp",), "g", w_output),
+        (("fsdp",), "g", lined(ffn_gain)),
+        (("fsdp",), "g", jnp.pad(w_router, ((0, 0), (0, 128 - experts)))),
+        (("ctx",), "f", grads_sent),
+    )
     output_w = output_w.reshape(width, -1)
+    gain_two = gain_two[:, :lines].reshape(width).astype(f32)
+    router_w = router_all.reshape(width, 128)[:, :experts]
+    grad_rows = grad_rows.reshape(n_ctx * CAP, width)
     total_rows = n_ctx * rows
     pairs_all = pairs_all.reshape(total_rows, 2 * pair_width)
     attended = attention(starts, ctx_at * rows, queries, pairs_all, pair_width)
@@ -708,14 +712,14 @@
     query_grad_rot, pair_grads = attention_back(
         starts, ctx_at * rows, queries, attended_grad, pairs_all, pair_width
     )
-    pieces, pair_grads = lax.optimization_barrier((pieces, pair_grads))
-    expert_all = lax.all_gather(pieces, "ctx", axis=0, tiled=True, axis_index_groups=rings)
     pair_got, mixed_parts, early_got = send(
         7,
         (("ctx",), "a", pair_grads.reshape(n_ctx, rows, 2 * pair_width)),
         (("tp",), "a", mixed_part.reshape(n_tp, quarter, width)),
         (("fsdp",), "a", early.reshape(n_fsdp, depth, -1)),
     )
+    pieces, pair_got = lax.optimization_barrier((pieces, pair_got))
+    expert_all = lax.all_gather(pieces, "ctx", axis=0, tiled=True, axis_index_groups=rings)
     pair_owned = jnp.sum(pair_got.astype(f32), axis=0)
     turned_back = turn(
         jnp.concatenate([query_grad_rot, pair_owned[:, :pair_width]], axis=1),

time: 377 us -> 389 us (1.032)
  Pallas kernels: 279 us -> 299 us
  waiting for transfers between devices: 6.89 us -> 1.38 us
    pallas_call x10, Pallas kernels: 179 us -> 198 us  [exchange(): pl.pallas_call(functools.partial(exchange_kernel, plan, sizes), out_shape...]
    all_gather x1, waiting for transfers between devices: 6.84 us -> 0.02 us  [local(): lax.all_gather(pieces, 'ctx', axis=0, tiled=True, axis_index_groups=pairs)]
    unnamed x93 -> x99, local copies, waits for them, and re-layouts: 9.45 us -> 10.2 us
  transfers between devices with their start and end apart: 3 -> 3, of which waited for: 1 -> 1; matrix products, arithmetic and copies ran while one was open for 13% -> 14% of each run, Pallas kernels for 36% -> 45%
where the time goes in v8:
time: 389 us; the launch traced here: 388 us
  Pallas kernels  299 us (77%)
  other arithmetic  29.4 us (8%)
  local copies, waits for them, and re-layouts  23.8 us (6%)
  matrix products  19.4 us (5%)
  between operations  14.7 us (4%)
    pallas_call x10, Pallas kernels, exchange(): pl.pallas_call(functools.partial(exchange_kernel, plan, sizes), out_shape...  198 us
    pallas_call x1, Pallas kernels, expert_of_place(): pl.pallas_call(functools.partial(expert_kernel, n, n_fsdp, part), out_sha...  82.7 us
    unnamed x99, local copies, waits for them, and re-layouts  10.2 us
    dot_general x6, matrix products, mm(): return jnp.dot(left, right, preferred_element_type=f32)  9.86 us
    pallas_call x1, Pallas kernels, attention_back(): pl.pallas_call(functools.partial(attention_back_kernel, groups), out_shap...  8.26 us
  transfers between devices with their start and end apart: 3, of which 1 were waited for; matrix products, arithmetic and copies ran while one was open for 14% of the time, Pallas kernels for 45%

profile of v8, /device:TPU:1, one launch (start us, length us, event | category | flops | bytes accessed | tf_op | source)
XLA Modules:
  0.0 387.9 jit_solution(18126109965612055969)
XLA Ops:
  7.3 1.5 copy-done
  9.0 1.5 constant_dynamic-slice_fusion.1
  11.9 1.0 pad_maximum_fusion.refs_2_
  12.9 19.9 %exchange_0.1 = (bf16[4,256,512]{2,1,0:T(8,128)(2,1)}, bf16[4,16,128]{2,1,0:T(8,128)(2,1)}, bf16[4,3,256,128]{3,2,1,0:T(8,128)(2,1)}) custom-call(bf16[256,512]{1,0:T(8,128)(2,1)} %pad_maximum_fusion.4.refs_0_, bf16[16,128]{1,0:T(8,128)(2,1)} %pad.20.refs_1_, bf16[4,3,256,128]{3,2,1,0:T(8,128)(2,1)} %pad_maximum_fusion.refs_2_), custom_call_target="tpu_custom_call" | custom-call | bytes 37027840 | tf_op jit(solution)/shard_map/exchange_0/pallas_call | solution.py:107
  33.9 1.7 fusion.20
  36.2 1.8 fusion.9
  41.7 2.0 convolution_convert_fusion.1
  43.8 41.5 %exchange_1.1 = (bf16[8,256,256]{2,1,0:T(8,128)(2,1)}, bf16[4,256,256]{2,1,0:T(8,128)(2,1)}, bf16[4,16,128]{2,1,0:T(8,128)(2,1)}, bf16[4,256,128]{2,1,0:T(8,128)(2,1)}, bf16[8,128,1024]{2,1,0:T(8,128)(2,1)}) custom-call(bf16[256,256]{1,0:T(8,128)(2,1)} %pad_maximum_fusion.8.refs_0_, bf16[256,256]{1,0:T(8,128)(2,1)} %refs_1_.1, bf16[16,128]{1,0:T(8,128)(2,1)} %pad.21.refs_2_, ...), custom_call_target="tpu_custom_call" | custom-call | bytes 78970880 | tf_op jit(solution)/shard_map/exchange_1/pallas_call | solution.py:107
  86.0 1.2 copy-done.5
  87.2 5.1 %attention.1 = bf16[256,256]{1,0:T(8,128)(2,1)S(1)} custom-call(s32[256,1]{1,0:T(8,128)S(1)} %copy.73.starts_ref, s32[1,1]{1,0:T(1,128)} %bitcast.4.first_ref, bf16[256,256]{1,0:T(8,128)(2,1)S(1)} %slice.124.queries_ref, bf16[2048,256]{1,0:T(8,128)(2,1)S(1)} %bitcast.113), custom_call_target="tpu_custom_call" | custom-call | flops 536870912 | bytes 4194304 | tf_op jit(solution)/shard_map/attention/pallas_call | solution.py:186
  92.3 1.1 convolution_convert_fusion.4
  93.5 9.4 %exchange_2.1 = bf16[4,64,1024]{2,1,0:T(8,128)(2,1)} custom-call(bf16[4,64,1024]{2,1,0:T(8,128)(2,1)} %bitcast.124), custom_call_target="tpu_custom_call" | custom-call | bytes 10485760 | tf_op jit(solution)/shard_map/exchange_2/pallas_call | solution.py:107
  102.9 1.1 convert_reduce_fusion.4
  105.5 8.5 %exchange_11.1 = bf16[4,64,1024]{2,1,0:T(8,128)(2,1)} custom-call(bf16[64,1024]{1,0:T(8,128)(2,1)} %multiply_convert_fusion.2.refs_0_), custom_call_target="tpu_custom_call" | custom-call | bytes 10485760 | tf_op jit(solution)/shard_map/exchange_11/pallas_call | solution.py:107
  114.0 1.3 fusion.49
  116.6 3.1 convolution_convert_fusion.rows_ref
  119.7 82.7 %expert_of_place.1 = (bf16[1024,1024]{1,0:T(8,128)(2,1)S(1)}, bf16[1024,1024]{1,0:T(8,128)(2,1)S(1)}, f32[8,8,128]{2,1,0:T(8,128)S(1)}, bf16[3072,128]{1,0:T(8,128)(2,1)S(1)}) custom-call(bf16[1024,1024]{1,0:T(8,128)(2,1)} %convolution_convert_fusion.rows_ref, f32[8,8,128]{2,1,0:T(8,128)S(1)} %broadcast_in_dim.82.probs_ref, bf16[1024,1024]{1,0:T(8,128)(2,1)} %bitcast.156, ...), custom_call_target="tpu_custom_call" | custom-call | flops 19327352832 | bytes 104857600 | tf_op jit(solution)/shard_map/expert_of_place/pallas_call | solution.py:481
  202.3 0.9 copy-done.4
  203.2 1.5 convolution_convert_fusion.6
  204.8 0.9 fusion.1.refs_1_
  205.6 18.0 %exchange_5.1 = (bf16[4,64,1024]{2,1,0:T(8,128)(2,1)}, f32[4,8,256]{2,1,0:T(8,128)}, bf16[4,3,256,128]{3,2,1,0:T(8,128)(2,1)}) custom-call(bf16[4,64,1024]{2,1,0:T(8,128)(2,1)} %bitcast.138, f32[8,256]{1,0:T(8,128)} %fusion.1.refs_1_, bf16[4,3,256,128]{3,2,1,0:T(8,128)(2,1)} %bitcast.112), custom_call_target="tpu_custom_call" | custom-call | bytes 26869760 | tf_op jit(solution)/shard_map/exchange_5/pallas_call | solution.py:107
  223.7 1.1 convert_reduce_fusion.3
  226.4 1.9 multiply_reduce_fusion.3
  230.3 1.9 multiply_convert_fusion.1
  232.2 8.5 %exchange_6.1 = bf16[4,64,1024]{2,1,0:T(8,128)(2,1)} custom-call(bf16[64,1024]{1,0:T(8,128)(2,1)} %get-tuple-element.80.refs_0_), custom_call_target="tpu_custom_call" | custom-call | bytes 10485760 | tf_op jit(solution)/shard_map/exchange_6/pallas_call | solution.py:107
  240.7 2.0 copy.74
  242.7 1.6 convolution_convert_fusion.7.grads_ref
  244.3 8.3 %attention_back.1 = (f32[256,256]{1,0:T(8,128)S(1)}, bf16[2048,256]{1,0:T(8,128)(2,1)S(1)}) custom-call(s32[256,1]{1,0:T(8,128)S(1)} %copy.73.starts_ref, s32[1,1]{1,0:T(1,128)} %bitcast.4.first_ref, bf16[256,256]{1,0:T(8,128)(2,1)S(1)} %slice.124.queries_ref, bf16[256,256]{1,0:T(8,128)(2,1)S(1)} %convolution_convert_fusion.7.grads_ref, ...), custom_call_target="tpu_custom_call" | custom-call | flops 1342177280 | bytes 8388608 | tf_op jit(solution)/shard_map/attention_back/pallas_call | solution.py:261
  253.0 1.0 pad_maximum_fusion.1.refs_2_
  253.9 0.9 copy-done.8
  254.9 1.6 convolution_convert_fusion.5
  256.4 35.9 %exchange_7.1 = (bf16[8,256,256]{2,1,0:T(8,128)(2,1)}, bf16[4,64,1024]{2,1,0:T(8,128)(2,1)}, bf16[4,256,384]{2,1,0:T(8,128)(2,1)}) custom-call(bf16[8,256,256]{2,1,0:T(8,128)(2,1)} %bitcast.111, bf16[4,64,1024]{2,1,0:T(8,128)(2,1)} %bitcast.139, bf16[4,256,384]{2,1,0:T(8,128)(2,1)} %pad_maximum_fusion.1.refs_2_), custom_call_target="tpu_custom_call" | custom-call | bytes 47185920 | tf_op jit(solution)/shard_map/exchange_7/pallas_call | solution.py:107
  293.1 2.0 reduce_sum.213
  295.0 1.1 convert_reduce_fusion.2
  297.4 2.0 fusion.11
  299.4 1.3 multiply_reduce_fusion
  301.4 1.5 convolution_convert_fusion.2
  302.9 21.9 %exchange_8.1 = (bf16[4,64,1024]{2,1,0:T(8,128)(2,1)}, bf16[4,256,512]{2,1,0:T(8,128)(2,1)}, f32[4,8,256]{2,1,0:T(8,128)}, bf16[4,64,1024]{2,1,0:T(8,128)(2,1)}) custom-call(bf16[4,64,1024]{2,1,0:T(8,128)(2,1)} %bitcast.137, bf16[4,256,512]{2,1,0:T(8,128)(2,1)} %bitcast.128, f32[4,8,256]{2,1,0:T(8,128)} %pad.24.refs_2_, bf16[64,1024]{1,0:T(8,128)(2,1)} %add_convert_fusion.refs_3_), custom_call_target="tpu_custom_call" | custom-call | bytes 42598400 | tf_op jit(solution)/shard_map/exchange_8/pallas_call | solution.py:107
  324.8 1.4 reduce_sum.214.refs_1_
  326.3 1.5 reduce_sum.212
  329.6 20.6 %exchange_9.1 = (bf16[8,32,896]{2,1,0:T(8,128)(2,1)}, f32[32,8,256]{2,1,0:T(8,128)}, bf16[4,64,1024]{2,1,0:T(8,128)(2,1)}) custom-call(bf16[8,32,896]{2,1,0:T(8,128)(2,1)} %bitcast.125, f32[8,256]{1,0:T(8,128)} %reduce_sum.214.refs_1_, bf16[64,1024]{1,0:T(8,128)(2,1)} %subtract_convert_fusion.refs_2_), custom_call_target="tpu_custom_call" | custom-call | bytes 24903680 | tf_op jit(solution)/shard_map/exchange_9/pallas_call | solution.py:107
  350.2 1.0 reduce_sum.217
  351.2 1.7 reduce_sum.218.refs_0_
  352.9 13.8 %exchange_10.1 = bf16[8,32,896]{2,1,0:T(8,128)(2,1)} custom-call(bf16[32,896]{1,0:T(8,128)(2,1)} %reduce_sum.218.refs_0_), custom_call_target="tpu_custom_call" | custom-call | bytes 9175040 | tf_op jit(solution)/shard_map/exchange_10/pallas_call | solution.py:107
  366.8 1.1 bitcast_convert_fusion
  370.7 1.3 all-gather.8.cloned.1.call-done.pieces_ref
  372.0 2.8 copy-done.2
  374.8 5.0 %spread.1 = (f32[8192,128]{1,0:T(8,128)}, f32[8192,128]{1,0:T(8,128)}, f32[8192,128]{1,0:T(8,128)}) custom-call(bf16[32,3,256,128]{3,2,1,0:T(8,128)(2,1)S(1)} %copy-done.2), custom_call_target="tpu_custom_call" | custom-call | tf_op jit(solution)/shard_map/spread/pallas_call | solution.py:132
  (182 shorter events, 22.8 us)
Async XLA Ops:
  7.2 1.6 copy-start
  7.2 3.4 copy-start.40
  7.2 4.0 %copy-start.26 = (bf16[256,128]{1,0:T(8,128)(2,1)S(1)}, bf16[256,128]{1,0:T(8,128)(2,1)}, u32[]{:S(2)}) copy-start(bf16[256,128]{1,0:T(8,128)(2,1)} %param.23) | copy-start | bytes 196612
  7.2 4.0 %copy-start.27 = (bf16[256,128]{1,0:T(8,128)(2,1)S(1)}, bf16[256,128]{1,0:T(8,128)(2,1)}, u32[]{:S(2)}) copy-start(bf16[256,128]{1,0:T(8,128)(2,1)} %param.22) | copy-start | bytes 196612
  7.2 4.0 %copy-start.25 = (bf16[256,256]{1,0:T(8,128)(2,1)S(1)}, bf16[256,256]{1,0:T(8,128)(2,1)}, u32[]{:S(2)}) copy-start(bf16[256,256]{1,0:T(8,128)(2,1)} %param.21) | copy-start | bytes 393220
  7.2 112.4 %all-gather.4.cloned.1.call-start = ((), (), s32[]{:S(2)}) async-start(), calls=%async_computation | async-start | bytes 3932160 | tf_op jit(solution)/shard_map/all_gather | solution.py:595
  10.6 22.4 %copy-start.11 = (bf16[256,1024]{1,0:T(8,128)(2,1)S(1)}, bf16[256,1024]{1,0:T(8,128)(2,1)}, u32[]{:S(2)}) copy-start(bf16[256,1024]{1,0:T(8,128)(2,1)} %param.16) | copy-start | bytes 1572868
  32.9 259.5 %all-gather.6.cloned.1.call-start = ((), (), s32[]{:S(2)}) async-start(), calls=%async_computation.1 | async-start | bytes 2359296 | tf_op jit(solution)/shard_map/all_gather | solution.py:683
  32.9 3.3 copy-start.38
  33.1 2.4 copy-start.33
  33.9 2.1 copy-start.42
  35.9 2.3 copy-start.41
  35.9 2.9 copy-start.29
  35.9 3.9 copy-start.9
  36.2 4.2 %copy-start.30 = (f32[256]{0:T(256)}, f32[256]{0:T(256)S(1)}, u32[]{:S(2)}) copy-start(f32[256]{0:T(256)S(1)} %subtract_convert_fusion.1) | copy-start | bytes 3076
  36.2 4.2 %copy-start.43 = (s32[8]{0:T(128)S(1)}, s32[8]{0:T(128)}, u32[]{:S(2)}) copy-start(s32[8]{0:T(128)} %constant.118.clone) | copy-start | bytes 100
  36.2 4.2 %copy-start.28 = (s32[256,8]{0,1:T(8,128)S(1)}, s32[256,8]{0,1:T(8,128)}, u32[]{:S(2)}) copy-start(s32[256,8]{0,1:T(8,128)} %param.19) | copy-start | bytes 24580
  38.0 3.7 copy-start.20
  41.0 162.2 %copy-start.18 = (pred[1024,256]{1,0:T(32,128)(4,1)}, pred[1024,256]{1,0:T(32,128)(4,1)S(1)}, u32[]{:S(2)}) copy-start(pred[1024,256]{1,0:T(32,128)(4,1)S(1)} %fusion.3) | copy-start | bytes 786436
  86.0 1.2 copy-start.5
  87.2 5.1 %copy-start.12 = (bf16[4,256,256]{2,1,0:T(8,128)(2,1)S(1)}, bf16[4,256,256]{2,1,0:T(8,128)(2,1)}, u32[]{:S(2)}) copy-start(bf16[4,256,256]{2,1,0:T(8,128)(2,1)} %get-tuple-element.47) | copy-start | bytes 1572868
  93.5 20.5 %copy-start.15 = (bf16[4,256,128]{2,1,0:T(8,128)(2,1)S(1)}, bf16[4,256,128]{2,1,0:T(8,128)(2,1)}, u32[]{:S(2)}) copy-start(bf16[4,256,128]{2,1,0:T(8,128)(2,1)} %get-tuple-element.49) | copy-start | bytes 786436
  104.7 121.7 %copy-start.32 = (f32[64]{0:T(128)}, f32[64]{0:T(128)S(1)}, u32[]{:S(2)}) copy-start(f32[64]{0:T(128)S(1)} %get-tuple-element.101) | copy-start | bytes 772
  202.3 0.9 copy-start.4
  203.2 1.6 copy-start.7
  205.6 22.6 %copy-start.10 = (bf16[4,64,1024]{2,1,0:T(8,128)(2,1)S(1)}, bf16[4,64,1024]{2,1,0:T(8,128)(2,1)}, u32[]{:S(2)}) copy-start(bf16[4,64,1024]{2,1,0:T(8,128)(2,1)} %exchange_11.1) | copy-start | bytes 1572868
  224.8 147.1 %all-gather.8.cloned.1.call-start = ((), (), s32[]{:S(2)}) async-start(), calls=%async_computation.2 | async-start | bytes 7864320 | tf_op jit(solution)/shard_map/all_gather | solution.py:722
  229.6 14.7 %copy-start.6 = (bf16[8,256,256]{2,1,0:T(8,128)(2,1)S(1)}, bf16[8,256,256]{2,1,0:T(8,128)(2,1)}, u32[]{:S(2)}) copy-start(bf16[8,256,256]{2,1,0:T(8,128)(2,1)} %get-tuple-element.46) | copy-start | bytes 3145732
  244.3 8.3 %copy-start.13 = (bf16[1024,256]{1,0:T(8,128)(2,1)S(1)}, bf16[1024,256]{1,0:T(8,128)(2,1)}, u32[]{:S(2)}) copy-start(bf16[1024,256]{1,0:T(8,128)(2,1)} %copy.74) | copy-start | bytes 1572868
  244.3 8.6 %copy-start.17 = (bf16[1024,128]{1,0:T(8,128)(2,1)S(1)}, bf16[1024,128]{1,0:T(8,128)(2,1)}, u32[]{:S(2)}) copy-start(bf16[1024,128]{1,0:T(8,128)(2,1)} %pad.23.clone) | copy-start | bytes 786436
  252.6 3.8 copy-start.3
  252.6 2.3 copy-start.8
  252.6 2.2 copy-start.19
  256.4 36.0 %copy-start.34 = (f32[256]{0:T(256)S(1)}, f32[256]{0:T(256)}, u32[]{:S(2)}) copy-start(f32[256]{0:T(256)} %copy-done.33) | copy-start | bytes 3076
  292.4 4.5 %copy-start.14 = (bf16[8,256,256]{2,1,0:T(8,128)(2,1)S(1)}, bf16[8,256,256]{2,1,0:T(8,128)(2,1)}, u32[]{:S(2)}) copy-start(bf16[8,256,256]{2,1,0:T(8,128)(2,1)} %get-tuple-element.62) | copy-start | bytes 3145732
  296.2 1.2 copy-start.31
  296.2 1.2 copy-start.39
  296.9 2.5 copy-start.35
  296.9 2.5 copy-start.44
  302.9 24.9 %copy-start.21 = (bf16[256,384]{1,0:T(8,128)(2,1)S(1)}, bf16[256,384]{1,0:T(8,128)(2,1)}, u32[]{:S(2)}) copy-start(bf16[256,384]{1,0:T(8,128)(2,1)} %reduce_sum.213) | copy-start | bytes 589828
  324.8 3.8 copy-start.22
  324.8 4.0 %copy-start.16 = (f32[64,1024]{1,0:T(8,128)S(1)}, f32[64,1024]{1,0:T(8,128)}, u32[]{:S(2)}) copy-start(f32[64,1024]{1,0:T(8,128)} %get-tuple-element.81) | copy-start | bytes 786436
  324.8 4.0 %copy-start.36 = (f32[64]{0:T(128)S(1)}, f32[64]{0:T(128)}, u32[]{:S(2)}) copy-start(f32[64]{0:T(128)} %get-tuple-element.78) | copy-start | bytes 772
  324.8 4.0 %copy-start.37 = (f32[64]{0:T(128)S(1)}, f32[64]{0:T(128)}, u32[]{:S(2)}) copy-start(f32[64]{0:T(128)} %get-tuple-element.79) | copy-start | bytes 772
  372.0 2.8 copy-start.2
  374.8 5.1 %copy-start.23 = (bf16[4,64,1024]{2,1,0:T(8,128)(2,1)S(1)}, bf16[4,64,1024]{2,1,0:T(8,128)(2,1)}, u32[]{:S(2)}) copy-start(bf16[4,64,1024]{2,1,0:T(8,128)(2,1)} %get-tuple-element.64) | copy-start | bytes 1572868
  374.8 5.8 %copy-start.24 = (bf16[4,64,1024]{2,1,0:T(8,128)(2,1)S(1)}, bf16[4,64,1024]{2,1,0:T(8,128)(2,1)}, u32[]{:S(2)}) copy-start(bf16[4,64,1024]{2,1,0:T(8,128)(2,1)} %get-tuple-element.69) | copy-start | bytes 1572868
  374.8 6.6 %copy-start.1 = (bf16[256,32,128]{2,1,0:T(8,128)(2,1)S(1)}, bf16[256,32,128]{2,1,0:T(8,128)(2,1)}, u32[]{:S(2)}) copy-start(bf16[256,32,128]{2,1,0:T(8,128)(2,1)} %param.27) | copy-start | bytes 6291460
Sparse Core Ops, SparseCore 0:
  33.0 48.4 all-gather.3
  225.0 40.8 all-gather.5
  292.6 79.3 all-gather.7

commit v9 on v8

--- a/solution.py
+++ b/solution.py
@@ -678,9 +678,8 @@
         (("tp",), "a", expert_grad.reshape(n_tp, 3, depth, ff)),
     )
 
-    pairs = [[2 * i, 2 * i + 1] for i in range(n_ctx // 2)]
     rings = [list(range(start, n_ctx, 2)) for start in range(2)]
-    pieces = lax.all_gather(pieces, "ctx", axis=0, tiled=True, axis_index_groups=pairs)
+    partner = lax.ppermute(pieces, "ctx", [(i, i + 1 - 2 * (i % 2)) for i in range(n_ctx)])
 
     slot_of = jnp.array([offsets.index(k) for k in range(n_ctx)], dtype=jnp.int32)
     back_order = slot_of[lax.rem(jnp.arange(n_ctx, dtype=jnp.int32) + n_ctx - ctx_at, n_ctx)]
@@ -712,14 +711,19 @@
     query_grad_rot, pair_grads = attention_back(
         starts, ctx_at * rows, queries, attended_grad, pairs_all, pair_width
     )
+    partner, pair_grads = lax.optimization_barrier((partner, pair_grads))
+    pieces = jnp.where(
+        lax.rem(ctx_at, 2) == 0,
+        jnp.concatenate([pieces, partner]),
+        jnp.concatenate([partner, pieces]),
+    )
+    expert_all = lax.all_gather(pieces, "ctx", axis=0, tiled=True, axis_index_groups=rings)
     pair_got, mixed_parts, early_got = send(
         7,
         (("ctx",), "a", pair_grads.reshape(n_ctx, rows, 2 * pair_width)),
         (("tp",), "a", mixed_part.reshape(n_tp, quarter, width)),
         (("fsdp",), "a", early.reshape(n_fsdp, depth, -1)),
     )
-    pieces, pair_got = lax.optimization_barrier((pieces, pair_got))
-    expert_all = lax.all_gather(pieces, "ctx", axis=0, tiled=True, axis_index_groups=rings)
     pair_owned = jnp.sum(pair_got.astype(f32), axis=0)
     turned_back = turn(
         jnp.concatenate([query_grad_rot, pair_owned[:, :pair_width]], axis=1),

time: 389 us -> 397 us (1.021)
  starting transfers between devices: 0.12 us -> 4.46 us
  Pallas kernels: 299 us -> 303 us
    ppermute x0 -> x1, starting transfers between devices: none -> 4.38 us  [local(): lax.ppermute(pieces, 'ctx', [(i, i + 1 - 2 * (i % 2)) for i in range(n_ct...]
    pallas_call x10, Pallas kernels: 198 us -> 202 us  [exchange(): pl.pallas_call(functools.partial(exchange_kernel, plan, sizes), out_shape...]
    unnamed x99 -> x101, local copies, waits for them, and re-layouts: 10.2 us -> 10.2 us
  transfers between devices with their start and end apart: 3 -> 3, of which waited for: 1 -> 0; matrix products, arithmetic and copies ran while one was open for 14% -> 13% of each run, Pallas kernels for 45% -> 45%
where the time goes in v9:
time: 397 us; the launch traced here: 396 us
  Pallas kernels  303 us (76%)
  other arithmetic  30.8 us (8%)
  local copies, waits for them, and re-layouts  23.5 us (6%)
  matrix products  19.8 us (5%)
  between operations  15 us (4%)
  starting transfers between devices  4.46 us (1%)
    pallas_call x10, Pallas kernels, exchange(): pl.pallas_call(functools.partial(exchange_kernel, plan, sizes), out_shape...  202 us
    pallas_call x1, Pallas kernels, expert_of_place(): pl.pallas_call(functools.partial(expert_kernel, n, n_fsdp, part), out_sha...  81.9 us
    unnamed x101, local copies, waits for them, and re-layouts  10.2 us
    dot_general x6, matrix products, mm(): return jnp.dot(left, right, preferred_element_type=f32)  9.63 us
    pallas_call x1, Pallas kernels, attention_back(): pl.pallas_call(functools.partial(attention_back_kernel, groups), out_shap...  8.3 us
  transfers between devices with their start and end apart: 3, of which 0 were waited for; matrix products, arithmetic and copies ran while one was open for 13% of the time, Pallas kernels for 45%

profile of v9, /device:TPU:1, one launch (start us, length us, event | category | flops | bytes accessed | tf_op | source)
XLA Modules:
  0.0 396.1 jit_solution(17710681957971269670)
XLA Ops:
  7.3 1.5 copy-done
  9.0 1.5 constant_dynamic-slice_fusion.1
  11.9 1.0 pad_maximum_fusion.refs_2_
  12.9 19.9 %exchange_0.1 = (bf16[4,256,512]{2,1,0:T(8,128)(2,1)}, bf16[4,16,128]{2,1,0:T(8,128)(2,1)}, bf16[4,3,256,128]{3,2,1,0:T(8,128)(2,1)}) custom-call(bf16[256,512]{1,0:T(8,128)(2,1)} %pad_maximum_fusion.4.refs_0_, bf16[16,128]{1,0:T(8,128)(2,1)} %pad.20.refs_1_, bf16[4,3,256,128]{3,2,1,0:T(8,128)(2,1)} %pad_maximum_fusion.refs_2_), custom_call_target="tpu_custom_call" | custom-call | bytes 37027840 | tf_op jit(solution)/shard_map/exchange_0/pallas_call | solution.py:107
  33.9 1.7 fusion.20
  36.2 1.8 fusion.9
  41.8 2.0 convolution_convert_fusion.1
  43.8 41.5 %exchange_1.1 = (bf16[8,256,256]{2,1,0:T(8,128)(2,1)}, bf16[4,256,256]{2,1,0:T(8,128)(2,1)}, bf16[4,16,128]{2,1,0:T(8,128)(2,1)}, bf16[4,256,128]{2,1,0:T(8,128)(2,1)}, bf16[8,128,1024]{2,1,0:T(8,128)(2,1)}) custom-call(bf16[256,256]{1,0:T(8,128)(2,1)} %pad_maximum_fusion.8.refs_0_, bf16[256,256]{1,0:T(8,128)(2,1)} %refs_1_.1, bf16[16,128]{1,0:T(8,128)(2,1)} %pad.21.refs_2_, ...), custom_call_target="tpu_custom_call" | custom-call | bytes 78970880 | tf_op jit(solution)/shard_map/exchange_1/pallas_call | solution.py:107
  86.1 1.2 copy-done.5
  87.3 5.1 %attention.1 = bf16[256,256]{1,0:T(8,128)(2,1)S(1)} custom-call(s32[256,1]{1,0:T(8,128)S(1)} %copy.73.starts_ref, s32[1,1]{1,0:T(1,128)} %bitcast.4.first_ref, bf16[256,256]{1,0:T(8,128)(2,1)S(1)} %slice.124.queries_ref, bf16[2048,256]{1,0:T(8,128)(2,1)S(1)} %bitcast.113), custom_call_target="tpu_custom_call" | custom-call | flops 536870912 | bytes 4194304 | tf_op jit(solution)/shard_map/attention/pallas_call | solution.py:186
  92.4 1.1 convolution_convert_fusion.4
  93.5 9.4 %exchange_2.1 = bf16[4,64,1024]{2,1,0:T(8,128)(2,1)} custom-call(bf16[4,64,1024]{2,1,0:T(8,128)(2,1)} %bitcast.124), custom_call_target="tpu_custom_call" | custom-call | bytes 10485760 | tf_op jit(solution)/shard_map/exchange_2/pallas_call | solution.py:107
  102.9 1.1 convert_reduce_fusion.4
  105.0 8.5 %exchange_11.1 = bf16[4,64,1024]{2,1,0:T(8,128)(2,1)} custom-call(bf16[64,1024]{1,0:T(8,128)(2,1)} %multiply_convert_fusion.2.refs_0_), custom_call_target="tpu_custom_call" | custom-call | bytes 10485760 | tf_op jit(solution)/shard_map/exchange_11/pallas_call | solution.py:107
  113.5 1.3 fusion.49
  116.1 3.1 convolution_convert_fusion.rows_ref
  119.2 81.9 %expert_of_place.1 = (bf16[1024,1024]{1,0:T(8,128)(2,1)S(1)}, bf16[1024,1024]{1,0:T(8,128)(2,1)S(1)}, f32[8,8,128]{2,1,0:T(8,128)S(1)}, bf16[3072,128]{1,0:T(8,128)(2,1)S(1)}) custom-call(bf16[1024,1024]{1,0:T(8,128)(2,1)} %convolution_convert_fusion.rows_ref, f32[8,8,128]{2,1,0:T(8,128)S(1)} %broadcast_in_dim.82.probs_ref, bf16[1024,1024]{1,0:T(8,128)(2,1)} %bitcast.156, ...), custom_call_target="tpu_custom_call" | custom-call | flops 19327352832 | bytes 104857600 | tf_op jit(solution)/shard_map/expert_of_place/pallas_call | solution.py:481
  201.2 0.9 copy-done.4
  202.0 1.6 convolution_convert_fusion.6
  203.6 0.9 fusion.1.refs_1_
  204.4 18.3 %exchange_5.1 = (bf16[4,64,1024]{2,1,0:T(8,128)(2,1)}, f32[4,8,256]{2,1,0:T(8,128)}, bf16[4,3,256,128]{3,2,1,0:T(8,128)(2,1)}) custom-call(bf16[4,64,1024]{2,1,0:T(8,128)(2,1)} %bitcast.138, f32[8,256]{1,0:T(8,128)} %fusion.1.refs_1_, bf16[4,3,256,128]{3,2,1,0:T(8,128)(2,1)} %bitcast.112), custom_call_target="tpu_custom_call" | custom-call | bytes 26869760 | tf_op jit(solution)/shard_map/exchange_5/pallas_call | solution.py:107
  222.7 1.1 convert_reduce_fusion.3
  225.4 4.4 %collective-permute-start = (bf16[4,3,256,128]{3,2,1,0:T(8,128)(2,1)}, bf16[4,3,256,128]{3,2,1,0:T(8,128)(2,1)}, u32[]{:S(2)}, u32[]{:S(2)}) collective-permute-start(bf16[4,3,256,128]{3,2,1,0:T(8,128)(2,1)} %get-tuple-element.58), channel_id=1, source_target_pairs={{0,4},{4,0},{8,12},{12,8},{16,20},{20,16},{24,28},{28,24},{1,5},{5... | collective-permute-start | bytes 2359304 | tf_op jit(solution)/shard_map/ppermute | solution.py:682
  230.4 1.7 multiply_convert_fusion.1
  232.1 21.3 %exchange_6.1 = bf16[4,64,1024]{2,1,0:T(8,128)(2,1)} custom-call(bf16[64,1024]{1,0:T(8,128)(2,1)} %get-tuple-element.80.refs_0_), custom_call_target="tpu_custom_call" | custom-call | bytes 10485760 | tf_op jit(solution)/shard_map/exchange_6/pallas_call | solution.py:107
  253.4 1.3 convolution_convert_fusion.7.grads_ref
  254.8 8.3 %attention_back.1 = (f32[256,256]{1,0:T(8,128)S(1)}, bf16[2048,256]{1,0:T(8,128)(2,1)S(1)}) custom-call(s32[256,1]{1,0:T(8,128)S(1)} %copy.73.starts_ref, s32[1,1]{1,0:T(1,128)} %bitcast.4.first_ref, bf16[256,256]{1,0:T(8,128)(2,1)S(1)} %slice.124.queries_ref, bf16[256,256]{1,0:T(8,128)(2,1)S(1)} %convolution_convert_fusion.7.grads_ref, ...), custom_call_target="tpu_custom_call" | custom-call | flops 1342177280 | bytes 8388608 | tf_op jit(solution)/shard_map/attention_back/pallas_call | solution.py:261
  263.1 1.0 copy-done.3
  264.1 2.8 maximum_select_fusion
  269.5 1.0 copy.74
  270.5 1.4 convolution_convert_fusion.3
  271.9 1.9 pad_maximum_fusion.1.refs_2_
  273.8 1.5 convolution_convert_fusion.5
  275.3 32.0 %exchange_7.1 = (bf16[8,256,256]{2,1,0:T(8,128)(2,1)}, bf16[4,64,1024]{2,1,0:T(8,128)(2,1)}, bf16[4,256,384]{2,1,0:T(8,128)(2,1)}) custom-call(bf16[8,256,256]{2,1,0:T(8,128)(2,1)} %bitcast.111, bf16[4,64,1024]{2,1,0:T(8,128)(2,1)} %bitcast.139, bf16[4,256,384]{2,1,0:T(8,128)(2,1)} %pad_maximum_fusion.1.refs_2_), custom_call_target="tpu_custom_call" | custom-call | bytes 47185920 | tf_op jit(solution)/shard_map/exchange_7/pallas_call | solution.py:107
  307.4 1.5 convert_reduce_fusion
  309.4 2.7 fusion.11
  312.1 2.0 multiply_reduce_fusion
  315.6 1.5 convolution_convert_fusion.2
  317.1 19.4 %exchange_8.1 = (bf16[4,64,1024]{2,1,0:T(8,128)(2,1)}, bf16[4,256,512]{2,1,0:T(8,128)(2,1)}, f32[4,8,256]{2,1,0:T(8,128)}, bf16[4,64,1024]{2,1,0:T(8,128)(2,1)}) custom-call(bf16[4,64,1024]{2,1,0:T(8,128)(2,1)} %bitcast.137, bf16[4,256,512]{2,1,0:T(8,128)(2,1)} %bitcast.128, f32[4,8,256]{2,1,0:T(8,128)} %pad.24.refs_2_, bf16[64,1024]{1,0:T(8,128)(2,1)} %add_convert_fusion.refs_3_), custom_call_target="tpu_custom_call" | custom-call | bytes 42598400 | tf_op jit(solution)/shard_map/exchange_8/pallas_call | solution.py:107
  336.6 1.4 reduce_sum.214.refs_1_
  338.0 1.5 reduce_sum.212
  341.3 21.2 %exchange_9.1 = (bf16[8,32,896]{2,1,0:T(8,128)(2,1)}, f32[32,8,256]{2,1,0:T(8,128)}, bf16[4,64,1024]{2,1,0:T(8,128)(2,1)}) custom-call(bf16[8,32,896]{2,1,0:T(8,128)(2,1)} %bitcast.125, f32[8,256]{1,0:T(8,128)} %reduce_sum.214.refs_1_, bf16[64,1024]{1,0:T(8,128)(2,1)} %subtract_convert_fusion.refs_2_), custom_call_target="tpu_custom_call" | custom-call | bytes 24903680 | tf_op jit(solution)/shard_map/exchange_9/pallas_call | solution.py:107
  362.5 1.0 reduce_sum.217
  363.5 1.7 reduce_sum.218.refs_0_
  365.2 10.7 %exchange_10.1 = bf16[8,32,896]{2,1,0:T(8,128)(2,1)} custom-call(bf16[32,896]{1,0:T(8,128)(2,1)} %reduce_sum.218.refs_0_), custom_call_target="tpu_custom_call" | custom-call | bytes 9175040 | tf_op jit(solution)/shard_map/exchange_10/pallas_call | solution.py:107
  375.9 1.1 bitcast_convert_fusion
  379.8 2.8 copy-done.2
  382.6 5.0 %spread.1 = (f32[8192,128]{1,0:T(8,128)}, f32[8192,128]{1,0:T(8,128)}, f32[8192,128]{1,0:T(8,128)}) custom-call(bf16[32,3,256,128]{3,2,1,0:T(8,128)(2,1)S(1)} %copy-done.2), custom_call_target="tpu_custom_call" | custom-call | tf_op jit(solution)/shard_map/spread/pallas_call | solution.py:132
  (184 shorter events, 22.6 us)
Async XLA Ops:
  7.2 1.6 copy-start
  7.2 3.4 copy-start.41
  7.2 4.0 %copy-start.31 = (bf16[256,128]{1,0:T(8,128)(2,1)S(1)}, bf16[256,128]{1,0:T(8,128)(2,1)}, u32[]{:S(2)}) copy-start(bf16[256,128]{1,0:T(8,128)(2,1)} %param.23) | copy-start | bytes 196612
  7.2 4.0 %copy-start.32 = (bf16[256,128]{1,0:T(8,128)(2,1)S(1)}, bf16[256,128]{1,0:T(8,128)(2,1)}, u32[]{:S(2)}) copy-start(bf16[256,128]{1,0:T(8,128)(2,1)} %param.22) | copy-start | bytes 196612
  7.2 4.0 %copy-start.30 = (bf16[256,256]{1,0:T(8,128)(2,1)S(1)}, bf16[256,256]{1,0:T(8,128)(2,1)}, u32[]{:S(2)}) copy-start(bf16[256,256]{1,0:T(8,128)(2,1)} %param.21) | copy-start | bytes 393220
  7.2 112.0 %all-gather.3.cloned.1.call-start = ((), (), s32[]{:S(2)}) async-start(), calls=%async_computation | async-start | bytes 3932160 | tf_op jit(solution)/shard_map/all_gather | solution.py:595
  10.6 22.4 %copy-start.14 = (bf16[256,1024]{1,0:T(8,128)(2,1)S(1)}, bf16[256,1024]{1,0:T(8,128)(2,1)}, u32[]{:S(2)}) copy-start(bf16[256,1024]{1,0:T(8,128)(2,1)} %param.16) | copy-start | bytes 1572868
  32.9 347.0 %all-gather.5.cloned.1.call-start = ((), (), s32[]{:S(2)}) async-start(), calls=%async_computation.1 | async-start | bytes 7864320 | tf_op jit(solution)/shard_map/all_gather | solution.py:720
  32.9 3.3 copy-start.40
  33.2 2.4 copy-start.35
  33.9 2.1 copy-start.43
  35.9 2.3 copy-start.42
  35.9 3.0 copy-start.34
  35.9 3.9 copy-start.9
  36.2 4.3 %copy-start.44 = (s32[8]{0:T(128)S(1)}, s32[8]{0:T(128)}, u32[]{:S(2)}) copy-start(s32[8]{0:T(128)} %constant.122.clone) | copy-start | bytes 100
  36.2 4.3 %copy-start.33 = (s32[256,8]{0,1:T(8,128)S(1)}, s32[256,8]{0,1:T(8,128)}, u32[]{:S(2)}) copy-start(s32[256,8]{0,1:T(8,128)} %param.19) | copy-start | bytes 24580
  38.0 3.8 copy-start.20
  38.2 65.9 %copy-start.12 = (f32[256,1024]{1,0:T(8,128)}, f32[256,1024]{1,0:T(8,128)S(1)}, u32[]{:S(2)}) copy-start(f32[256,1024]{1,0:T(8,128)S(1)} %convert_element_type.134) | copy-start | bytes 3145732
  41.0 161.0 %copy-start.18 = (pred[1024,256]{1,0:T(32,128)(4,1)}, pred[1024,256]{1,0:T(32,128)(4,1)S(1)}, u32[]{:S(2)}) copy-start(pred[1024,256]{1,0:T(32,128)(4,1)S(1)} %fusion.3) | copy-start | bytes 786436
  86.1 1.2 copy-start.5
  87.3 5.1 %copy-start.16 = (bf16[4,256,256]{2,1,0:T(8,128)(2,1)S(1)}, bf16[4,256,256]{2,1,0:T(8,128)(2,1)}, u32[]{:S(2)}) copy-start(bf16[4,256,256]{2,1,0:T(8,128)(2,1)} %get-tuple-element.47) | copy-start | bytes 1572868
  93.5 20.0 %copy-start.17 = (bf16[4,256,128]{2,1,0:T(8,128)(2,1)S(1)}, bf16[4,256,128]{2,1,0:T(8,128)(2,1)}, u32[]{:S(2)}) copy-start(bf16[4,256,128]{2,1,0:T(8,128)(2,1)} %get-tuple-element.49) | copy-start | bytes 786436
  202.0 1.6 copy-start.7
  225.3 29.5 %copy-start.6 = (bf16[8,256,256]{2,1,0:T(8,128)(2,1)S(1)}, bf16[8,256,256]{2,1,0:T(8,128)(2,1)}, u32[]{:S(2)}) copy-start(bf16[8,256,256]{2,1,0:T(8,128)(2,1)} %get-tuple-element.46) | copy-start | bytes 3145732
  225.4 6.8 %copy-start.28 = (f32[256,32]{0,1:T(8,128)}, f32[256,32]{0,1:T(8,128)S(1)}, u32[]{:S(2)}) copy-start(f32[256,32]{0,1:T(8,128)S(1)} %subtract_multiply_fusion) | copy-start | bytes 98308
  225.4 38.7 %collective-permute-start = (bf16[4,3,256,128]{3,2,1,0:T(8,128)(2,1)}, bf16[4,3,256,128]{3,2,1,0:T(8,128)(2,1)}, u32[]{:S(2)}, u32[]{:S(2)}) collective-permute-start(bf16[4,3,256,128]{3,2,1,0:T(8,128)(2,1)} %get-tuple-element.58), channel_id=1, source_target_pairs={{0,4},{4,0},{8,12},{12,8},{16,20},{20,16},{24,28},{28,24},{1,5},{5... | collective-permute-start | bytes 2359304 | tf_op jit(solution)/shard_map/ppermute | solution.py:682
  254.8 9.3 %copy-start.22 = (bf16[4,3,256,128]{3,2,1,0:T(8,128)(2,1)S(1)}, bf16[4,3,256,128]{3,2,1,0:T(8,128)(2,1)}, u32[]{:S(2)}) copy-start(bf16[4,3,256,128]{3,2,1,0:T(8,128)(2,1)} %get-tuple-element.58) | copy-start | bytes 2359300
  263.1 1.0 copy-start.3
  264.1 2.9 copy-start.36
  264.1 3.5 copy-start.10
  264.1 3.5 copy-start.29
  266.9 2.6 copy-start.11
  268.8 5.0 %copy-start.8 = (bf16[1024,1024]{1,0:T(8,128)(2,1)S(1)}, bf16[1024,1024]{1,0:T(8,128)(2,1)}, u32[]{:S(2)}) copy-start(bf16[1024,1024]{1,0:T(8,128)(2,1)} %copy-done.7) | copy-start | bytes 6291460
  270.5 3.3 copy-start.19
  307.4 1.7 copy-start.21
  307.4 2.0 copy-start.27
  308.9 3.2 copy-start.15
  309.2 2.9 copy-start.45
  309.4 5.4 %copy-start.23 = (bf16[4,64,1024]{2,1,0:T(8,128)(2,1)S(1)}, bf16[4,64,1024]{2,1,0:T(8,128)(2,1)}, u32[]{:S(2)}) copy-start(bf16[4,64,1024]{2,1,0:T(8,128)(2,1)} %get-tuple-element.63) | copy-start | bytes 1572868
  312.1 3.4 copy-start.37
  317.1 23.2 %copy-start.13 = (f32[256,1024]{1,0:T(8,128)S(1)}, f32[256,1024]{1,0:T(8,128)}, u32[]{:S(2)}) copy-start(f32[256,1024]{1,0:T(8,128)} %copy-done.12) | copy-start | bytes 3145732
  336.5 3.7 copy-start.24
  336.6 3.9 copy-start.38
  336.6 3.9 copy-start.39
  379.8 2.8 copy-start.2
  382.6 5.1 %copy-start.25 = (bf16[4,64,1024]{2,1,0:T(8,128)(2,1)S(1)}, bf16[4,64,1024]{2,1,0:T(8,128)(2,1)}, u32[]{:S(2)}) copy-start(bf16[4,64,1024]{2,1,0:T(8,128)(2,1)} %get-tuple-element.64) | copy-start | bytes 1572868
  382.6 5.8 %copy-start.26 = (bf16[4,64,1024]{2,1,0:T(8,128)(2,1)S(1)}, bf16[4,64,1024]{2,1,0:T(8,128)(2,1)}, u32[]{:S(2)}) copy-start(bf16[4,64,1024]{2,1,0:T(8,128)(2,1)} %get-tuple-element.69) | copy-start | bytes 1572868
  382.6 6.6 %copy-start.1 = (bf16[256,32,128]{2,1,0:T(8,128)(2,1)S(1)}, bf16[256,32,128]{2,1,0:T(8,128)(2,1)}, u32[]{:S(2)}) copy-start(bf16[256,32,128]{2,1,0:T(8,128)(2,1)} %param.27) | copy-start | bytes 6291460
  (1 other events, 0.9 us)
Sparse Core Ops, SparseCore 0:
  33.0 48.4 all-gather.2
  267.0 79.5 all-gather.4

commit v10 on v8

--- a/solution.py
+++ b/solution.py
@@ -712,14 +712,16 @@
     query_grad_rot, pair_grads = attention_back(
         starts, ctx_at * rows, queries, attended_grad, pairs_all, pair_width
     )
+    pieces, pair_grads, mixed_part, early = lax.optimization_barrier(
+        (pieces, pair_grads, mixed_part, early)
+    )
+    expert_all = lax.all_gather(pieces, "ctx", axis=0, tiled=True, axis_index_groups=rings)
     pair_got, mixed_parts, early_got = send(
         7,
         (("ctx",), "a", pair_grads.reshape(n_ctx, rows, 2 * pair_width)),
         (("tp",), "a", mixed_part.reshape(n_tp, quarter, width)),
         (("fsdp",), "a", early.reshape(n_fsdp, depth, -1)),
     )
-    pieces, pair_got = lax.optimization_barrier((pieces, pair_got))
-    expert_all = lax.all_gather(pieces, "ctx", axis=0, tiled=True, axis_index_groups=rings)
     pair_owned = jnp.sum(pair_got.astype(f32), axis=0)
     turned_back = turn(
         jnp.concatenate([query_grad_rot, pair_owned[:, :pair_width]], axis=1),

time: 389 us -> 388 us (level)
  Pallas kernels: 299 us -> 287 us
  waiting for transfers between devices: 1.38 us -> 10.4 us
    pallas_call x10, Pallas kernels: 198 us -> 186 us  [exchange(): pl.pallas_call(functools.partial(exchange_kernel, plan, sizes), out_shape...]
    all_gather x1, waiting for transfers between devices: 0.02 us -> 10.4 us  [local(): lax.all_gather(pieces, 'ctx', axis=0, tiled=True, axis_index_groups=pairs)]
    unnamed x99 -> x106, local copies, waits for them, and re-layouts: 10.2 us -> 12.5 us
  transfers between devices with their start and end apart: 3 -> 3, of which waited for: 1 -> 1; matrix products, arithmetic and copies ran while one was open for 14% -> 14% of each run, Pallas kernels for 45% -> 42%
where the time goes in v10:
time: 388 us; the launch traced here: 387 us
  Pallas kernels  287 us (74%)
  other arithmetic  28.9 us (7%)
  local copies, waits for them, and re-layouts  27.2 us (7%)
  matrix products  19.1 us (5%)
  between operations  14.6 us (4%)
  waiting for transfers between devices  10.4 us (3%)
    pallas_call x10, Pallas kernels, exchange(): pl.pallas_call(functools.partial(exchange_kernel, plan, sizes), out_shape...  186 us
    pallas_call x1, Pallas kernels, expert_of_place(): pl.pallas_call(functools.partial(expert_kernel, n, n_fsdp, part), out_sha...  81.9 us
    unnamed x106, local copies, waits for them, and re-layouts  12.5 us
    all_gather x1, waiting for transfers between devices, local(): lax.all_gather(pieces, 'ctx', axis=0, tiled=True, axis_index_groups=pairs)  10.4 us
    dot_general x6, matrix products, mm(): return jnp.dot(left, right, preferred_element_type=f32)  9.78 us
    pallas_call x1, Pallas kernels, attention_back(): pl.pallas_call(functools.partial(attention_back_kernel, groups), out_shap...  8.27 us
  transfers between devices with their start and end apart: 3, of which 1 were waited for; matrix products, arithmetic and copies ran while one was open for 14% of the time, Pallas kernels for 42%

profile of v10, /device:TPU:1, one launch (start us, length us, event | category | flops | bytes accessed | tf_op | source)
XLA Modules:
  0.0 387.0 jit_solution(10875227014503940978)
XLA Ops:
  7.3 1.5 copy-done
  9.0 1.5 constant_dynamic-slice_fusion.1
  11.9 1.0 pad_maximum_fusion.refs_2_
  12.9 19.9 %exchange_0.1 = (bf16[4,256,512]{2,1,0:T(8,128)(2,1)}, bf16[4,16,128]{2,1,0:T(8,128)(2,1)}, bf16[4,3,256,128]{3,2,1,0:T(8,128)(2,1)}) custom-call(bf16[256,512]{1,0:T(8,128)(2,1)} %pad_maximum_fusion.3.refs_0_, bf16[16,128]{1,0:T(8,128)(2,1)} %pad.20.refs_1_, bf16[4,3,256,128]{3,2,1,0:T(8,128)(2,1)} %pad_maximum_fusion.refs_2_), custom_call_target="tpu_custom_call" | custom-call | bytes 37027840 | tf_op jit(solution)/shard_map/exchange_0/pallas_call | solution.py:107
  33.9 1.7 fusion.22
  36.2 1.8 fusion.11
  41.7 2.0 convolution_convert_fusion.1
  43.7 41.5 %exchange_1.1 = (bf16[8,256,256]{2,1,0:T(8,128)(2,1)}, bf16[4,256,256]{2,1,0:T(8,128)(2,1)}, bf16[4,16,128]{2,1,0:T(8,128)(2,1)}, bf16[4,256,128]{2,1,0:T(8,128)(2,1)}, bf16[8,128,1024]{2,1,0:T(8,128)(2,1)}) custom-call(bf16[256,256]{1,0:T(8,128)(2,1)} %pad_maximum_fusion.7.refs_0_, bf16[256,256]{1,0:T(8,128)(2,1)} %refs_1_.1, bf16[16,128]{1,0:T(8,128)(2,1)} %pad.21.refs_2_, ...), custom_call_target="tpu_custom_call" | custom-call | bytes 78970880 | tf_op jit(solution)/shard_map/exchange_1/pallas_call | solution.py:107
  86.0 1.2 copy-done.5
  87.2 5.1 %attention.1 = bf16[256,256]{1,0:T(8,128)(2,1)S(1)} custom-call(s32[256,1]{1,0:T(8,128)S(1)} %copy.64.starts_ref, s32[1,1]{1,0:T(1,128)} %bitcast.4.first_ref, bf16[256,256]{1,0:T(8,128)(2,1)S(1)} %slice.124.queries_ref, bf16[2048,256]{1,0:T(8,128)(2,1)S(1)} %bitcast.108), custom_call_target="tpu_custom_call" | custom-call | flops 536870912 | bytes 4194304 | tf_op jit(solution)/shard_map/attention/pallas_call | solution.py:186
  92.3 1.1 convolution_convert_fusion.4
  93.5 9.4 %exchange_2.1 = bf16[4,64,1024]{2,1,0:T(8,128)(2,1)} custom-call(bf16[4,64,1024]{2,1,0:T(8,128)(2,1)} %bitcast.119), custom_call_target="tpu_custom_call" | custom-call | bytes 10485760 | tf_op jit(solution)/shard_map/exchange_2/pallas_call | solution.py:107
  102.9 1.1 convert_reduce_fusion.4
  105.4 8.5 %exchange_11.1 = bf16[4,64,1024]{2,1,0:T(8,128)(2,1)} custom-call(bf16[64,1024]{1,0:T(8,128)(2,1)} %multiply_convert_fusion.2.refs_0_), custom_call_target="tpu_custom_call" | custom-call | bytes 10485760 | tf_op jit(solution)/shard_map/exchange_11/pallas_call | solution.py:107
  114.0 1.3 fusion.50
  117.7 3.1 convolution_convert_fusion.rows_ref
  120.8 81.9 %expert_of_place.1 = (bf16[1024,1024]{1,0:T(8,128)(2,1)S(1)}, bf16[1024,1024]{1,0:T(8,128)(2,1)S(1)}, f32[8,8,128]{2,1,0:T(8,128)S(1)}, bf16[3072,128]{1,0:T(8,128)(2,1)S(1)}) custom-call(bf16[1024,1024]{1,0:T(8,128)(2,1)} %convolution_convert_fusion.rows_ref, f32[8,8,128]{2,1,0:T(8,128)S(1)} %broadcast_in_dim.82.probs_ref, bf16[1024,1024]{1,0:T(8,128)(2,1)} %bitcast.150, ...), custom_call_target="tpu_custom_call" | custom-call | flops 19327352832 | bytes 104857600 | tf_op jit(solution)/shard_map/expert_of_place/pallas_call | solution.py:481
  202.7 0.9 copy-done.4
  203.6 1.6 convolution_convert_fusion.6
  205.2 0.9 fusion.2.refs_1_
  206.0 18.3 %exchange_5.1 = (bf16[4,64,1024]{2,1,0:T(8,128)(2,1)}, f32[4,8,256]{2,1,0:T(8,128)}, bf16[4,3,256,128]{3,2,1,0:T(8,128)(2,1)}) custom-call(bf16[4,64,1024]{2,1,0:T(8,128)(2,1)} %bitcast.132, f32[8,256]{1,0:T(8,128)} %fusion.2.refs_1_, bf16[4,3,256,128]{3,2,1,0:T(8,128)(2,1)} %bitcast.107), custom_call_target="tpu_custom_call" | custom-call | bytes 26869760 | tf_op jit(solution)/shard_map/exchange_5/pallas_call | solution.py:107
  224.3 1.1 convert_reduce_fusion.3
  227.6 1.5 reshape.372
  230.7 1.6 multiply_reduce_fusion.3
  232.3 1.8 multiply_convert_fusion.1
  234.1 8.5 %exchange_6.1 = bf16[4,64,1024]{2,1,0:T(8,128)(2,1)} custom-call(bf16[64,1024]{1,0:T(8,128)(2,1)} %get-tuple-element.84.refs_0_), custom_call_target="tpu_custom_call" | custom-call | bytes 10485760 | tf_op jit(solution)/shard_map/exchange_6/pallas_call | solution.py:107
  242.6 1.5 convolution_convert_fusion.7.grads_ref
  244.1 8.3 %attention_back.1 = (f32[256,256]{1,0:T(8,128)S(1)}, bf16[2048,256]{1,0:T(8,128)(2,1)S(1)}) custom-call(s32[256,1]{1,0:T(8,128)S(1)} %copy.64.starts_ref, s32[1,1]{1,0:T(1,128)} %bitcast.4.first_ref, bf16[256,256]{1,0:T(8,128)(2,1)S(1)} %slice.124.queries_ref, bf16[256,256]{1,0:T(8,128)(2,1)S(1)} %convolution_convert_fusion.7.grads_ref, ...), custom_call_target="tpu_custom_call" | custom-call | flops 1342177280 | bytes 8388608 | tf_op jit(solution)/shard_map/attention_back/pallas_call | solution.py:261
  252.4 1.0 copy-done.3
  255.0 1.6 convolution_convert_fusion.5
  256.5 10.4 %all-gather.6.cloned.1.call-done = bf16[8,3,256,128]{3,2,1,0:T(8,128)(2,1)} async-done(((bf16[4,3,256,128]{3,2,1,0:T(8,128)(2,1)}), bf16[8,3,256,128]{3,2,1,0:T(8,128)(2,1)}) %all-gather.6.cloned.1.call-update) | async-done | bytes 1572880 | tf_op jit(solution)/shard_map/all_gather | solution.py:683
  268.2 1.2 copy.65
  269.3 27.8 %exchange_7.1 = (bf16[8,256,256]{2,1,0:T(8,128)(2,1)}, bf16[4,64,1024]{2,1,0:T(8,128)(2,1)}, bf16[4,256,384]{2,1,0:T(8,128)(2,1)}) custom-call(bf16[8,256,256]{2,1,0:T(8,128)(2,1)} %bitcast.106, bf16[4,64,1024]{2,1,0:T(8,128)(2,1)} %bitcast.133, bf16[4,256,384]{2,1,0:T(8,128)(2,1)} %bitcast.116), custom_call_target="tpu_custom_call" | custom-call | bytes 47185920 | tf_op jit(solution)/shard_map/exchange_7/pallas_call | solution.py:107
  297.2 1.5 convert_reduce_fusion
  300.3 2.7 fusion.13
  303.0 1.3 multiply_reduce_fusion
  305.7 1.5 convolution_convert_fusion.2
  307.3 22.6 %exchange_8.1 = (bf16[4,64,1024]{2,1,0:T(8,128)(2,1)}, bf16[4,256,512]{2,1,0:T(8,128)(2,1)}, f32[4,8,256]{2,1,0:T(8,128)}, bf16[4,64,1024]{2,1,0:T(8,128)(2,1)}) custom-call(bf16[4,64,1024]{2,1,0:T(8,128)(2,1)} %bitcast.131, bf16[4,256,512]{2,1,0:T(8,128)(2,1)} %bitcast.123, f32[4,8,256]{2,1,0:T(8,128)} %pad.24.refs_2_, bf16[64,1024]{1,0:T(8,128)(2,1)} %add_convert_fusion.refs_3_), custom_call_target="tpu_custom_call" | custom-call | bytes 42598400 | tf_op jit(solution)/shard_map/exchange_8/pallas_call | solution.py:107
  329.9 1.4 reduce_sum.214.refs_1_
  331.3 1.5 reduce_sum.212
  334.6 18.7 %exchange_9.1 = (bf16[8,32,896]{2,1,0:T(8,128)(2,1)}, f32[32,8,256]{2,1,0:T(8,128)}, bf16[4,64,1024]{2,1,0:T(8,128)(2,1)}) custom-call(bf16[8,32,896]{2,1,0:T(8,128)(2,1)} %bitcast.120, f32[8,256]{1,0:T(8,128)} %reduce_sum.214.refs_1_, bf16[64,1024]{1,0:T(8,128)(2,1)} %subtract_convert_fusion.refs_2_), custom_call_target="tpu_custom_call" | custom-call | bytes 24903680 | tf_op jit(solution)/shard_map/exchange_9/pallas_call | solution.py:107
  353.3 1.0 reduce_sum.217
  354.3 1.7 reduce_sum.218.refs_0_
  356.0 11.1 %exchange_10.1 = bf16[8,32,896]{2,1,0:T(8,128)(2,1)} custom-call(bf16[32,896]{1,0:T(8,128)(2,1)} %reduce_sum.218.refs_0_), custom_call_target="tpu_custom_call" | custom-call | bytes 9175040 | tf_op jit(solution)/shard_map/exchange_10/pallas_call | solution.py:107
  367.1 1.1 bitcast_convert_fusion
  370.2 0.8 fusion.45
  371.0 2.8 copy-done.2
  373.8 5.0 %spread.1 = (f32[8192,128]{1,0:T(8,128)}, f32[8192,128]{1,0:T(8,128)}, f32[8192,128]{1,0:T(8,128)}) custom-call(bf16[32,3,256,128]{3,2,1,0:T(8,128)(2,1)S(1)} %copy-done.2), custom_call_target="tpu_custom_call" | custom-call | tf_op jit(solution)/shard_map/spread/pallas_call | solution.py:132
  (188 shorter events, 26.4 us)
Async XLA Ops:
  7.2 1.6 copy-start
  7.2 3.4 copy-start.44
  7.2 4.0 %copy-start.29 = (bf16[256,128]{1,0:T(8,128)(2,1)S(1)}, bf16[256,128]{1,0:T(8,128)(2,1)}, u32[]{:S(2)}) copy-start(bf16[256,128]{1,0:T(8,128)(2,1)} %param.23) | copy-start | bytes 196612
  7.2 4.0 %copy-start.30 = (bf16[256,128]{1,0:T(8,128)(2,1)S(1)}, bf16[256,128]{1,0:T(8,128)(2,1)}, u32[]{:S(2)}) copy-start(bf16[256,128]{1,0:T(8,128)(2,1)} %param.22) | copy-start | bytes 196612
  7.2 4.0 %copy-start.28 = (bf16[256,256]{1,0:T(8,128)(2,1)S(1)}, bf16[256,256]{1,0:T(8,128)(2,1)}, u32[]{:S(2)}) copy-start(bf16[256,256]{1,0:T(8,128)(2,1)} %param.21) | copy-start | bytes 393220
  7.2 113.6 %all-gather.4.cloned.1.call-start = ((), (), s32[]{:S(2)}) async-start(), calls=%async_computation | async-start | bytes 3932160 | tf_op jit(solution)/shard_map/all_gather | solution.py:595
  10.6 22.4 %copy-start.12 = (bf16[256,1024]{1,0:T(8,128)(2,1)S(1)}, bf16[256,1024]{1,0:T(8,128)(2,1)}, u32[]{:S(2)}) copy-start(bf16[256,1024]{1,0:T(8,128)(2,1)} %param.16) | copy-start | bytes 1572868
  32.9 234.0 %all-gather.6.cloned.1.call-start = ((), (), s32[]{:S(2)}) async-start(), calls=%async_computation.1 | async-start | bytes 2359296 | tf_op jit(solution)/shard_map/all_gather | solution.py:683
  32.9 3.3 copy-start.43
  33.1 2.4 copy-start.37
  33.9 2.1 copy-start.46
  35.9 2.3 copy-start.45
  35.9 2.9 copy-start.33
  35.9 3.9 copy-start.9
  36.2 3.4 copy-start.34
  36.2 4.2 %copy-start.47 = (s32[8]{0:T(128)S(1)}, s32[8]{0:T(128)}, u32[]{:S(2)}) copy-start(s32[8]{0:T(128)} %constant.118.clone) | copy-start | bytes 100
  36.2 4.2 %copy-start.31 = (s32[256,8]{0,1:T(8,128)S(1)}, s32[256,8]{0,1:T(8,128)}, u32[]{:S(2)}) copy-start(s32[256,8]{0,1:T(8,128)} %param.19) | copy-start | bytes 24580
  38.0 3.7 copy-start.19
  41.0 162.6 %copy-start.16 = (pred[1024,256]{1,0:T(32,128)(4,1)}, pred[1024,256]{1,0:T(32,128)(4,1)S(1)}, u32[]{:S(2)}) copy-start(pred[1024,256]{1,0:T(32,128)(4,1)S(1)} %fusion.4) | copy-start | bytes 786436
  86.0 1.2 copy-start.5
  87.2 5.1 %copy-start.13 = (bf16[4,256,256]{2,1,0:T(8,128)(2,1)S(1)}, bf16[4,256,256]{2,1,0:T(8,128)(2,1)}, u32[]{:S(2)}) copy-start(bf16[4,256,256]{2,1,0:T(8,128)(2,1)} %get-tuple-element.49) | copy-start | bytes 1572868
  93.5 20.5 %copy-start.14 = (bf16[4,256,128]{2,1,0:T(8,128)(2,1)S(1)}, bf16[4,256,128]{2,1,0:T(8,128)(2,1)}, u32[]{:S(2)}) copy-start(bf16[4,256,128]{2,1,0:T(8,128)(2,1)} %get-tuple-element.51) | copy-start | bytes 786436
  104.7 9.3 %copy-start.36 = (f32[64]{0:T(128)}, f32[64]{0:T(128)S(1)}, u32[]{:S(2)}) copy-start(f32[64]{0:T(128)S(1)} %get-tuple-element.105) | copy-start | bytes 772
  203.6 1.6 copy-start.7
  225.5 145.6 %all-gather.8.cloned.1.call-start = ((), (), s32[]{:S(2)}) async-start(), calls=%async_computation.2 | async-start | bytes 7864320 | tf_op jit(solution)/shard_map/all_gather | solution.py:718
  227.6 16.5 %copy-start.6 = (bf16[8,256,256]{2,1,0:T(8,128)(2,1)S(1)}, bf16[8,256,256]{2,1,0:T(8,128)(2,1)}, u32[]{:S(2)}) copy-start(bf16[8,256,256]{2,1,0:T(8,128)(2,1)} %get-tuple-element.48) | copy-start | bytes 3145732
  230.7 3.4 copy-start.26
  244.1 9.3 %copy-start.10 = (bf16[4,64,1024]{2,1,0:T(8,128)(2,1)S(1)}, bf16[4,64,1024]{2,1,0:T(8,128)(2,1)}, u32[]{:S(2)}) copy-start(bf16[4,64,1024]{2,1,0:T(8,128)(2,1)} %exchange_11.1) | copy-start | bytes 1572868
  244.1 9.3 %copy-start.27 = (f32[256,32]{0,1:T(8,128)S(1)}, f32[256,32]{0,1:T(8,128)}, u32[]{:S(2)}) copy-start(f32[256,32]{0,1:T(8,128)} %copy-done.26) | copy-start | bytes 98308
  244.1 9.6 %copy-start.11 = (bf16[4,64,1024]{2,1,0:T(8,128)(2,1)S(1)}, bf16[4,64,1024]{2,1,0:T(8,128)(2,1)}, u32[]{:S(2)}) copy-start(bf16[4,64,1024]{2,1,0:T(8,128)(2,1)} %exchange_6.1) | copy-start | bytes 1572868
  252.4 1.0 copy-start.3
  253.4 1.6 copy-start.8
  253.4 1.6 copy-start.17
  255.0 12.0 %copy-start.38 = (f32[256]{0:T(256)S(1)}, f32[256]{0:T(256)}, u32[]{:S(2)}) copy-start(f32[256]{0:T(256)} %copy-done.37) | copy-start | bytes 3076
  297.2 2.3 copy-start.20
  297.2 2.6 copy-start.35
  299.4 3.6 copy-start.39
  299.6 3.4 copy-start.48
  300.3 4.6 %copy-start.21 = (bf16[4,64,1024]{2,1,0:T(8,128)(2,1)S(1)}, bf16[4,64,1024]{2,1,0:T(8,128)(2,1)}, u32[]{:S(2)}) copy-start(bf16[4,64,1024]{2,1,0:T(8,128)(2,1)} %get-tuple-element.67) | copy-start | bytes 1572868
  303.0 2.7 copy-start.40
  329.9 3.7 copy-start.22
  329.9 4.0 %copy-start.15 = (f32[64,1024]{1,0:T(8,128)S(1)}, f32[64,1024]{1,0:T(8,128)}, u32[]{:S(2)}) copy-start(f32[64,1024]{1,0:T(8,128)} %get-tuple-element.85) | copy-start | bytes 786436
  329.9 3.9 %copy-start.41 = (f32[64]{0:T(128)S(1)}, f32[64]{0:T(128)}, u32[]{:S(2)}) copy-start(f32[64]{0:T(128)} %get-tuple-element.82) | copy-start | bytes 772
  329.9 3.9 %copy-start.42 = (f32[64]{0:T(128)S(1)}, f32[64]{0:T(128)}, u32[]{:S(2)}) copy-start(f32[64]{0:T(128)} %get-tuple-element.83) | copy-start | bytes 772
  371.0 2.8 copy-start.2
  373.8 5.1 %copy-start.23 = (bf16[4,64,1024]{2,1,0:T(8,128)(2,1)S(1)}, bf16[4,64,1024]{2,1,0:T(8,128)(2,1)}, u32[]{:S(2)}) copy-start(bf16[4,64,1024]{2,1,0:T(8,128)(2,1)} %get-tuple-element.68) | copy-start | bytes 1572868
  373.8 5.8 %copy-start.24 = (bf16[4,64,1024]{2,1,0:T(8,128)(2,1)S(1)}, bf16[4,64,1024]{2,1,0:T(8,128)(2,1)}, u32[]{:S(2)}) copy-start(bf16[4,64,1024]{2,1,0:T(8,128)(2,1)} %get-tuple-element.73) | copy-start | bytes 1572868
  373.8 6.6 %copy-start.1 = (bf16[256,32,128]{2,1,0:T(8,128)(2,1)S(1)}, bf16[256,32,128]{2,1,0:T(8,128)(2,1)}, u32[]{:S(2)}) copy-start(bf16[256,32,128]{2,1,0:T(8,128)(2,1)} %param.27) | copy-start | bytes 6291460
  (4 other events, 3.0 us)
Sparse Core Ops, SparseCore 0:
  33.0 48.4 all-gather.3
  225.6 41.2 all-gather.5
  268.6 80.0 all-gather.7
